TPU v7x, 32 devices: a whole 2x2x4 slice. The times are simulated.
32 devices in a mesh: rep: 4 (over z), blk: 8 (over y, x, core).
Axes of the slice: x: 2, y: 2, z: 4, core: 2. Of those that a mesh axis runs over, the one named last changes fastest.
Arguments:
- feats: bfloat16 [4096, 256], P(('blk', 'rep')), may hold values from -6 to 6
- weight: bfloat16 [256, 256], replicated, may hold values from -0.375 to 0.375
- cotangent: bfloat16 [4096, 256], P(('blk', 'rep')), may hold values from -6 to 6
- block_vals: bfloat16 [8, 4, 2, 3, 128, 128], P('blk', 'rep'), may hold values from -0.109375 to 0.109375
- block_rows: int32 [8, 4, 2, 3], P('blk', 'rep'), may hold values from 0 to 3
- block_cols: int32 [8, 4, 2, 3], P('blk', 'rep'), may hold values from 0 to 3
- step_counts: int32 [8, 4, 2], P('blk', 'rep'), may hold values from 0 to 3, as said below
Outputs:
- out_rows: bfloat16 [4096, 256], P(('blk', 'rep'))
- grad_weight: float32 [256, 256], replicated
- grad_feats: float32 [4096, 256], P(('blk', 'rep'))
Inputs may be any that keep to these rules, and one draw needn't show every extreme that they name: `step_counts`: every list (g, m) reaches 3 live slots at one or more of its j.
All inputs are finite; a program needn't handle non-finite values.
Results may differ from a plain program's by a relative error of at most 0.0055.
Values may be sent and summed in bfloat16 or wider, within the bound.
No kernel may reach another device: no remote copies, remote signals or barrier semaphores. Data moves between devices by JAX's collectives and lax.ppermute only.
A program may use at most 64 MiB of HBM per device.

v0:
```python
import jax
import jax.numpy as jnp
from jax import lax
from jax.sharding import PartitionSpec as P


def shifted_2(array, axis, by):
    peers = lax.axis_size(axis)
    return lax.ppermute(array, axis, [(i, (i + by) % peers) for i in range(peers)])


def pick_rows(index, live_mask, count):
    selector = (index[:, None] == jnp.arange(count, dtype=jnp.int32)[None, :]).astype(jnp.float32)
    return selector * live_mask[:, None]


def per_device(feats, weight, cotangent, block_vals, block_rows, block_cols, step_counts):
    rep_size = lax.axis_size("rep")
    cycle_size = lax.axis_size("blk")
    cycle_steps = cycle_size // rep_size
    member = lax.axis_index("rep")
    adjacency = block_vals[0, 0]
    row_index = block_rows[0, 0]
    col_index = block_cols[0, 0]
    live_counts = step_counts[0, 0]
    slots = adjacency.shape[1]
    block_size = adjacency.shape[2]
    feat_width = feats.shape[1]
    cycle_blocks = feats.shape[0] * rep_size // block_size
    slot_ids = jnp.arange(slots, dtype=jnp.int32)
    bit_count = (rep_size - 1).bit_length()

    def live_at(offset):
        return (slot_ids < live_counts[offset]).astype(jnp.float32)

    gathered = lax.all_gather(feats, "rep", axis=0, tiled=True)
    current = gathered
    for bit_pos in range(bit_count):
        shifted = shifted_2(current, "blk", cycle_steps << bit_pos)
        current = jnp.where((member >> bit_pos) % 2 == 1, shifted, current)
    partial_value = jnp.zeros((cycle_blocks, block_size, feat_width), jnp.float32)
    for step_index in range(cycle_steps):
        forward_operand = current.reshape(cycle_blocks, block_size, feat_width)[
            col_index[step_index]
        ]
        forward_products = jnp.einsum(
            "kij,kjf->kif",
            adjacency[step_index],
            forward_operand,
            preferred_element_type=jnp.float32,
        )
        forward_selector = pick_rows(row_index[step_index], live_at(step_index), cycle_blocks)
        partial_value = partial_value + jnp.einsum(
            "kr,kif->rif", forward_selector, forward_products, precision=lax.Precision.HIGHEST
        )
        if step_index + 1 < cycle_steps:
            current = shifted_2(current, "blk", 1)
    aggregate = lax.psum_scatter(
        partial_value.reshape(-1, feat_width), "rep", scatter_dimension=0, tiled=True
    )
    agg_low = aggregate.astype(jnp.bfloat16)
    pre = jnp.dot(agg_low, weight, preferred_element_type=jnp.float32)
    sigma = jax.nn.sigmoid(pre)
    out_rows = (pre * sigma).astype(jnp.bfloat16)
    slope = sigma * (1.0 + pre * (1.0 - sigma))
    dpre = (cotangent.astype(jnp.float32) * slope).astype(jnp.bfloat16)
    weight_part = jnp.einsum("nf,ng->fg", agg_low, dpre, preferred_element_type=jnp.float32)
    grad_weight = lax.psum(weight_part, ("rep", "blk"))
    dagg = jnp.einsum("ng,fg->nf", dpre, weight, preferred_element_type=jnp.float32).astype(
        jnp.bfloat16
    )
    grad_cycle = lax.all_gather(dagg, "rep", axis=0, tiled=True).reshape(
        cycle_blocks, block_size, feat_width
    )
    empty = jnp.zeros((cycle_blocks, block_size, feat_width), jnp.float32)
    accumulator = empty
    for step_index in range(cycle_steps):
        backward_offset = cycle_steps - 1 - step_index
        operand = grad_cycle[row_index[backward_offset]]
        products = jnp.einsum(
            "kji,kjf->kif", adjacency[backward_offset], operand, preferred_element_type=jnp.float32
        )
        selector = pick_rows(col_index[backward_offset], live_at(backward_offset), cycle_blocks)
        accumulator = accumulator + jnp.einsum(
            "kr,kif->rif", selector, products, precision=lax.Precision.HIGHEST
        )
        if step_index + 1 < cycle_steps:
            accumulator = shifted_2(accumulator.astype(jnp.bfloat16), "blk", -1).astype(
                accumulator.dtype
            )
    for bit_pos in range(bit_count):
        shifted = shifted_2(
            accumulator.astype(jnp.bfloat16), "blk", -(cycle_steps << bit_pos)
        ).astype(accumulator.dtype)
        accumulator = jnp.where((member >> bit_pos) % 2 == 1, shifted, accumulator)
    grad_feats = lax.psum_scatter(
        accumulator.reshape(-1, feat_width), "rep", scatter_dimension=0, tiled=True
    )
    return (out_rows, grad_weight, grad_feats)


def solution(mesh):
    return jax.shard_map(
        per_device,
        mesh=mesh,
        in_specs=(
            P(("blk", "rep"), None),
            P(),
            P(("blk", "rep"), None),
            P("blk", "rep", None, None, None, None),
            P("blk", "rep", None, None),
            P("blk", "rep", None, None),
            P("blk", "rep", None),
        ),
        out_specs=(P(("blk", "rep"), None), P(), P(("blk", "rep"), None)),
        check_vma=False,
    )
```

profile of v0, /device:TPU:0, one launch (start us, length us, event | category | flops | bytes accessed | tf_op | source)
XLA Modules:
  0.0 259.4 jit_solution(11412845454726279309)
XLA Ops:
  7.2 16.0 %all_gather.6 = bf16[512,256]{1,0:T(8,128)(2,1)S(1)} all-gather(bf16[128,256]{1,0:T(8,128)(2,1)} %param.7), channel_id=1, replica_groups=mesh['rep'=4,'blk'=8] {'rep'}, dimensions={0}, use_global_device_ids=true | all-gather | bytes 327680 | tf_op jit(solution)/shard_map/all_gather | solution.py:36
  23.2 1.5 collective-permute-start
  24.7 0.6 fusion.52
  25.3 0.7 compare_convert_fusion
  26.0 4.5 %collective-permute-done = bf16[512,256]{1,0:T(8,128)(2,1)S(1)} collective-permute-done((bf16[512,256]{1,0:T(8,128)(2,1)S(1)}, bf16[512,256]{1,0:T(8,128)(2,1)S(1)}, u32[]{:S(2)}, u32[]{:S(2)}) %collective-permute-start) | collective-permute-done | bytes 262176 | tf_op jit(solution)/shard_map/ppermute | solution.py:9
  30.5 1.6 collective-permute-start.1
  32.1 0.6 compare_convert_fusion.1
  32.8 0.7 copy-done.2
  33.5 3.5 %collective-permute-done.1 = bf16[512,256]{1,0:T(8,128)(2,1)S(1)} collective-permute-done((bf16[512,256]{1,0:T(8,128)(2,1)S(1)}, bf16[512,256]{1,0:T(8,128)(2,1)S(1)}, u32[]{:S(2)}, u32[]{:S(2)}) %collective-permute-start.1) | collective-permute-done | bytes 262176 | tf_op jit(solution)/shard_map/ppermute | solution.py:9
  37.0 0.1 collective-permute-start.2
  37.1 0.6 gather_fusion
  37.7 0.4 copy-done.1
  38.0 0.3 fusion.14
  38.3 0.2 copy.12
  38.5 1.0 fusion.4
  39.5 4.2 %collective-permute-done.2 = bf16[512,256]{1,0:T(8,128)(2,1)S(1)} collective-permute-done((bf16[512,256]{1,0:T(8,128)(2,1)S(1)}, bf16[512,256]{1,0:T(8,128)(2,1)S(1)}, u32[]{:S(2)}, u32[]{:S(2)}) %collective-permute-start.2) | collective-permute-done | bytes 262176 | tf_op jit(solution)/shard_map/ppermute | solution.py:9
  43.8 0.6 gather_fusion.1
  44.3 0.3 fusion.10
  44.6 0.2 copy.13
  44.8 1.0 convolution_add_fusion
  45.9 0.9 copy.10
  46.8 0.0 all-reduce.2.cloned.1.call-start
  46.9 22.4 %reduce-scatter.3.cloned.1.call-done = f32[128,256]{1,0:T(8,128)} async-done(((f32[512,256]{1,0:T(8,128)}), f32[128,256]{1,0:T(8,128)}) %reduce-scatter.3.cloned.1.call-update) | async-done | bytes 131088 | tf_op jit(solution)/shard_map/reduce_scatter | solution.py:58
  69.3 1.7 multiply_convert_fusion.1
  71.0 0.2 convolution_convert_fusion.1
  71.2 14.1 %all_gather.7 = bf16[512,256]{1,0:T(8,128)(2,1)S(1)} all-gather(bf16[128,256]{1,0:T(8,128)(2,1)S(1)} %convolution_convert_fusion.1), channel_id=1, replica_groups=mesh['rep'=4,'blk'=8] {'rep'}, dimensions={0}, use_global_device_ids=true | all-gather | bytes 327680 | tf_op jit(solution)/shard_map/all_gather | solution.py:72
  85.3 0.6 gather_fusion.2
  85.9 0.3 fusion.8
  86.1 0.2 copy.14
  86.4 1.0 convolution_convert_fusion
  87.4 0.1 collective-permute-start.3
  87.4 0.6 gather_fusion.3
  88.0 0.3 fusion.12
  88.3 0.2 copy.15
  88.5 2.8 %collective-permute-done.3 = bf16[4,128,256]{2,0,1:T(4,128)(2,1)S(1)} collective-permute-done((bf16[4,128,256]{2,0,1:T(4,128)(2,1)S(1)}, bf16[4,128,256]{2,0,1:T(4,128)(2,1)S(1)}, u32[]{:S(2)}, u32[]{:S(2)}) %collective-permute-start.3) | collective-permute-done | bytes 262176 | tf_op jit(solution)/shard_map/ppermute | solution.py:9
  91.3 1.1 fusion.6
  92.4 2.4 collective-permute-start.4
  94.8 6.6 %collective-permute-done.4 = bf16[4,128,256]{2,0,1:T(4,128)(2,1)S(1)} collective-permute-done((bf16[4,128,256]{2,0,1:T(4,128)(2,1)S(1)}, bf16[4,128,256]{2,0,1:T(4,128)(2,1)S(1)}, u32[]{:S(2)}, u32[]{:S(2)}) %collective-permute-start.4) | collective-permute-done | bytes 262176 | tf_op jit(solution)/shard_map/ppermute | solution.py:9
  101.4 0.2 fusion.7
  101.6 1.0 collective-permute-start.5
  102.6 0.9 fusion.20
  103.5 0.0 reduce-scatter.5.cloned.1.call-start
  103.6 6.4 %collective-permute-done.5 = bf16[4,128,256]{2,0,1:T(4,128)(2,1)S(1)} collective-permute-done((bf16[4,128,256]{2,0,1:T(4,128)(2,1)S(1)}, bf16[4,128,256]{2,0,1:T(4,128)(2,1)S(1)}, u32[]{:S(2)}, u32[]{:S(2)}) %collective-permute-start.5) | collective-permute-done | bytes 262176 | tf_op jit(solution)/shard_map/ppermute | solution.py:9
  109.9 0.1 convert_select_fusion
  110.0 0.9 copy.11
  110.9 116.7 %all-reduce.2.cloned.1.call-done = f32[256,256]{1,0:T(8,128)} async-done(((f32[256,256]{1,0:T(8,128)}), f32[256,256]{1,0:T(8,128)}) %all-reduce.2.cloned.1.call-update) | async-done | bytes 262160 | tf_op jit(solution)/shard_map/psum | solution.py:68
  227.6 23.6 %reduce-scatter.5.cloned.1.call-done = f32[128,256]{1,0:T(8,128)} async-done(((f32[512,256]{1,0:T(8,128)}), f32[128,256]{1,0:T(8,128)}) %reduce-scatter.5.cloned.1.call-update) | async-done | bytes 131088 | tf_op jit(solution)/shard_map/reduce_scatter | solution.py:96
  251.2 1.7 copy.17
  (25 shorter events, 0.2 us)
Async XLA Ops:
  7.2 62.1 %copy-start = (bf16[256,256]{1,0:T(8,128)(2,1)S(1)}, bf16[256,256]{1,0:T(8,128)(2,1)}, u32[]{:S(2)}) copy-start(bf16[256,256]{1,0:T(8,128)(2,1)} %param.8) | copy-start | bytes 393220
  7.2 17.5 %copy-start.4 = (s32[1,1,2]{2,1,0:T(1,128)S(1)}, s32[1,1,2]{2,1,0:T(1,128)}, u32[]{:S(2)}) copy-start(s32[1,1,2]{2,1,0:T(1,128)} %param.13) | copy-start | bytes 28
  7.2 62.1 %reduce-scatter.3.cloned.1.call-start = ((), (), s32[]{:S(2)}) async-start(), calls=%async_computation.2 | async-start | bytes 655360 | tf_op jit(solution)/shard_map/reduce_scatter | solution.py:58
  23.2 2.1 copy-start.3
  23.2 7.3 %collective-permute-start = (bf16[512,256]{1,0:T(8,128)(2,1)S(1)}, bf16[512,256]{1,0:T(8,128)(2,1)S(1)}, u32[]{:S(2)}, u32[]{:S(2)}) collective-permute-start(bf16[512,256]{1,0:T(8,128)(2,1)S(1)} %all_gather.6), channel_id=1, source_target_pairs={{0,2},{1,3},{2,4},{3,5},{4,6},{5,7},{6,0},{7,1},{8,10},{9,11},{10,... | collective-permute-start | bytes 786440 | tf_op jit(solution)/shard_map/ppermute | solution.py:9
  30.5 6.4 %collective-permute-start.1 = (bf16[512,256]{1,0:T(8,128)(2,1)S(1)}, bf16[512,256]{1,0:T(8,128)(2,1)S(1)}, u32[]{:S(2)}, u32[]{:S(2)}) collective-permute-start(bf16[512,256]{1,0:T(8,128)(2,1)S(1)} %broadcast_select_fusion), channel_id=1, source_target_pairs={{0,4},{1,5},{2,6},{3,7},{4,0},{5,1},{6,2},{7,3},{8,12},{9,13},{10,... | collective-permute-start | bytes 786440 | tf_op jit(solution)/shard_map/ppermute | solution.py:9
  32.8 0.7 copy-start.2
  37.0 6.7 %collective-permute-start.2 = (bf16[512,256]{1,0:T(8,128)(2,1)S(1)}, bf16[512,256]{1,0:T(8,128)(2,1)S(1)}, u32[]{:S(2)}, u32[]{:S(2)}) collective-permute-start(bf16[512,256]{1,0:T(8,128)(2,1)S(1)} %broadcast_select_fusion.1), channel_id=1, source_target_pairs={{0,1},{1,2},{2,3},{3,4},{4,5},{5,6},{6,7},{7,0},{8,9},{9,10},{10,1... | collective-permute-start | bytes 786440 | tf_op jit(solution)/shard_map/ppermute | solution.py:9
  37.1 0.9 copy-start.1
  46.8 180.8 %all-reduce.2.cloned.1.call-start = ((), (), s32[]{:S(2)}) async-start(), calls=%async_computation.3 | async-start | bytes 524288 | tf_op jit(solution)/shard_map/psum | solution.py:68
  46.9 24.1 %copy-start.6 = (bf16[128,256]{1,0:T(8,128)(2,1)S(1)}, bf16[128,256]{1,0:T(8,128)(2,1)}, u32[]{:S(2)}) copy-start(bf16[128,256]{1,0:T(8,128)(2,1)} %param.9) | copy-start | bytes 196612
  87.4 3.9 %collective-permute-start.3 = (bf16[4,128,256]{2,0,1:T(4,128)(2,1)S(1)}, bf16[4,128,256]{2,0,1:T(4,128)(2,1)S(1)}, u32[]{:S(2)}, u32[]{:S(2)}) collective-permute-start(bf16[4,128,256]{2,0,1:T(4,128)(2,1)S(1)} %convolution_convert_fusion), channel_id=1, source_target_pairs={{0,7},{1,0},{2,1},{3,2},{4,3},{5,4},{6,5},{7,6},{8,15},{9,8},{10,9... | collective-permute-start | bytes 786440 | tf_op jit(solution)/shard_map/ppermute | solution.py:9
  92.4 9.0 %collective-permute-start.4 = (bf16[4,128,256]{2,0,1:T(4,128)(2,1)S(1)}, bf16[4,128,256]{2,0,1:T(4,128)(2,1)S(1)}, u32[]{:S(2)}, u32[]{:S(2)}) collective-permute-start(bf16[4,128,256]{2,0,1:T(4,128)(2,1)S(1)} %get-tuple-element.15), channel_id=1, source_target_pairs={{0,6},{1,7},{2,0},{3,1},{4,2},{5,3},{6,4},{7,5},{8,14},{9,15},{10,... | collective-permute-start | bytes 786440 | tf_op jit(solution)/shard_map/ppermute | solution.py:9
  101.4 1.2 copy-start.5
  101.6 8.3 %collective-permute-start.5 = (bf16[4,128,256]{2,0,1:T(4,128)(2,1)S(1)}, bf16[4,128,256]{2,0,1:T(4,128)(2,1)S(1)}, u32[]{:S(2)}, u32[]{:S(2)}) collective-permute-start(bf16[4,128,256]{2,0,1:T(4,128)(2,1)S(1)} %fusion.7), channel_id=1, source_target_pairs={{0,4},{1,5},{2,6},{3,7},{4,0},{5,1},{6,2},{7,3},{8,12},{9,13},{10,... | collective-permute-start | bytes 786440 | tf_op jit(solution)/shard_map/ppermute | solution.py:9
  103.5 147.7 %reduce-scatter.5.cloned.1.call-start = ((), (), s32[]{:S(2)}) async-start(), calls=%async_computation.4 | async-start | bytes 655360 | tf_op jit(solution)/shard_map/reduce_scatter | solution.py:96
Sparse Core Ops, SparseCore 0:
  46.9 22.3 reduce-scatter.2
  103.6 123.9 all-reduce.1
  230.5 20.6 reduce-scatter.4
where the time goes:
time: 260 us; the launch traced here: 259 us
  waiting for transfers between devices  191 us (73%)
  blocking collectives  30.1 us (12%)
  between operations  14 us (5%)
  local copies, waits for them, and re-layouts  8.28 us (3%)
  matrix products  7.97 us (3%)
  starting transfers between devices  6.66 us (3%)
    psum x1, waiting for transfers between devices, per_device(): grad_weight = lax.psum(weight_part, ('rep', 'blk'))  117 us
    ppermute x6, waiting for transfers between devices, shifted_2(): lax.ppermute(array, axis, [(i, (i + by) % peers) for i in range(peers)])  28 us
    reduce_scatter x1, waiting for transfers between devices, per_device(): lax.psum_scatter(accumulator.reshape(-1, feat_width), 'rep', scatter_dime...  23.6 us
    reduce_scatter x1, waiting for transfers between devices, per_device(): lax.psum_scatter(partial_value.reshape(-1, feat_width), 'rep', scatter_di...  22.4 us
    all_gather x1, blocking collectives, per_device(): gathered = lax.all_gather(feats, 'rep', axis=0, tiled=True)  16 us
    all_gather x1, blocking collectives, per_device(): lax.all_gather(dagg, 'rep', axis=0, tiled=True)  14.1 us
    ppermute x6, starting transfers between devices, shifted_2(): lax.ppermute(array, axis, [(i, (i + by) % peers) for i in range(peers)])  6.54 us
  transfers between devices with their start and end apart: 9, of which 9 were waited for; matrix products, arithmetic and copies ran while one was open for 3% of the time, Pallas kernels for 0%

commit v1 on v0

v1 whole, which is shorter than its diff:
```python
import functools

import jax
import jax.numpy as jnp
from jax import lax
from jax.experimental import pallas as pl
from jax.experimental.pallas import tpu as pltpu
from jax.sharding import PartitionSpec as P

F32 = jnp.float32
BF16 = jnp.bfloat16
VMEM = pl.BlockSpec(memory_space=pltpu.VMEM)
SMEM = pl.BlockSpec(memory_space=pltpu.SMEM)


def shift(array, axis, by):
    peers = lax.axis_size(axis)
    return lax.ppermute(array, axis, [(i, (i + by) % peers) for i in range(peers)])


def call(body, outs, in_specs, scratch=(), flops=0, moved=0):
    return pl.pallas_call(
        body,
        out_shape=outs,
        in_specs=in_specs,
        out_specs=jax.tree.map(lambda _: VMEM, outs),
        scratch_shapes=list(scratch),
        compiler_params=pltpu.CompilerParams(vmem_limit_bytes=48 * 1024 * 1024),
        cost_estimate=pl.CostEstimate(flops=flops, bytes_accessed=moved, transcendentals=0),
    )


def member_and(by, reps):
    return lax.rem(lax.axis_index("rep") + by, reps)


def split_features(reps, width, feats, *rest):
    outs, turned = rest[:-1], rest[-1]
    turned[...] = feats[...].astype(F32).T.astype(BF16).reshape(turned.shape)
    for t in range(reps):
        outs[t][...] = turned[member_and(t, reps)]


def slot_of(index, lists, cap, j, c):
    k = j * cap + c
    row = index[k]
    col = index[lists * cap + k]
    live = c < index[2 * lists * cap + j]
    return row, col, live


def aggregate(reps, lists, cap, *refs):
    groups = reps * lists
    index = refs[:reps]
    blocks = refs[reps : 2 * reps]
    parts = refs[2 * reps : 2 * reps + groups]
    outs = refs[2 * reps + groups : 3 * reps + groups]
    held, total = refs[3 * reps + groups :]
    for s in range(groups):
        held[s] = parts[s][...]
    total[...] = jnp.zeros_like(total)
    for t in range(reps):
        origin = member_and(reps - t, reps)
        for j in range(lists):
            s = origin * lists + j
            for c in range(cap):
                row, col, live = slot_of(index[t], lists, cap, j, c)
                place = member_and(reps - col, reps)
                product = lax.dot_general(
                    held[s, place],
                    blocks[t][j * cap + c],
                    (((1,), (1,)), ((), ())),
                    preferred_element_type=F32,
                )
                total[row] += jnp.where(live, product, 0.0)
    for t in range(reps):
        outs[t][...] = total[member_and(t, reps)].astype(BF16)


def dense_layer(reps, *refs):
    chunks = refs[:reps]
    weight, cotangent, out, agg_out, dpre_out = refs[reps : reps + 5]
    dagg_outs = refs[reps + 5 : 2 * reps + 5]
    agg, dagg = refs[2 * reps + 5 :]
    for t in range(reps):
        agg[member_and(reps - t, reps)] = chunks[t][...]
    turned = agg[...].reshape(-1, agg.shape[2])
    agg_out[...] = turned
    pre = lax.dot_general(
        turned, weight[...], (((0,), (0,)), ((), ())), preferred_element_type=F32
    )
    sigma = jax.nn.sigmoid(pre)
    out[...] = (pre * sigma).astype(BF16)
    slope = sigma * (1.0 + pre * (1.0 - sigma))
    dpre = (cotangent[...].astype(F32) * slope).astype(BF16)
    dpre_out[...] = dpre
    dagg[...] = (
        lax.dot_general(
            weight[...], dpre, (((1,), (1,)), ((), ())), preferred_element_type=F32
        )
        .astype(BF16)
        .reshape(dagg.shape)
    )
    for t in range(reps):
        dagg_outs[t][...] = dagg[member_and(t, reps)]


def weight_terms(reps, agg, dpre, *rest):
    outs, terms = rest[:-1], rest[-1]
    product = jnp.dot(agg[...], dpre[...], preferred_element_type=F32)
    terms[...] = product.astype(BF16).reshape(terms.shape)
    for t in range(reps):
        outs[t][...] = terms[member_and(t, reps)]


def feature_grads(reps, lists, cap, *refs):
    groups = reps * lists
    index = refs[:reps]
    blocks = refs[reps : 2 * reps]
    chunks = refs[2 * reps : 3 * reps]
    outs = refs[3 * reps : 3 * reps + groups]
    dagg, total = refs[3 * reps + groups :]
    for t in range(reps):
        dagg[member_and(reps - t, reps)] = chunks[t][...]
    total[...] = jnp.zeros_like(total)
    for t in range(reps):
        origin = member_and(reps - t, reps)
        for j in range(lists):
            s = origin * lists + j
            for c in range(cap):
                row, col, live = slot_of(index[t], lists, cap, j, c)
                product = jnp.dot(
                    dagg[row], blocks[t][j * cap + c], preferred_element_type=F32
                )
                total[s, col] += jnp.where(live, product, 0.0)
    for s in range(groups):
        outs[s][...] = total[s].astype(BF16)


def sum_all(*refs):
    out = refs[-1]
    total = refs[0][...].astype(F32)
    for ref in refs[1:-1]:
        total += ref[...].astype(F32)
    out[...] = total.astype(out.dtype)


def sum_groups(reps, groups, *refs):
    parts = refs[:groups]
    outs = refs[groups : groups + reps]
    for t in range(reps):
        place = member_and(t, reps)
        total = parts[0][place].astype(F32)
        for part in parts[1:]:
            total += part[place].astype(F32)
        outs[t][...] = total.astype(BF16)


def join_rows(reps, *refs):
    chunks, out, joined = refs[:reps], refs[reps], refs[reps + 1]
    for t in range(reps):
        joined[member_and(reps - t, reps)] = chunks[t][...].astype(F32)
    out[...] = joined[...].reshape(-1, joined.shape[2]).T


def join_weight(reps, *refs):
    chunks, out = refs[:reps], refs[reps]
    part = out.shape[0] // reps
    for t in range(reps):
        start = pl.multiple_of(member_and(reps - t, reps) * part, part)
        out[pl.ds(start, part), :] = chunks[t][...].astype(F32)


def per_device(feats, weight, cotangent, block_vals, block_rows, block_cols, step_counts):
    reps = lax.axis_size("rep")
    groups = lax.axis_size("blk")
    lists, cap, block = block_vals.shape[2:5]
    nodes, width = feats.shape
    part = width // reps
    like = jax.ShapeDtypeStruct
    chunk = like((part, block), BF16)
    wchunk = like((part, width), BF16)
    group = like((reps, part, block), BF16)

    def over_rep(arrays):
        return [arrays[0]] + [shift(arrays[t], "rep", t) for t in range(1, reps)]

    index = jnp.concatenate(
        [block_rows.reshape(-1), block_cols.reshape(-1), step_counts.reshape(-1)]
    )
    blocks = block_vals.reshape(lists * cap, block, block)

    quarters = call(
        functools.partial(split_features, reps, width),
        [chunk] * reps,
        [VMEM],
        [pltpu.VMEM((reps, part, block), BF16)],
        moved=2 * nodes * width * 2,
    )(feats)
    quarters = over_rep(quarters)
    all_index = over_rep([index] * reps)
    all_blocks = over_rep([blocks] * reps)
    mine = jnp.stack(quarters)
    feats_parts = [mine] + [shift(mine, "blk", s) for s in range(1, groups)]
    slots = groups * cap
    slot_flops = 2 * slots * part * block * block
    slot_bytes = 2 * (slots * block * block + groups * reps * part * block)

    chunks = call(
        functools.partial(aggregate, reps, lists, cap),
        [chunk] * reps,
        [SMEM] * reps + [VMEM] * (reps + groups),
        [
            pltpu.VMEM((groups, reps, part, block), BF16),
            pltpu.VMEM((reps, part, block), F32),
        ],
        flops=slot_flops,
        moved=slot_bytes,
    )(*all_index, *all_blocks, *feats_parts)
    chunks = over_rep(chunks)

    out_rows, agg, dpre, *dagg = call(
        functools.partial(dense_layer, reps),
        [
            like((nodes, width), BF16),
            like((width, nodes), BF16),
            like((nodes, width), BF16),
        ]
        + [chunk] * reps,
        [VMEM] * (reps + 2),
        [pltpu.VMEM((reps, part, block), BF16)] * 2,
        flops=4 * nodes * width * width,
        moved=14 * nodes * width,
    )(*chunks, weight, cotangent)
    dagg = over_rep(dagg)

    terms = call(
        functools.partial(weight_terms, reps),
        [wchunk] * reps,
        [VMEM] * 2,
        [pltpu.VMEM((reps, part, width), BF16)],
        flops=2 * nodes * width * width,
        moved=8 * nodes * width,
    )(agg, dpre)
    terms = over_rep(terms)

    grads = call(
        functools.partial(feature_grads, reps, lists, cap),
        [group] * groups,
        [SMEM] * reps + [VMEM] * (2 * reps),
        [
            pltpu.VMEM((reps, part, block), BF16),
            pltpu.VMEM((groups, reps, part, block), F32),
        ],
        flops=slot_flops,
        moved=slot_bytes,
    )(*all_index, *all_blocks, *dagg)
    grads = [grads[0]] + [shift(grads[s], "blk", -s) for s in range(1, groups)]

    term = call(sum_all, wchunk, [VMEM] * reps, moved=5 * 2 * part * width)(*terms)
    group_terms = [term] + [shift(term, "blk", s) for s in range(1, groups)]

    rows = call(
        functools.partial(sum_groups, reps, groups),
        [chunk] * reps,
        [VMEM] * groups,
        moved=2 * groups * reps * part * block,
    )(*grads)
    rows = over_rep(rows)

    gw_part = call(sum_all, wchunk, [VMEM] * groups, moved=2 * groups * part * width)(*group_terms)
    gw_parts = over_rep([gw_part] * reps)

    grad_feats = call(
        functools.partial(join_rows, reps),
        like((nodes, width), F32),
        [VMEM] * reps,
        [pltpu.VMEM((reps, part, block), F32)],
        moved=6 * nodes * width,
    )(*rows)
    grad_weight = call(
        functools.partial(join_weight, reps),
        like((width, width), F32),
        [VMEM] * reps,
        moved=6 * width * width,
    )(*gw_parts)
    return (out_rows, grad_weight, grad_feats)


def solution(mesh):
    return jax.shard_map(
        per_device,
        mesh=mesh,
        in_specs=(
            P(("blk", "rep"), None),
            P(),
            P(("blk", "rep"), None),
            P("blk", "rep", None, None, None, None),
            P("blk", "rep", None, None),
            P("blk", "rep", None, None),
            P("blk", "rep", None),
        ),
        out_specs=(P(("blk", "rep"), None), P(), P(("blk", "rep"), None)),
        check_vma=False,
    )
```

time: 260 us -> 90.7 us (0.35)
  waiting for transfers between devices: 191 us -> 31 us
  starting transfers between devices: 6.66 us -> 51.1 us
  blocking collectives: 30.1 us -> 0 us
  between operations: 14 us -> 0.77 us
  matrix products: 7.97 us -> 0 us
  local copies, waits for them, and re-layouts: 8.28 us -> 2.52 us
  Pallas kernels: 0 us -> 4.98 us
    psum x1 -> x0, waiting for transfers between devices: 117 us -> none  [per_device(): grad_weight = lax.psum(weight_part, ('rep', 'blk'))]
    reduce_scatter x2 -> x0, waiting for transfers between devices: 45.9 us -> none  [the longest x1 23.6 us: per_device(): lax.psum_scatter(accumulator.reshape(-1, feat_width), 'rep', scatter_dime...]
    ppermute x6 -> x45, starting transfers between devices: 6.54 us -> 51.1 us  [shift(): lax.ppermute(array, axis, [(i, (i + by) % peers) for i in range(peers)])]
    all_gather x2 -> x0, blocking collectives: 30.1 us -> none  [the longest x1 16 us: per_device(): gathered = lax.all_gather(feats, 'rep', axis=0, tiled=True)]
    dot_general x11 -> x0, matrix products: 7.97 us -> none  [the longest x2 2.05 us: per_device(): jnp.einsum('kr,kif->rif', selector, products, precision=lax.Precision.HIG...]
    pallas_call x0 -> x10, Pallas kernels: none -> 4.98 us  [the longest x1 1.21 us: per_device(): call(functools.partial(aggregate, reps, lists, cap), [chunk] * reps, [SME...]
    ppermute x6 -> x45, waiting for transfers between devices: 28 us -> 31 us  [shift(): lax.ppermute(array, axis, [(i, (i + by) % peers) for i in range(peers)])]
  transfers between devices with their start and end apart: 9 -> 45, of which waited for: 9 -> 20; matrix products, arithmetic and copies ran while one was open for 3% -> 2% of each run, Pallas kernels for 0% -> 2%
where the time goes in v1:
time: 90.7 us; the launch traced here: 90.5 us
  starting transfers between devices  51.1 us (56%)
  waiting for transfers between devices  31 us (34%)
  Pallas kernels  4.98 us (5%)
  local copies, waits for them, and re-layouts  2.52 us (3%)
    ppermute x45, starting transfers between devices, shift(): lax.ppermute(array, axis, [(i, (i + by) % peers) for i in range(peers)])  51.1 us
    ppermute x45, waiting for transfers between devices, shift(): lax.ppermute(array, axis, [(i, (i + by) % peers) for i in range(peers)])  31 us
  transfers between devices with their start and end apart: 45, of which 20 were waited for; matrix products, arithmetic and copies ran while one was open for 2% of the time, Pallas kernels for 2%

profile of v1, /device:TPU:0, one launch (start us, length us, event | category | flops | bytes accessed | tf_op | source)
XLA Modules:
  0.0 90.5 jit_solution(8546373254411085767)
XLA Ops:
  0.6 0.9 copy-done.2
  1.6 3.1 %collective-permute-start.6 = (bf16[64,128]{1,0:T(8,128)(2,1)S(1)}, bf16[64,128]{1,0:T(8,128)(2,1)S(1)}, u32[]{:S(2)}, u32[]{:S(2)}) collective-permute-start(bf16[64,128]{1,0:T(8,128)(2,1)S(1)} %get-tuple-element.35), channel_id=1, source_target_pairs={{0,8},{8,16},{16,24},{24,0},{1,9},{9,17},{17,25},{25,1},{2,10},{10... | collective-permute-start | bytes 49160 | tf_op jit(solution)/shard_map/ppermute | solution.py:18
  4.7 2.6 %collective-permute-start.7 = (bf16[64,128]{1,0:T(8,128)(2,1)S(1)}, bf16[64,128]{1,0:T(8,128)(2,1)S(1)}, u32[]{:S(2)}, u32[]{:S(2)}) collective-permute-start(bf16[64,128]{1,0:T(8,128)(2,1)S(1)} %get-tuple-element.36), channel_id=1, source_target_pairs={{0,16},{8,24},{16,0},{24,8},{1,17},{9,25},{17,1},{25,9},{2,18},{10... | collective-permute-start | bytes 49160 | tf_op jit(solution)/shard_map/ppermute | solution.py:18
  7.3 1.3 %collective-permute-start.8 = (bf16[64,128]{1,0:T(8,128)(2,1)S(1)}, bf16[64,128]{1,0:T(8,128)(2,1)S(1)}, u32[]{:S(2)}, u32[]{:S(2)}) collective-permute-start(bf16[64,128]{1,0:T(8,128)(2,1)S(1)} %get-tuple-element.37), channel_id=1, source_target_pairs={{0,24},{8,0},{16,8},{24,16},{1,25},{9,1},{17,9},{25,17},{2,26},{10... | collective-permute-start | bytes 49160 | tf_op jit(solution)/shard_map/ppermute | solution.py:18
  8.6 0.8 reshape.18
  9.4 0.8 reshape.19
  10.2 0.9 collective-permute-done.8
  11.8 3.1 %collective-permute-start.2 = (s32[14]{0:T(128)S(1)}, s32[14]{0:T(128)S(1)}, u32[]{:S(2)}, u32[]{:S(2)}) collective-permute-start(s32[14]{0:T(128)S(1)} %pad_add_fusion.refs_0_), channel_id=1, source_target_pairs={{0,24},{8,0},{16,8},{24,16},{1,25},{9,1},{17,9},{25,17},{2,26},{10... | collective-permute-start | bytes 176 | tf_op jit(solution)/shard_map/ppermute | solution.py:18
  15.6 2.4 %collective-permute-start.14 = (bf16[4,64,128]{2,1,0:T(8,128)(2,1)S(1)}, bf16[4,64,128]{2,1,0:T(8,128)(2,1)S(1)}, u32[]{:S(2)}, u32[]{:S(2)}) collective-permute-start(bf16[4,64,128]{2,1,0:T(8,128)(2,1)S(1)} %pad_maximum_fusion.refs_8_), channel_id=1, source_target_pairs={{0,6},{1,7},{2,0},{3,1},{4,2},{5,3},{6,4},{7,5},{8,14},{9,15},{10,... | collective-permute-start | bytes 196616 | tf_op jit(solution)/shard_map/ppermute | solution.py:18
  18.0 1.4 %collective-permute-done.1.refs_2_ = s32[14]{0:T(128)S(1)} collective-permute-done((s32[14]{0:T(128)S(1)}, s32[14]{0:T(128)S(1)}, u32[]{:S(2)}, u32[]{:S(2)}) %collective-permute-start.1) | collective-permute-done | bytes 88 | tf_op jit(solution)/shard_map/ppermute | solution.py:18
  19.4 1.9 %collective-permute-start.5 = (bf16[6,128,128]{2,1,0:T(8,128)(2,1)S(1)}, bf16[6,128,128]{2,1,0:T(8,128)(2,1)S(1)}, u32[]{:S(2)}, u32[]{:S(2)}) collective-permute-start(bf16[6,128,128]{2,1,0:T(8,128)(2,1)S(1)} %bitcast.6), channel_id=1, source_target_pairs={{0,24},{8,0},{16,8},{24,16},{1,25},{9,1},{17,9},{25,17},{2,26},{10... | collective-permute-start | bytes 589832 | tf_op jit(solution)/shard_map/ppermute | solution.py:18
  21.3 1.1 %collective-permute-start.4 = (bf16[6,128,128]{2,1,0:T(8,128)(2,1)S(1)}, bf16[6,128,128]{2,1,0:T(8,128)(2,1)S(1)}, u32[]{:S(2)}, u32[]{:S(2)}) collective-permute-start(bf16[6,128,128]{2,1,0:T(8,128)(2,1)S(1)} %bitcast.7), channel_id=1, source_target_pairs={{0,16},{8,24},{16,0},{24,8},{1,17},{9,25},{17,1},{25,9},{2,18},{10... | collective-permute-start | bytes 589832 | tf_op jit(solution)/shard_map/ppermute | solution.py:18
  22.5 0.7 collective-permute-start.12
  23.2 0.8 collective-permute-start.11
  23.9 3.5 %collective-permute-done.12.refs_12_ = bf16[4,64,128]{2,1,0:T(8,128)(2,1)S(1)} collective-permute-done((bf16[4,64,128]{2,1,0:T(8,128)(2,1)S(1)}, bf16[4,64,128]{2,1,0:T(8,128)(2,1)S(1)}, u32[]{:S(2)}, u32[]{:S(2)}) %collective-permute-start.12) | collective-permute-done | bytes 65568 | tf_op jit(solution)/shard_map/ppermute | solution.py:18
  28.4 4.5 %collective-permute-done.10.refs_10_ = bf16[4,64,128]{2,1,0:T(8,128)(2,1)S(1)} collective-permute-done((bf16[4,64,128]{2,1,0:T(8,128)(2,1)S(1)}, bf16[4,64,128]{2,1,0:T(8,128)(2,1)S(1)}, u32[]{:S(2)}, u32[]{:S(2)}) %collective-permute-start.10) | collective-permute-done | bytes 65568 | tf_op jit(solution)/shard_map/ppermute | solution.py:18
  33.3 7.2 %collective-permute-done.4.refs_6_ = bf16[6,128,128]{2,1,0:T(8,128)(2,1)S(1)} collective-permute-done((bf16[6,128,128]{2,1,0:T(8,128)(2,1)S(1)}, bf16[6,128,128]{2,1,0:T(8,128)(2,1)S(1)}, u32[]{:S(2)}, u32[]{:S(2)}) %collective-permute-start.4) | collective-permute-done | bytes 196640 | tf_op jit(solution)/shard_map/ppermute | solution.py:18
  40.5 1.2 %shard_map.95 = (bf16[64,128]{1,0:T(8,128)(2,1)S(1)}, bf16[64,128]{1,0:T(8,128)(2,1)S(1)}, bf16[64,128]{1,0:T(8,128)(2,1)S(1)}, bf16[64,128]{1,0:T(8,128)(2,1)S(1)}) custom-call(s32[14]{0:T(128)S(1)} %pad_add_fusion.refs_0_, s32[14]{0:T(128)S(1)} %collective-permute-done.refs_1_, s32[14]{0:T(128)S(1)} %collective-permute-done.1.refs_2_, ...), custom_call_target="tpu_custom_call" | custom-call | flops 50331648 | bytes 1310720 | tf_op jit(solution)/shard_map/pallas_call | solution.py:209
  41.8 1.8 %collective-permute-start.17 = (bf16[64,128]{1,0:T(8,128)(2,1)S(1)}, bf16[64,128]{1,0:T(8,128)(2,1)S(1)}, u32[]{:S(2)}, u32[]{:S(2)}) collective-permute-start(bf16[64,128]{1,0:T(8,128)(2,1)S(1)} %get-tuple-element.40), channel_id=1, source_target_pairs={{0,16},{8,24},{16,0},{24,8},{1,17},{9,25},{17,1},{25,9},{2,18},{10... | collective-permute-start | bytes 49160 | tf_op jit(solution)/shard_map/ppermute | solution.py:18
  43.5 2.8 %collective-permute-start.18 = (bf16[64,128]{1,0:T(8,128)(2,1)S(1)}, bf16[64,128]{1,0:T(8,128)(2,1)S(1)}, u32[]{:S(2)}, u32[]{:S(2)}) collective-permute-start(bf16[64,128]{1,0:T(8,128)(2,1)S(1)} %get-tuple-element.41), channel_id=1, source_target_pairs={{0,24},{8,0},{16,8},{24,16},{1,25},{9,1},{17,9},{25,17},{2,26},{10... | collective-permute-start | bytes 49160 | tf_op jit(solution)/shard_map/ppermute | solution.py:18
  46.4 0.9 %collective-permute-done.16.refs_1_ = bf16[64,128]{1,0:T(8,128)(2,1)S(1)} collective-permute-done((bf16[64,128]{1,0:T(8,128)(2,1)S(1)}, bf16[64,128]{1,0:T(8,128)(2,1)S(1)}, u32[]{:S(2)}, u32[]{:S(2)}) %collective-permute-start.16) | collective-permute-done | bytes 16416 | tf_op jit(solution)/shard_map/ppermute | solution.py:18
  47.9 0.9 shard_map.96
  48.9 2.1 %collective-permute-start.19 = (bf16[64,256]{1,0:T(8,128)(2,1)S(1)}, bf16[64,256]{1,0:T(8,128)(2,1)S(1)}, u32[]{:S(2)}, u32[]{:S(2)}) collective-permute-start(bf16[64,256]{1,0:T(8,128)(2,1)S(1)} %get-tuple-element.46), channel_id=1, source_target_pairs={{0,8},{8,16},{16,24},{24,0},{1,9},{9,17},{17,25},{25,1},{2,10},{10... | collective-permute-start | bytes 98312 | tf_op jit(solution)/shard_map/ppermute | solution.py:18
  51.0 2.6 %collective-permute-start.20 = (bf16[64,256]{1,0:T(8,128)(2,1)S(1)}, bf16[64,256]{1,0:T(8,128)(2,1)S(1)}, u32[]{:S(2)}, u32[]{:S(2)}) collective-permute-start(bf16[64,256]{1,0:T(8,128)(2,1)S(1)} %get-tuple-element.47), channel_id=1, source_target_pairs={{0,16},{8,24},{16,0},{24,8},{1,17},{9,25},{17,1},{25,9},{2,18},{10... | collective-permute-start | bytes 98312 | tf_op jit(solution)/shard_map/ppermute | solution.py:18
  53.6 1.3 %collective-permute-done.19.refs_1_ = bf16[64,256]{1,0:T(8,128)(2,1)S(1)} collective-permute-done((bf16[64,256]{1,0:T(8,128)(2,1)S(1)}, bf16[64,256]{1,0:T(8,128)(2,1)S(1)}, u32[]{:S(2)}, u32[]{:S(2)}) %collective-permute-start.19) | collective-permute-done | bytes 32800 | tf_op jit(solution)/shard_map/ppermute | solution.py:18
  54.9 0.9 collective-permute-done.20.refs_2_
  55.8 1.7 %collective-permute-done.21.refs_3_ = bf16[64,256]{1,0:T(8,128)(2,1)S(1)} collective-permute-done((bf16[64,256]{1,0:T(8,128)(2,1)S(1)}, bf16[64,256]{1,0:T(8,128)(2,1)S(1)}, u32[]{:S(2)}, u32[]{:S(2)}) %collective-permute-start.21) | collective-permute-done | bytes 32800 | tf_op jit(solution)/shard_map/ppermute | solution.py:18
  57.8 2.6 %collective-permute-start.33 = (bf16[64,128]{1,0:T(8,128)(2,1)S(1)}, bf16[64,128]{1,0:T(8,128)(2,1)S(1)}, u32[]{:S(2)}, u32[]{:S(2)}) collective-permute-start(bf16[64,128]{1,0:T(8,128)(2,1)S(1)} %get-tuple-element.51), channel_id=1, source_target_pairs={{0,16},{8,24},{16,0},{24,8},{1,17},{9,25},{17,1},{25,9},{2,18},{10... | collective-permute-start | bytes 49160 | tf_op jit(solution)/shard_map/ppermute | solution.py:18
  60.4 1.0 %collective-permute-start.27 = (bf16[64,256]{1,0:T(8,128)(2,1)S(1)}, bf16[64,256]{1,0:T(8,128)(2,1)S(1)}, u32[]{:S(2)}, u32[]{:S(2)}) collective-permute-start(bf16[64,256]{1,0:T(8,128)(2,1)S(1)} %shard_map.98.refs_0_), channel_id=1, source_target_pairs={{0,6},{1,7},{2,0},{3,1},{4,2},{5,3},{6,4},{7,5},{8,14},{9,15},{10,... | collective-permute-start | bytes 98312 | tf_op jit(solution)/shard_map/ppermute | solution.py:18
  61.3 1.1 %collective-permute-start.34 = (bf16[64,128]{1,0:T(8,128)(2,1)S(1)}, bf16[64,128]{1,0:T(8,128)(2,1)S(1)}, u32[]{:S(2)}, u32[]{:S(2)}) collective-permute-start(bf16[64,128]{1,0:T(8,128)(2,1)S(1)} %get-tuple-element.52), channel_id=1, source_target_pairs={{0,24},{8,0},{16,8},{24,16},{1,25},{9,1},{17,9},{25,17},{2,26},{10... | collective-permute-start | bytes 49160 | tf_op jit(solution)/shard_map/ppermute | solution.py:18
  62.5 0.8 collective-permute-done.32.refs_9_
  63.2 0.9 %collective-permute-start.25 = (bf16[64,256]{1,0:T(8,128)(2,1)S(1)}, bf16[64,256]{1,0:T(8,128)(2,1)S(1)}, u32[]{:S(2)}, u32[]{:S(2)}) collective-permute-start(bf16[64,256]{1,0:T(8,128)(2,1)S(1)} %shard_map.98.refs_0_), channel_id=1, source_target_pairs={{0,4},{1,5},{2,6},{3,7},{4,0},{5,1},{6,2},{7,3},{8,12},{9,13},{10,... | collective-permute-start | bytes 98312 | tf_op jit(solution)/shard_map/ppermute | solution.py:18
  64.1 0.9 %collective-permute-done.34.refs_11_ = bf16[64,128]{1,0:T(8,128)(2,1)S(1)} collective-permute-done((bf16[64,128]{1,0:T(8,128)(2,1)S(1)}, bf16[64,128]{1,0:T(8,128)(2,1)S(1)}, u32[]{:S(2)}, u32[]{:S(2)}) %collective-permute-start.34) | collective-permute-done | bytes 16416 | tf_op jit(solution)/shard_map/ppermute | solution.py:18
  65.1 1.0 %shard_map.101 = (bf16[4,64,128]{2,1,0:T(8,128)(2,1)S(1)}, bf16[4,64,128]{2,1,0:T(8,128)(2,1)S(1)}, bf16[4,64,128]{2,1,0:T(8,128)(2,1)S(1)}, bf16[4,64,128]{2,1,...) custom-call(s32[14]{0:T(128)S(1)} %pad_add_fusion.refs_0_, ...), custom_call_target="tpu_custom_call" | custom-call | flops 50331648 | bytes 1310720 | tf_op jit(solution)/shard_map/pallas_call | solution.py:247
  66.1 1.1 %collective-permute-start.35 = (bf16[4,64,128]{2,1,0:T(8,128)(2,1)S(1)}, bf16[4,64,128]{2,1,0:T(8,128)(2,1)S(1)}, u32[]{:S(2)}, u32[]{:S(2)}) collective-permute-start(bf16[4,64,128]{2,1,0:T(8,128)(2,1)S(1)} %get-tuple-element.54), channel_id=1, source_target_pairs={{0,7},{1,0},{2,1},{3,2},{4,3},{5,4},{6,5},{7,6},{8,15},{9,8},{10,9... | collective-permute-start | bytes 196616 | tf_op jit(solution)/shard_map/ppermute | solution.py:18
  67.2 1.0 %collective-permute-start.36 = (bf16[4,64,128]{2,1,0:T(8,128)(2,1)S(1)}, bf16[4,64,128]{2,1,0:T(8,128)(2,1)S(1)}, u32[]{:S(2)}, u32[]{:S(2)}) collective-permute-start(bf16[4,64,128]{2,1,0:T(8,128)(2,1)S(1)} %get-tuple-element.55), channel_id=1, source_target_pairs={{0,6},{1,7},{2,0},{3,1},{4,2},{5,3},{6,4},{7,5},{8,14},{9,15},{10,... | collective-permute-start | bytes 196616 | tf_op jit(solution)/shard_map/ppermute | solution.py:18
  68.1 1.8 %collective-permute-start.23 = (bf16[64,256]{1,0:T(8,128)(2,1)S(1)}, bf16[64,256]{1,0:T(8,128)(2,1)S(1)}, u32[]{:S(2)}, u32[]{:S(2)}) collective-permute-start(bf16[64,256]{1,0:T(8,128)(2,1)S(1)} %shard_map.98.refs_0_), channel_id=1, source_target_pairs={{0,2},{1,3},{2,4},{3,5},{4,6},{5,7},{6,0},{7,1},{8,10},{9,11},{10,... | collective-permute-start | bytes 98312 | tf_op jit(solution)/shard_map/ppermute | solution.py:18
  70.0 1.5 %collective-permute-done.24.refs_3_ = bf16[64,256]{1,0:T(8,128)(2,1)S(1)} collective-permute-done((bf16[64,256]{1,0:T(8,128)(2,1)S(1)}, bf16[64,256]{1,0:T(8,128)(2,1)S(1)}, u32[]{:S(2)}, u32[]{:S(2)}) %collective-permute-start.24) | collective-permute-done | bytes 32800 | tf_op jit(solution)/shard_map/ppermute | solution.py:18
  71.5 1.3 %collective-permute-start.37 = (bf16[4,64,128]{2,1,0:T(8,128)(2,1)S(1)}, bf16[4,64,128]{2,1,0:T(8,128)(2,1)S(1)}, u32[]{:S(2)}, u32[]{:S(2)}) collective-permute-start(bf16[4,64,128]{2,1,0:T(8,128)(2,1)S(1)} %get-tuple-element.56), channel_id=1, source_target_pairs={{0,5},{1,6},{2,7},{3,0},{4,1},{5,2},{6,3},{7,4},{8,13},{9,14},{10,... | collective-permute-start | bytes 196616 | tf_op jit(solution)/shard_map/ppermute | solution.py:18
  74.2 2.6 %collective-permute-start.40 = (bf16[4,64,128]{2,1,0:T(8,128)(2,1)S(1)}, bf16[4,64,128]{2,1,0:T(8,128)(2,1)S(1)}, u32[]{:S(2)}, u32[]{:S(2)}) collective-permute-start(bf16[4,64,128]{2,1,0:T(8,128)(2,1)S(1)} %get-tuple-element.59), channel_id=1, source_target_pairs={{0,2},{1,3},{2,4},{3,5},{4,6},{5,7},{6,0},{7,1},{8,10},{9,11},{10,... | collective-permute-start | bytes 196616 | tf_op jit(solution)/shard_map/ppermute | solution.py:18
  76.9 2.3 %collective-permute-start.31 = (bf16[64,256]{1,0:T(8,128)(2,1)S(1)}, bf16[64,256]{1,0:T(8,128)(2,1)S(1)}, u32[]{:S(2)}, u32[]{:S(2)}) collective-permute-start(bf16[64,256]{1,0:T(8,128)(2,1)S(1)} %shard_map.99.refs_0_), channel_id=1, source_target_pairs={{0,24},{8,0},{16,8},{24,16},{1,25},{9,1},{17,9},{25,17},{2,26},{10... | collective-permute-start | bytes 98312 | tf_op jit(solution)/shard_map/ppermute | solution.py:18
  79.2 2.3 %collective-permute-start.30 = (bf16[64,256]{1,0:T(8,128)(2,1)S(1)}, bf16[64,256]{1,0:T(8,128)(2,1)S(1)}, u32[]{:S(2)}, u32[]{:S(2)}) collective-permute-start(bf16[64,256]{1,0:T(8,128)(2,1)S(1)} %shard_map.99.refs_0_), channel_id=1, source_target_pairs={{0,16},{8,24},{16,0},{24,8},{1,17},{9,25},{17,1},{25,9},{2,18},{10... | collective-permute-start | bytes 98312 | tf_op jit(solution)/shard_map/ppermute | solution.py:18
  81.7 1.2 %collective-permute-start.42 = (bf16[64,128]{1,0:T(8,128)(2,1)S(1)}, bf16[64,128]{1,0:T(8,128)(2,1)S(1)}, u32[]{:S(2)}, u32[]{:S(2)}) collective-permute-start(bf16[64,128]{1,0:T(8,128)(2,1)S(1)} %get-tuple-element.62), channel_id=1, source_target_pairs={{0,8},{8,16},{16,24},{24,0},{1,9},{9,17},{17,25},{25,1},{2,10},{10... | collective-permute-start | bytes 49160 | tf_op jit(solution)/shard_map/ppermute | solution.py:18
  82.9 3.1 %collective-permute-start.43 = (bf16[64,128]{1,0:T(8,128)(2,1)S(1)}, bf16[64,128]{1,0:T(8,128)(2,1)S(1)}, u32[]{:S(2)}, u32[]{:S(2)}) collective-permute-start(bf16[64,128]{1,0:T(8,128)(2,1)S(1)} %get-tuple-element.63), channel_id=1, source_target_pairs={{0,16},{8,24},{16,0},{24,8},{1,17},{9,25},{17,1},{25,9},{2,18},{10... | collective-permute-start | bytes 49160 | tf_op jit(solution)/shard_map/ppermute | solution.py:18
  86.0 1.4 %collective-permute-done.29.refs_1_ = bf16[64,256]{1,0:T(8,128)(2,1)S(1)} collective-permute-done((bf16[64,256]{1,0:T(8,128)(2,1)S(1)}, bf16[64,256]{1,0:T(8,128)(2,1)S(1)}, u32[]{:S(2)}, u32[]{:S(2)}) %collective-permute-start.29) | collective-permute-done | bytes 32800 | tf_op jit(solution)/shard_map/ppermute | solution.py:18
  87.4 0.7 shard_map.100
  88.1 1.6 %collective-permute-done.44.refs_3_ = bf16[64,128]{1,0:T(8,128)(2,1)S(1)} collective-permute-done((bf16[64,128]{1,0:T(8,128)(2,1)S(1)}, bf16[64,128]{1,0:T(8,128)(2,1)S(1)}, u32[]{:S(2)}, u32[]{:S(2)}) %collective-permute-start.44) | collective-permute-done | bytes 16416 | tf_op jit(solution)/shard_map/ppermute | solution.py:18
  89.7 0.8 shard_map.103
  (66 shorter events, 5.6 us)
Async XLA Ops:
  0.6 18.7 %copy-start = (bf16[1,1,2,3,128,128]{5,4,3,2,1,0:T(8,128)(2,1)S(1)}, bf16[1,1,2,3,128,128]{5,4,3,2,1,0:T(8,128)(2,1)}, u32[]{:S(2)}) copy-start(bf16[1,1,2,3,128,128]{5,4,3,2,1,0:T(8,128)(2,1)} %param.10) | copy-start | bytes 589828
  1.6 8.5 %collective-permute-start.6 = (bf16[64,128]{1,0:T(8,128)(2,1)S(1)}, bf16[64,128]{1,0:T(8,128)(2,1)S(1)}, u32[]{:S(2)}, u32[]{:S(2)}) collective-permute-start(bf16[64,128]{1,0:T(8,128)(2,1)S(1)} %get-tuple-element.35), channel_id=1, source_target_pairs={{0,8},{8,16},{16,24},{24,0},{1,9},{9,17},{17,25},{25,1},{2,10},{10... | collective-permute-start | bytes 49160 | tf_op jit(solution)/shard_map/ppermute | solution.py:18
  4.7 5.5 %collective-permute-start.7 = (bf16[64,128]{1,0:T(8,128)(2,1)S(1)}, bf16[64,128]{1,0:T(8,128)(2,1)S(1)}, u32[]{:S(2)}, u32[]{:S(2)}) collective-permute-start(bf16[64,128]{1,0:T(8,128)(2,1)S(1)} %get-tuple-element.36), channel_id=1, source_target_pairs={{0,16},{8,24},{16,0},{24,8},{1,17},{9,25},{17,1},{25,9},{2,18},{10... | collective-permute-start | bytes 49160 | tf_op jit(solution)/shard_map/ppermute | solution.py:18
  7.3 3.7 %collective-permute-start.8 = (bf16[64,128]{1,0:T(8,128)(2,1)S(1)}, bf16[64,128]{1,0:T(8,128)(2,1)S(1)}, u32[]{:S(2)}, u32[]{:S(2)}) collective-permute-start(bf16[64,128]{1,0:T(8,128)(2,1)S(1)} %get-tuple-element.37), channel_id=1, source_target_pairs={{0,24},{8,0},{16,8},{24,16},{1,25},{9,1},{17,9},{25,17},{2,26},{10... | collective-permute-start | bytes 49160 | tf_op jit(solution)/shard_map/ppermute | solution.py:18
  11.1 11.4 %collective-permute-start.15 = (bf16[4,64,128]{2,1,0:T(8,128)(2,1)S(1)}, bf16[4,64,128]{2,1,0:T(8,128)(2,1)S(1)}, u32[]{:S(2)}, u32[]{:S(2)}) collective-permute-start(bf16[4,64,128]{2,1,0:T(8,128)(2,1)S(1)} %pad_maximum_fusion.refs_8_), channel_id=1, source_target_pairs={{0,7},{1,0},{2,1},{3,2},{4,3},{5,4},{6,5},{7,6},{8,15},{9,8},{10,9... | collective-permute-start | bytes 196616 | tf_op jit(solution)/shard_map/ppermute | solution.py:18
  11.8 6.2 %collective-permute-start.2 = (s32[14]{0:T(128)S(1)}, s32[14]{0:T(128)S(1)}, u32[]{:S(2)}, u32[]{:S(2)}) collective-permute-start(s32[14]{0:T(128)S(1)} %pad_add_fusion.refs_0_), channel_id=1, source_target_pairs={{0,24},{8,0},{16,8},{24,16},{1,25},{9,1},{17,9},{25,17},{2,26},{10... | collective-permute-start | bytes 176 | tf_op jit(solution)/shard_map/ppermute | solution.py:18
  14.9 4.4 %collective-permute-start.1 = (s32[14]{0:T(128)S(1)}, s32[14]{0:T(128)S(1)}, u32[]{:S(2)}, u32[]{:S(2)}) collective-permute-start(s32[14]{0:T(128)S(1)} %pad_add_fusion.refs_0_), channel_id=1, source_target_pairs={{0,16},{8,24},{16,0},{24,8},{1,17},{9,25},{17,1},{25,9},{2,18},{10... | collective-permute-start | bytes 176 | tf_op jit(solution)/shard_map/ppermute | solution.py:18
  14.9 6.4 %collective-permute-start = (s32[14]{0:T(128)S(1)}, s32[14]{0:T(128)S(1)}, u32[]{:S(2)}, u32[]{:S(2)}) collective-permute-start(s32[14]{0:T(128)S(1)} %pad_add_fusion.refs_0_), channel_id=1, source_target_pairs={{0,8},{8,16},{16,24},{24,0},{1,9},{9,17},{17,25},{25,1},{2,10},{10... | collective-permute-start | bytes 176 | tf_op jit(solution)/shard_map/ppermute | solution.py:18
  15.6 6.9 %collective-permute-start.14 = (bf16[4,64,128]{2,1,0:T(8,128)(2,1)S(1)}, bf16[4,64,128]{2,1,0:T(8,128)(2,1)S(1)}, u32[]{:S(2)}, u32[]{:S(2)}) collective-permute-start(bf16[4,64,128]{2,1,0:T(8,128)(2,1)S(1)} %pad_maximum_fusion.refs_8_), channel_id=1, source_target_pairs={{0,6},{1,7},{2,0},{3,1},{4,2},{5,3},{6,4},{7,5},{8,14},{9,15},{10,... | collective-permute-start | bytes 196616 | tf_op jit(solution)/shard_map/ppermute | solution.py:18
  18.0 5.1 %collective-permute-start.13 = (bf16[4,64,128]{2,1,0:T(8,128)(2,1)S(1)}, bf16[4,64,128]{2,1,0:T(8,128)(2,1)S(1)}, u32[]{:S(2)}, u32[]{:S(2)}) collective-permute-start(bf16[4,64,128]{2,1,0:T(8,128)(2,1)S(1)} %pad_maximum_fusion.refs_8_), channel_id=1, source_target_pairs={{0,5},{1,6},{2,7},{3,0},{4,1},{5,2},{6,3},{7,4},{8,13},{9,14},{10,... | collective-permute-start | bytes 196616 | tf_op jit(solution)/shard_map/ppermute | solution.py:18
  19.4 28.5 %copy-start.1 = (bf16[256,256]{1,0:T(8,128)(2,1)S(1)}, bf16[256,256]{1,0:T(8,128)(2,1)}, u32[]{:S(2)}) copy-start(bf16[256,256]{1,0:T(8,128)(2,1)} %refs_4_.1) | copy-start | bytes 393220
  19.4 28.5 %copy-start.3 = (bf16[128,256]{1,0:T(8,128)(2,1)S(1)}, bf16[128,256]{1,0:T(8,128)(2,1)}, u32[]{:S(2)}) copy-start(bf16[128,256]{1,0:T(8,128)(2,1)} %refs_5_.1) | copy-start | bytes 196612
  19.4 13.9 %collective-permute-start.5 = (bf16[6,128,128]{2,1,0:T(8,128)(2,1)S(1)}, bf16[6,128,128]{2,1,0:T(8,128)(2,1)S(1)}, u32[]{:S(2)}, u32[]{:S(2)}) collective-permute-start(bf16[6,128,128]{2,1,0:T(8,128)(2,1)S(1)} %bitcast.6), channel_id=1, source_target_pairs={{0,24},{8,0},{16,8},{24,16},{1,25},{9,1},{17,9},{25,17},{2,26},{10... | collective-permute-start | bytes 589832 | tf_op jit(solution)/shard_map/ppermute | solution.py:18
  21.3 19.2 %collective-permute-start.4 = (bf16[6,128,128]{2,1,0:T(8,128)(2,1)S(1)}, bf16[6,128,128]{2,1,0:T(8,128)(2,1)S(1)}, u32[]{:S(2)}, u32[]{:S(2)}) collective-permute-start(bf16[6,128,128]{2,1,0:T(8,128)(2,1)S(1)} %bitcast.7), channel_id=1, source_target_pairs={{0,16},{8,24},{16,0},{24,8},{1,17},{9,25},{17,1},{25,9},{2,18},{10... | collective-permute-start | bytes 589832 | tf_op jit(solution)/shard_map/ppermute | solution.py:18
  22.4 18.0 %collective-permute-start.3 = (bf16[6,128,128]{2,1,0:T(8,128)(2,1)S(1)}, bf16[6,128,128]{2,1,0:T(8,128)(2,1)S(1)}, u32[]{:S(2)}, u32[]{:S(2)}) collective-permute-start(bf16[6,128,128]{2,1,0:T(8,128)(2,1)S(1)} %bitcast.8), channel_id=1, source_target_pairs={{0,8},{8,16},{16,24},{24,0},{1,9},{9,17},{17,25},{25,1},{2,10},{10... | collective-permute-start | bytes 589832 | tf_op jit(solution)/shard_map/ppermute | solution.py:18
  22.5 5.0 %collective-permute-start.12 = (bf16[4,64,128]{2,1,0:T(8,128)(2,1)S(1)}, bf16[4,64,128]{2,1,0:T(8,128)(2,1)S(1)}, u32[]{:S(2)}, u32[]{:S(2)}) collective-permute-start(bf16[4,64,128]{2,1,0:T(8,128)(2,1)S(1)} %pad_maximum_fusion.refs_8_), channel_id=1, source_target_pairs={{0,4},{1,5},{2,6},{3,7},{4,0},{5,1},{6,2},{7,3},{8,12},{9,13},{10,... | collective-permute-start | bytes 196616 | tf_op jit(solution)/shard_map/ppermute | solution.py:18
  23.2 5.3 %collective-permute-start.11 = (bf16[4,64,128]{2,1,0:T(8,128)(2,1)S(1)}, bf16[4,64,128]{2,1,0:T(8,128)(2,1)S(1)}, u32[]{:S(2)}, u32[]{:S(2)}) collective-permute-start(bf16[4,64,128]{2,1,0:T(8,128)(2,1)S(1)} %pad_maximum_fusion.refs_8_), channel_id=1, source_target_pairs={{0,3},{1,4},{2,5},{3,6},{4,7},{5,0},{6,1},{7,2},{8,11},{9,12},{10,... | collective-permute-start | bytes 196616 | tf_op jit(solution)/shard_map/ppermute | solution.py:18
  27.4 5.5 %collective-permute-start.10 = (bf16[4,64,128]{2,1,0:T(8,128)(2,1)S(1)}, bf16[4,64,128]{2,1,0:T(8,128)(2,1)S(1)}, u32[]{:S(2)}, u32[]{:S(2)}) collective-permute-start(bf16[4,64,128]{2,1,0:T(8,128)(2,1)S(1)} %pad_maximum_fusion.refs_8_), channel_id=1, source_target_pairs={{0,2},{1,3},{2,4},{3,5},{4,6},{5,7},{6,0},{7,1},{8,10},{9,11},{10,... | collective-permute-start | bytes 196616 | tf_op jit(solution)/shard_map/ppermute | solution.py:18
  28.4 4.9 %collective-permute-start.9 = (bf16[4,64,128]{2,1,0:T(8,128)(2,1)S(1)}, bf16[4,64,128]{2,1,0:T(8,128)(2,1)S(1)}, u32[]{:S(2)}, u32[]{:S(2)}) collective-permute-start(bf16[4,64,128]{2,1,0:T(8,128)(2,1)S(1)} %pad_maximum_fusion.refs_8_), channel_id=1, source_target_pairs={{0,1},{1,2},{2,3},{3,4},{4,5},{5,6},{6,7},{7,0},{8,9},{9,10},{10,1... | collective-permute-start | bytes 196616 | tf_op jit(solution)/shard_map/ppermute | solution.py:18
  41.7 5.6 %collective-permute-start.16 = (bf16[64,128]{1,0:T(8,128)(2,1)S(1)}, bf16[64,128]{1,0:T(8,128)(2,1)S(1)}, u32[]{:S(2)}, u32[]{:S(2)}) collective-permute-start(bf16[64,128]{1,0:T(8,128)(2,1)S(1)} %get-tuple-element.39), channel_id=1, source_target_pairs={{0,8},{8,16},{16,24},{24,0},{1,9},{9,17},{17,25},{25,1},{2,10},{10... | collective-permute-start | bytes 49160 | tf_op jit(solution)/shard_map/ppermute | solution.py:18
  41.8 5.6 %collective-permute-start.17 = (bf16[64,128]{1,0:T(8,128)(2,1)S(1)}, bf16[64,128]{1,0:T(8,128)(2,1)S(1)}, u32[]{:S(2)}, u32[]{:S(2)}) collective-permute-start(bf16[64,128]{1,0:T(8,128)(2,1)S(1)} %get-tuple-element.40), channel_id=1, source_target_pairs={{0,16},{8,24},{16,0},{24,8},{1,17},{9,25},{17,1},{25,9},{2,18},{10... | collective-permute-start | bytes 49160 | tf_op jit(solution)/shard_map/ppermute | solution.py:18
  43.5 4.3 %collective-permute-start.18 = (bf16[64,128]{1,0:T(8,128)(2,1)S(1)}, bf16[64,128]{1,0:T(8,128)(2,1)S(1)}, u32[]{:S(2)}, u32[]{:S(2)}) collective-permute-start(bf16[64,128]{1,0:T(8,128)(2,1)S(1)} %get-tuple-element.41), channel_id=1, source_target_pairs={{0,24},{8,0},{16,8},{24,16},{1,25},{9,1},{17,9},{25,17},{2,26},{10... | collective-permute-start | bytes 49160 | tf_op jit(solution)/shard_map/ppermute | solution.py:18
  48.9 6.0 %collective-permute-start.19 = (bf16[64,256]{1,0:T(8,128)(2,1)S(1)}, bf16[64,256]{1,0:T(8,128)(2,1)S(1)}, u32[]{:S(2)}, u32[]{:S(2)}) collective-permute-start(bf16[64,256]{1,0:T(8,128)(2,1)S(1)} %get-tuple-element.46), channel_id=1, source_target_pairs={{0,8},{8,16},{16,24},{24,0},{1,9},{9,17},{17,25},{25,1},{2,10},{10... | collective-permute-start | bytes 98312 | tf_op jit(solution)/shard_map/ppermute | solution.py:18
  51.0 4.8 %collective-permute-start.20 = (bf16[64,256]{1,0:T(8,128)(2,1)S(1)}, bf16[64,256]{1,0:T(8,128)(2,1)S(1)}, u32[]{:S(2)}, u32[]{:S(2)}) collective-permute-start(bf16[64,256]{1,0:T(8,128)(2,1)S(1)} %get-tuple-element.47), channel_id=1, source_target_pairs={{0,16},{8,24},{16,0},{24,8},{1,17},{9,25},{17,1},{25,9},{2,18},{10... | collective-permute-start | bytes 98312 | tf_op jit(solution)/shard_map/ppermute | solution.py:18
  53.6 3.9 %collective-permute-start.21 = (bf16[64,256]{1,0:T(8,128)(2,1)S(1)}, bf16[64,256]{1,0:T(8,128)(2,1)S(1)}, u32[]{:S(2)}, u32[]{:S(2)}) collective-permute-start(bf16[64,256]{1,0:T(8,128)(2,1)S(1)} %get-tuple-element.48), channel_id=1, source_target_pairs={{0,24},{8,0},{16,8},{24,16},{1,25},{9,1},{17,9},{25,17},{2,26},{10... | collective-permute-start | bytes 98312 | tf_op jit(solution)/shard_map/ppermute | solution.py:18
  57.6 9.6 %collective-permute-start.28 = (bf16[64,256]{1,0:T(8,128)(2,1)S(1)}, bf16[64,256]{1,0:T(8,128)(2,1)S(1)}, u32[]{:S(2)}, u32[]{:S(2)}) collective-permute-start(bf16[64,256]{1,0:T(8,128)(2,1)S(1)} %shard_map.98.refs_0_), channel_id=1, source_target_pairs={{0,7},{1,0},{2,1},{3,2},{4,3},{5,4},{6,5},{7,6},{8,15},{9,8},{10,9... | collective-permute-start | bytes 98312 | tf_op jit(solution)/shard_map/ppermute | solution.py:18
  57.6 5.6 %collective-permute-start.32 = (bf16[64,128]{1,0:T(8,128)(2,1)S(1)}, bf16[64,128]{1,0:T(8,128)(2,1)S(1)}, u32[]{:S(2)}, u32[]{:S(2)}) collective-permute-start(bf16[64,128]{1,0:T(8,128)(2,1)S(1)} %get-tuple-element.50), channel_id=1, source_target_pairs={{0,8},{8,16},{16,24},{24,0},{1,9},{9,17},{17,25},{25,1},{2,10},{10... | collective-permute-start | bytes 49160 | tf_op jit(solution)/shard_map/ppermute | solution.py:18
  57.8 5.5 %collective-permute-start.33 = (bf16[64,128]{1,0:T(8,128)(2,1)S(1)}, bf16[64,128]{1,0:T(8,128)(2,1)S(1)}, u32[]{:S(2)}, u32[]{:S(2)}) collective-permute-start(bf16[64,128]{1,0:T(8,128)(2,1)S(1)} %get-tuple-element.51), channel_id=1, source_target_pairs={{0,16},{8,24},{16,0},{24,8},{1,17},{9,25},{17,1},{25,9},{2,18},{10... | collective-permute-start | bytes 49160 | tf_op jit(solution)/shard_map/ppermute | solution.py:18
  60.4 7.7 %collective-permute-start.27 = (bf16[64,256]{1,0:T(8,128)(2,1)S(1)}, bf16[64,256]{1,0:T(8,128)(2,1)S(1)}, u32[]{:S(2)}, u32[]{:S(2)}) collective-permute-start(bf16[64,256]{1,0:T(8,128)(2,1)S(1)} %shard_map.98.refs_0_), channel_id=1, source_target_pairs={{0,6},{1,7},{2,0},{3,1},{4,2},{5,3},{6,4},{7,5},{8,14},{9,15},{10,... | collective-permute-start | bytes 98312 | tf_op jit(solution)/shard_map/ppermute | solution.py:18
  61.3 3.7 %collective-permute-start.34 = (bf16[64,128]{1,0:T(8,128)(2,1)S(1)}, bf16[64,128]{1,0:T(8,128)(2,1)S(1)}, u32[]{:S(2)}, u32[]{:S(2)}) collective-permute-start(bf16[64,128]{1,0:T(8,128)(2,1)S(1)} %get-tuple-element.52), channel_id=1, source_target_pairs={{0,24},{8,0},{16,8},{24,16},{1,25},{9,1},{17,9},{25,17},{2,26},{10... | collective-permute-start | bytes 49160 | tf_op jit(solution)/shard_map/ppermute | solution.py:18
  63.2 4.9 %collective-permute-start.26 = (bf16[64,256]{1,0:T(8,128)(2,1)S(1)}, bf16[64,256]{1,0:T(8,128)(2,1)S(1)}, u32[]{:S(2)}, u32[]{:S(2)}) collective-permute-start(bf16[64,256]{1,0:T(8,128)(2,1)S(1)} %shard_map.98.refs_0_), channel_id=1, source_target_pairs={{0,5},{1,6},{2,7},{3,0},{4,1},{5,2},{6,3},{7,4},{8,13},{9,14},{10,... | collective-permute-start | bytes 98312 | tf_op jit(solution)/shard_map/ppermute | solution.py:18
  63.2 6.7 %collective-permute-start.25 = (bf16[64,256]{1,0:T(8,128)(2,1)S(1)}, bf16[64,256]{1,0:T(8,128)(2,1)S(1)}, u32[]{:S(2)}, u32[]{:S(2)}) collective-permute-start(bf16[64,256]{1,0:T(8,128)(2,1)S(1)} %shard_map.98.refs_0_), channel_id=1, source_target_pairs={{0,4},{1,5},{2,6},{3,7},{4,0},{5,1},{6,2},{7,3},{8,12},{9,13},{10,... | collective-permute-start | bytes 98312 | tf_op jit(solution)/shard_map/ppermute | solution.py:18
  66.1 8.1 %collective-permute-start.35 = (bf16[4,64,128]{2,1,0:T(8,128)(2,1)S(1)}, bf16[4,64,128]{2,1,0:T(8,128)(2,1)S(1)}, u32[]{:S(2)}, u32[]{:S(2)}) collective-permute-start(bf16[4,64,128]{2,1,0:T(8,128)(2,1)S(1)} %get-tuple-element.54), channel_id=1, source_target_pairs={{0,7},{1,0},{2,1},{3,2},{4,3},{5,4},{6,5},{7,6},{8,15},{9,8},{10,9... | collective-permute-start | bytes 196616 | tf_op jit(solution)/shard_map/ppermute | solution.py:18
  67.2 9.7 %collective-permute-start.36 = (bf16[4,64,128]{2,1,0:T(8,128)(2,1)S(1)}, bf16[4,64,128]{2,1,0:T(8,128)(2,1)S(1)}, u32[]{:S(2)}, u32[]{:S(2)}) collective-permute-start(bf16[4,64,128]{2,1,0:T(8,128)(2,1)S(1)} %get-tuple-element.55), channel_id=1, source_target_pairs={{0,6},{1,7},{2,0},{3,1},{4,2},{5,3},{6,4},{7,5},{8,14},{9,15},{10,... | collective-permute-start | bytes 196616 | tf_op jit(solution)/shard_map/ppermute | solution.py:18
  68.1 3.3 %collective-permute-start.24 = (bf16[64,256]{1,0:T(8,128)(2,1)S(1)}, bf16[64,256]{1,0:T(8,128)(2,1)S(1)}, u32[]{:S(2)}, u32[]{:S(2)}) collective-permute-start(bf16[64,256]{1,0:T(8,128)(2,1)S(1)} %shard_map.98.refs_0_), channel_id=1, source_target_pairs={{0,3},{1,4},{2,5},{3,6},{4,7},{5,0},{6,1},{7,2},{8,11},{9,12},{10,... | collective-permute-start | bytes 98312 | tf_op jit(solution)/shard_map/ppermute | solution.py:18
  68.1 5.1 %collective-permute-start.23 = (bf16[64,256]{1,0:T(8,128)(2,1)S(1)}, bf16[64,256]{1,0:T(8,128)(2,1)S(1)}, u32[]{:S(2)}, u32[]{:S(2)}) collective-permute-start(bf16[64,256]{1,0:T(8,128)(2,1)S(1)} %shard_map.98.refs_0_), channel_id=1, source_target_pairs={{0,2},{1,3},{2,4},{3,5},{4,6},{5,7},{6,0},{7,1},{8,10},{9,11},{10,... | collective-permute-start | bytes 98312 | tf_op jit(solution)/shard_map/ppermute | solution.py:18
  70.0 4.2 %collective-permute-start.22 = (bf16[64,256]{1,0:T(8,128)(2,1)S(1)}, bf16[64,256]{1,0:T(8,128)(2,1)S(1)}, u32[]{:S(2)}, u32[]{:S(2)}) collective-permute-start(bf16[64,256]{1,0:T(8,128)(2,1)S(1)} %shard_map.98.refs_0_), channel_id=1, source_target_pairs={{0,1},{1,2},{2,3},{3,4},{4,5},{5,6},{6,7},{7,0},{8,9},{9,10},{10,1... | collective-permute-start | bytes 98312 | tf_op jit(solution)/shard_map/ppermute | solution.py:18
  71.5 5.4 %collective-permute-start.37 = (bf16[4,64,128]{2,1,0:T(8,128)(2,1)S(1)}, bf16[4,64,128]{2,1,0:T(8,128)(2,1)S(1)}, u32[]{:S(2)}, u32[]{:S(2)}) collective-permute-start(bf16[4,64,128]{2,1,0:T(8,128)(2,1)S(1)} %get-tuple-element.56), channel_id=1, source_target_pairs={{0,5},{1,6},{2,7},{3,0},{4,1},{5,2},{6,3},{7,4},{8,13},{9,14},{10,... | collective-permute-start | bytes 196616 | tf_op jit(solution)/shard_map/ppermute | solution.py:18
  73.3 5.9 %collective-permute-start.38 = (bf16[4,64,128]{2,1,0:T(8,128)(2,1)S(1)}, bf16[4,64,128]{2,1,0:T(8,128)(2,1)S(1)}, u32[]{:S(2)}, u32[]{:S(2)}) collective-permute-start(bf16[4,64,128]{2,1,0:T(8,128)(2,1)S(1)} %get-tuple-element.57), channel_id=1, source_target_pairs={{0,4},{1,5},{2,6},{3,7},{4,0},{5,1},{6,2},{7,3},{8,12},{9,13},{10,... | collective-permute-start | bytes 196616 | tf_op jit(solution)/shard_map/ppermute | solution.py:18
  74.2 7.3 %collective-permute-start.39 = (bf16[4,64,128]{2,1,0:T(8,128)(2,1)S(1)}, bf16[4,64,128]{2,1,0:T(8,128)(2,1)S(1)}, u32[]{:S(2)}, u32[]{:S(2)}) collective-permute-start(bf16[4,64,128]{2,1,0:T(8,128)(2,1)S(1)} %get-tuple-element.58), channel_id=1, source_target_pairs={{0,3},{1,4},{2,5},{3,6},{4,7},{5,0},{6,1},{7,2},{8,11},{9,12},{10,... | collective-permute-start | bytes 196616 | tf_op jit(solution)/shard_map/ppermute | solution.py:18
  74.2 7.3 %collective-permute-start.40 = (bf16[4,64,128]{2,1,0:T(8,128)(2,1)S(1)}, bf16[4,64,128]{2,1,0:T(8,128)(2,1)S(1)}, u32[]{:S(2)}, u32[]{:S(2)}) collective-permute-start(bf16[4,64,128]{2,1,0:T(8,128)(2,1)S(1)} %get-tuple-element.59), channel_id=1, source_target_pairs={{0,2},{1,3},{2,4},{3,5},{4,6},{5,7},{6,0},{7,1},{8,10},{9,11},{10,... | collective-permute-start | bytes 196616 | tf_op jit(solution)/shard_map/ppermute | solution.py:18
  76.8 4.8 %collective-permute-start.41 = (bf16[4,64,128]{2,1,0:T(8,128)(2,1)S(1)}, bf16[4,64,128]{2,1,0:T(8,128)(2,1)S(1)}, u32[]{:S(2)}, u32[]{:S(2)}) collective-permute-start(bf16[4,64,128]{2,1,0:T(8,128)(2,1)S(1)} %get-tuple-element.60), channel_id=1, source_target_pairs={{0,1},{1,2},{2,3},{3,4},{4,5},{5,6},{6,7},{7,0},{8,9},{9,10},{10,1... | collective-permute-start | bytes 196616 | tf_op jit(solution)/shard_map/ppermute | solution.py:18
  76.9 9.1 %collective-permute-start.31 = (bf16[64,256]{1,0:T(8,128)(2,1)S(1)}, bf16[64,256]{1,0:T(8,128)(2,1)S(1)}, u32[]{:S(2)}, u32[]{:S(2)}) collective-permute-start(bf16[64,256]{1,0:T(8,128)(2,1)S(1)} %shard_map.99.refs_0_), channel_id=1, source_target_pairs={{0,24},{8,0},{16,8},{24,16},{1,25},{9,1},{17,9},{25,17},{2,26},{10... | collective-permute-start | bytes 98312 | tf_op jit(solution)/shard_map/ppermute | solution.py:18
  79.2 6.9 %collective-permute-start.30 = (bf16[64,256]{1,0:T(8,128)(2,1)S(1)}, bf16[64,256]{1,0:T(8,128)(2,1)S(1)}, u32[]{:S(2)}, u32[]{:S(2)}) collective-permute-start(bf16[64,256]{1,0:T(8,128)(2,1)S(1)} %shard_map.99.refs_0_), channel_id=1, source_target_pairs={{0,16},{8,24},{16,0},{24,8},{1,17},{9,25},{17,1},{25,9},{2,18},{10... | collective-permute-start | bytes 98312 | tf_op jit(solution)/shard_map/ppermute | solution.py:18
  81.5 5.9 %collective-permute-start.29 = (bf16[64,256]{1,0:T(8,128)(2,1)S(1)}, bf16[64,256]{1,0:T(8,128)(2,1)S(1)}, u32[]{:S(2)}, u32[]{:S(2)}) collective-permute-start(bf16[64,256]{1,0:T(8,128)(2,1)S(1)} %shard_map.99.refs_0_), channel_id=1, source_target_pairs={{0,8},{8,16},{16,24},{24,0},{1,9},{9,17},{17,25},{25,1},{2,10},{10... | collective-permute-start | bytes 98312 | tf_op jit(solution)/shard_map/ppermute | solution.py:18
  81.7 6.4 %collective-permute-start.42 = (bf16[64,128]{1,0:T(8,128)(2,1)S(1)}, bf16[64,128]{1,0:T(8,128)(2,1)S(1)}, u32[]{:S(2)}, u32[]{:S(2)}) collective-permute-start(bf16[64,128]{1,0:T(8,128)(2,1)S(1)} %get-tuple-element.62), channel_id=1, source_target_pairs={{0,8},{8,16},{16,24},{24,0},{1,9},{9,17},{17,25},{25,1},{2,10},{10... | collective-permute-start | bytes 49160 | tf_op jit(solution)/shard_map/ppermute | solution.py:18
  82.9 5.2 %collective-permute-start.43 = (bf16[64,128]{1,0:T(8,128)(2,1)S(1)}, bf16[64,128]{1,0:T(8,128)(2,1)S(1)}, u32[]{:S(2)}, u32[]{:S(2)}) collective-permute-start(bf16[64,128]{1,0:T(8,128)(2,1)S(1)} %get-tuple-element.63), channel_id=1, source_target_pairs={{0,16},{8,24},{16,0},{24,8},{1,17},{9,25},{17,1},{25,9},{2,18},{10... | collective-permute-start | bytes 49160 | tf_op jit(solution)/shard_map/ppermute | solution.py:18
  86.0 3.7 %collective-permute-start.44 = (bf16[64,128]{1,0:T(8,128)(2,1)S(1)}, bf16[64,128]{1,0:T(8,128)(2,1)S(1)}, u32[]{:S(2)}, u32[]{:S(2)}) collective-permute-start(bf16[64,128]{1,0:T(8,128)(2,1)S(1)} %get-tuple-element.64), channel_id=1, source_target_pairs={{0,24},{8,0},{16,8},{24,16},{1,25},{9,1},{17,9},{25,17},{2,26},{10... | collective-permute-start | bytes 49160 | tf_op jit(solution)/shard_map/ppermute | solution.py:18
  (2 other events, 1.5 us)

commit v2 on v0

v2 whole, which is shorter than its diff:
```python
import functools

import jax
import jax.numpy as jnp
from jax import lax
from jax.experimental import pallas as pl
from jax.experimental.pallas import tpu as pltpu
from jax.sharding import PartitionSpec as P

F32 = jnp.float32
BF16 = jnp.bfloat16
VMEM = pl.BlockSpec(memory_space=pltpu.VMEM)
SMEM = pl.BlockSpec(memory_space=pltpu.SMEM)
PAD = 16


def shift(array, axis, by):
    peers = lax.axis_size(axis)
    return lax.ppermute(array, axis, [(i, (i + by) % peers) for i in range(peers)])


def exchange(array, axis):
    return lax.all_to_all(array, axis, 0, 0, tiled=True)


def call(body, outs, in_specs, scratch=(), flops=0, moved=0):
    return pl.pallas_call(
        body,
        out_shape=outs,
        in_specs=in_specs,
        out_specs=jax.tree.map(lambda _: VMEM, outs),
        scratch_shapes=list(scratch),
        compiler_params=pltpu.CompilerParams(vmem_limit_bytes=48 * 1024 * 1024),
        cost_estimate=pl.CostEstimate(flops=flops, bytes_accessed=moved, transcendentals=0),
    )


def split_features(reps, lists, cap, feats, rows, cols, counts, out):
    nodes = feats.shape[0]
    part = feats.shape[1] // reps
    turned = feats[...].astype(F32).T.astype(BF16)
    lane = lax.broadcasted_iota(jnp.int32, (PAD, nodes), 1)
    index = jnp.zeros((PAD, nodes), jnp.int32)
    slots = lists * cap
    for j in range(lists):
        for c in range(cap):
            k = j * cap + c
            index = jnp.where(lane == k, rows[j, c], index)
            index = jnp.where(lane == slots + k, cols[j, c], index)
        index = jnp.where(lane == 2 * slots + j, counts[j], index)
    index = index.astype(F32).astype(BF16)
    for q in range(reps):
        out[q, :part] = turned[q * part : (q + 1) * part]
        out[q, part:] = index


def spread(groups, part, mine, out):
    own = mine[:, :part]
    for g in range(groups):
        out[g] = own


def slot_of(index, lists, cap, t, j, c):
    k = j * cap + c
    slots = lists * cap
    return index[t, k], index[t, slots + k], c < index[t, 2 * slots + j]


def aggregate(reps, groups, lists, cap, index, *refs):
    blocks = refs[:reps]
    held, out, total = refs[reps:]
    me = lax.axis_index("rep")
    mine = lax.axis_index("blk")
    total[...] = jnp.zeros_like(total)
    for t in range(reps):
        origin = lax.rem(me + reps - t, reps)
        for j in range(lists):
            source = lax.rem(mine + groups - origin * lists - j, groups)
            for c in range(cap):
                row, col, live = slot_of(index, lists, cap, origin, j, c)
                product = lax.dot_general(
                    held[source, col],
                    blocks[t][j * cap + c],
                    (((1,), (1,)), ((), ())),
                    preferred_element_type=F32,
                )
                total[row] += jnp.where(live, product, 0.0)
    out[...] = total[...].astype(BF16)


def dense_layer(reps, agg, weight, cotangent, out, send):
    part = agg.shape[1]
    nodes = agg.shape[2]
    turned = agg[...].reshape(reps * part, nodes)
    pre = lax.dot_general(
        turned, weight[...], (((0,), (0,)), ((), ())), preferred_element_type=F32
    )
    sigma = jax.nn.sigmoid(pre)
    out[...] = (pre * sigma).astype(BF16)
    slope = sigma * (1.0 + pre * (1.0 - sigma))
    dpre = (cotangent[...].astype(F32) * slope).astype(BF16)
    dagg = lax.dot_general(
        weight[...], dpre, (((1,), (1,)), ((), ())), preferred_element_type=F32
    )
    send[:, :, :nodes] = dagg.astype(BF16).reshape(reps, part, nodes)
    terms = jnp.dot(turned, dpre, preferred_element_type=F32)
    send[:, :, nodes:] = terms.astype(BF16).reshape(reps, part, reps * part)


def feature_grads(reps, groups, lists, cap, index, *refs):
    blocks = refs[:reps]
    arrived, out, total = refs[reps:]
    nodes = blocks[0].shape[1]
    me = lax.axis_index("rep")
    mine = lax.axis_index("blk")
    total[...] = jnp.zeros_like(total)
    for t in range(reps):
        origin = lax.rem(me + reps - t, reps)
        for j in range(lists):
            target = lax.rem(mine + groups - origin * lists - j, groups)
            for c in range(cap):
                row, col, live = slot_of(index, lists, cap, origin, j, c)
                product = jnp.dot(
                    arrived[row, :, :nodes], blocks[t][j * cap + c], preferred_element_type=F32
                )
                total[target, col] += jnp.where(live, product, 0.0)
    terms = arrived[0, :, nodes:].astype(F32)
    for t in range(1, reps):
        terms += arrived[t, :, nodes:].astype(F32)
    terms = terms.astype(BF16)
    for g in range(groups):
        for b in range(reps):
            out[g, :, b * nodes : (b + 1) * nodes] = total[g, b].astype(BF16)
        out[g, :, reps * nodes :] = terms


def sum_groups(reps, groups, arrived, out):
    nodes = (arrived.shape[2] - out.shape[2]) // (reps - 1)
    total = arrived[0].astype(F32)
    for g in range(1, groups):
        total += arrived[g].astype(F32)
    total = total.astype(BF16)
    for b in range(reps):
        out[b, :, :nodes] = total[:, b * nodes : (b + 1) * nodes]
        out[b, :, nodes:] = total[:, reps * nodes :]


def finish(reps, arrived, grad_feats, grad_weight):
    part = arrived.shape[1]
    nodes = grad_feats.shape[0]
    turned = arrived[:, :, :nodes].astype(F32).reshape(reps * part, nodes)
    grad_feats[...] = turned.T
    grad_weight[...] = arrived[:, :, nodes:].astype(F32).reshape(reps * part, -1)


def per_device(feats, weight, cotangent, block_vals, block_rows, block_cols, step_counts):
    reps = lax.axis_size("rep")
    groups = lax.axis_size("blk")
    lists, cap, block = block_vals.shape[2:5]
    nodes, width = feats.shape
    part = width // reps
    like = jax.ShapeDtypeStruct
    slots = lists * cap
    blocks = block_vals.reshape(slots, block, block)

    quarters = call(
        functools.partial(split_features, reps, lists, cap),
        like((reps, part + PAD, nodes), BF16),
        [VMEM, SMEM, SMEM, SMEM],
        moved=4 * nodes * width,
    )(feats, block_rows[0, 0], block_cols[0, 0], step_counts[0, 0])
    quarters = exchange(quarters, "rep")
    all_blocks = [blocks] + [shift(blocks, "rep", t) for t in range(1, reps)]
    index = quarters[:, part, : 2 * slots + lists].astype(jnp.int32)

    held = call(
        functools.partial(spread, groups, part),
        like((groups, reps, part, nodes), BF16),
        [VMEM],
        moved=2 * (groups + 1) * nodes * width,
    )(quarters)
    held = exchange(held, "blk")
    slot_flops = 2 * groups * cap * part * block * block
    slot_bytes = 2 * (groups * cap * block * block + groups * nodes * width)

    agg = call(
        functools.partial(aggregate, reps, groups, lists, cap),
        like((reps, part, nodes), BF16),
        [SMEM] + [VMEM] * (reps + 1),
        [pltpu.VMEM((reps, part, nodes), F32)],
        flops=slot_flops,
        moved=slot_bytes,
    )(index, *all_blocks, held)
    agg = exchange(agg, "rep")

    out_rows, send = call(
        functools.partial(dense_layer, reps),
        [like((nodes, width), BF16), like((reps, part, nodes + width), BF16)],
        [VMEM] * 3,
        flops=6 * nodes * width * width,
        moved=14 * nodes * width,
    )(agg, weight, cotangent)
    arrived = exchange(send, "rep")

    grads = call(
        functools.partial(feature_grads, reps, groups, lists, cap),
        like((groups, part, reps * nodes + width), BF16),
        [SMEM] + [VMEM] * (reps + 1),
        [pltpu.VMEM((groups, reps, part, nodes), F32)],
        flops=slot_flops,
        moved=slot_bytes,
    )(index, *all_blocks, arrived)
    grads = exchange(grads, "blk")

    rows = call(
        functools.partial(sum_groups, reps, groups),
        like((reps, part, nodes + width), BF16),
        [VMEM],
        moved=3 * groups * nodes * width,
    )(grads)
    rows = exchange(rows, "rep")

    grad_feats, grad_weight = call(
        functools.partial(finish, reps),
        [like((nodes, width), F32), like((width, width), F32)],
        [VMEM],
        moved=12 * nodes * width,
    )(rows)
    return (out_rows, grad_weight, grad_feats)


def solution(mesh):
    return jax.shard_map(
        per_device,
        mesh=mesh,
        in_specs=(
            P(("blk", "rep"), None),
            P(),
            P(("blk", "rep"), None),
            P("blk", "rep", None, None, None, None),
            P("blk", "rep", None, None),
            P("blk", "rep", None, None),
            P("blk", "rep", None),
        ),
        out_specs=(P(("blk", "rep"), None), P(), P(("blk", "rep"), None)),
        check_vma=False,
    )
```

time: 260 us -> 87.6 us (0.34)
  waiting for transfers between devices: 191 us -> 17.5 us
  blocking collectives: 30.1 us -> 55.2 us
  between operations: 14 us -> 0.7 us
  matrix products: 7.97 us -> 0 us
  local copies, waits for them, and re-layouts: 8.28 us -> 1.53 us
  Pallas kernels: 0 us -> 5.48 us
    psum x1 -> x0, waiting for transfers between devices: 117 us -> none  [per_device(): grad_weight = lax.psum(weight_part, ('rep', 'blk'))]
    all_to_all x0 -> x5, blocking collectives: none -> 55.2 us  [exchange(): return lax.all_to_all(array, axis, 0, 0, tiled=True)]
    reduce_scatter x2 -> x0, waiting for transfers between devices: 45.9 us -> none  [the longest x1 23.6 us: per_device(): lax.psum_scatter(accumulator.reshape(-1, feat_width), 'rep', scatter_dime...]
    all_gather x2 -> x0, blocking collectives: 30.1 us -> none  [the longest x1 16 us: per_device(): gathered = lax.all_gather(feats, 'rep', axis=0, tiled=True)]
    ppermute x6 -> x3, waiting for transfers between devices: 28 us -> 17.5 us  [shift(): lax.ppermute(array, axis, [(i, (i + by) % peers) for i in range(peers)])]
    dot_general x11 -> x0, matrix products: 7.97 us -> none  [the longest x2 2.05 us: per_device(): jnp.einsum('kr,kif->rif', selector, products, precision=lax.Precision.HIG...]
    pallas_call x0 -> x7, Pallas kernels: none -> 5.48 us  [the longest x1 1.22 us: per_device(): call(functools.partial(aggregate, reps, groups, lists, cap), like((reps,...]
    all_to_all x0 -> x1, starting transfers between devices: none -> 3.85 us  [exchange(): return lax.all_to_all(array, axis, 0, 0, tiled=True)]
  transfers between devices with their start and end apart: 9 -> 4, of which waited for: 9 -> 2; matrix products, arithmetic and copies ran while one was open for 3% -> 0% of each run, Pallas kernels for 0% -> 0%
where the time goes in v2:
time: 87.6 us; the launch traced here: 87.2 us
  blocking collectives  55.2 us (63%)
  waiting for transfers between devices  17.5 us (20%)
  starting transfers between devices  6.72 us (8%)
  Pallas kernels  5.48 us (6%)
  local copies, waits for them, and re-layouts  1.53 us (2%)
    all_to_all x5, blocking collectives, exchange(): return lax.all_to_all(array, axis, 0, 0, tiled=True)  55.2 us
    ppermute x3, waiting for transfers between devices, shift(): lax.ppermute(array, axis, [(i, (i + by) % peers) for i in range(peers)])  17.5 us
    all_to_all x1, starting transfers between devices, exchange(): return lax.all_to_all(array, axis, 0, 0, tiled=True)  3.85 us
    ppermute x3, starting transfers between devices, shift(): lax.ppermute(array, axis, [(i, (i + by) % peers) for i in range(peers)])  2.86 us
  transfers between devices with their start and end apart: 4, of which 2 were waited for; matrix products, arithmetic and copies ran while one was open for 0% of the time, Pallas kernels for 0%

profile of v2, /device:TPU:0, one launch (start us, length us, event | category | flops | bytes accessed | tf_op | source)
XLA Modules:
  0.0 87.2 jit_solution(16499860149842080463)
XLA Ops:
  0.6 0.0 copy-start.5
  0.6 0.0 copy-start.4
  0.7 0.0 copy-start.6
  0.7 0.7 copy-done.5
  1.3 0.0 copy-done.4
  1.3 0.0 copy-done.6
  1.3 0.0 copy-start.2
  1.3 0.8 copy-done.2
  2.2 0.7 shard_map.94
  2.8 11.9 %all_to_all.30.mine = bf16[4,80,128]{2,1,0:T(8,128)(2,1)S(1)} all-to-all(bf16[4,80,128]{2,1,0:T(8,128)(2,1)S(1)} %shard_map.94), channel_id=1, replica_groups=mesh['rep'=4,'blk'=8] {'rep'}, dimensions={0} | all-to-all | bytes 163840 | tf_op jit(solution)/shard_map/all_to_all | solution.py:23
  14.7 0.9 shard_map.95
  15.6 0.0 copy-start
  15.6 3.9 %all-to-all-start.1 = ((bf16[8,4,64,128]{3,2,1,0:T(8,128)(2,1)}), bf16[8,4,64,128]{3,2,1,0:T(8,128)(2,1)S(1)}, u32[]{:S(2)}, u32[]{:S(2)}) async-start(bf16[8,4,64,128]{3,2,1,0:T(8,128)(2,1)} %shard_map.95), calls=%async_computation.1 | async-start | bytes 1048576 | tf_op jit(solution)/shard_map/all_to_all | solution.py:23
  19.5 0.0 copy-done
  19.5 0.9 %collective-permute-start.2 = (bf16[6,128,128]{2,1,0:T(8,128)(2,1)S(1)}, bf16[6,128,128]{2,1,0:T(8,128)(2,1)S(1)}, u32[]{:S(2)}, u32[]{:S(2)}) collective-permute-start(bf16[6,128,128]{2,1,0:T(8,128)(2,1)S(1)} %bitcast.5), channel_id=1, source_target_pairs={{0,24},{8,0},{16,8},{24,16},{1,25},{9,1},{17,9},{25,17},{2,26},{10... | collective-permute-start | bytes 589832 | tf_op jit(solution)/shard_map/ppermute | solution.py:19
  20.4 1.6 %collective-permute-start.1 = (bf16[6,128,128]{2,1,0:T(8,128)(2,1)S(1)}, bf16[6,128,128]{2,1,0:T(8,128)(2,1)S(1)}, u32[]{:S(2)}, u32[]{:S(2)}) collective-permute-start(bf16[6,128,128]{2,1,0:T(8,128)(2,1)S(1)} %bitcast.6), channel_id=1, source_target_pairs={{0,16},{8,24},{16,0},{24,8},{1,17},{9,25},{17,1},{25,9},{2,18},{10... | collective-permute-start | bytes 589832 | tf_op jit(solution)/shard_map/ppermute | solution.py:19
  22.0 0.3 collective-permute-start
  22.3 4.4 %collective-permute-done.2.refs_3_ = bf16[6,128,128]{2,1,0:T(8,128)(2,1)S(1)} collective-permute-done((bf16[6,128,128]{2,1,0:T(8,128)(2,1)S(1)}, bf16[6,128,128]{2,1,0:T(8,128)(2,1)S(1)}, u32[]{:S(2)}, u32[]{:S(2)}) %collective-permute-start.2) | collective-permute-done | bytes 196640 | tf_op jit(solution)/shard_map/ppermute | solution.py:19
  26.8 13.1 %collective-permute-done.1.refs_2_ = bf16[6,128,128]{2,1,0:T(8,128)(2,1)S(1)} collective-permute-done((bf16[6,128,128]{2,1,0:T(8,128)(2,1)S(1)}, bf16[6,128,128]{2,1,0:T(8,128)(2,1)S(1)}, u32[]{:S(2)}, u32[]{:S(2)}) %collective-permute-start.1) | collective-permute-done | bytes 196640 | tf_op jit(solution)/shard_map/ppermute | solution.py:19
  39.9 0.0 collective-permute-done.refs_1_
  39.9 0.0 all-to-all-done.1.refs_4_
  39.9 0.0 copy-start.3
  39.9 1.2 %shard_map.96 = bf16[4,64,128]{2,1,0:T(8,128)(2,1)S(1)} custom-call(s32[4,14]{1,0:T(4,128)S(1)} %bitcast.10, bf16[6,128,128]{2,1,0:T(8,128)(2,1)S(1)} %bitcast.8, bf16[6,128,128]{2,1,0:T(8,128)(2,1)S(1)} %collective-permute-done.refs_1_, bf16[6,128,128]{2,1,0:T(8,128)(2,1)S(1)} %collective-permute-done.1.refs_2_, ...), custom_call_target="tpu_custom_call" | custom-call | flops 50331648 | bytes 1310720 | tf_op jit(solution)/shard_map/pallas_call | solution.py:186
  41.1 0.0 copy-start.1
  41.1 8.3 %all_to_all.31.agg = bf16[4,64,128]{2,1,0:T(8,128)(2,1)S(1)} all-to-all(bf16[4,64,128]{2,1,0:T(8,128)(2,1)S(1)} %shard_map.96), channel_id=1, replica_groups=mesh['rep'=4,'blk'=8] {'rep'}, dimensions={0} | all-to-all | bytes 131072 | tf_op jit(solution)/shard_map/all_to_all | solution.py:23
  49.4 0.0 copy-done.3
  49.4 0.0 copy-done.1
  49.4 0.8 shard_map.97
  50.3 9.2 %all_to_all.32.refs_4_ = bf16[4,64,384]{2,1,0:T(8,128)(2,1)S(1)} all-to-all(bf16[4,64,384]{2,1,0:T(8,128)(2,1)S(1)} %get-tuple-element.8), channel_id=1, replica_groups=mesh['rep'=4,'blk'=8] {'rep'}, dimensions={0} | all-to-all | bytes 393216 | tf_op jit(solution)/shard_map/all_to_all | solution.py:23
  59.4 1.0 %shard_map.98 = bf16[8,64,768]{2,1,0:T(8,128)(2,1)S(1)} custom-call(s32[4,14]{1,0:T(4,128)S(1)} %bitcast.11, bf16[6,128,128]{2,1,0:T(8,128)(2,1)S(1)} %bitcast.9, bf16[6,128,128]{2,1,0:T(8,128)(2,1)S(1)} %collective-permute-done.refs_1_, bf16[6,128,128]{2,1,0:T(8,128)(2,1)S(1)} %collective-permute-done.1.refs_2_, ...), custom_call_target="tpu_custom_call" | custom-call | flops 50331648 | bytes 1310720 | tf_op jit(solution)/shard_map/pallas_call | solution.py:205
  60.4 16.2 %all_to_all.33.arrived = bf16[8,64,768]{2,1,0:T(8,128)(2,1)S(1)} all-to-all(bf16[8,64,768]{2,1,0:T(8,128)(2,1)S(1)} %shard_map.98), channel_id=1, replica_groups=mesh['rep'=4,'blk'=8] {'blk'}, dimensions={0} | all-to-all | bytes 1572864 | tf_op jit(solution)/shard_map/all_to_all | solution.py:23
  76.6 0.1 shard_map.99
  76.7 9.7 %all_to_all.34.arrived = bf16[4,64,384]{2,1,0:T(8,128)(2,1)S(1)} all-to-all(bf16[4,64,384]{2,1,0:T(8,128)(2,1)S(1)} %shard_map.99), channel_id=1, replica_groups=mesh['rep'=4,'blk'=8] {'rep'}, dimensions={0} | all-to-all | bytes 393216 | tf_op jit(solution)/shard_map/all_to_all | solution.py:23
  86.4 0.8 shard_map.100
  (1 shorter events, 0.0 us)
Async XLA Ops:
  0.6 0.7 copy-start.5
  0.6 0.7 copy-start.4
  0.7 0.7 copy-start.6
  1.3 0.8 copy-start.2
  15.6 3.9 %copy-start = (bf16[1,1,2,3,128,128]{5,4,3,2,1,0:T(8,128)(2,1)S(1)}, bf16[1,1,2,3,128,128]{5,4,3,2,1,0:T(8,128)(2,1)}, u32[]{:S(2)}) copy-start(bf16[1,1,2,3,128,128]{5,4,3,2,1,0:T(8,128)(2,1)} %param.10) | copy-start | bytes 589828
  15.6 24.3 %all-to-all-start.1 = ((bf16[8,4,64,128]{3,2,1,0:T(8,128)(2,1)}), bf16[8,4,64,128]{3,2,1,0:T(8,128)(2,1)S(1)}, u32[]{:S(2)}, u32[]{:S(2)}) async-start(bf16[8,4,64,128]{3,2,1,0:T(8,128)(2,1)} %shard_map.95), calls=%async_computation.1 | async-start | bytes 1048576 | tf_op jit(solution)/shard_map/all_to_all | solution.py:23
  19.5 7.3 %collective-permute-start.2 = (bf16[6,128,128]{2,1,0:T(8,128)(2,1)S(1)}, bf16[6,128,128]{2,1,0:T(8,128)(2,1)S(1)}, u32[]{:S(2)}, u32[]{:S(2)}) collective-permute-start(bf16[6,128,128]{2,1,0:T(8,128)(2,1)S(1)} %bitcast.5), channel_id=1, source_target_pairs={{0,24},{8,0},{16,8},{24,16},{1,25},{9,1},{17,9},{25,17},{2,26},{10... | collective-permute-start | bytes 589832 | tf_op jit(solution)/shard_map/ppermute | solution.py:19
  20.4 19.5 %collective-permute-start.1 = (bf16[6,128,128]{2,1,0:T(8,128)(2,1)S(1)}, bf16[6,128,128]{2,1,0:T(8,128)(2,1)S(1)}, u32[]{:S(2)}, u32[]{:S(2)}) collective-permute-start(bf16[6,128,128]{2,1,0:T(8,128)(2,1)S(1)} %bitcast.6), channel_id=1, source_target_pairs={{0,16},{8,24},{16,0},{24,8},{1,17},{9,25},{17,1},{25,9},{2,18},{10... | collective-permute-start | bytes 589832 | tf_op jit(solution)/shard_map/ppermute | solution.py:19
  22.0 17.9 %collective-permute-start = (bf16[6,128,128]{2,1,0:T(8,128)(2,1)S(1)}, bf16[6,128,128]{2,1,0:T(8,128)(2,1)S(1)}, u32[]{:S(2)}, u32[]{:S(2)}) collective-permute-start(bf16[6,128,128]{2,1,0:T(8,128)(2,1)S(1)} %bitcast.7), channel_id=1, source_target_pairs={{0,8},{8,16},{16,24},{24,0},{1,9},{9,17},{17,25},{25,1},{2,10},{10... | collective-permute-start | bytes 589832 | tf_op jit(solution)/shard_map/ppermute | solution.py:19
  39.9 9.6 %copy-start.3 = (bf16[128,256]{1,0:T(8,128)(2,1)S(1)}, bf16[128,256]{1,0:T(8,128)(2,1)}, u32[]{:S(2)}) copy-start(bf16[128,256]{1,0:T(8,128)(2,1)} %cotangent.1) | copy-start | bytes 196612
  41.1 8.3 %copy-start.1 = (bf16[256,256]{1,0:T(8,128)(2,1)S(1)}, bf16[256,256]{1,0:T(8,128)(2,1)}, u32[]{:S(2)}) copy-start(bf16[256,256]{1,0:T(8,128)(2,1)} %weight.1) | copy-start | bytes 393220

commit v3 on v2

v3 whole, which is shorter than its diff:
```python
import functools

import jax
import jax.numpy as jnp
from jax import lax
from jax.experimental import pallas as pl
from jax.experimental.pallas import tpu as pltpu
from jax.sharding import PartitionSpec as P

F32 = jnp.float32
BF16 = jnp.bfloat16
VMEM = pl.BlockSpec(memory_space=pltpu.VMEM)
SMEM = pl.BlockSpec(memory_space=pltpu.SMEM)
PAD = 16


def shift(array, by):
    peers = lax.axis_size("rep")
    return lax.ppermute(array, "rep", [(i, (i + by) % peers) for i in range(peers)])


def swap(array, bit):
    peers = lax.axis_size("blk")
    return lax.ppermute(array, "blk", [(i, i ^ bit) for i in range(peers)])


def call(body, outs, in_specs, scratch=(), flops=0, moved=0):
    return pl.pallas_call(
        body,
        out_shape=outs,
        in_specs=in_specs,
        out_specs=jax.tree.map(lambda _: VMEM, outs),
        scratch_shapes=list(scratch),
        compiler_params=pltpu.CompilerParams(vmem_limit_bytes=48 * 1024 * 1024),
        cost_estimate=pl.CostEstimate(flops=flops, bytes_accessed=moved, transcendentals=0),
    )


def dot(a, b, a_dim, b_dim):
    return lax.dot_general(a, b, (((a_dim,), (b_dim,)), ((), ())), preferred_element_type=F32)


def member_and(by, reps):
    return lax.rem(lax.axis_index("rep") + by, reps)


def split_features(reps, lists, cap, feats, rows, cols, counts, *rest):
    outs, turned = rest[:-1], rest[-1]
    nodes = feats.shape[0]
    part = feats.shape[1] // reps
    turned[...] = feats[...].astype(F32).T.astype(BF16).reshape(turned.shape)
    lane = lax.broadcasted_iota(jnp.int32, (PAD, nodes), 1)
    index = jnp.zeros((PAD, nodes), jnp.int32)
    slots = lists * cap
    for j in range(lists):
        for c in range(cap):
            k = j * cap + c
            index = jnp.where(lane == k, rows[j, c], index)
            index = jnp.where(lane == slots + k, cols[j, c], index)
        index = jnp.where(lane == 2 * slots + j, counts[j], index)
    index = index.astype(F32).astype(BF16)
    for t in range(reps):
        outs[t][:part] = turned[member_and(t, reps)]
        outs[t][part:] = index


def order_chunks(reps, part, *refs):
    chunks, mine, index = refs[:reps], refs[reps], refs[reps + 1]
    for t in range(reps):
        origin = member_and(reps - t, reps)
        mine[0, origin] = chunks[t][:part]
        index[origin] = chunks[t][part:].astype(F32).astype(jnp.int32)


def join(first, second, out):
    half = first.shape[0]
    out[:half] = first[...]
    out[half:] = second[...]


def slot_of(index, lists, cap, t, j, c):
    k = j * cap + c
    slots = lists * cap
    return index[t, 0, k], index[t, 0, slots + k], c < index[t, 0, 2 * slots + j]


def relative(groups, lists, origin, j):
    mine = lax.axis_index("blk")
    return lax.bitwise_xor(mine, lax.rem(mine + groups - origin * lists - j, groups))


def aggregate(reps, groups, lists, cap, index, *refs):
    blocks = refs[:reps]
    near, far, out, held, total = refs[reps:]
    half = groups // 2
    held[0] = near[...]
    held[1] = far[...]
    total[...] = jnp.zeros_like(total)
    for t in range(reps):
        origin = member_and(reps - t, reps)
        for j in range(lists):
            place = relative(groups, lists, origin, j)
            for c in range(cap):
                row, col, live = slot_of(index, lists, cap, origin, j, c)
                source = held[lax.rem(place, 2), lax.div(place, 2), col]
                product = dot(source, blocks[t][j * cap + c], 1, 1)
                total[row] += jnp.where(live, product, 0.0)
    out[...] = total[...].astype(BF16)


def dense_and_back(reps, groups, lists, cap, index, *refs):
    blocks = refs[:reps]
    chunks = refs[reps : 2 * reps]
    cotangents = refs[2 * reps : 3 * reps]
    weight, out, keep, send = refs[3 * reps : 3 * reps + 4]
    agg, cot, outs, dagg, total = refs[3 * reps + 4 :]
    nodes, width = out.shape
    me = lax.axis_index("rep")
    half = groups // 2
    for t in range(reps):
        origin = member_and(reps - t, reps)
        cot[origin] = cotangents[t][...]
        for b in range(reps):
            agg[b, origin] = chunks[t][b]
    total[...] = jnp.zeros_like(total)
    gw = jnp.zeros((width, width), F32)
    for b in range(reps):
        turned = agg[b].reshape(width, nodes)
        pre = dot(turned, weight[...], 0, 0)
        sigma = jax.nn.sigmoid(pre)
        outs[b] = (pre * sigma).astype(BF16)
        slope = sigma * (1.0 + pre * (1.0 - sigma))
        dpre = (cot[b].astype(F32) * slope).astype(BF16)
        dagg[b] = dot(dpre, weight[...], 1, 1).astype(BF16)
        gw += dot(turned, dpre, 1, 0)
    out[...] = outs[me]
    gw = gw.astype(BF16).reshape(-1, nodes, width)
    keep[half:] = gw.astype(F32)
    send[half:] = gw
    for t in range(reps):
        origin = member_and(reps - t, reps)
        for j in range(lists):
            place = relative(groups, lists, origin, j)
            for c in range(cap):
                row, col, live = slot_of(index, lists, cap, origin, j, c)

                @pl.when(jnp.logical_and(live, col == me))
                def _():
                    total[lax.rem(place, 2), lax.div(place, 2)] += dot(
                        blocks[t][j * cap + c], dagg[row], 0, 0
                    )

    keep[:half] = total[0]
    send[:half] = total[1].astype(BF16)


def add_and_halve(half, keep, arrived, next_keep, next_send):
    next_keep[:half] = keep[:half] + arrived[:half].astype(F32)
    next_send[:half] = (keep[half : 2 * half] + arrived[half : 2 * half].astype(F32)).astype(BF16)
    gw = (keep[2 * half :] + arrived[2 * half :].astype(F32)).astype(BF16)
    next_keep[half:] = gw.astype(F32)
    next_send[half:] = gw


def finish(keep, arrived, grad_feats, grad_weight):
    total = keep[...] + arrived[...].astype(F32)
    grad_feats[...] = total[0]
    grad_weight[...] = total[1:].reshape(grad_weight.shape)


def per_device(feats, weight, cotangent, block_vals, block_rows, block_cols, step_counts):
    reps = lax.axis_size("rep")
    groups = lax.axis_size("blk")
    lists, cap, block = block_vals.shape[2:5]
    nodes, width = feats.shape
    part = width // reps
    extra = width // nodes
    like = jax.ShapeDtypeStruct
    blocks = block_vals.reshape(lists * cap, block, block)

    def over_rep(arrays):
        return [arrays[0]] + [shift(arrays[t], t) for t in range(1, reps)]

    all_blocks = over_rep([blocks] * reps)
    chunks = call(
        functools.partial(split_features, reps, lists, cap),
        [like((part + PAD, nodes), BF16)] * reps,
        [VMEM, SMEM, SMEM, SMEM],
        [pltpu.VMEM((reps, part, nodes), BF16)],
        moved=4 * nodes * width,
    )(feats, block_rows[0, 0], block_cols[0, 0], step_counts[0, 0])
    near, index = call(
        functools.partial(order_chunks, reps, part),
        [like((1, reps, part, nodes), BF16), like((reps, PAD, nodes), jnp.int32)],
        [VMEM] * reps,
        moved=4 * nodes * width,
    )(*over_rep(chunks))
    all_cotangents = over_rep([cotangent] * reps)

    bit = 2
    while bit < groups:
        near = call(
            join,
            like((2 * near.shape[0],) + near.shape[1:], BF16),
            [VMEM] * 2,
            moved=8 * near.size,
        )(near, swap(near, bit))
        bit *= 2
    far = swap(near, 1)
    slot_flops = 2 * groups * cap * part * block * block
    slot_bytes = 2 * (groups * cap * block * block + groups * nodes * width)

    agg = call(
        functools.partial(aggregate, reps, groups, lists, cap),
        like((reps, part, nodes), BF16),
        [SMEM] + [VMEM] * (reps + 2),
        [
            pltpu.VMEM((2, groups // 2, reps, part, nodes), BF16),
            pltpu.VMEM((reps, part, nodes), F32),
        ],
        flops=slot_flops,
        moved=slot_bytes,
    )(index, *all_blocks, near, far)
    aggs = over_rep([agg] * reps)

    half = groups // 2
    out_rows, keep, send = call(
        functools.partial(dense_and_back, reps, groups, lists, cap),
        [
            like((nodes, width), BF16),
            like((half + extra, nodes, width), F32),
            like((half + extra, nodes, width), BF16),
        ],
        [SMEM] + [VMEM] * (3 * reps + 1),
        [
            pltpu.VMEM((reps, reps, part, nodes), BF16),
            pltpu.VMEM((reps, nodes, width), BF16),
            pltpu.VMEM((reps, nodes, width), BF16),
            pltpu.VMEM((reps, nodes, width), BF16),
            pltpu.VMEM((2, half, nodes, width), F32),
        ],
        flops=slot_flops + 6 * reps * nodes * width * width,
        moved=2 * slot_bytes,
    )(index, *all_blocks, *aggs, *all_cotangents, weight)
    arrived = swap(send, 1)
    bit = groups // 2
    while bit > 1:
        half = half // 2
        keep, send = call(
            functools.partial(add_and_halve, half),
            [
                like((half + extra, nodes, width), F32),
                like((half + extra, nodes, width), BF16),
            ],
            [VMEM] * 2,
            moved=12 * (half + extra) * nodes * width,
        )(keep, arrived)
        arrived = swap(send, bit)
        bit = bit // 2

    grad_feats, grad_weight = call(
        finish,
        [like((nodes, width), F32), like((width, width), F32)],
        [VMEM] * 2,
        moved=30 * nodes * width,
    )(keep, arrived)
    return (out_rows, grad_weight, grad_feats)


def solution(mesh):
    return jax.shard_map(
        per_device,
        mesh=mesh,
        in_specs=(
            P(("blk", "rep"), None),
            P(),
            P(("blk", "rep"), None),
            P("blk", "rep", None, None, None, None),
            P("blk", "rep", None, None),
            P("blk", "rep", None, None),
            P("blk", "rep", None),
        ),
        out_specs=(P(("blk", "rep"), None), P(), P(("blk", "rep"), None)),
        check_vma=False,
    )
```

time: 87.6 us -> 78.2 us (0.89)
  blocking collectives: 55.2 us -> 0 us
  waiting for transfers between devices: 17.5 us -> 45.2 us
  starting transfers between devices: 6.72 us -> 23.5 us
  Pallas kernels: 5.48 us -> 7.56 us
    all_to_all x5 -> x0, blocking collectives: 55.2 us -> none  [exchange(): return lax.all_to_all(array, axis, 0, 0, tiled=True)]
    ppermute x3 -> x18, waiting for transfers between devices: 17.5 us -> 45.2 us  [the longest x12 25 us: shift(): lax.ppermute(array, 'rep', [(i, (i + by) % peers) for i in range(peers)])]
    ppermute x3 -> x18, starting transfers between devices: 2.86 us -> 23.5 us  [the longest x12 17.2 us: shift(): lax.ppermute(array, 'rep', [(i, (i + by) % peers) for i in range(peers)])]
    all_to_all x1 -> x0, starting transfers between devices: 3.85 us -> none  [exchange(): return lax.all_to_all(array, axis, 0, 0, tiled=True)]
    pallas_call x6 -> x8, Pallas kernels: 4.26 us -> 5.84 us  [the longest x1 4.19 us: per_device(): call(functools.partial(dense_and_back, reps, groups, lists, cap), [like((...]
  transfers between devices with their start and end apart: 4 -> 18, of which waited for: 2 -> 12; matrix products, arithmetic and copies ran while one was open for 0% -> 0% of each run, Pallas kernels for 0% -> 2%
where the time goes in v3:
time: 78.2 us; the launch traced here: 78.5 us
  waiting for transfers between devices  45.2 us (58%)
  starting transfers between devices  23.5 us (30%)
  Pallas kernels  7.56 us (10%)
  local copies, waits for them, and re-layouts  1.53 us (2%)
    ppermute x12, waiting for transfers between devices, shift(): lax.ppermute(array, 'rep', [(i, (i + by) % peers) for i in range(peers)])  25 us
    ppermute x6, waiting for transfers between devices, swap(): return lax.ppermute(array, 'blk', [(i, i ^ bit) for i in range(peers)])  20.2 us
    ppermute x12, starting transfers between devices, shift(): lax.ppermute(array, 'rep', [(i, (i + by) % peers) for i in range(peers)])  17.2 us
    ppermute x6, starting transfers between devices, swap(): return lax.ppermute(array, 'blk', [(i, i ^ bit) for i in range(peers)])  6.24 us
    pallas_call x1, Pallas kernels, per_device(): call(functools.partial(dense_and_back, reps, groups, lists, cap), [like((...  4.19 us
    pallas_call x1, Pallas kernels, per_device(): call(functools.partial(aggregate, reps, groups, lists, cap), like((reps,...  1.72 us
  transfers between devices with their start and end apart: 18, of which 12 were waited for; matrix products, arithmetic and copies ran while one was open for 0% of the time, Pallas kernels for 2%

profile of v3, /device:TPU:0, one launch (start us, length us, event | category | flops | bytes accessed | tf_op | source)
XLA Modules:
  0.0 78.5 jit_solution(17444871816108471864)
XLA Ops:
  0.7 0.7 copy-done.5
  1.3 0.0 copy-done.4
  1.3 0.8 %copy-done.3 = bf16[128,256]{1,0:T(8,128)(2,1)S(1)} copy-done((bf16[128,256]{1,0:T(8,128)(2,1)S(1)}, bf16[128,256]{1,0:T(8,128)(2,1)}, u32[]{:S(2)}) %copy-start.3) | copy-done | bytes 65560
  2.2 0.7 shard_map.94
  2.9 3.1 %collective-permute-start = (bf16[80,128]{1,0:T(8,128)(2,1)S(1)}, bf16[80,128]{1,0:T(8,128)(2,1)S(1)}, u32[]{:S(2)}, u32[]{:S(2)}) collective-permute-start(bf16[80,128]{1,0:T(8,128)(2,1)S(1)} %get-tuple-element.19), channel_id=1, source_target_pairs={{0,8},{8,16},{16,24},{24,0},{1,9},{9,17},{17,25},{25,1},{2,10},{10... | collective-permute-start | bytes 61448 | tf_op jit(solution)/shard_map/ppermute | solution.py:19
  5.9 2.6 %collective-permute-start.1 = (bf16[80,128]{1,0:T(8,128)(2,1)S(1)}, bf16[80,128]{1,0:T(8,128)(2,1)S(1)}, u32[]{:S(2)}, u32[]{:S(2)}) collective-permute-start(bf16[80,128]{1,0:T(8,128)(2,1)S(1)} %get-tuple-element.20), channel_id=1, source_target_pairs={{0,16},{8,24},{16,0},{24,8},{1,17},{9,25},{17,1},{25,9},{2,18},{10... | collective-permute-start | bytes 61448 | tf_op jit(solution)/shard_map/ppermute | solution.py:19
  8.5 1.3 %collective-permute-start.2 = (bf16[80,128]{1,0:T(8,128)(2,1)S(1)}, bf16[80,128]{1,0:T(8,128)(2,1)S(1)}, u32[]{:S(2)}, u32[]{:S(2)}) collective-permute-start(bf16[80,128]{1,0:T(8,128)(2,1)S(1)} %get-tuple-element.21), channel_id=1, source_target_pairs={{0,24},{8,0},{16,8},{24,16},{1,25},{9,1},{17,9},{25,17},{2,26},{10... | collective-permute-start | bytes 61448 | tf_op jit(solution)/shard_map/ppermute | solution.py:19
  9.9 0.0 collective-permute-done.refs_1_
  9.9 0.9 %collective-permute-done.1.refs_2_ = bf16[80,128]{1,0:T(8,128)(2,1)S(1)} collective-permute-done((bf16[80,128]{1,0:T(8,128)(2,1)S(1)}, bf16[80,128]{1,0:T(8,128)(2,1)S(1)}, u32[]{:S(2)}, u32[]{:S(2)}) %collective-permute-start.1) | collective-permute-done | bytes 20512 | tf_op jit(solution)/shard_map/ppermute | solution.py:19
  10.8 1.5 %collective-permute-done.2.refs_3_ = bf16[80,128]{1,0:T(8,128)(2,1)S(1)} collective-permute-done((bf16[80,128]{1,0:T(8,128)(2,1)S(1)}, bf16[80,128]{1,0:T(8,128)(2,1)S(1)}, u32[]{:S(2)}, u32[]{:S(2)}) %collective-permute-start.2) | collective-permute-done | bytes 20512 | tf_op jit(solution)/shard_map/ppermute | solution.py:19
  12.3 1.6 %collective-permute-start.6 = (bf16[1,4,64,128]{3,2,1,0:T(8,128)(2,1)S(1)}, bf16[1,4,64,128]{3,2,1,0:T(8,128)(2,1)S(1)}, u32[]{:S(2)}, u32[]{:S(2)}) collective-permute-start(bf16[1,4,64,128]{3,2,1,0:T(8,128)(2,1)S(1)} %get-tuple-element.23.first), channel_id=1, source_target_pairs={{0,2},{1,3},{2,0},{3,1},{4,6},{5,7},{6,4},{7,5},{8,10},{9,11},{10,... | collective-permute-start | bytes 196616 | tf_op jit(solution)/shard_map/ppermute | solution.py:24
  13.9 2.8 %collective-permute-done.6.second = bf16[1,4,64,128]{3,2,1,0:T(8,128)(2,1)S(1)} collective-permute-done((bf16[1,4,64,128]{3,2,1,0:T(8,128)(2,1)S(1)}, bf16[1,4,64,128]{3,2,1,0:T(8,128)(2,1)S(1)}, u32[]{:S(2)}, u32[]{:S(2)}) %collective-permute-start.6) | collective-permute-done | bytes 65568 | tf_op jit(solution)/shard_map/ppermute | solution.py:24
  16.7 0.0 copy-start
  16.7 0.0 copy-start.2
  16.7 1.6 %collective-permute-start.7 = (bf16[2,4,64,128]{3,2,1,0:T(8,128)(2,1)S(1)}, bf16[2,4,64,128]{3,2,1,0:T(8,128)(2,1)S(1)}, u32[]{:S(2)}, u32[]{:S(2)}) collective-permute-start(bf16[2,4,64,128]{3,2,1,0:T(8,128)(2,1)S(1)} %shard_map.96.first), channel_id=1, source_target_pairs={{0,4},{1,5},{2,6},{3,7},{4,0},{5,1},{6,2},{7,3},{8,12},{9,13},{10,... | collective-permute-start | bytes 393224 | tf_op jit(solution)/shard_map/ppermute | solution.py:24
  18.3 3.4 %collective-permute-done.7.second = bf16[2,4,64,128]{3,2,1,0:T(8,128)(2,1)S(1)} collective-permute-done((bf16[2,4,64,128]{3,2,1,0:T(8,128)(2,1)S(1)}, bf16[2,4,64,128]{3,2,1,0:T(8,128)(2,1)S(1)}, u32[]{:S(2)}, u32[]{:S(2)}) %collective-permute-start.7) | collective-permute-done | bytes 131104 | tf_op jit(solution)/shard_map/ppermute | solution.py:24
  21.7 0.1 collective-permute-start.8
  21.8 3.2 %collective-permute-start.5 = (bf16[6,128,128]{2,1,0:T(8,128)(2,1)S(1)}, bf16[6,128,128]{2,1,0:T(8,128)(2,1)S(1)}, u32[]{:S(2)}, u32[]{:S(2)}) collective-permute-start(bf16[6,128,128]{2,1,0:T(8,128)(2,1)S(1)} %bitcast.4), channel_id=1, source_target_pairs={{0,24},{8,0},{16,8},{24,16},{1,25},{9,1},{17,9},{25,17},{2,26},{10... | collective-permute-start | bytes 589832 | tf_op jit(solution)/shard_map/ppermute | solution.py:19
  25.0 0.0 collective-permute-start.4
  25.0 0.7 collective-permute-start.3
  25.7 2.3 %collective-permute-start.13 = (bf16[128,256]{1,0:T(8,128)(2,1)S(1)}, bf16[128,256]{1,0:T(8,128)(2,1)S(1)}, u32[]{:S(2)}, u32[]{:S(2)}) collective-permute-start(bf16[128,256]{1,0:T(8,128)(2,1)S(1)} %copy-done.2), channel_id=1, source_target_pairs={{0,16},{8,24},{16,0},{24,8},{1,17},{9,25},{17,1},{25,9},{2,18},{10... | collective-permute-start | bytes 196616 | tf_op jit(solution)/shard_map/ppermute | solution.py:19
  28.0 3.1 %collective-permute-done.5.refs_3_ = bf16[6,128,128]{2,1,0:T(8,128)(2,1)S(1)} collective-permute-done((bf16[6,128,128]{2,1,0:T(8,128)(2,1)S(1)}, bf16[6,128,128]{2,1,0:T(8,128)(2,1)S(1)}, u32[]{:S(2)}, u32[]{:S(2)}) %collective-permute-start.5) | collective-permute-done | bytes 196640 | tf_op jit(solution)/shard_map/ppermute | solution.py:19
  31.0 0.0 collective-permute-start.12
  31.0 13.9 %collective-permute-done.4.refs_2_ = bf16[6,128,128]{2,1,0:T(8,128)(2,1)S(1)} collective-permute-done((bf16[6,128,128]{2,1,0:T(8,128)(2,1)S(1)}, bf16[6,128,128]{2,1,0:T(8,128)(2,1)S(1)}, u32[]{:S(2)}, u32[]{:S(2)}) %collective-permute-start.4) | collective-permute-done | bytes 196640 | tf_op jit(solution)/shard_map/ppermute | solution.py:19
  45.0 0.0 collective-permute-start.14
  45.0 0.0 collective-permute-done.3.refs_1_
  45.0 0.0 collective-permute-done.8.refs_5_
  45.0 0.0 copy-start.1
  45.0 1.7 %shard_map.98.refs_4_ = bf16[4,64,128]{2,1,0:T(8,128)(2,1)S(1)} custom-call(s32[4,16,128]{2,1,0:T(8,128)S(1)} %get-tuple-element.22.index, bf16[6,128,128]{2,1,0:T(8,128)(2,1)S(1)} %bitcast.7, bf16[6,128,128]{2,1,0:T(8,128)(2,1)S(1)} %collective-permute-done.3.refs_1_, bf16[6,128,128]{2,1,0:T(8,128)(2,1)S(1)} %collective-permute-done.4.refs_2_, ...), custom_call_target="tpu_custom_call" | custom-call | flops 50331648 | bytes 1310720 | tf_op jit(solution)/shard_map/pallas_call | solution.py:213
  46.7 1.0 %collective-permute-start.11 = (bf16[4,64,128]{2,1,0:T(8,128)(2,1)S(1)}, bf16[4,64,128]{2,1,0:T(8,128)(2,1)S(1)}, u32[]{:S(2)}, u32[]{:S(2)}) collective-permute-start(bf16[4,64,128]{2,1,0:T(8,128)(2,1)S(1)} %shard_map.98.refs_4_), channel_id=1, source_target_pairs={{0,24},{8,0},{16,8},{24,16},{1,25},{9,1},{17,9},{25,17},{2,26},{10... | collective-permute-start | bytes 196616 | tf_op jit(solution)/shard_map/ppermute | solution.py:19
  47.8 2.5 %collective-permute-start.10 = (bf16[4,64,128]{2,1,0:T(8,128)(2,1)S(1)}, bf16[4,64,128]{2,1,0:T(8,128)(2,1)S(1)}, u32[]{:S(2)}, u32[]{:S(2)}) collective-permute-start(bf16[4,64,128]{2,1,0:T(8,128)(2,1)S(1)} %shard_map.98.refs_4_), channel_id=1, source_target_pairs={{0,16},{8,24},{16,0},{24,8},{1,17},{9,25},{17,1},{25,9},{2,18},{10... | collective-permute-start | bytes 196616 | tf_op jit(solution)/shard_map/ppermute | solution.py:19
  50.3 0.0 collective-permute-done.13.refs_10_
  50.3 0.5 collective-permute-start.9
  50.8 0.0 collective-permute-done.12.refs_9_
  50.8 0.0 collective-permute-done.14.refs_11_
  50.8 0.4 collective-permute-done.11.refs_7_
  51.2 3.4 %collective-permute-done.10.refs_6_ = bf16[4,64,128]{2,1,0:T(8,128)(2,1)S(1)} collective-permute-done((bf16[4,64,128]{2,1,0:T(8,128)(2,1)S(1)}, bf16[4,64,128]{2,1,0:T(8,128)(2,1)S(1)}, u32[]{:S(2)}, u32[]{:S(2)}) %collective-permute-start.10) | collective-permute-done | bytes 65568 | tf_op jit(solution)/shard_map/ppermute | solution.py:19
  54.6 1.7 %collective-permute-done.9.refs_5_ = bf16[4,64,128]{2,1,0:T(8,128)(2,1)S(1)} collective-permute-done((bf16[4,64,128]{2,1,0:T(8,128)(2,1)S(1)}, bf16[4,64,128]{2,1,0:T(8,128)(2,1)S(1)}, u32[]{:S(2)}, u32[]{:S(2)}) %collective-permute-start.9) | collective-permute-done | bytes 65568 | tf_op jit(solution)/shard_map/ppermute | solution.py:19
  56.3 4.2 %shard_map.99 = (bf16[128,256]{1,0:T(8,128)(2,1)}, f32[6,128,256]{2,1,0:T(8,128)S(1)}, bf16[6,128,256]{2,1,0:T(8,128)(2,1)S(1)}) custom-call(s32[4,16,128]{2,1,0:T(8,128)S(1)} %get-tuple-element.22.index, bf16[6,128,128]{2,1,0:T(8,128)(2,1)S(1)} %bitcast.8, bf16[6,128,128]{2,1,0:T(8,128)(2,1)S(1)} %collective-permute-done.3.refs_1_, ...), custom_call_target="tpu_custom_call" | custom-call | flops 251658240 | bytes 2621440 | tf_op jit(solution)/shard_map/pallas_call | solution.py:227
  60.5 0.0 collective-permute-start.15
  60.5 1.7 %collective-permute-done.15.arrived = bf16[6,128,256]{2,1,0:T(8,128)(2,1)S(1)} collective-permute-done((bf16[6,128,256]{2,1,0:T(8,128)(2,1)S(1)}, bf16[6,128,256]{2,1,0:T(8,128)(2,1)S(1)}, u32[]{:S(2)}, u32[]{:S(2)}) %collective-permute-start.15) | collective-permute-done | bytes 393248 | tf_op jit(solution)/shard_map/ppermute | solution.py:24
  62.2 0.1 shard_map.100
  62.3 2.2 %collective-permute-start.16 = (bf16[4,128,256]{2,1,0:T(8,128)(2,1)S(1)}, bf16[4,128,256]{2,1,0:T(8,128)(2,1)S(1)}, u32[]{:S(2)}, u32[]{:S(2)}) collective-permute-start(bf16[4,128,256]{2,1,0:T(8,128)(2,1)S(1)} %get-tuple-element.28), channel_id=1, source_target_pairs={{0,4},{1,5},{2,6},{3,7},{4,0},{5,1},{6,2},{7,3},{8,12},{9,13},{10,... | collective-permute-start | bytes 786440 | tf_op jit(solution)/shard_map/ppermute | solution.py:24
  64.5 6.6 %collective-permute-done.16.arrived = bf16[4,128,256]{2,1,0:T(8,128)(2,1)S(1)} collective-permute-done((bf16[4,128,256]{2,1,0:T(8,128)(2,1)S(1)}, bf16[4,128,256]{2,1,0:T(8,128)(2,1)S(1)}, u32[]{:S(2)}, u32[]{:S(2)}) %collective-permute-start.16) | collective-permute-done | bytes 262176 | tf_op jit(solution)/shard_map/ppermute | solution.py:24
  71.1 0.1 shard_map.101
  71.2 0.9 %collective-permute-start.17 = (bf16[3,128,256]{2,1,0:T(8,128)(2,1)S(1)}, bf16[3,128,256]{2,1,0:T(8,128)(2,1)S(1)}, u32[]{:S(2)}, u32[]{:S(2)}) collective-permute-start(bf16[3,128,256]{2,1,0:T(8,128)(2,1)S(1)} %get-tuple-element.30), channel_id=1, source_target_pairs={{0,2},{1,3},{2,0},{3,1},{4,6},{5,7},{6,4},{7,5},{8,10},{9,11},{10,... | collective-permute-start | bytes 589832 | tf_op jit(solution)/shard_map/ppermute | solution.py:24
  72.0 5.6 %collective-permute-done.17.arrived = bf16[3,128,256]{2,1,0:T(8,128)(2,1)S(1)} collective-permute-done((bf16[3,128,256]{2,1,0:T(8,128)(2,1)S(1)}, bf16[3,128,256]{2,1,0:T(8,128)(2,1)S(1)}, u32[]{:S(2)}, u32[]{:S(2)}) %collective-permute-start.17) | collective-permute-done | bytes 196640 | tf_op jit(solution)/shard_map/ppermute | solution.py:24
  77.7 0.8 shard_map.102
  (11 shorter events, 0.1 us)
Async XLA Ops:
  0.6 0.7 copy-start.5
  0.6 0.7 copy-start.4
  0.7 0.7 copy-start.6
  1.3 0.8 %copy-start.3 = (bf16[128,256]{1,0:T(8,128)(2,1)S(1)}, bf16[128,256]{1,0:T(8,128)(2,1)}, u32[]{:S(2)}) copy-start(bf16[128,256]{1,0:T(8,128)(2,1)} %feats.1) | copy-start | bytes 196612
  2.9 7.0 %collective-permute-start = (bf16[80,128]{1,0:T(8,128)(2,1)S(1)}, bf16[80,128]{1,0:T(8,128)(2,1)S(1)}, u32[]{:S(2)}, u32[]{:S(2)}) collective-permute-start(bf16[80,128]{1,0:T(8,128)(2,1)S(1)} %get-tuple-element.19), channel_id=1, source_target_pairs={{0,8},{8,16},{16,24},{24,0},{1,9},{9,17},{17,25},{25,1},{2,10},{10... | collective-permute-start | bytes 61448 | tf_op jit(solution)/shard_map/ppermute | solution.py:19
  5.9 4.8 %collective-permute-start.1 = (bf16[80,128]{1,0:T(8,128)(2,1)S(1)}, bf16[80,128]{1,0:T(8,128)(2,1)S(1)}, u32[]{:S(2)}, u32[]{:S(2)}) collective-permute-start(bf16[80,128]{1,0:T(8,128)(2,1)S(1)} %get-tuple-element.20), channel_id=1, source_target_pairs={{0,16},{8,24},{16,0},{24,8},{1,17},{9,25},{17,1},{25,9},{2,18},{10... | collective-permute-start | bytes 61448 | tf_op jit(solution)/shard_map/ppermute | solution.py:19
  8.5 3.8 %collective-permute-start.2 = (bf16[80,128]{1,0:T(8,128)(2,1)S(1)}, bf16[80,128]{1,0:T(8,128)(2,1)S(1)}, u32[]{:S(2)}, u32[]{:S(2)}) collective-permute-start(bf16[80,128]{1,0:T(8,128)(2,1)S(1)} %get-tuple-element.21), channel_id=1, source_target_pairs={{0,24},{8,0},{16,8},{24,16},{1,25},{9,1},{17,9},{25,17},{2,26},{10... | collective-permute-start | bytes 61448 | tf_op jit(solution)/shard_map/ppermute | solution.py:19
  12.3 4.3 %collective-permute-start.6 = (bf16[1,4,64,128]{3,2,1,0:T(8,128)(2,1)S(1)}, bf16[1,4,64,128]{3,2,1,0:T(8,128)(2,1)S(1)}, u32[]{:S(2)}, u32[]{:S(2)}) collective-permute-start(bf16[1,4,64,128]{3,2,1,0:T(8,128)(2,1)S(1)} %get-tuple-element.23.first), channel_id=1, source_target_pairs={{0,2},{1,3},{2,0},{3,1},{4,6},{5,7},{6,4},{7,5},{8,10},{9,11},{10,... | collective-permute-start | bytes 196616 | tf_op jit(solution)/shard_map/ppermute | solution.py:24
  16.7 5.2 %copy-start = (bf16[1,1,2,3,128,128]{5,4,3,2,1,0:T(8,128)(2,1)S(1)}, bf16[1,1,2,3,128,128]{5,4,3,2,1,0:T(8,128)(2,1)}, u32[]{:S(2)}) copy-start(bf16[1,1,2,3,128,128]{5,4,3,2,1,0:T(8,128)(2,1)} %param.10) | copy-start | bytes 589828
  16.7 9.0 %copy-start.2 = (bf16[128,256]{1,0:T(8,128)(2,1)S(1)}, bf16[128,256]{1,0:T(8,128)(2,1)}, u32[]{:S(2)}) copy-start(bf16[128,256]{1,0:T(8,128)(2,1)} %refs_8_.1) | copy-start | bytes 196612
  16.7 5.0 %collective-permute-start.7 = (bf16[2,4,64,128]{3,2,1,0:T(8,128)(2,1)S(1)}, bf16[2,4,64,128]{3,2,1,0:T(8,128)(2,1)S(1)}, u32[]{:S(2)}, u32[]{:S(2)}) collective-permute-start(bf16[2,4,64,128]{3,2,1,0:T(8,128)(2,1)S(1)} %shard_map.96.first), channel_id=1, source_target_pairs={{0,4},{1,5},{2,6},{3,7},{4,0},{5,1},{6,2},{7,3},{8,12},{9,13},{10,... | collective-permute-start | bytes 393224 | tf_op jit(solution)/shard_map/ppermute | solution.py:24
  21.7 23.2 %collective-permute-start.8 = (bf16[4,4,64,128]{3,2,1,0:T(8,128)(2,1)S(1)}, bf16[4,4,64,128]{3,2,1,0:T(8,128)(2,1)S(1)}, u32[]{:S(2)}, u32[]{:S(2)}) collective-permute-start(bf16[4,4,64,128]{3,2,1,0:T(8,128)(2,1)S(1)} %shard_map.97.refs_4_), channel_id=1, source_target_pairs={{0,1},{1,0},{2,3},{3,2},{4,5},{5,4},{6,7},{7,6},{8,9},{9,8},{10,11... | collective-permute-start | bytes 786440 | tf_op jit(solution)/shard_map/ppermute | solution.py:24
  21.8 9.2 %collective-permute-start.5 = (bf16[6,128,128]{2,1,0:T(8,128)(2,1)S(1)}, bf16[6,128,128]{2,1,0:T(8,128)(2,1)S(1)}, u32[]{:S(2)}, u32[]{:S(2)}) collective-permute-start(bf16[6,128,128]{2,1,0:T(8,128)(2,1)S(1)} %bitcast.4), channel_id=1, source_target_pairs={{0,24},{8,0},{16,8},{24,16},{1,25},{9,1},{17,9},{25,17},{2,26},{10... | collective-permute-start | bytes 589832 | tf_op jit(solution)/shard_map/ppermute | solution.py:19
  25.0 19.9 %collective-permute-start.4 = (bf16[6,128,128]{2,1,0:T(8,128)(2,1)S(1)}, bf16[6,128,128]{2,1,0:T(8,128)(2,1)S(1)}, u32[]{:S(2)}, u32[]{:S(2)}) collective-permute-start(bf16[6,128,128]{2,1,0:T(8,128)(2,1)S(1)} %bitcast.5), channel_id=1, source_target_pairs={{0,16},{8,24},{16,0},{24,8},{1,17},{9,25},{17,1},{25,9},{2,18},{10... | collective-permute-start | bytes 589832 | tf_op jit(solution)/shard_map/ppermute | solution.py:19
  25.0 19.9 %collective-permute-start.3 = (bf16[6,128,128]{2,1,0:T(8,128)(2,1)S(1)}, bf16[6,128,128]{2,1,0:T(8,128)(2,1)S(1)}, u32[]{:S(2)}, u32[]{:S(2)}) collective-permute-start(bf16[6,128,128]{2,1,0:T(8,128)(2,1)S(1)} %bitcast.6), channel_id=1, source_target_pairs={{0,8},{8,16},{16,24},{24,0},{1,9},{9,17},{17,25},{25,1},{2,10},{10... | collective-permute-start | bytes 589832 | tf_op jit(solution)/shard_map/ppermute | solution.py:19
  25.7 24.6 %collective-permute-start.13 = (bf16[128,256]{1,0:T(8,128)(2,1)S(1)}, bf16[128,256]{1,0:T(8,128)(2,1)S(1)}, u32[]{:S(2)}, u32[]{:S(2)}) collective-permute-start(bf16[128,256]{1,0:T(8,128)(2,1)S(1)} %copy-done.2), channel_id=1, source_target_pairs={{0,16},{8,24},{16,0},{24,8},{1,17},{9,25},{17,1},{25,9},{2,18},{10... | collective-permute-start | bytes 196616 | tf_op jit(solution)/shard_map/ppermute | solution.py:19
  31.0 19.8 %collective-permute-start.12 = (bf16[128,256]{1,0:T(8,128)(2,1)S(1)}, bf16[128,256]{1,0:T(8,128)(2,1)S(1)}, u32[]{:S(2)}, u32[]{:S(2)}) collective-permute-start(bf16[128,256]{1,0:T(8,128)(2,1)S(1)} %copy-done.2), channel_id=1, source_target_pairs={{0,8},{8,16},{16,24},{24,0},{1,9},{9,17},{17,25},{25,1},{2,10},{10... | collective-permute-start | bytes 196616 | tf_op jit(solution)/shard_map/ppermute | solution.py:19
  45.0 5.8 %collective-permute-start.14 = (bf16[128,256]{1,0:T(8,128)(2,1)S(1)}, bf16[128,256]{1,0:T(8,128)(2,1)S(1)}, u32[]{:S(2)}, u32[]{:S(2)}) collective-permute-start(bf16[128,256]{1,0:T(8,128)(2,1)S(1)} %copy-done.2), channel_id=1, source_target_pairs={{0,24},{8,0},{16,8},{24,16},{1,25},{9,1},{17,9},{25,17},{2,26},{10... | collective-permute-start | bytes 196616 | tf_op jit(solution)/shard_map/ppermute | solution.py:19
  45.0 11.3 %copy-start.1 = (bf16[256,256]{1,0:T(8,128)(2,1)S(1)}, bf16[256,256]{1,0:T(8,128)(2,1)}, u32[]{:S(2)}) copy-start(bf16[256,256]{1,0:T(8,128)(2,1)} %refs_12_.1) | copy-start | bytes 393220
  46.7 4.5 %collective-permute-start.11 = (bf16[4,64,128]{2,1,0:T(8,128)(2,1)S(1)}, bf16[4,64,128]{2,1,0:T(8,128)(2,1)S(1)}, u32[]{:S(2)}, u32[]{:S(2)}) collective-permute-start(bf16[4,64,128]{2,1,0:T(8,128)(2,1)S(1)} %shard_map.98.refs_4_), channel_id=1, source_target_pairs={{0,24},{8,0},{16,8},{24,16},{1,25},{9,1},{17,9},{25,17},{2,26},{10... | collective-permute-start | bytes 196616 | tf_op jit(solution)/shard_map/ppermute | solution.py:19
  47.8 6.8 %collective-permute-start.10 = (bf16[4,64,128]{2,1,0:T(8,128)(2,1)S(1)}, bf16[4,64,128]{2,1,0:T(8,128)(2,1)S(1)}, u32[]{:S(2)}, u32[]{:S(2)}) collective-permute-start(bf16[4,64,128]{2,1,0:T(8,128)(2,1)S(1)} %shard_map.98.refs_4_), channel_id=1, source_target_pairs={{0,16},{8,24},{16,0},{24,8},{1,17},{9,25},{17,1},{25,9},{2,18},{10... | collective-permute-start | bytes 196616 | tf_op jit(solution)/shard_map/ppermute | solution.py:19
  50.3 6.1 %collective-permute-start.9 = (bf16[4,64,128]{2,1,0:T(8,128)(2,1)S(1)}, bf16[4,64,128]{2,1,0:T(8,128)(2,1)S(1)}, u32[]{:S(2)}, u32[]{:S(2)}) collective-permute-start(bf16[4,64,128]{2,1,0:T(8,128)(2,1)S(1)} %shard_map.98.refs_4_), channel_id=1, source_target_pairs={{0,8},{8,16},{16,24},{24,0},{1,9},{9,17},{17,25},{25,1},{2,10},{10... | collective-permute-start | bytes 196616 | tf_op jit(solution)/shard_map/ppermute | solution.py:19
  60.5 1.7 %collective-permute-start.15 = (bf16[6,128,256]{2,1,0:T(8,128)(2,1)S(1)}, bf16[6,128,256]{2,1,0:T(8,128)(2,1)S(1)}, u32[]{:S(2)}, u32[]{:S(2)}) collective-permute-start(bf16[6,128,256]{2,1,0:T(8,128)(2,1)S(1)} %get-tuple-element.26), channel_id=1, source_target_pairs={{0,1},{1,0},{2,3},{3,2},{4,5},{5,4},{6,7},{7,6},{8,9},{9,8},{10,11... | collective-permute-start | bytes 1179656 | tf_op jit(solution)/shard_map/ppermute | solution.py:24
  62.3 8.8 %collective-permute-start.16 = (bf16[4,128,256]{2,1,0:T(8,128)(2,1)S(1)}, bf16[4,128,256]{2,1,0:T(8,128)(2,1)S(1)}, u32[]{:S(2)}, u32[]{:S(2)}) collective-permute-start(bf16[4,128,256]{2,1,0:T(8,128)(2,1)S(1)} %get-tuple-element.28), channel_id=1, source_target_pairs={{0,4},{1,5},{2,6},{3,7},{4,0},{5,1},{6,2},{7,3},{8,12},{9,13},{10,... | collective-permute-start | bytes 786440 | tf_op jit(solution)/shard_map/ppermute | solution.py:24
  71.2 6.5 %collective-permute-start.17 = (bf16[3,128,256]{2,1,0:T(8,128)(2,1)S(1)}, bf16[3,128,256]{2,1,0:T(8,128)(2,1)S(1)}, u32[]{:S(2)}, u32[]{:S(2)}) collective-permute-start(bf16[3,128,256]{2,1,0:T(8,128)(2,1)S(1)} %get-tuple-element.30), channel_id=1, source_target_pairs={{0,2},{1,3},{2,0},{3,1},{4,6},{5,7},{6,4},{7,5},{8,10},{9,11},{10,... | collective-permute-start | bytes 589832 | tf_op jit(solution)/shard_map/ppermute | solution.py:24

commit v4 on v3

v4 whole, which is shorter than its diff:
```python
import functools

import jax
import jax.numpy as jnp
from jax import lax
from jax.experimental import pallas as pl
from jax.experimental.pallas import tpu as pltpu
from jax.sharding import PartitionSpec as P

F32 = jnp.float32
BF16 = jnp.bfloat16
VMEM = pl.BlockSpec(memory_space=pltpu.VMEM)
SMEM = pl.BlockSpec(memory_space=pltpu.SMEM)
PAD = 16


def shift(array, by):
    peers = lax.axis_size("rep")
    return lax.ppermute(array, "rep", [(i, (i + by) % peers) for i in range(peers)])


def swap(array, axis, bit):
    peers = lax.axis_size(axis)
    return lax.ppermute(array, axis, [(i, i ^ bit) for i in range(peers)])


def relay(array):
    peers = lax.axis_size("rep")
    below, above = [array], [array]
    for step in range(1, peers):
        up = [(i, i + 1) for i in range(step - 1, peers - 1)]
        down = [(i, i - 1) for i in range(1, peers - step + 1)]
        below.append(lax.ppermute(below[-1], "rep", up))
        above.append(lax.ppermute(above[-1], "rep", down))
    return below + above[1:]


def call(body, outs, in_specs, scratch=(), flops=0, moved=0):
    return pl.pallas_call(
        body,
        out_shape=outs,
        in_specs=in_specs,
        out_specs=jax.tree.map(lambda _: VMEM, outs),
        scratch_shapes=list(scratch),
        compiler_params=pltpu.CompilerParams(vmem_limit_bytes=48 * 1024 * 1024),
        cost_estimate=pl.CostEstimate(flops=flops, bytes_accessed=moved, transcendentals=0),
    )


def dot(a, b, a_dim, b_dim):
    return lax.dot_general(a, b, (((a_dim,), (b_dim,)), ((), ())), preferred_element_type=F32)


def member_and(by, reps):
    return lax.rem(lax.axis_index("rep") + by, reps)


def pack(blocks, cotangent, out):
    slots, block = blocks.shape[:2]
    out[:slots] = blocks[...]
    for k in range(cotangent.shape[1] // block):
        out[slots + k] = cotangent[:, k * block : (k + 1) * block]


def split_features(reps, lists, cap, feats, rows, cols, counts, keep, send, turned):
    nodes = feats.shape[0]
    part = feats.shape[1] // reps
    turned[...] = feats[...].astype(F32).T.astype(BF16).reshape(turned.shape)
    lane = lax.broadcasted_iota(jnp.int32, (PAD, nodes), 1)
    index = jnp.zeros((PAD, nodes), jnp.int32)
    slots = lists * cap
    for j in range(lists):
        for c in range(cap):
            k = j * cap + c
            index = jnp.where(lane == k, rows[j, c], index)
            index = jnp.where(lane == slots + k, cols[j, c], index)
        index = jnp.where(lane == 2 * slots + j, counts[j], index)
    index = index.astype(F32).astype(BF16)
    me = lax.axis_index("rep")
    half = reps // 2
    for d in range(reps):
        out = send if d >= half else keep
        out[d % half, :part] = turned[lax.bitwise_xor(me, d)]
        out[d % half, part:] = index


def regroup(held, gone, keep, arrived, next_keep, next_send):
    half = gone // 2
    for o in range(held):
        for source, base in ((keep, 0), (arrived, held)):
            for d in range(half):
                next_keep[(base + o) * half + d] = source[o * gone + d]
                next_send[(base + o) * half + d] = source[o * gone + half + d]


def order_chunks(reps, part, keep, arrived, mine, index):
    me = lax.axis_index("rep")
    half = reps // 2
    for k in range(reps):
        source = arrived if k >= half else keep
        origin = lax.bitwise_xor(me, origin_bits(k, reps))
        mine[0, origin] = source[k % half, :part]
        index[origin] = source[k % half, part:].astype(F32).astype(jnp.int32)


def origin_bits(k, reps):
    bits, value, origin = reps.bit_length() - 1, k, 0
    for i in range(bits):
        if value >> i & 1:
            origin |= 1 << (bits - 1 - i)
    return origin


def join(first, second, out):
    half = first.shape[0]
    out[:half] = first[...]
    out[half:] = second[...]


def slot_of(index, lists, cap, t, j, c):
    k = j * cap + c
    slots = lists * cap
    return index[t, 0, k], index[t, 0, slots + k], c < index[t, 0, 2 * slots + j]


def relative(groups, lists, origin, j):
    mine = lax.axis_index("blk")
    return lax.bitwise_xor(mine, lax.rem(mine + groups - origin * lists - j, groups))


def aggregate(reps, groups, lists, cap, index, *refs):
    arrays = refs[: 2 * reps - 1]
    near, far, out, blocks, cotangents, held, total = refs[2 * reps - 1 :]
    slots = lists * cap
    block = blocks.shape[2]
    me = lax.axis_index("rep")

    def place_at(origin, array):
        blocks[origin] = array[:slots]
        for k in range(cotangents.shape[2] // block):
            cotangents[origin, :, k * block : (k + 1) * block] = array[slots + k]

    place_at(me, arrays[0])
    for step in range(1, reps):
        pl.when(me >= step)(functools.partial(place_at, me - step, arrays[step]))
        pl.when(me + step < reps)(
            functools.partial(place_at, me + step, arrays[reps - 1 + step])
        )
    held[0] = near[...]
    held[1] = far[...]
    total[...] = jnp.zeros_like(total)
    for origin in range(reps):
        for j in range(lists):
            place = relative(groups, lists, origin, j)
            for c in range(cap):
                row, col, live = slot_of(index, lists, cap, origin, j, c)
                source = held[lax.rem(place, 2), lax.div(place, 2), col]
                product = dot(source, blocks[origin, j * cap + c], 1, 1)
                total[row] += jnp.where(live, product, 0.0)
    out[...] = total[...].astype(BF16)


def dense_layer(reps, *refs):
    chunks = refs[:reps]
    cot, weight, out, dagg, terms, agg, outs = refs[reps:]
    nodes, width = out.shape
    for t in range(reps):
        origin = member_and(reps - t, reps)
        for b in range(reps):
            agg[b, origin] = chunks[t][b]
    gw = jnp.zeros((width, width), F32)
    for b in range(reps):
        turned = agg[b].reshape(width, nodes)
        pre = dot(turned, weight[...], 0, 0)
        sigma = jax.nn.sigmoid(pre)
        outs[b] = (pre * sigma).astype(BF16)
        slope = sigma * (1.0 + pre * (1.0 - sigma))
        dpre = (cot[b].astype(F32) * slope).astype(BF16)
        dagg[b] = dot(dpre, weight[...], 1, 1).astype(BF16)
        gw += dot(turned, dpre, 1, 0)
    out[...] = outs[lax.axis_index("rep")]
    terms[...] = gw.astype(BF16)


def feature_grads(reps, groups, lists, cap, index, blocks, dagg, keep, send, total):
    me = lax.axis_index("rep")
    total[...] = jnp.zeros_like(total)
    for origin in range(reps):
        for j in range(lists):
            place = relative(groups, lists, origin, j)
            for c in range(cap):
                row, col, live = slot_of(index, lists, cap, origin, j, c)

                @pl.when(jnp.logical_and(live, col == me))
                def _():
                    total[lax.rem(place, 2), lax.div(place, 2)] += dot(
                        blocks[origin, j * cap + c], dagg[row], 0, 0
                    )

    keep[...] = total[0]
    send[...] = total[1].astype(BF16)


def add_terms(mine, arrived, out):
    out[...] = (mine[...].astype(F32) + arrived[...].astype(F32)).astype(out.dtype)


def add_and_halve(half, keep, arrived, next_keep, next_send):
    next_keep[...] = keep[:half] + arrived[:half].astype(F32)
    next_send[...] = (keep[half:] + arrived[half:].astype(F32)).astype(BF16)


def add_last(keep, arrived, grad_feats):
    grad_feats[...] = keep[0] + arrived[0].astype(F32)


def per_device(feats, weight, cotangent, block_vals, block_rows, block_cols, step_counts):
    reps = lax.axis_size("rep")
    groups = lax.axis_size("blk")
    lists, cap, block = block_vals.shape[2:5]
    nodes, width = feats.shape
    part = width // reps
    extra = width // block
    slots = lists * cap
    like = jax.ShapeDtypeStruct

    packed = call(
        pack,
        like((slots + extra, block, block), BF16),
        [VMEM] * 2,
        moved=4 * (slots + extra) * block * block,
    )(block_vals.reshape(slots, block, block), cotangent)
    relayed = relay(packed)

    piece = like((reps // 2, part + PAD, nodes), BF16)
    keep, send = call(
        functools.partial(split_features, reps, lists, cap),
        [piece] * 2,
        [VMEM, SMEM, SMEM, SMEM],
        [pltpu.VMEM((reps, part, nodes), BF16)],
        moved=4 * nodes * width,
    )(feats, block_rows[0, 0], block_cols[0, 0], step_counts[0, 0])
    bit, origins = reps // 2, 1
    arrived = swap(send, "rep", bit)
    while bit > 1:
        keep, send = call(
            functools.partial(regroup, origins, bit),
            [piece] * 2,
            [VMEM] * 2,
            moved=4 * nodes * width,
        )(keep, arrived)
        bit, origins = bit // 2, origins * 2
        arrived = swap(send, "rep", bit)
    near, index = call(
        functools.partial(order_chunks, reps, part),
        [like((1, reps, part, nodes), BF16), like((reps, PAD, nodes), jnp.int32)],
        [VMEM] * 2,
        moved=4 * nodes * width,
    )(keep, arrived)

    bit = 2
    while bit < groups:
        near = call(
            join,
            like((2 * near.shape[0],) + near.shape[1:], BF16),
            [VMEM] * 2,
            moved=8 * near.size,
        )(near, swap(near, "blk", bit))
        bit *= 2
    far = swap(near, "blk", 1)
    slot_flops = 2 * groups * cap * part * block * block
    slot_bytes = 2 * (groups * cap * block * block + groups * nodes * width)

    agg, blocks, cotangents = call(
        functools.partial(aggregate, reps, groups, lists, cap),
        [
            like((reps, part, nodes), BF16),
            like((reps, slots, block, block), BF16),
            like((reps, nodes, width), BF16),
        ],
        [SMEM] + [VMEM] * (2 * reps + 1),
        [
            pltpu.VMEM((2, groups // 2, reps, part, nodes), BF16),
            pltpu.VMEM((reps, part, nodes), F32),
        ],
        flops=slot_flops,
        moved=slot_bytes,
    )(index, *relayed, near, far)
    aggs = [agg] + [shift(agg, t) for t in range(1, reps)]

    out_rows, dagg, terms = call(
        functools.partial(dense_layer, reps),
        [
            like((nodes, width), BF16),
            like((reps, nodes, width), BF16),
            like((width, width), BF16),
        ],
        [VMEM] * (reps + 2),
        [
            pltpu.VMEM((reps, reps, part, nodes), BF16),
            pltpu.VMEM((reps, nodes, width), BF16),
        ],
        flops=6 * reps * nodes * width * width,
        moved=2 * reps * 5 * nodes * width,
    )(*aggs, cotangents, weight)

    half = groups // 2
    keep, send = call(
        functools.partial(feature_grads, reps, groups, lists, cap),
        [like((half, nodes, width), F32), like((half, nodes, width), BF16)],
        [SMEM] + [VMEM] * 2,
        [pltpu.VMEM((2, half, nodes, width), F32)],
        flops=slot_flops,
        moved=slot_bytes,
    )(index, blocks, dagg)

    bit = 1
    while bit < groups:
        other = swap(terms, "blk", bit)
        bit *= 2
        terms = call(
            add_terms,
            like((width, width), BF16 if bit < groups else F32),
            [VMEM] * 2,
            moved=6 * width * width,
        )(terms, other)

    arrived = swap(send, "blk", 1)
    bit = groups // 2
    while bit > 1:
        half = half // 2
        keep, send = call(
            functools.partial(add_and_halve, half),
            [like((half, nodes, width), F32), like((half, nodes, width), BF16)],
            [VMEM] * 2,
            moved=12 * half * nodes * width,
        )(keep, arrived)
        arrived = swap(send, "blk", bit)
        bit = bit // 2
    grad_feats = call(
        add_last, like((nodes, width), F32), [VMEM] * 2, moved=10 * nodes * width
    )(keep, arrived)
    return (out_rows, terms, grad_feats)


def solution(mesh):
    return jax.shard_map(
        per_device,
        mesh=mesh,
        in_specs=(
            P(("blk", "rep"), None),
            P(),
            P(("blk", "rep"), None),
            P("blk", "rep", None, None, None, None),
            P("blk", "rep", None, None),
            P("blk", "rep", None, None),
            P("blk", "rep", None),
        ),
        out_specs=(P(("blk", "rep"), None), P(), P(("blk", "rep"), None)),
        check_vma=False,
    )
```

time: 78.2 us -> 76.1 us (0.973)
  waiting for transfers between devices: 45.2 us -> 28.8 us
  starting transfers between devices: 23.5 us -> 35.9 us
  local copies, waits for them, and re-layouts: 1.53 us -> 2.42 us
    ppermute x6 -> x17, starting transfers between devices: 6.24 us -> 29.7 us  [the longest x11 18.8 us: swap(): return lax.ppermute(array, axis, [(i, i ^ bit) for i in range(peers)])]
    ppermute x12 -> x3, waiting for transfers between devices: 25 us -> 5.52 us  [shift(): lax.ppermute(array, 'rep', [(i, (i + by) % peers) for i in range(peers)])]
    ppermute x12 -> x3, starting transfers between devices: 17.2 us -> 6.21 us  [shift(): lax.ppermute(array, 'rep', [(i, (i + by) % peers) for i in range(peers)])]
    ppermute x6 -> x17, waiting for transfers between devices: 20.2 us -> 23.3 us  [the longest x11 14.5 us: swap(): return lax.ppermute(array, axis, [(i, i ^ bit) for i in range(peers)])]
    unnamed x14, local copies, waits for them, and re-layouts: 1.53 us -> 2.42 us
    pallas_call x6 -> x12, Pallas kernels: 7.52 us -> 7.58 us  [the longest x1 2.15 us: per_device(): call(functools.partial(feature_grads, reps, groups, lists, cap), [like((h...]
  transfers between devices with their start and end apart: 18 -> 20, of which waited for: 12 -> 12; matrix products, arithmetic and copies ran while one was open for 0% -> 0% of each run, Pallas kernels for 2% -> 2%
where the time goes in v4:
time: 76.1 us; the launch traced here: 75.6 us
  starting transfers between devices  35.9 us (47%)
  waiting for transfers between devices  28.8 us (38%)
  Pallas kernels  7.61 us (10%)
  local copies, waits for them, and re-layouts  2.42 us (3%)
  between operations  0.83 us (1%)
    ppermute x11, starting transfers between devices, swap(): return lax.ppermute(array, axis, [(i, i ^ bit) for i in range(peers)])  18.8 us
    ppermute x11, waiting for transfers between devices, swap(): return lax.ppermute(array, axis, [(i, i ^ bit) for i in range(peers)])  14.5 us
    ppermute x3, waiting for transfers between devices, relay(): above.append(lax.ppermute(above[-1], 'rep', down))  8.58 us
    ppermute x3, starting transfers between devices, relay(): below.append(lax.ppermute(below[-1], 'rep', up))  6.91 us
    ppermute x3, starting transfers between devices, shift(): lax.ppermute(array, 'rep', [(i, (i + by) % peers) for i in range(peers)])  6.21 us
    ppermute x3, waiting for transfers between devices, shift(): lax.ppermute(array, 'rep', [(i, (i + by) % peers) for i in range(peers)])  5.52 us
    ppermute x3, starting transfers between devices, relay(): above.append(lax.ppermute(above[-1], 'rep', down))  4 us
    unnamed x14, local copies, waits for them, and re-layouts  2.42 us
  transfers between devices with their start and end apart: 20, of which 12 were waited for; matrix products, arithmetic and copies ran while one was open for 0% of the time, Pallas kernels for 2%

profile of v4, /device:TPU:0, one launch (start us, length us, event | category | flops | bytes accessed | tf_op | source)
XLA Modules:
  0.0 75.6 jit_solution(2545908668614833035)
XLA Ops:
  0.6 0.9 %copy-done = bf16[1,1,2,3,128,128]{5,4,3,2,1,0:T(8,128)(2,1)S(1)} copy-done((bf16[1,1,2,3,128,128]{5,4,3,2,1,0:T(8,128)(2,1)S(1)}, bf16[1,1,2,3,128,128]{5,4,3,2,1,0:T(8,128)(2,1)}, u32[]{:S(2)}) %copy-start) | copy-done | bytes 196632
  1.6 0.8 %copy-done.2 = bf16[128,256]{1,0:T(8,128)(2,1)S(1)} copy-done((bf16[128,256]{1,0:T(8,128)(2,1)S(1)}, bf16[128,256]{1,0:T(8,128)(2,1)}, u32[]{:S(2)}) %copy-start.2) | copy-done | bytes 65560
  2.4 1.4 %collective-permute-start.5 = (bf16[8,128,128]{2,1,0:T(8,128)(2,1)S(1)}, bf16[8,128,128]{2,1,0:T(8,128)(2,1)S(1)}, u32[]{:S(2)}, u32[]{:S(2)}) collective-permute-start(bf16[8,128,128]{2,1,0:T(8,128)(2,1)S(1)} %shard_map.97.refs_0_), channel_id=1, source_target_pairs={{8,0},{16,8},{24,16},{9,1},{17,9},{25,17},{10,2},{18,10},{26,18},{... | collective-permute-start | bytes 786440 | tf_op jit(solution)/shard_map/ppermute | solution.py:34
  3.9 5.6 %collective-permute-start.2 = (bf16[8,128,128]{2,1,0:T(8,128)(2,1)S(1)}, bf16[8,128,128]{2,1,0:T(8,128)(2,1)S(1)}, u32[]{:S(2)}, u32[]{:S(2)}) collective-permute-start(bf16[8,128,128]{2,1,0:T(8,128)(2,1)S(1)} %shard_map.97.refs_0_), channel_id=1, source_target_pairs={{0,8},{8,16},{16,24},{1,9},{9,17},{17,25},{2,10},{10,18},{18,26},{... | collective-permute-start | bytes 786440 | tf_op jit(solution)/shard_map/ppermute | solution.py:33
  9.4 0.0 copy-start.3
  9.5 0.0 copy-start.5
  9.5 0.6 copy-done.3
  10.1 0.7 shard_map.94
  10.8 3.1 %collective-permute-start = (bf16[2,80,128]{2,1,0:T(8,128)(2,1)S(1)}, bf16[2,80,128]{2,1,0:T(8,128)(2,1)S(1)}, u32[]{:S(2)}, u32[]{:S(2)}) collective-permute-start(bf16[2,80,128]{2,1,0:T(8,128)(2,1)S(1)} %get-tuple-element.22), channel_id=1, source_target_pairs={{0,16},{8,24},{16,0},{24,8},{1,17},{9,25},{17,1},{25,9},{2,18},{10... | collective-permute-start | bytes 122888 | tf_op jit(solution)/shard_map/ppermute | solution.py:24
  13.9 0.0 collective-permute-done.5.refs_4_
  13.9 1.3 %collective-permute-start.6 = (bf16[8,128,128]{2,1,0:T(8,128)(2,1)S(1)}, bf16[8,128,128]{2,1,0:T(8,128)(2,1)S(1)}, u32[]{:S(2)}, u32[]{:S(2)}) collective-permute-start(bf16[8,128,128]{2,1,0:T(8,128)(2,1)S(1)} %collective-permute-done.5.refs_4_), channel_id=1, source_target_pairs={{8,0},{16,8},{9,1},{17,9},{10,2},{18,10},{11,3},{19,11},{12,4},{20... | collective-permute-start | bytes 786440 | tf_op jit(solution)/shard_map/ppermute | solution.py:34
  15.2 0.2 collective-permute-done.2.refs_1_
  15.4 0.7 collective-permute-start.3
  16.1 0.2 collective-permute-done.arrived
  16.3 6.2 %collective-permute-start.1 = (bf16[2,80,128]{2,1,0:T(8,128)(2,1)S(1)}, bf16[2,80,128]{2,1,0:T(8,128)(2,1)S(1)}, u32[]{:S(2)}, u32[]{:S(2)}) collective-permute-start(bf16[2,80,128]{2,1,0:T(8,128)(2,1)S(1)} %get-tuple-element.24), channel_id=1, source_target_pairs={{0,8},{8,0},{16,24},{24,16},{1,9},{9,1},{17,25},{25,17},{2,10},{10... | collective-permute-start | bytes 122888 | tf_op jit(solution)/shard_map/ppermute | solution.py:24
  22.5 2.0 %collective-permute-done.1.arrived = bf16[2,80,128]{2,1,0:T(8,128)(2,1)S(1)} collective-permute-done((bf16[2,80,128]{2,1,0:T(8,128)(2,1)S(1)}, bf16[2,80,128]{2,1,0:T(8,128)(2,1)S(1)}, u32[]{:S(2)}, u32[]{:S(2)}) %collective-permute-start.1) | collective-permute-done | bytes 40992 | tf_op jit(solution)/shard_map/ppermute | solution.py:24
  24.5 1.6 %collective-permute-start.8 = (bf16[1,4,64,128]{3,2,1,0:T(8,128)(2,1)S(1)}, bf16[1,4,64,128]{3,2,1,0:T(8,128)(2,1)S(1)}, u32[]{:S(2)}, u32[]{:S(2)}) collective-permute-start(bf16[1,4,64,128]{3,2,1,0:T(8,128)(2,1)S(1)} %get-tuple-element.26.first), channel_id=1, source_target_pairs={{0,2},{1,3},{2,0},{3,1},{4,6},{5,7},{6,4},{7,5},{8,10},{9,11},{10,... | collective-permute-start | bytes 196616 | tf_op jit(solution)/shard_map/ppermute | solution.py:24
  26.1 2.8 %collective-permute-done.8.second = bf16[1,4,64,128]{3,2,1,0:T(8,128)(2,1)S(1)} collective-permute-done((bf16[1,4,64,128]{3,2,1,0:T(8,128)(2,1)S(1)}, bf16[1,4,64,128]{3,2,1,0:T(8,128)(2,1)S(1)}, u32[]{:S(2)}, u32[]{:S(2)}) %collective-permute-start.8) | collective-permute-done | bytes 65568 | tf_op jit(solution)/shard_map/ppermute | solution.py:24
  28.9 1.6 %collective-permute-start.9 = (bf16[2,4,64,128]{3,2,1,0:T(8,128)(2,1)S(1)}, bf16[2,4,64,128]{3,2,1,0:T(8,128)(2,1)S(1)}, u32[]{:S(2)}, u32[]{:S(2)}) collective-permute-start(bf16[2,4,64,128]{3,2,1,0:T(8,128)(2,1)S(1)} %shard_map.98.first), channel_id=1, source_target_pairs={{0,4},{1,5},{2,6},{3,7},{4,0},{5,1},{6,2},{7,3},{8,12},{9,13},{10,... | collective-permute-start | bytes 393224 | tf_op jit(solution)/shard_map/ppermute | solution.py:24
  30.4 3.4 %collective-permute-done.9.second = bf16[2,4,64,128]{3,2,1,0:T(8,128)(2,1)S(1)} collective-permute-done((bf16[2,4,64,128]{3,2,1,0:T(8,128)(2,1)S(1)}, bf16[2,4,64,128]{3,2,1,0:T(8,128)(2,1)S(1)}, u32[]{:S(2)}, u32[]{:S(2)}) %collective-permute-start.9) | collective-permute-done | bytes 131104 | tf_op jit(solution)/shard_map/ppermute | solution.py:24
  33.9 0.1 collective-permute-start.10
  34.0 0.0 collective-permute-done.6.refs_5_
  34.0 1.3 %collective-permute-start.7 = (bf16[8,128,128]{2,1,0:T(8,128)(2,1)S(1)}, bf16[8,128,128]{2,1,0:T(8,128)(2,1)S(1)}, u32[]{:S(2)}, u32[]{:S(2)}) collective-permute-start(bf16[8,128,128]{2,1,0:T(8,128)(2,1)S(1)} %collective-permute-done.6.refs_5_), channel_id=1, source_target_pairs={{8,0},{9,1},{10,2},{11,3},{12,4},{13,5},{14,6},{15,7}} | collective-permute-start | bytes 786440 | tf_op jit(solution)/shard_map/ppermute | solution.py:34
  35.3 0.0 collective-permute-done.3.refs_2_
  35.3 0.7 collective-permute-start.4
  36.0 0.0 collective-permute-done.10.refs_8_
  36.0 8.6 %collective-permute-done.7.refs_6_ = bf16[8,128,128]{2,1,0:T(8,128)(2,1)S(1)} collective-permute-done((bf16[8,128,128]{2,1,0:T(8,128)(2,1)S(1)}, bf16[8,128,128]{2,1,0:T(8,128)(2,1)S(1)}, u32[]{:S(2)}, u32[]{:S(2)}) %collective-permute-start.7) | collective-permute-done | bytes 262176 | tf_op jit(solution)/shard_map/ppermute | solution.py:34
  44.6 0.0 collective-permute-done.4.refs_3_
  44.6 1.8 %shard_map.100 = (bf16[4,64,128]{2,1,0:T(8,128)(2,1)S(1)}, bf16[4,6,128,128]{3,2,1,0:T(8,128)(2,1)S(1)}, bf16[4,128,256]{2,1,0:T(8,128)(2,1)S(1)}) custom-call(s32[4,16,128]{2,1,0:T(8,128)S(1)} %get-tuple-element.25.index, bf16[8,128,128]{2,1,0:T(8,128)(2,1)S(1)} %shard_map.97.refs_0_, bf16[8,128,128]{2,1,0:T(8,128)(2,1)S(1)} %collective-permute-done.2.refs_1_, ...), custom_call_target="tpu_custom_call" | custom-call | flops 50331648 | bytes 1310720 | tf_op jit(solution)/shard_map/pallas_call | solution.py:274
  46.4 5.6 %collective-permute-start.13 = (bf16[4,64,128]{2,1,0:T(8,128)(2,1)S(1)}, bf16[4,64,128]{2,1,0:T(8,128)(2,1)S(1)}, u32[]{:S(2)}, u32[]{:S(2)}) collective-permute-start(bf16[4,64,128]{2,1,0:T(8,128)(2,1)S(1)} %get-tuple-element.27.refs_0_), channel_id=1, source_target_pairs={{0,24},{8,0},{16,8},{24,16},{1,25},{9,1},{17,9},{25,17},{2,26},{10... | collective-permute-start | bytes 196616 | tf_op jit(solution)/shard_map/ppermute | solution.py:19
  52.0 0.6 collective-permute-start.11
  52.7 1.9 %collective-permute-done.13.refs_3_ = bf16[4,64,128]{2,1,0:T(8,128)(2,1)S(1)} collective-permute-done((bf16[4,64,128]{2,1,0:T(8,128)(2,1)S(1)}, bf16[4,64,128]{2,1,0:T(8,128)(2,1)S(1)}, u32[]{:S(2)}, u32[]{:S(2)}) %collective-permute-start.13) | collective-permute-done | bytes 65568 | tf_op jit(solution)/shard_map/ppermute | solution.py:19
  54.5 3.0 %collective-permute-done.12.refs_2_ = bf16[4,64,128]{2,1,0:T(8,128)(2,1)S(1)} collective-permute-done((bf16[4,64,128]{2,1,0:T(8,128)(2,1)S(1)}, bf16[4,64,128]{2,1,0:T(8,128)(2,1)S(1)}, u32[]{:S(2)}, u32[]{:S(2)}) %collective-permute-start.12) | collective-permute-done | bytes 65568 | tf_op jit(solution)/shard_map/ppermute | solution.py:19
  57.5 0.7 collective-permute-done.11.refs_1_
  58.2 1.3 %shard_map.101 = (bf16[128,256]{1,0:T(8,128)(2,1)}, bf16[4,128,256]{2,1,0:T(8,128)(2,1)S(1)}, bf16[256,256]{1,0:T(8,128)(2,1)S(1)}) custom-call(bf16[4,64,128]{2,1,0:T(8,128)(2,1)S(1)} %get-tuple-element.27.refs_0_, bf16[4,64,128]{2,1,0:T(8,128)(2,1)S(1)} %collective-permute-done.11.refs_1_, bf16[4,64,128]{2,1,0:T(8,128)(2,1)S(1)} %collective-permute-done.12.refs_2_, ...), custom_call_target="tpu_custom_call" | custom-call | flops 201326592 | bytes 1310720 | tf_op jit(solution)/shard_map/pallas_call | solution.py:291
  59.5 2.2 %shard_map.105 = (f32[4,128,256]{2,1,0:T(8,128)S(1)}, bf16[4,128,256]{2,1,0:T(8,128)(2,1)S(1)}) custom-call(s32[4,16,128]{2,1,0:T(8,128)S(1)} %get-tuple-element.25.index, bf16[4,6,128,128]{3,2,1,0:T(8,128)(2,1)S(1)} %get-tuple-element.31.blocks, bf16[4,128,256]{2,1,0:T(8,128)(2,1)S(1)} %get-tuple-element.32.dagg), custom_call_target="tpu_custom_call" | custom-call | flops 50331648 | bytes 1310720 | tf_op jit(solution)/shard_map/pallas_call | solution.py:308
  61.7 0.1 collective-permute-start.17
  61.8 0.5 collective-permute-start.14
  62.3 1.2 %collective-permute-done.14.arrived = bf16[256,256]{1,0:T(8,128)(2,1)S(1)} collective-permute-done((bf16[256,256]{1,0:T(8,128)(2,1)S(1)}, bf16[256,256]{1,0:T(8,128)(2,1)S(1)}, u32[]{:S(2)}, u32[]{:S(2)}) %collective-permute-start.14) | collective-permute-done | bytes 131104 | tf_op jit(solution)/shard_map/ppermute | solution.py:24
  63.5 1.5 %collective-permute-start.15 = (bf16[256,256]{1,0:T(8,128)(2,1)S(1)}, bf16[256,256]{1,0:T(8,128)(2,1)S(1)}, u32[]{:S(2)}, u32[]{:S(2)}) collective-permute-start(bf16[256,256]{1,0:T(8,128)(2,1)S(1)} %shard_map.102.mine), channel_id=1, source_target_pairs={{0,2},{1,3},{2,0},{3,1},{4,6},{5,7},{6,4},{7,5},{8,10},{9,11},{10,... | collective-permute-start | bytes 393224 | tf_op jit(solution)/shard_map/ppermute | solution.py:24
  65.0 0.0 collective-permute-done.17.arrived
  65.1 1.3 %collective-permute-start.18 = (bf16[2,128,256]{2,1,0:T(8,128)(2,1)S(1)}, bf16[2,128,256]{2,1,0:T(8,128)(2,1)S(1)}, u32[]{:S(2)}, u32[]{:S(2)}) collective-permute-start(bf16[2,128,256]{2,1,0:T(8,128)(2,1)S(1)} %get-tuple-element.36), channel_id=1, source_target_pairs={{0,4},{1,5},{2,6},{3,7},{4,0},{5,1},{6,2},{7,3},{8,12},{9,13},{10,... | collective-permute-start | bytes 393224 | tf_op jit(solution)/shard_map/ppermute | solution.py:24
  66.4 2.7 %collective-permute-done.15.arrived = bf16[256,256]{1,0:T(8,128)(2,1)S(1)} collective-permute-done((bf16[256,256]{1,0:T(8,128)(2,1)S(1)}, bf16[256,256]{1,0:T(8,128)(2,1)S(1)}, u32[]{:S(2)}, u32[]{:S(2)}) %collective-permute-start.15) | collective-permute-done | bytes 131104 | tf_op jit(solution)/shard_map/ppermute | solution.py:24
  69.1 1.4 %collective-permute-start.16 = (bf16[256,256]{1,0:T(8,128)(2,1)S(1)}, bf16[256,256]{1,0:T(8,128)(2,1)S(1)}, u32[]{:S(2)}, u32[]{:S(2)}) collective-permute-start(bf16[256,256]{1,0:T(8,128)(2,1)S(1)} %shard_map.103.mine), channel_id=1, source_target_pairs={{0,4},{1,5},{2,6},{3,7},{4,0},{5,1},{6,2},{7,3},{8,12},{9,13},{10,... | collective-permute-start | bytes 393224 | tf_op jit(solution)/shard_map/ppermute | solution.py:24
  70.5 1.5 %collective-permute-start.19 = (bf16[1,128,256]{2,1,0:T(8,128)(2,1)S(1)}, bf16[1,128,256]{2,1,0:T(8,128)(2,1)S(1)}, u32[]{:S(2)}, u32[]{:S(2)}) collective-permute-start(bf16[1,128,256]{2,1,0:T(8,128)(2,1)S(1)} %get-tuple-element.38), channel_id=1, source_target_pairs={{0,2},{1,3},{2,0},{3,1},{4,6},{5,7},{6,4},{7,5},{8,10},{9,11},{10,... | collective-permute-start | bytes 196616 | tf_op jit(solution)/shard_map/ppermute | solution.py:24
  72.0 2.1 %collective-permute-done.16.arrived = bf16[256,256]{1,0:T(8,128)(2,1)S(1)} collective-permute-done((bf16[256,256]{1,0:T(8,128)(2,1)S(1)}, bf16[256,256]{1,0:T(8,128)(2,1)S(1)}, u32[]{:S(2)}, u32[]{:S(2)}) %collective-permute-start.16) | collective-permute-done | bytes 131104 | tf_op jit(solution)/shard_map/ppermute | solution.py:24
  74.2 0.7 shard_map.104
  74.9 0.7 shard_map.108
  (21 shorter events, 0.2 us)
Async XLA Ops:
  0.6 0.9 %copy-start = (bf16[1,1,2,3,128,128]{5,4,3,2,1,0:T(8,128)(2,1)S(1)}, bf16[1,1,2,3,128,128]{5,4,3,2,1,0:T(8,128)(2,1)}, u32[]{:S(2)}) copy-start(bf16[1,1,2,3,128,128]{5,4,3,2,1,0:T(8,128)(2,1)} %param.10) | copy-start | bytes 589828
  1.6 0.8 %copy-start.2 = (bf16[128,256]{1,0:T(8,128)(2,1)S(1)}, bf16[128,256]{1,0:T(8,128)(2,1)}, u32[]{:S(2)}) copy-start(bf16[128,256]{1,0:T(8,128)(2,1)} %cotangent.1) | copy-start | bytes 196612
  2.4 7.1 %copy-start.1 = (bf16[128,256]{1,0:T(8,128)(2,1)S(1)}, bf16[128,256]{1,0:T(8,128)(2,1)}, u32[]{:S(2)}) copy-start(bf16[128,256]{1,0:T(8,128)(2,1)} %feats.1) | copy-start | bytes 196612
  2.4 7.1 %copy-start.4 = (s32[1,1,2,3]{3,2,1,0:T(2,128)S(1)}, s32[1,1,2,3]{3,2,1,0:T(2,128)}, u32[]{:S(2)}) copy-start(s32[1,1,2,3]{3,2,1,0:T(2,128)} %param.12) | copy-start | bytes 76
  2.4 11.5 %collective-permute-start.5 = (bf16[8,128,128]{2,1,0:T(8,128)(2,1)S(1)}, bf16[8,128,128]{2,1,0:T(8,128)(2,1)S(1)}, u32[]{:S(2)}, u32[]{:S(2)}) collective-permute-start(bf16[8,128,128]{2,1,0:T(8,128)(2,1)S(1)} %shard_map.97.refs_0_), channel_id=1, source_target_pairs={{8,0},{16,8},{24,16},{9,1},{17,9},{25,17},{10,2},{18,10},{26,18},{... | collective-permute-start | bytes 786440 | tf_op jit(solution)/shard_map/ppermute | solution.py:34
  3.9 11.5 %collective-permute-start.2 = (bf16[8,128,128]{2,1,0:T(8,128)(2,1)S(1)}, bf16[8,128,128]{2,1,0:T(8,128)(2,1)S(1)}, u32[]{:S(2)}, u32[]{:S(2)}) collective-permute-start(bf16[8,128,128]{2,1,0:T(8,128)(2,1)S(1)} %shard_map.97.refs_0_), channel_id=1, source_target_pairs={{0,8},{8,16},{16,24},{1,9},{9,17},{17,25},{2,10},{10,18},{18,26},{... | collective-permute-start | bytes 786440 | tf_op jit(solution)/shard_map/ppermute | solution.py:33
  9.4 0.7 copy-start.3
  9.5 0.7 copy-start.5
  10.8 5.5 %collective-permute-start = (bf16[2,80,128]{2,1,0:T(8,128)(2,1)S(1)}, bf16[2,80,128]{2,1,0:T(8,128)(2,1)S(1)}, u32[]{:S(2)}, u32[]{:S(2)}) collective-permute-start(bf16[2,80,128]{2,1,0:T(8,128)(2,1)S(1)} %get-tuple-element.22), channel_id=1, source_target_pairs={{0,16},{8,24},{16,0},{24,8},{1,17},{9,25},{17,1},{25,9},{2,18},{10... | collective-permute-start | bytes 122888 | tf_op jit(solution)/shard_map/ppermute | solution.py:24
  13.9 20.1 %collective-permute-start.6 = (bf16[8,128,128]{2,1,0:T(8,128)(2,1)S(1)}, bf16[8,128,128]{2,1,0:T(8,128)(2,1)S(1)}, u32[]{:S(2)}, u32[]{:S(2)}) collective-permute-start(bf16[8,128,128]{2,1,0:T(8,128)(2,1)S(1)} %collective-permute-done.5.refs_4_), channel_id=1, source_target_pairs={{8,0},{16,8},{9,1},{17,9},{10,2},{18,10},{11,3},{19,11},{12,4},{20... | collective-permute-start | bytes 786440 | tf_op jit(solution)/shard_map/ppermute | solution.py:34
  15.4 19.9 %collective-permute-start.3 = (bf16[8,128,128]{2,1,0:T(8,128)(2,1)S(1)}, bf16[8,128,128]{2,1,0:T(8,128)(2,1)S(1)}, u32[]{:S(2)}, u32[]{:S(2)}) collective-permute-start(bf16[8,128,128]{2,1,0:T(8,128)(2,1)S(1)} %collective-permute-done.2.refs_1_), channel_id=1, source_target_pairs={{8,16},{16,24},{9,17},{17,25},{10,18},{18,26},{11,19},{19,27},{12,... | collective-permute-start | bytes 786440 | tf_op jit(solution)/shard_map/ppermute | solution.py:33
  16.3 8.2 %collective-permute-start.1 = (bf16[2,80,128]{2,1,0:T(8,128)(2,1)S(1)}, bf16[2,80,128]{2,1,0:T(8,128)(2,1)S(1)}, u32[]{:S(2)}, u32[]{:S(2)}) collective-permute-start(bf16[2,80,128]{2,1,0:T(8,128)(2,1)S(1)} %get-tuple-element.24), channel_id=1, source_target_pairs={{0,8},{8,0},{16,24},{24,16},{1,9},{9,1},{17,25},{25,17},{2,10},{10... | collective-permute-start | bytes 122888 | tf_op jit(solution)/shard_map/ppermute | solution.py:24
  24.5 4.3 %collective-permute-start.8 = (bf16[1,4,64,128]{3,2,1,0:T(8,128)(2,1)S(1)}, bf16[1,4,64,128]{3,2,1,0:T(8,128)(2,1)S(1)}, u32[]{:S(2)}, u32[]{:S(2)}) collective-permute-start(bf16[1,4,64,128]{3,2,1,0:T(8,128)(2,1)S(1)} %get-tuple-element.26.first), channel_id=1, source_target_pairs={{0,2},{1,3},{2,0},{3,1},{4,6},{5,7},{6,4},{7,5},{8,10},{9,11},{10,... | collective-permute-start | bytes 196616 | tf_op jit(solution)/shard_map/ppermute | solution.py:24
  28.9 5.0 %collective-permute-start.9 = (bf16[2,4,64,128]{3,2,1,0:T(8,128)(2,1)S(1)}, bf16[2,4,64,128]{3,2,1,0:T(8,128)(2,1)S(1)}, u32[]{:S(2)}, u32[]{:S(2)}) collective-permute-start(bf16[2,4,64,128]{3,2,1,0:T(8,128)(2,1)S(1)} %shard_map.98.first), channel_id=1, source_target_pairs={{0,4},{1,5},{2,6},{3,7},{4,0},{5,1},{6,2},{7,3},{8,12},{9,13},{10,... | collective-permute-start | bytes 393224 | tf_op jit(solution)/shard_map/ppermute | solution.py:24
  33.9 2.1 %collective-permute-start.10 = (bf16[4,4,64,128]{3,2,1,0:T(8,128)(2,1)S(1)}, bf16[4,4,64,128]{3,2,1,0:T(8,128)(2,1)S(1)}, u32[]{:S(2)}, u32[]{:S(2)}) collective-permute-start(bf16[4,4,64,128]{3,2,1,0:T(8,128)(2,1)S(1)} %shard_map.99.refs_7_), channel_id=1, source_target_pairs={{0,1},{1,0},{2,3},{3,2},{4,5},{5,4},{6,7},{7,6},{8,9},{9,8},{10,11... | collective-permute-start | bytes 786440 | tf_op jit(solution)/shard_map/ppermute | solution.py:24
  34.0 10.6 %collective-permute-start.7 = (bf16[8,128,128]{2,1,0:T(8,128)(2,1)S(1)}, bf16[8,128,128]{2,1,0:T(8,128)(2,1)S(1)}, u32[]{:S(2)}, u32[]{:S(2)}) collective-permute-start(bf16[8,128,128]{2,1,0:T(8,128)(2,1)S(1)} %collective-permute-done.6.refs_5_), channel_id=1, source_target_pairs={{8,0},{9,1},{10,2},{11,3},{12,4},{13,5},{14,6},{15,7}} | collective-permute-start | bytes 786440 | tf_op jit(solution)/shard_map/ppermute | solution.py:34
  35.3 9.3 %collective-permute-start.4 = (bf16[8,128,128]{2,1,0:T(8,128)(2,1)S(1)}, bf16[8,128,128]{2,1,0:T(8,128)(2,1)S(1)}, u32[]{:S(2)}, u32[]{:S(2)}) collective-permute-start(bf16[8,128,128]{2,1,0:T(8,128)(2,1)S(1)} %collective-permute-done.3.refs_2_), channel_id=1, source_target_pairs={{16,24},{17,25},{18,26},{19,27},{20,28},{21,29},{22,30},{23,31}} | collective-permute-start | bytes 786440 | tf_op jit(solution)/shard_map/ppermute | solution.py:33
  44.6 13.6 %copy-start.6 = (bf16[256,256]{1,0:T(8,128)(2,1)S(1)}, bf16[256,256]{1,0:T(8,128)(2,1)}, u32[]{:S(2)}) copy-start(bf16[256,256]{1,0:T(8,128)(2,1)} %refs_5_.1) | copy-start | bytes 393220
  46.4 8.1 %collective-permute-start.13 = (bf16[4,64,128]{2,1,0:T(8,128)(2,1)S(1)}, bf16[4,64,128]{2,1,0:T(8,128)(2,1)S(1)}, u32[]{:S(2)}, u32[]{:S(2)}) collective-permute-start(bf16[4,64,128]{2,1,0:T(8,128)(2,1)S(1)} %get-tuple-element.27.refs_0_), channel_id=1, source_target_pairs={{0,24},{8,0},{16,8},{24,16},{1,25},{9,1},{17,9},{25,17},{2,26},{10... | collective-permute-start | bytes 196616 | tf_op jit(solution)/shard_map/ppermute | solution.py:19
  52.0 5.5 %collective-permute-start.12 = (bf16[4,64,128]{2,1,0:T(8,128)(2,1)S(1)}, bf16[4,64,128]{2,1,0:T(8,128)(2,1)S(1)}, u32[]{:S(2)}, u32[]{:S(2)}) collective-permute-start(bf16[4,64,128]{2,1,0:T(8,128)(2,1)S(1)} %get-tuple-element.27.refs_0_), channel_id=1, source_target_pairs={{0,16},{8,24},{16,0},{24,8},{1,17},{9,25},{17,1},{25,9},{2,18},{10... | collective-permute-start | bytes 196616 | tf_op jit(solution)/shard_map/ppermute | solution.py:19
  52.0 6.2 %collective-permute-start.11 = (bf16[4,64,128]{2,1,0:T(8,128)(2,1)S(1)}, bf16[4,64,128]{2,1,0:T(8,128)(2,1)S(1)}, u32[]{:S(2)}, u32[]{:S(2)}) collective-permute-start(bf16[4,64,128]{2,1,0:T(8,128)(2,1)S(1)} %get-tuple-element.27.refs_0_), channel_id=1, source_target_pairs={{0,8},{8,16},{16,24},{24,0},{1,9},{9,17},{17,25},{25,1},{2,10},{10... | collective-permute-start | bytes 196616 | tf_op jit(solution)/shard_map/ppermute | solution.py:19
  61.7 3.3 %collective-permute-start.17 = (bf16[4,128,256]{2,1,0:T(8,128)(2,1)S(1)}, bf16[4,128,256]{2,1,0:T(8,128)(2,1)S(1)}, u32[]{:S(2)}, u32[]{:S(2)}) collective-permute-start(bf16[4,128,256]{2,1,0:T(8,128)(2,1)S(1)} %get-tuple-element.34), channel_id=1, source_target_pairs={{0,1},{1,0},{2,3},{3,2},{4,5},{5,4},{6,7},{7,6},{8,9},{9,8},{10,11... | collective-permute-start | bytes 786440 | tf_op jit(solution)/shard_map/ppermute | solution.py:24
  61.8 1.7 %collective-permute-start.14 = (bf16[256,256]{1,0:T(8,128)(2,1)S(1)}, bf16[256,256]{1,0:T(8,128)(2,1)S(1)}, u32[]{:S(2)}, u32[]{:S(2)}) collective-permute-start(bf16[256,256]{1,0:T(8,128)(2,1)S(1)} %get-tuple-element.30.mine), channel_id=1, source_target_pairs={{0,1},{1,0},{2,3},{3,2},{4,5},{5,4},{6,7},{7,6},{8,9},{9,8},{10,11... | collective-permute-start | bytes 393224 | tf_op jit(solution)/shard_map/ppermute | solution.py:24
  63.5 5.6 %collective-permute-start.15 = (bf16[256,256]{1,0:T(8,128)(2,1)S(1)}, bf16[256,256]{1,0:T(8,128)(2,1)S(1)}, u32[]{:S(2)}, u32[]{:S(2)}) collective-permute-start(bf16[256,256]{1,0:T(8,128)(2,1)S(1)} %shard_map.102.mine), channel_id=1, source_target_pairs={{0,2},{1,3},{2,0},{3,1},{4,6},{5,7},{6,4},{7,5},{8,10},{9,11},{10,... | collective-permute-start | bytes 393224 | tf_op jit(solution)/shard_map/ppermute | solution.py:24
  65.1 5.4 %collective-permute-start.18 = (bf16[2,128,256]{2,1,0:T(8,128)(2,1)S(1)}, bf16[2,128,256]{2,1,0:T(8,128)(2,1)S(1)}, u32[]{:S(2)}, u32[]{:S(2)}) collective-permute-start(bf16[2,128,256]{2,1,0:T(8,128)(2,1)S(1)} %get-tuple-element.36), channel_id=1, source_target_pairs={{0,4},{1,5},{2,6},{3,7},{4,0},{5,1},{6,2},{7,3},{8,12},{9,13},{10,... | collective-permute-start | bytes 393224 | tf_op jit(solution)/shard_map/ppermute | solution.py:24
  69.1 5.0 %collective-permute-start.16 = (bf16[256,256]{1,0:T(8,128)(2,1)S(1)}, bf16[256,256]{1,0:T(8,128)(2,1)S(1)}, u32[]{:S(2)}, u32[]{:S(2)}) collective-permute-start(bf16[256,256]{1,0:T(8,128)(2,1)S(1)} %shard_map.103.mine), channel_id=1, source_target_pairs={{0,4},{1,5},{2,6},{3,7},{4,0},{5,1},{6,2},{7,3},{8,12},{9,13},{10,... | collective-permute-start | bytes 393224 | tf_op jit(solution)/shard_map/ppermute | solution.py:24
  70.5 4.4 %collective-permute-start.19 = (bf16[1,128,256]{2,1,0:T(8,128)(2,1)S(1)}, bf16[1,128,256]{2,1,0:T(8,128)(2,1)S(1)}, u32[]{:S(2)}, u32[]{:S(2)}) collective-permute-start(bf16[1,128,256]{2,1,0:T(8,128)(2,1)S(1)} %get-tuple-element.38), channel_id=1, source_target_pairs={{0,2},{1,3},{2,0},{3,1},{4,6},{5,7},{6,4},{7,5},{8,10},{9,11},{10,... | collective-permute-start | bytes 196616 | tf_op jit(solution)/shard_map/ppermute | solution.py:24

commit v5 on v4

v5 whole, which is shorter than its diff:
```python
import functools

import jax
import jax.numpy as jnp
from jax import lax
from jax.experimental import pallas as pl
from jax.experimental.pallas import tpu as pltpu
from jax.sharding import PartitionSpec as P

F32 = jnp.float32
BF16 = jnp.bfloat16
VMEM = pl.BlockSpec(memory_space=pltpu.VMEM)
SMEM = pl.BlockSpec(memory_space=pltpu.SMEM)
PAD = 16


def shift(array, by):
    peers = lax.axis_size("rep")
    return lax.ppermute(array, "rep", [(i, (i + by) % peers) for i in range(peers)])


def swap(array, axis, bit):
    peers = lax.axis_size(axis)
    return lax.ppermute(array, axis, [(i, i ^ bit) for i in range(peers)])


def call(body, outs, in_specs, scratch=(), flops=0, moved=0):
    return pl.pallas_call(
        body,
        out_shape=outs,
        in_specs=in_specs,
        out_specs=jax.tree.map(lambda _: VMEM, outs),
        scratch_shapes=list(scratch),
        compiler_params=pltpu.CompilerParams(vmem_limit_bytes=48 * 1024 * 1024),
        cost_estimate=pl.CostEstimate(flops=flops, bytes_accessed=moved, transcendentals=0),
    )


def dot(a, b, a_dim, b_dim):
    return lax.dot_general(a, b, (((a_dim,), (b_dim,)), ((), ())), preferred_element_type=F32)


def member_and(by, reps):
    return lax.rem(lax.axis_index("rep") + by, reps)


def pack(blocks, cotangent, out):
    slots, block = blocks.shape[:2]
    for q in range(out.shape[0]):
        out[q, :slots] = blocks[...]
        for k in range(cotangent.shape[1] // block):
            out[q, slots + k] = cotangent[:, k * block : (k + 1) * block]


def split_features(reps, lists, cap, feats, rows, cols, counts, keep, send, turned):
    nodes = feats.shape[0]
    part = feats.shape[1] // reps
    turned[...] = feats[...].astype(F32).T.astype(BF16).reshape(turned.shape)
    lane = lax.broadcasted_iota(jnp.int32, (PAD, nodes), 1)
    index = jnp.zeros((PAD, nodes), jnp.int32)
    slots = lists * cap
    for j in range(lists):
        for c in range(cap):
            k = j * cap + c
            index = jnp.where(lane == k, rows[j, c], index)
            index = jnp.where(lane == slots + k, cols[j, c], index)
        index = jnp.where(lane == 2 * slots + j, counts[j], index)
    index = index.astype(F32).astype(BF16)
    me = lax.axis_index("rep")
    half = reps // 2
    for d in range(reps):
        out = send if d >= half else keep
        out[d % half, :part] = turned[lax.bitwise_xor(me, d)]
        out[d % half, part:] = index


def regroup(held, gone, keep, arrived, next_keep, next_send):
    half = gone // 2
    for o in range(held):
        for source, base in ((keep, 0), (arrived, held)):
            for d in range(half):
                next_keep[(base + o) * half + d] = source[o * gone + d]
                next_send[(base + o) * half + d] = source[o * gone + half + d]


def order_chunks(reps, part, keep, arrived, mine, index):
    me = lax.axis_index("rep")
    half = reps // 2
    for k in range(reps):
        source = arrived if k >= half else keep
        origin = lax.bitwise_xor(me, origin_bits(k, reps))
        mine[origin] = source[k % half, :part]
        index[origin] = source[k % half, part:].astype(F32).astype(jnp.int32)


def origin_bits(k, reps):
    bits, value, origin = reps.bit_length() - 1, k, 0
    for i in range(bits):
        if value >> i & 1:
            origin |= 1 << (bits - 1 - i)
    return origin


def join(*refs):
    out = refs[-1]
    for k, ref in enumerate(refs[:-1]):
        out[k] = ref[...]


def slot_of(index, lists, cap, t, j, c):
    k = j * cap + c
    slots = lists * cap
    return index[t, 0, k], index[t, 0, slots + k], c < index[t, 0, 2 * slots + j]


def relative(groups, offset):
    mine = lax.axis_index("blk")
    return lax.bitwise_xor(mine, lax.rem(mine + groups - offset, groups))


def aggregate(reps, groups, lists, cap, index, blocks, near, far, out, total):
    total[...] = jnp.zeros_like(total)
    for origin in range(reps):
        for j in range(lists):
            offset = origin * lists + j
            held = far if offset % 2 else near
            place = lax.div(relative(groups, offset), 2)
            for c in range(cap):
                row, col, live = slot_of(index, lists, cap, origin, j, c)
                product = dot(held[place, col], blocks[origin, j * cap + c], 1, 1)
                total[row] += jnp.where(live, product, 0.0)
    out[...] = total[...].astype(BF16)


def dense_layer(reps, *refs):
    chunks = refs[:reps]
    packed, weight, out, dagg, terms, agg, outs = refs[reps:]
    nodes, width = out.shape
    slots = packed.shape[1] - width // packed.shape[3]
    for t in range(reps):
        origin = member_and(reps - t, reps)
        for b in range(reps):
            agg[b, origin] = chunks[t][b]
    gw = jnp.zeros((width, width), F32)
    for b in range(reps):
        turned = agg[b].reshape(width, nodes)
        pre = dot(turned, weight[...], 0, 0)
        sigma = jax.nn.sigmoid(pre)
        outs[b] = (pre * sigma).astype(BF16)
        slope = sigma * (1.0 + pre * (1.0 - sigma))
        cot = jnp.concatenate(
            [packed[b, k] for k in range(slots, packed.shape[1])], axis=1
        ).astype(F32)
        dpre = (cot * slope).astype(BF16)
        dagg[b] = dot(dpre, weight[...], 1, 1).astype(BF16)
        gw += dot(turned, dpre, 1, 0)
    out[...] = outs[lax.axis_index("rep")]
    terms[...] = gw.astype(BF16)


def feature_grads(reps, groups, lists, cap, index, blocks, dagg, terms, keep, send, total):
    me = lax.axis_index("rep")
    half = groups // 2
    keep[...] = jnp.zeros_like(keep)
    total[...] = jnp.zeros_like(total)
    for origin in range(reps):
        for j in range(lists):
            offset = origin * lists + j
            target = total if offset % 2 else keep
            place = lax.div(relative(groups, offset), 2)
            for c in range(cap):
                row, col, live = slot_of(index, lists, cap, origin, j, c)

                @pl.when(jnp.logical_and(live, col == me))
                def _():
                    target[place] += dot(blocks[origin, j * cap + c], dagg[row], 0, 0)

    send[:half] = total[...].astype(BF16)
    send[half:] = terms[...].reshape(-1, *send.shape[1:])


def add_core(half, keep, terms, arrived, own, gw, *sends):
    own[...] = keep[0] + arrived[0].astype(F32)
    for k in range(1, half):
        sends[k - 1][...] = (keep[k] + arrived[k].astype(F32)).astype(BF16)
    other = arrived[half:].reshape(terms.shape).astype(F32)
    gw[...] = (terms[...].astype(F32) + other).astype(BF16)


def add_terms(mine, arrived, out):
    out[...] = (mine[...].astype(F32) + arrived[...].astype(F32)).astype(out.dtype)


def add_last(own, *refs):
    total = own[...]
    for ref in refs[:-1]:
        total += ref[...].astype(F32)
    refs[-1][...] = total


def per_device(feats, weight, cotangent, block_vals, block_rows, block_cols, step_counts):
    reps = lax.axis_size("rep")
    groups = lax.axis_size("blk")
    lists, cap, block = block_vals.shape[2:5]
    nodes, width = feats.shape
    part = width // reps
    extra = width // block
    slots = lists * cap
    half = groups // 2
    like = jax.ShapeDtypeStruct

    packed = call(
        pack,
        like((reps, slots + extra, block, block), BF16),
        [VMEM] * 2,
        moved=2 * (1 + reps) * (slots + extra) * block * block,
    )(block_vals.reshape(slots, block, block), cotangent)
    packed = lax.all_to_all(packed, "rep", 0, 0, tiled=True)

    piece = like((reps // 2, part + PAD, nodes), BF16)
    keep, send = call(
        functools.partial(split_features, reps, lists, cap),
        [piece] * 2,
        [VMEM, SMEM, SMEM, SMEM],
        [pltpu.VMEM((reps, part, nodes), BF16)],
        moved=4 * nodes * width,
    )(feats, block_rows[0, 0], block_cols[0, 0], step_counts[0, 0])
    bit, origins = reps // 2, 1
    arrived = swap(send, "rep", bit)
    while bit > 1:
        keep, send = call(
            functools.partial(regroup, origins, bit),
            [piece] * 2,
            [VMEM] * 2,
            moved=4 * nodes * width,
        )(keep, arrived)
        bit, origins = bit // 2, origins * 2
        arrived = swap(send, "rep", bit)
    mine, index = call(
        functools.partial(order_chunks, reps, part),
        [like((reps, part, nodes), BF16), like((reps, PAD, nodes), jnp.int32)],
        [VMEM] * 2,
        moved=4 * nodes * width,
    )(keep, arrived)

    near = call(
        join,
        like((half, reps, part, nodes), BF16),
        [VMEM] * half,
        moved=4 * half * nodes * width,
    )(mine, *[swap(mine, "blk", 2 * k) for k in range(1, half)])
    far = swap(near, "blk", 1)
    slot_flops = 2 * groups * cap * part * block * block
    slot_bytes = 2 * (groups * cap * block * block + groups * nodes * width)

    agg = call(
        functools.partial(aggregate, reps, groups, lists, cap),
        like((reps, part, nodes), BF16),
        [SMEM] + [VMEM] * 3,
        [pltpu.VMEM((reps, part, nodes), F32)],
        flops=slot_flops,
        moved=slot_bytes,
    )(index, packed, near, far)
    aggs = [agg] + [shift(agg, t) for t in range(1, reps)]

    out_rows, dagg, terms = call(
        functools.partial(dense_layer, reps),
        [
            like((nodes, width), BF16),
            like((reps, nodes, width), BF16),
            like((width, width), BF16),
        ],
        [VMEM] * (reps + 2),
        [
            pltpu.VMEM((reps, reps, part, nodes), BF16),
            pltpu.VMEM((reps, nodes, width), BF16),
        ],
        flops=6 * reps * nodes * width * width,
        moved=2 * reps * 5 * nodes * width,
    )(*aggs, packed, weight)

    keep, send = call(
        functools.partial(feature_grads, reps, groups, lists, cap),
        [
            like((half, nodes, width), F32),
            like((half + width // nodes, nodes, width), BF16),
        ],
        [SMEM] + [VMEM] * 3,
        [pltpu.VMEM((half, nodes, width), F32)],
        flops=slot_flops,
        moved=slot_bytes,
    )(index, packed, dagg, terms)
    own, terms, *sends = call(
        functools.partial(add_core, half),
        [like((nodes, width), F32), like((width, width), BF16)]
        + [like((nodes, width), BF16)] * (half - 1),
        [VMEM] * 3,
        moved=10 * half * nodes * width,
    )(keep, terms, swap(send, "blk", 1))
    rest = [swap(sends[k - 1], "blk", 2 * k) for k in range(1, half)]

    bit = 2
    while bit < groups:
        other = swap(terms, "blk", bit)
        bit *= 2
        terms = call(
            add_terms,
            like((width, width), BF16 if bit < groups else F32),
            [VMEM] * 2,
            moved=6 * width * width,
        )(terms, other)
    grad_feats = call(
        add_last,
        like((nodes, width), F32),
        [VMEM] * half,
        moved=(6 + 2 * half) * nodes * width,
    )(own, *rest)
    return (out_rows, terms, grad_feats)


def solution(mesh):
    return jax.shard_map(
        per_device,
        mesh=mesh,
        in_specs=(
            P(("blk", "rep"), None),
            P(),
            P(("blk", "rep"), None),
            P("blk", "rep", None, None, None, None),
            P("blk", "rep", None, None),
            P("blk", "rep", None, None),
            P("blk", "rep", None),
        ),
        out_specs=(P(("blk", "rep"), None), P(), P(("blk", "rep"), None)),
        check_vma=False,
    )
```

time: 76.1 us -> 82.4 us (1.083)
  waiting for transfers between devices: 28.8 us -> 48.8 us
  starting transfers between devices: 35.9 us -> 21.3 us
  Pallas kernels: 7.61 us -> 9.08 us
    ppermute x11 -> x12, waiting for transfers between devices: 14.5 us -> 44 us  [swap(): return lax.ppermute(array, axis, [(i, i ^ bit) for i in range(peers)])]
    ppermute x6 -> x0, starting transfers between devices: 10.9 us -> none  [the longest x3 6.91 us: relay(): below.append(lax.ppermute(below[-1], 'rep', up))]
    ppermute x6 -> x0, waiting for transfers between devices: 8.81 us -> none  [the longest x3 8.58 us: relay(): above.append(lax.ppermute(above[-1], 'rep', down))]
    ppermute x11 -> x12, starting transfers between devices: 18.8 us -> 10.9 us  [swap(): return lax.ppermute(array, axis, [(i, i ^ bit) for i in range(peers)])]
    all_to_all x0 -> x1, starting transfers between devices: none -> 6.45 us  [per_device(): packed = lax.all_to_all(packed, 'rep', 0, 0, tiled=True)]
    ppermute x3, starting transfers between devices: 6.21 us -> 3.87 us  [shift(): lax.ppermute(array, 'rep', [(i, (i + by) % peers) for i in range(peers)])]
    pallas_call x8 -> x6, Pallas kernels: 2.65 us -> 3.62 us  [the longest x1 1.72 us: per_device(): call(functools.partial(aggregate, reps, groups, lists, cap), like((reps,...]
  transfers between devices with their start and end apart: 20 -> 16, of which waited for: 12 -> 13; matrix products, arithmetic and copies ran while one was open for 0% -> 0% of each run, Pallas kernels for 2% -> 2%
where the time goes in v5:
time: 82.4 us; the launch traced here: 82.3 us
  waiting for transfers between devices  48.8 us (59%)
  starting transfers between devices  21.3 us (26%)
  Pallas kernels  9.08 us (11%)
  local copies, waits for them, and re-layouts  2.43 us (3%)
    ppermute x12, waiting for transfers between devices, swap(): return lax.ppermute(array, axis, [(i, i ^ bit) for i in range(peers)])  44 us
    ppermute x12, starting transfers between devices, swap(): return lax.ppermute(array, axis, [(i, i ^ bit) for i in range(peers)])  10.9 us
    all_to_all x1, starting transfers between devices, per_device(): packed = lax.all_to_all(packed, 'rep', 0, 0, tiled=True)  6.45 us
    ppermute x3, waiting for transfers between devices, shift(): lax.ppermute(array, 'rep', [(i, (i + by) % peers) for i in range(peers)])  4.82 us
    ppermute x3, starting transfers between devices, shift(): lax.ppermute(array, 'rep', [(i, (i + by) % peers) for i in range(peers)])  3.87 us
    pallas_call x1, Pallas kernels, per_device(): call(functools.partial(feature_grads, reps, groups, lists, cap), [like((h...  2.68 us
    unnamed x14, local copies, waits for them, and re-layouts  2.43 us
    pallas_call x1, Pallas kernels, per_device(): call(functools.partial(aggregate, reps, groups, lists, cap), like((reps,...  1.72 us
  transfers between devices with their start and end apart: 16, of which 13 were waited for; matrix products, arithmetic and copies ran while one was open for 0% of the time, Pallas kernels for 2%

profile of v5, /device:TPU:0, one launch (start us, length us, event | category | flops | bytes accessed | tf_op | source)
XLA Modules:
  0.0 82.3 jit_solution(9338590336969524733)
XLA Ops:
  0.6 0.0 copy-start
  0.6 0.9 %copy-done = bf16[1,1,2,3,128,128]{5,4,3,2,1,0:T(8,128)(2,1)S(1)} copy-done((bf16[1,1,2,3,128,128]{5,4,3,2,1,0:T(8,128)(2,1)S(1)}, bf16[1,1,2,3,128,128]{5,4,3,2,1,0:T(8,128)(2,1)}, u32[]{:S(2)}) %copy-start) | copy-done | bytes 196632
  1.6 0.8 %copy-done.2 = bf16[128,256]{1,0:T(8,128)(2,1)S(1)} copy-done((bf16[128,256]{1,0:T(8,128)(2,1)S(1)}, bf16[128,256]{1,0:T(8,128)(2,1)}, u32[]{:S(2)}) %copy-start.2) | copy-done | bytes 65560
  2.4 1.1 %shard_map.97 = bf16[4,8,128,128]{3,2,1,0:T(8,128)(2,1)} custom-call(bf16[6,128,128]{2,1,0:T(8,128)(2,1)S(1)} %bitcast.4, bf16[128,256]{1,0:T(8,128)(2,1)S(1)} %copy-done.2), custom_call_target="tpu_custom_call" | custom-call | bytes 1310720 | tf_op jit(solution)/shard_map/pallas_call | solution.py:212
  3.5 6.4 %all-to-all-start = ((bf16[4,8,128,128]{3,2,1,0:T(8,128)(2,1)}), bf16[4,8,128,128]{3,2,1,0:T(8,128)(2,1)S(1)}, u32[]{:S(2)}, u32[]{:S(2)}) async-start(bf16[4,8,128,128]{3,2,1,0:T(8,128)(2,1)} %shard_map.97), calls=%async_computation | async-start | bytes 2097152 | tf_op jit(solution)/shard_map/all_to_all | solution.py:218
  10.0 0.0 copy-done.3
  10.0 0.0 copy-done.5
  10.0 0.7 copy-done.4
  10.6 0.0 copy-done.6
  10.6 0.7 shard_map.94
  11.3 3.0 %collective-permute-start = (bf16[2,80,128]{2,1,0:T(8,128)(2,1)S(1)}, bf16[2,80,128]{2,1,0:T(8,128)(2,1)S(1)}, u32[]{:S(2)}, u32[]{:S(2)}) collective-permute-start(bf16[2,80,128]{2,1,0:T(8,128)(2,1)S(1)} %get-tuple-element.20), channel_id=1, source_target_pairs={{0,16},{8,24},{16,0},{24,8},{1,17},{9,25},{17,1},{25,9},{2,18},{10... | collective-permute-start | bytes 122888 | tf_op jit(solution)/shard_map/ppermute | solution.py:24
  14.3 23.1 %collective-permute-done.arrived = bf16[2,80,128]{2,1,0:T(8,128)(2,1)S(1)} collective-permute-done((bf16[2,80,128]{2,1,0:T(8,128)(2,1)S(1)}, bf16[2,80,128]{2,1,0:T(8,128)(2,1)S(1)}, u32[]{:S(2)}, u32[]{:S(2)}) %collective-permute-start) | collective-permute-done | bytes 40992 | tf_op jit(solution)/shard_map/ppermute | solution.py:24
  37.5 0.0 collective-permute-start.1
  37.5 4.0 %collective-permute-done.1.arrived = bf16[2,80,128]{2,1,0:T(8,128)(2,1)S(1)} collective-permute-done((bf16[2,80,128]{2,1,0:T(8,128)(2,1)S(1)}, bf16[2,80,128]{2,1,0:T(8,128)(2,1)S(1)}, u32[]{:S(2)}, u32[]{:S(2)}) %collective-permute-start.1) | collective-permute-done | bytes 40992 | tf_op jit(solution)/shard_map/ppermute | solution.py:24
  41.5 1.6 %collective-permute-start.2 = (bf16[4,64,128]{2,1,0:T(8,128)(2,1)S(1)}, bf16[4,64,128]{2,1,0:T(8,128)(2,1)S(1)}, u32[]{:S(2)}, u32[]{:S(2)}) collective-permute-start(bf16[4,64,128]{2,1,0:T(8,128)(2,1)S(1)} %get-tuple-element.24.refs_0_), channel_id=1, source_target_pairs={{0,2},{1,3},{2,0},{3,1},{4,6},{5,7},{6,4},{7,5},{8,10},{9,11},{10,... | collective-permute-start | bytes 196616 | tf_op jit(solution)/shard_map/ppermute | solution.py:24
  43.0 1.5 %collective-permute-start.3 = (bf16[4,64,128]{2,1,0:T(8,128)(2,1)S(1)}, bf16[4,64,128]{2,1,0:T(8,128)(2,1)S(1)}, u32[]{:S(2)}, u32[]{:S(2)}) collective-permute-start(bf16[4,64,128]{2,1,0:T(8,128)(2,1)S(1)} %get-tuple-element.24.refs_0_), channel_id=1, source_target_pairs={{0,4},{1,5},{2,6},{3,7},{4,0},{5,1},{6,2},{7,3},{8,12},{9,13},{10,... | collective-permute-start | bytes 196616 | tf_op jit(solution)/shard_map/ppermute | solution.py:24
  44.5 0.5 collective-permute-start.4
  45.0 0.8 collective-permute-done.2.refs_1_
  45.8 1.5 %collective-permute-done.3.refs_2_ = bf16[4,64,128]{2,1,0:T(8,128)(2,1)S(1)} collective-permute-done((bf16[4,64,128]{2,1,0:T(8,128)(2,1)S(1)}, bf16[4,64,128]{2,1,0:T(8,128)(2,1)S(1)}, u32[]{:S(2)}, u32[]{:S(2)}) %collective-permute-start.3) | collective-permute-done | bytes 65568 | tf_op jit(solution)/shard_map/ppermute | solution.py:24
  47.3 2.4 %collective-permute-done.4.refs_3_ = bf16[4,64,128]{2,1,0:T(8,128)(2,1)S(1)} collective-permute-done((bf16[4,64,128]{2,1,0:T(8,128)(2,1)S(1)}, bf16[4,64,128]{2,1,0:T(8,128)(2,1)S(1)}, u32[]{:S(2)}, u32[]{:S(2)}) %collective-permute-start.4) | collective-permute-done | bytes 65568 | tf_op jit(solution)/shard_map/ppermute | solution.py:24
  49.7 0.1 collective-permute-start.5
  49.8 1.5 %collective-permute-done.5.far = bf16[4,4,64,128]{3,2,1,0:T(8,128)(2,1)S(1)} collective-permute-done((bf16[4,4,64,128]{3,2,1,0:T(8,128)(2,1)S(1)}, bf16[4,4,64,128]{3,2,1,0:T(8,128)(2,1)S(1)}, u32[]{:S(2)}, u32[]{:S(2)}) %collective-permute-start.5) | collective-permute-done | bytes 262176 | tf_op jit(solution)/shard_map/ppermute | solution.py:24
  51.3 0.0 all-to-all-done.blocks.refs_4_
  51.3 1.7 %shard_map.99.refs_0_ = bf16[4,64,128]{2,1,0:T(8,128)(2,1)S(1)} custom-call(s32[4,16,128]{2,1,0:T(8,128)S(1)} %get-tuple-element.23.index, bf16[4,8,128,128]{3,2,1,0:T(8,128)(2,1)S(1)} %all-to-all-done.blocks.refs_4_, bf16[4,4,64,128]{3,2,1,0:T(8,128)(2,1)S(1)} %shard_map.98.near, bf16[4,4,64,128]{3,2,1,0:T(8,128)(2,1)S(1)} %collective-permute-done.5.far), custom_call_target="tpu_custom_call" | custom-call | flops 50331648 | bytes 1310720 | tf_op jit(solution)/shard_map/pallas_call | solution.py:256
  53.1 0.1 collective-permute-start.6
  53.1 2.0 %collective-permute-start.7 = (bf16[4,64,128]{2,1,0:T(8,128)(2,1)S(1)}, bf16[4,64,128]{2,1,0:T(8,128)(2,1)S(1)}, u32[]{:S(2)}, u32[]{:S(2)}) collective-permute-start(bf16[4,64,128]{2,1,0:T(8,128)(2,1)S(1)} %shard_map.99.refs_0_), channel_id=1, source_target_pairs={{0,16},{8,24},{16,0},{24,8},{1,17},{9,25},{17,1},{25,9},{2,18},{10... | collective-permute-start | bytes 196616 | tf_op jit(solution)/shard_map/ppermute | solution.py:19
  55.1 1.8 %collective-permute-start.8 = (bf16[4,64,128]{2,1,0:T(8,128)(2,1)S(1)}, bf16[4,64,128]{2,1,0:T(8,128)(2,1)S(1)}, u32[]{:S(2)}, u32[]{:S(2)}) collective-permute-start(bf16[4,64,128]{2,1,0:T(8,128)(2,1)S(1)} %shard_map.99.refs_0_), channel_id=1, source_target_pairs={{0,24},{8,0},{16,8},{24,16},{1,25},{9,1},{17,9},{25,17},{2,26},{10... | collective-permute-start | bytes 196616 | tf_op jit(solution)/shard_map/ppermute | solution.py:19
  56.9 3.0 %collective-permute-done.6.refs_1_ = bf16[4,64,128]{2,1,0:T(8,128)(2,1)S(1)} collective-permute-done((bf16[4,64,128]{2,1,0:T(8,128)(2,1)S(1)}, bf16[4,64,128]{2,1,0:T(8,128)(2,1)S(1)}, u32[]{:S(2)}, u32[]{:S(2)}) %collective-permute-start.6) | collective-permute-done | bytes 65568 | tf_op jit(solution)/shard_map/ppermute | solution.py:19
  59.9 1.9 %collective-permute-done.7.refs_2_ = bf16[4,64,128]{2,1,0:T(8,128)(2,1)S(1)} collective-permute-done((bf16[4,64,128]{2,1,0:T(8,128)(2,1)S(1)}, bf16[4,64,128]{2,1,0:T(8,128)(2,1)S(1)}, u32[]{:S(2)}, u32[]{:S(2)}) %collective-permute-start.7) | collective-permute-done | bytes 65568 | tf_op jit(solution)/shard_map/ppermute | solution.py:19
  61.8 0.0 collective-permute-done.8.refs_3_
  61.8 0.0 copy-done.1
  61.8 1.3 %shard_map.100 = (bf16[128,256]{1,0:T(8,128)(2,1)}, bf16[4,128,256]{2,1,0:T(8,128)(2,1)S(1)}, bf16[256,256]{1,0:T(8,128)(2,1)S(1)}) custom-call(bf16[4,64,128]{2,1,0:T(8,128)(2,1)S(1)} %shard_map.99.refs_0_, bf16[4,64,128]{2,1,0:T(8,128)(2,1)S(1)} %collective-permute-done.6.refs_1_, bf16[4,64,128]{2,1,0:T(8,128)(2,1)S(1)} %collective-permute-done.7.refs_2_, ...), custom_call_target="tpu_custom_call" | custom-call | flops 201326592 | bytes 1310720 | tf_op jit(solution)/shard_map/pallas_call | solution.py:266
  63.1 2.7 %shard_map.101 = (f32[4,128,256]{2,1,0:T(8,128)S(1)}, bf16[6,128,256]{2,1,0:T(8,128)(2,1)S(1)}) custom-call(s32[4,16,128]{2,1,0:T(8,128)S(1)} %get-tuple-element.23.index, bf16[4,8,128,128]{3,2,1,0:T(8,128)(2,1)S(1)} %all-to-all-done.blocks.refs_4_, bf16[4,128,256]{2,1,0:T(8,128)(2,1)S(1)} %get-tuple-element.26.dagg, ...), custom_call_target="tpu_custom_call" | custom-call | flops 50331648 | bytes 1310720 | tf_op jit(solution)/shard_map/pallas_call | solution.py:282
  65.8 0.1 collective-permute-start.9
  65.9 1.7 %collective-permute-done.9.arrived = bf16[6,128,256]{2,1,0:T(8,128)(2,1)S(1)} collective-permute-done((bf16[6,128,256]{2,1,0:T(8,128)(2,1)S(1)}, bf16[6,128,256]{2,1,0:T(8,128)(2,1)S(1)}, u32[]{:S(2)}, u32[]{:S(2)}) %collective-permute-start.9) | collective-permute-done | bytes 393248 | tf_op jit(solution)/shard_map/ppermute | solution.py:24
  67.6 0.1 shard_map.102
  67.7 0.2 collective-permute-start.10
  67.9 5.4 %collective-permute-done.10.arrived = bf16[256,256]{1,0:T(8,128)(2,1)S(1)} collective-permute-done((bf16[256,256]{1,0:T(8,128)(2,1)S(1)}, bf16[256,256]{1,0:T(8,128)(2,1)S(1)}, u32[]{:S(2)}, u32[]{:S(2)}) %collective-permute-start.10) | collective-permute-done | bytes 131104 | tf_op jit(solution)/shard_map/ppermute | solution.py:24
  73.3 0.6 collective-permute-start.11
  73.9 0.3 collective-permute-start.12
  74.2 1.5 %collective-permute-start.13 = (bf16[128,256]{1,0:T(8,128)(2,1)S(1)}, bf16[128,256]{1,0:T(8,128)(2,1)S(1)}, u32[]{:S(2)}, u32[]{:S(2)}) collective-permute-start(bf16[128,256]{1,0:T(8,128)(2,1)S(1)} %get-tuple-element.33), channel_id=1, source_target_pairs={{0,4},{1,5},{2,6},{3,7},{4,0},{5,1},{6,2},{7,3},{8,12},{9,13},{10,... | collective-permute-start | bytes 196616 | tf_op jit(solution)/shard_map/ppermute | solution.py:24
  75.7 1.7 %collective-permute-start.14 = (bf16[128,256]{1,0:T(8,128)(2,1)S(1)}, bf16[128,256]{1,0:T(8,128)(2,1)S(1)}, u32[]{:S(2)}, u32[]{:S(2)}) collective-permute-start(bf16[128,256]{1,0:T(8,128)(2,1)S(1)} %get-tuple-element.34), channel_id=1, source_target_pairs={{0,6},{1,7},{2,4},{3,5},{4,2},{5,3},{6,0},{7,1},{8,14},{9,15},{10,... | collective-permute-start | bytes 196616 | tf_op jit(solution)/shard_map/ppermute | solution.py:24
  77.4 1.0 %collective-permute-done.12.refs_0_ = bf16[128,256]{1,0:T(8,128)(2,1)S(1)} collective-permute-done((bf16[128,256]{1,0:T(8,128)(2,1)S(1)}, bf16[128,256]{1,0:T(8,128)(2,1)S(1)}, u32[]{:S(2)}, u32[]{:S(2)}) %collective-permute-start.12) | collective-permute-done | bytes 65568 | tf_op jit(solution)/shard_map/ppermute | solution.py:24
  78.4 1.8 %collective-permute-done.13.refs_1_ = bf16[128,256]{1,0:T(8,128)(2,1)S(1)} collective-permute-done((bf16[128,256]{1,0:T(8,128)(2,1)S(1)}, bf16[128,256]{1,0:T(8,128)(2,1)S(1)}, u32[]{:S(2)}, u32[]{:S(2)}) %collective-permute-start.13) | collective-permute-done | bytes 65568 | tf_op jit(solution)/shard_map/ppermute | solution.py:24
  80.2 0.7 collective-permute-done.14.refs_2_
  80.9 0.7 shard_map.105
  81.6 0.0 collective-permute-done.11.arrived
  81.6 0.7 shard_map.104
  (10 shorter events, 0.1 us)
Async XLA Ops:
  0.6 0.9 %copy-start = (bf16[1,1,2,3,128,128]{5,4,3,2,1,0:T(8,128)(2,1)S(1)}, bf16[1,1,2,3,128,128]{5,4,3,2,1,0:T(8,128)(2,1)}, u32[]{:S(2)}) copy-start(bf16[1,1,2,3,128,128]{5,4,3,2,1,0:T(8,128)(2,1)} %param.10) | copy-start | bytes 589828
  1.6 0.8 %copy-start.2 = (bf16[128,256]{1,0:T(8,128)(2,1)S(1)}, bf16[128,256]{1,0:T(8,128)(2,1)}, u32[]{:S(2)}) copy-start(bf16[128,256]{1,0:T(8,128)(2,1)} %cotangent.1) | copy-start | bytes 196612
  3.5 6.5 %copy-start.3 = (bf16[128,256]{1,0:T(8,128)(2,1)S(1)}, bf16[128,256]{1,0:T(8,128)(2,1)}, u32[]{:S(2)}) copy-start(bf16[128,256]{1,0:T(8,128)(2,1)} %feats.1) | copy-start | bytes 196612
  3.5 6.5 %copy-start.5 = (s32[1,1,2,3]{3,2,1,0:T(2,128)S(1)}, s32[1,1,2,3]{3,2,1,0:T(2,128)}, u32[]{:S(2)}) copy-start(s32[1,1,2,3]{3,2,1,0:T(2,128)} %param.12) | copy-start | bytes 76
  3.5 47.8 %all-to-all-start = ((bf16[4,8,128,128]{3,2,1,0:T(8,128)(2,1)}), bf16[4,8,128,128]{3,2,1,0:T(8,128)(2,1)S(1)}, u32[]{:S(2)}, u32[]{:S(2)}) async-start(bf16[4,8,128,128]{3,2,1,0:T(8,128)(2,1)} %shard_map.97), calls=%async_computation | async-start | bytes 2097152 | tf_op jit(solution)/shard_map/all_to_all | solution.py:218
  10.0 0.7 copy-start.4
  10.0 0.7 copy-start.6
  11.3 26.1 %collective-permute-start = (bf16[2,80,128]{2,1,0:T(8,128)(2,1)S(1)}, bf16[2,80,128]{2,1,0:T(8,128)(2,1)S(1)}, u32[]{:S(2)}, u32[]{:S(2)}) collective-permute-start(bf16[2,80,128]{2,1,0:T(8,128)(2,1)S(1)} %get-tuple-element.20), channel_id=1, source_target_pairs={{0,16},{8,24},{16,0},{24,8},{1,17},{9,25},{17,1},{25,9},{2,18},{10... | collective-permute-start | bytes 122888 | tf_op jit(solution)/shard_map/ppermute | solution.py:24
  37.5 4.0 %collective-permute-start.1 = (bf16[2,80,128]{2,1,0:T(8,128)(2,1)S(1)}, bf16[2,80,128]{2,1,0:T(8,128)(2,1)S(1)}, u32[]{:S(2)}, u32[]{:S(2)}) collective-permute-start(bf16[2,80,128]{2,1,0:T(8,128)(2,1)S(1)} %get-tuple-element.22), channel_id=1, source_target_pairs={{0,8},{8,0},{16,24},{24,16},{1,9},{9,1},{17,25},{25,17},{2,10},{10... | collective-permute-start | bytes 122888 | tf_op jit(solution)/shard_map/ppermute | solution.py:24
  41.5 4.4 %collective-permute-start.2 = (bf16[4,64,128]{2,1,0:T(8,128)(2,1)S(1)}, bf16[4,64,128]{2,1,0:T(8,128)(2,1)S(1)}, u32[]{:S(2)}, u32[]{:S(2)}) collective-permute-start(bf16[4,64,128]{2,1,0:T(8,128)(2,1)S(1)} %get-tuple-element.24.refs_0_), channel_id=1, source_target_pairs={{0,2},{1,3},{2,0},{3,1},{4,6},{5,7},{6,4},{7,5},{8,10},{9,11},{10,... | collective-permute-start | bytes 196616 | tf_op jit(solution)/shard_map/ppermute | solution.py:24
  43.0 4.3 %collective-permute-start.3 = (bf16[4,64,128]{2,1,0:T(8,128)(2,1)S(1)}, bf16[4,64,128]{2,1,0:T(8,128)(2,1)S(1)}, u32[]{:S(2)}, u32[]{:S(2)}) collective-permute-start(bf16[4,64,128]{2,1,0:T(8,128)(2,1)S(1)} %get-tuple-element.24.refs_0_), channel_id=1, source_target_pairs={{0,4},{1,5},{2,6},{3,7},{4,0},{5,1},{6,2},{7,3},{8,12},{9,13},{10,... | collective-permute-start | bytes 196616 | tf_op jit(solution)/shard_map/ppermute | solution.py:24
  44.5 5.2 %collective-permute-start.4 = (bf16[4,64,128]{2,1,0:T(8,128)(2,1)S(1)}, bf16[4,64,128]{2,1,0:T(8,128)(2,1)S(1)}, u32[]{:S(2)}, u32[]{:S(2)}) collective-permute-start(bf16[4,64,128]{2,1,0:T(8,128)(2,1)S(1)} %get-tuple-element.24.refs_0_), channel_id=1, source_target_pairs={{0,6},{1,7},{2,4},{3,5},{4,2},{5,3},{6,0},{7,1},{8,14},{9,15},{10,... | collective-permute-start | bytes 196616 | tf_op jit(solution)/shard_map/ppermute | solution.py:24
  49.7 1.6 %collective-permute-start.5 = (bf16[4,4,64,128]{3,2,1,0:T(8,128)(2,1)S(1)}, bf16[4,4,64,128]{3,2,1,0:T(8,128)(2,1)S(1)}, u32[]{:S(2)}, u32[]{:S(2)}) collective-permute-start(bf16[4,4,64,128]{3,2,1,0:T(8,128)(2,1)S(1)} %shard_map.98.near), channel_id=1, source_target_pairs={{0,1},{1,0},{2,3},{3,2},{4,5},{5,4},{6,7},{7,6},{8,9},{9,8},{10,11... | collective-permute-start | bytes 786440 | tf_op jit(solution)/shard_map/ppermute | solution.py:24
  51.3 10.4 %copy-start.1 = (bf16[256,256]{1,0:T(8,128)(2,1)S(1)}, bf16[256,256]{1,0:T(8,128)(2,1)}, u32[]{:S(2)}) copy-start(bf16[256,256]{1,0:T(8,128)(2,1)} %refs_5_.1) | copy-start | bytes 393220
  53.1 6.8 %collective-permute-start.6 = (bf16[4,64,128]{2,1,0:T(8,128)(2,1)S(1)}, bf16[4,64,128]{2,1,0:T(8,128)(2,1)S(1)}, u32[]{:S(2)}, u32[]{:S(2)}) collective-permute-start(bf16[4,64,128]{2,1,0:T(8,128)(2,1)S(1)} %shard_map.99.refs_0_), channel_id=1, source_target_pairs={{0,8},{8,16},{16,24},{24,0},{1,9},{9,17},{17,25},{25,1},{2,10},{10... | collective-permute-start | bytes 196616 | tf_op jit(solution)/shard_map/ppermute | solution.py:19
  53.1 8.6 %collective-permute-start.7 = (bf16[4,64,128]{2,1,0:T(8,128)(2,1)S(1)}, bf16[4,64,128]{2,1,0:T(8,128)(2,1)S(1)}, u32[]{:S(2)}, u32[]{:S(2)}) collective-permute-start(bf16[4,64,128]{2,1,0:T(8,128)(2,1)S(1)} %shard_map.99.refs_0_), channel_id=1, source_target_pairs={{0,16},{8,24},{16,0},{24,8},{1,17},{9,25},{17,1},{25,9},{2,18},{10... | collective-permute-start | bytes 196616 | tf_op jit(solution)/shard_map/ppermute | solution.py:19
  55.1 6.6 %collective-permute-start.8 = (bf16[4,64,128]{2,1,0:T(8,128)(2,1)S(1)}, bf16[4,64,128]{2,1,0:T(8,128)(2,1)S(1)}, u32[]{:S(2)}, u32[]{:S(2)}) collective-permute-start(bf16[4,64,128]{2,1,0:T(8,128)(2,1)S(1)} %shard_map.99.refs_0_), channel_id=1, source_target_pairs={{0,24},{8,0},{16,8},{24,16},{1,25},{9,1},{17,9},{25,17},{2,26},{10... | collective-permute-start | bytes 196616 | tf_op jit(solution)/shard_map/ppermute | solution.py:19
  65.8 1.8 %collective-permute-start.9 = (bf16[6,128,256]{2,1,0:T(8,128)(2,1)S(1)}, bf16[6,128,256]{2,1,0:T(8,128)(2,1)S(1)}, u32[]{:S(2)}, u32[]{:S(2)}) collective-permute-start(bf16[6,128,256]{2,1,0:T(8,128)(2,1)S(1)} %get-tuple-element.29), channel_id=1, source_target_pairs={{0,1},{1,0},{2,3},{3,2},{4,5},{5,4},{6,7},{7,6},{8,9},{9,8},{10,11... | collective-permute-start | bytes 1179656 | tf_op jit(solution)/shard_map/ppermute | solution.py:24
  67.7 5.6 %collective-permute-start.10 = (bf16[256,256]{1,0:T(8,128)(2,1)S(1)}, bf16[256,256]{1,0:T(8,128)(2,1)S(1)}, u32[]{:S(2)}, u32[]{:S(2)}) collective-permute-start(bf16[256,256]{1,0:T(8,128)(2,1)S(1)} %get-tuple-element.30.mine), channel_id=1, source_target_pairs={{0,2},{1,3},{2,0},{3,1},{4,6},{5,7},{6,4},{7,5},{8,10},{9,11},{10,... | collective-permute-start | bytes 393224 | tf_op jit(solution)/shard_map/ppermute | solution.py:24
  73.3 8.3 %collective-permute-start.11 = (bf16[256,256]{1,0:T(8,128)(2,1)S(1)}, bf16[256,256]{1,0:T(8,128)(2,1)S(1)}, u32[]{:S(2)}, u32[]{:S(2)}) collective-permute-start(bf16[256,256]{1,0:T(8,128)(2,1)S(1)} %shard_map.103.mine), channel_id=1, source_target_pairs={{0,4},{1,5},{2,6},{3,7},{4,0},{5,1},{6,2},{7,3},{8,12},{9,13},{10,... | collective-permute-start | bytes 393224 | tf_op jit(solution)/shard_map/ppermute | solution.py:24
  73.9 4.5 %collective-permute-start.12 = (bf16[128,256]{1,0:T(8,128)(2,1)S(1)}, bf16[128,256]{1,0:T(8,128)(2,1)S(1)}, u32[]{:S(2)}, u32[]{:S(2)}) collective-permute-start(bf16[128,256]{1,0:T(8,128)(2,1)S(1)} %get-tuple-element.32), channel_id=1, source_target_pairs={{0,2},{1,3},{2,0},{3,1},{4,6},{5,7},{6,4},{7,5},{8,10},{9,11},{10,... | collective-permute-start | bytes 196616 | tf_op jit(solution)/shard_map/ppermute | solution.py:24
  74.2 6.0 %collective-permute-start.13 = (bf16[128,256]{1,0:T(8,128)(2,1)S(1)}, bf16[128,256]{1,0:T(8,128)(2,1)S(1)}, u32[]{:S(2)}, u32[]{:S(2)}) collective-permute-start(bf16[128,256]{1,0:T(8,128)(2,1)S(1)} %get-tuple-element.33), channel_id=1, source_target_pairs={{0,4},{1,5},{2,6},{3,7},{4,0},{5,1},{6,2},{7,3},{8,12},{9,13},{10,... | collective-permute-start | bytes 196616 | tf_op jit(solution)/shard_map/ppermute | solution.py:24
  75.7 5.2 %collective-permute-start.14 = (bf16[128,256]{1,0:T(8,128)(2,1)S(1)}, bf16[128,256]{1,0:T(8,128)(2,1)S(1)}, u32[]{:S(2)}, u32[]{:S(2)}) collective-permute-start(bf16[128,256]{1,0:T(8,128)(2,1)S(1)} %get-tuple-element.34), channel_id=1, source_target_pairs={{0,6},{1,7},{2,4},{3,5},{4,2},{5,3},{6,0},{7,1},{8,14},{9,15},{10,... | collective-permute-start | bytes 196616 | tf_op jit(solution)/shard_map/ppermute | solution.py:24

commit v6 on v5

v6 whole, which is shorter than its diff:
```python
import functools

import jax
import jax.numpy as jnp
from jax import lax
from jax.experimental import pallas as pl
from jax.experimental.pallas import tpu as pltpu
from jax.sharding import PartitionSpec as P

F32 = jnp.float32
BF16 = jnp.bfloat16
VMEM = pl.BlockSpec(memory_space=pltpu.VMEM)
SMEM = pl.BlockSpec(memory_space=pltpu.SMEM)
PAD = 16


def swap(array, axis, bit):
    peers = lax.axis_size(axis)
    return lax.ppermute(array, axis, [(i, i ^ bit) for i in range(peers)])


def spread(array):
    reps = lax.axis_size("rep")
    held = {0: array}
    bit = reps // 2
    while bit:
        held.update({x | bit: swap(part, "rep", bit) for x, part in held.items()})
        bit //= 2
    return [held[x] for x in range(reps)]


def call(body, outs, in_specs, scratch=(), flops=0, moved=0):
    return pl.pallas_call(
        body,
        out_shape=outs,
        in_specs=in_specs,
        out_specs=jax.tree.map(lambda _: VMEM, outs),
        scratch_shapes=list(scratch),
        compiler_params=pltpu.CompilerParams(vmem_limit_bytes=48 * 1024 * 1024),
        cost_estimate=pl.CostEstimate(flops=flops, bytes_accessed=moved, transcendentals=0),
    )


def dot(a, b, a_dim, b_dim):
    return lax.dot_general(a, b, (((a_dim,), (b_dim,)), ((), ())), preferred_element_type=F32)


def other(axis, by):
    return lax.bitwise_xor(lax.axis_index(axis), by)


def split_features(reps, lists, cap, feats, rows, cols, counts, *rest):
    outs, turned = rest[:-1], rest[-1]
    nodes = feats.shape[0]
    part = feats.shape[1] // reps
    turned[...] = feats[...].astype(F32).T.astype(BF16).reshape(turned.shape)
    lane = lax.broadcasted_iota(jnp.int32, (PAD, nodes), 1)
    index = jnp.zeros((PAD, nodes), jnp.int32)
    slots = lists * cap
    for j in range(lists):
        for c in range(cap):
            k = j * cap + c
            index = jnp.where(lane == k, rows[j, c], index)
            index = jnp.where(lane == slots + k, cols[j, c], index)
        index = jnp.where(lane == 2 * slots + j, counts[j], index)
    index = index.astype(F32).astype(BF16)
    for x in range(reps):
        outs[x][:part] = turned[other("rep", x)]
        outs[x][part:] = index


def order_chunks(reps, part, *refs):
    chunks, unread, mine, index = refs[:reps], refs[reps], refs[-2], refs[-1]
    for x in range(reps):
        mine[other("rep", x)] = chunks[x][:part]
        index[x] = chunks[x][part:].astype(F32).astype(jnp.int32)


def join(*refs):
    out = refs[-1]
    for k, ref in enumerate(refs[:-1]):
        out[k] = ref[...]


def slot_of(index, lists, cap, t, j, c):
    k = j * cap + c
    slots = lists * cap
    return index[t, 0, k], index[t, 0, slots + k], c < index[t, 0, 2 * slots + j]


def relative(groups, lists, x, j):
    mine = lax.axis_index("blk")
    offset = other("rep", x) * lists + j
    return lax.div(lax.bitwise_xor(mine, lax.rem(mine + groups - offset, groups)), 2)


def aggregate(reps, groups, lists, cap, index, *refs):
    blocks = refs[:reps]
    near, far, out, total = refs[reps:]
    total[...] = jnp.zeros_like(total)
    for x in range(reps):
        for j in range(lists):
            held = far if j % 2 else near
            place = relative(groups, lists, x, j)
            for c in range(cap):
                row, col, live = slot_of(index, lists, cap, x, j, c)
                product = dot(held[place, col], blocks[x][j * cap + c], 1, 1)
                total[row] += jnp.where(live, product, 0.0)
    out[...] = total[...].astype(BF16)


def dense_layer(reps, *refs):
    chunks = refs[:reps]
    cotangents = refs[reps : 2 * reps]
    weight, out, dagg, terms, agg, cot, outs = refs[2 * reps :]
    nodes, width = out.shape
    for x in range(reps):
        origin = other("rep", x)
        cot[origin] = cotangents[x][...]
        for b in range(reps):
            agg[b, origin] = chunks[x][b]
    gw = jnp.zeros((width, width), F32)
    for b in range(reps):
        turned = agg[b].reshape(width, nodes)
        pre = dot(turned, weight[...], 0, 0)
        sigma = jax.nn.sigmoid(pre)
        outs[b] = (pre * sigma).astype(BF16)
        slope = sigma * (1.0 + pre * (1.0 - sigma))
        dpre = (cot[b].astype(F32) * slope).astype(BF16)
        dagg[b] = dot(dpre, weight[...], 1, 1).astype(BF16)
        gw += dot(turned, dpre, 1, 0)
    out[...] = outs[lax.axis_index("rep")]
    terms[...] = gw.astype(BF16).reshape(terms.shape)


def feature_grads(reps, groups, lists, cap, index, *refs):
    blocks = refs[:reps]
    dagg, terms, keep, send, total = refs[reps:]
    me = lax.axis_index("rep")
    half = groups // 2
    keep[...] = jnp.zeros_like(keep)
    total[...] = jnp.zeros_like(total)
    for x in range(reps):
        for j in range(lists):
            target = total if j % 2 else keep
            place = relative(groups, lists, x, j)
            for c in range(cap):
                row, col, live = slot_of(index, lists, cap, x, j, c)

                @pl.when(jnp.logical_and(live, col == me))
                def _():
                    target[place] += dot(blocks[x][j * cap + c], dagg[row], 0, 0)

    send[:half] = total[...].astype(BF16)
    core = lax.rem(lax.axis_index("blk"), 2)
    send[half:] = terms[1 - core].reshape(-1, *send.shape[1:])


def add_core(half, keep, terms, arrived, own, own_terms, *sends):
    nodes = own.shape[0]
    own[...] = keep[0] + arrived[0].astype(F32)
    core = lax.rem(lax.axis_index("blk"), 2)
    mine = terms[core].astype(F32)
    gw = (mine + arrived[half:].reshape(mine.shape).astype(F32)).astype(BF16)
    own_terms[...] = gw
    for k in range(1, half):
        sends[k - 1][:nodes] = (keep[k] + arrived[k].astype(F32)).astype(BF16)
        sends[k - 1][nodes:] = gw


def add_chips(half, own, own_terms, *refs):
    parts, grads, terms, held = refs[: half - 1], refs[-3], refs[-2], refs[-1]
    nodes = own.shape[0]
    chip = lax.div(lax.axis_index("blk"), 2)
    total = own[...]
    held[chip] = own_terms[...].astype(F32)
    for k in range(1, half):
        total += parts[k - 1][:nodes].astype(F32)
        held[lax.bitwise_xor(chip, k)] = parts[k - 1][nodes:].astype(F32)
    grads[...] = total
    gw = held[0]
    for k in range(1, half):
        gw += held[k]
    terms[...] = gw


def join_cores(mine, arrived, out):
    core = lax.rem(lax.axis_index("blk"), 2)
    rows = mine.shape[0]
    out[pl.ds(pl.multiple_of(core * rows, rows), rows), :] = mine[...]
    out[pl.ds(pl.multiple_of((1 - core) * rows, rows), rows), :] = arrived[...]


def per_device(feats, weight, cotangent, block_vals, block_rows, block_cols, step_counts):
    reps = lax.axis_size("rep")
    groups = lax.axis_size("blk")
    lists, cap, block = block_vals.shape[2:5]
    nodes, width = feats.shape
    part = width // reps
    slots = lists * cap
    half = groups // 2
    like = jax.ShapeDtypeStruct

    def direct(arrays):
        return [arrays[0]] + [swap(arrays[x], "rep", x) for x in range(1, reps)]

    blocks = spread(block_vals.reshape(slots, block, block))
    chunks = call(
        functools.partial(split_features, reps, lists, cap),
        [like((part + PAD, nodes), BF16)] * reps,
        [VMEM, SMEM, SMEM, SMEM],
        [pltpu.VMEM((reps, part, nodes), BF16)],
        moved=4 * nodes * width,
    )(feats, block_rows[0, 0], block_cols[0, 0], step_counts[0, 0])
    mine, index = call(
        functools.partial(order_chunks, reps, part),
        [like((reps, part, nodes), BF16), like((reps, PAD, nodes), jnp.int32)],
        [VMEM] * reps + [pl.BlockSpec(memory_space=pl.ANY)],
        moved=4 * nodes * width,
    )(*direct(chunks), blocks[1])

    near = call(
        join,
        like((half, reps, part, nodes), BF16),
        [VMEM] * half,
        moved=4 * half * nodes * width,
    )(mine, *[swap(mine, "blk", 2 * k) for k in range(1, half)])
    far = swap(near, "blk", 1)
    slot_flops = 2 * groups * cap * part * block * block
    slot_bytes = 2 * (groups * cap * block * block + groups * nodes * width)

    agg = call(
        functools.partial(aggregate, reps, groups, lists, cap),
        like((reps, part, nodes), BF16),
        [SMEM] + [VMEM] * (reps + 2),
        [pltpu.VMEM((reps, part, nodes), F32)],
        flops=slot_flops,
        moved=slot_bytes,
    )(index, *blocks, near, far)

    out_rows, dagg, terms = call(
        functools.partial(dense_layer, reps),
        [
            like((nodes, width), BF16),
            like((reps, nodes, width), BF16),
            like((2, width // 2, width), BF16),
        ],
        [VMEM] * (2 * reps + 1),
        [
            pltpu.VMEM((reps, reps, part, nodes), BF16),
            pltpu.VMEM((reps, nodes, width), BF16),
            pltpu.VMEM((reps, nodes, width), BF16),
        ],
        flops=6 * reps * nodes * width * width,
        moved=2 * reps * 5 * nodes * width,
    )(*direct([agg] * reps), *spread(cotangent), weight)

    keep, send = call(
        functools.partial(feature_grads, reps, groups, lists, cap),
        [
            like((half, nodes, width), F32),
            like((half + width // 2 // nodes, nodes, width), BF16),
        ],
        [SMEM] + [VMEM] * (reps + 2),
        [pltpu.VMEM((half, nodes, width), F32)],
        flops=slot_flops,
        moved=slot_bytes,
    )(index, *blocks, dagg, terms)
    own, own_terms, *sends = call(
        functools.partial(add_core, half),
        [like((nodes, width), F32), like((width // 2, width), BF16)]
        + [like((nodes + width // 2, width), BF16)] * (half - 1),
        [VMEM] * 3,
        moved=10 * half * nodes * width,
    )(keep, terms, swap(send, "blk", 1))
    grad_feats, terms = call(
        functools.partial(add_chips, half),
        [like((nodes, width), F32), like((width // 2, width), F32)],
        [VMEM] * (half + 1),
        [pltpu.VMEM((half, width // 2, width), F32)],
        moved=8 * half * nodes * width,
    )(own, own_terms, *[swap(sends[k - 1], "blk", 2 * k) for k in range(1, half)])
    grad_weight = call(
        join_cores, like((width, width), F32), [VMEM] * 2, moved=8 * width * width
    )(terms, swap(terms, "blk", 1))
    return (out_rows, grad_weight, grad_feats)


def solution(mesh):
    return jax.shard_map(
        per_device,
        mesh=mesh,
        in_specs=(
            P(("blk", "rep"), None),
            P(),
            P(("blk", "rep"), None),
            P("blk", "rep", None, None, None, None),
            P("blk", "rep", None, None),
            P("blk", "rep", None, None),
            P("blk", "rep", None),
        ),
        out_specs=(P(("blk", "rep"), None), P(), P(("blk", "rep"), None)),
        check_vma=False,
    )
```

time: 82.4 us -> 62.9 us (0.76)
  waiting for transfers between devices: 48.8 us -> 23.5 us
  starting transfers between devices: 21.3 us -> 29.2 us
  Pallas kernels: 9.08 us -> 7.52 us
  local copies, waits for them, and re-layouts: 2.43 us -> 1.55 us
    ppermute x12 -> x21, waiting for transfers between devices: 44 us -> 23.5 us  [swap(): return lax.ppermute(array, axis, [(i, i ^ bit) for i in range(peers)])]
    ppermute x12 -> x21, starting transfers between devices: 10.9 us -> 29.2 us  [swap(): return lax.ppermute(array, axis, [(i, i ^ bit) for i in range(peers)])]
    all_to_all x1 -> x0, starting transfers between devices: 6.45 us -> none  [per_device(): packed = lax.all_to_all(packed, 'rep', 0, 0, tiled=True)]
    ppermute x3 -> x0, waiting for transfers between devices: 4.82 us -> none  [shift(): lax.ppermute(array, 'rep', [(i, (i + by) % peers) for i in range(peers)])]
    ppermute x3 -> x0, starting transfers between devices: 3.87 us -> none  [shift(): lax.ppermute(array, 'rep', [(i, (i + by) % peers) for i in range(peers)])]
    pallas_call x6 -> x3, Pallas kernels: 3.24 us -> 2.11 us  [the longest x1 0.73 us: per_device(): call(join_cores, like((width, width), F32), [VMEM] * 2, moved=8 * width *...]
    unnamed x14, local copies, waits for them, and re-layouts: 2.43 us -> 1.55 us
  transfers between devices with their start and end apart: 16 -> 21, of which waited for: 13 -> 13; matrix products, arithmetic and copies ran while one was open for 0% -> 0% of each run, Pallas kernels for 2% -> 4%
where the time goes in v6:
time: 62.9 us; the launch traced here: 62.5 us
  starting transfers between devices  29.2 us (46%)
  waiting for transfers between devices  23.5 us (37%)
  Pallas kernels  7.52 us (12%)
  local copies, waits for them, and re-layouts  1.55 us (2%)
  between operations  0.74 us (1%)
    ppermute x21, starting transfers between devices, swap(): return lax.ppermute(array, axis, [(i, i ^ bit) for i in range(peers)])  29.2 us
    ppermute x21, waiting for transfers between devices, swap(): return lax.ppermute(array, axis, [(i, i ^ bit) for i in range(peers)])  23.5 us
    pallas_call x1, Pallas kernels, per_device(): call(functools.partial(feature_grads, reps, groups, lists, cap), [like((h...  2.27 us
    pallas_call x1, Pallas kernels, per_device(): call(functools.partial(aggregate, reps, groups, lists, cap), like((reps,...  1.72 us
    unnamed x14, local copies, waits for them, and re-layouts  1.55 us
    pallas_call x1, Pallas kernels, per_device(): call(functools.partial(dense_layer, reps), [like((nodes, width), BF16), l...  1.33 us
  transfers between devices with their start and end apart: 21, of which 13 were waited for; matrix products, arithmetic and copies ran while one was open for 0% of the time, Pallas kernels for 4%

profile of v6, /device:TPU:0, one launch (start us, length us, event | category | flops | bytes accessed | tf_op | source)
XLA Modules:
  0.0 62.5 jit_solution(4850428960365681656)
XLA Ops:
  0.6 3.1 %collective-permute-start.3 = (bf16[6,128,128]{2,1,0:T(8,128)(2,1)}, bf16[6,128,128]{2,1,0:T(8,128)(2,1)S(1)}, u32[]{:S(2)}, u32[]{:S(2)}) collective-permute-start(bf16[6,128,128]{2,1,0:T(8,128)(2,1)} %bitcast.4), channel_id=1, source_target_pairs={{0,8},{8,0},{16,24},{24,16},{1,9},{9,1},{17,25},{25,17},{2,10},{10... | collective-permute-start | bytes 589832 | tf_op jit(solution)/shard_map/ppermute | solution.py:19
  3.7 2.6 %collective-permute-start.4 = (bf16[6,128,128]{2,1,0:T(8,128)(2,1)}, bf16[6,128,128]{2,1,0:T(8,128)(2,1)S(1)}, u32[]{:S(2)}, u32[]{:S(2)}) collective-permute-start(bf16[6,128,128]{2,1,0:T(8,128)(2,1)} %bitcast.5), channel_id=1, source_target_pairs={{0,16},{8,24},{16,0},{24,8},{1,17},{9,25},{17,1},{25,9},{2,18},{10... | collective-permute-start | bytes 589832 | tf_op jit(solution)/shard_map/ppermute | solution.py:19
  6.3 0.7 %copy-done.3 = s32[1,1,2,3]{3,2,1,0:T(2,128)S(1)} copy-done((s32[1,1,2,3]{3,2,1,0:T(2,128)S(1)}, s32[1,1,2,3]{3,2,1,0:T(2,128)}, u32[]{:S(2)}) %copy-start.3) | copy-done | bytes 48
  7.0 0.0 copy-done.2
  7.0 0.8 %copy-done.1 = bf16[128,256]{1,0:T(8,128)(2,1)S(1)} copy-done((bf16[128,256]{1,0:T(8,128)(2,1)S(1)}, bf16[128,256]{1,0:T(8,128)(2,1)}, u32[]{:S(2)}) %copy-start.1) | copy-done | bytes 65560
  7.8 0.7 %shard_map.94 = (bf16[80,128]{1,0:T(8,128)(2,1)S(1)}, bf16[80,128]{1,0:T(8,128)(2,1)S(1)}, bf16[80,128]{1,0:T(8,128)(2,1)S(1)}, bf16[80,128]{1,0:T(8,128)(2,1)S(1)}) custom-call(bf16[128,256]{1,0:T(8,128)(2,1)S(1)} %copy-done.1, s32[2,3]{1,0:T(2,128)S(1)} %bitcast.8, s32[2,3]{1,0:T(2,128)S(1)} %bitcast.9, s32[2]{0:T(128)S(1)} %bitcast.10), custom_call_target="tpu_custom_call" | custom-call | bytes 131072 | tf_op jit(solution)/shard_map/pallas_call | solution.py:208
  8.5 0.5 collective-permute-start
  9.0 0.0 collective-permute-start.1
  9.0 3.9 %collective-permute-start.2 = (bf16[80,128]{1,0:T(8,128)(2,1)S(1)}, bf16[80,128]{1,0:T(8,128)(2,1)S(1)}, u32[]{:S(2)}, u32[]{:S(2)}) collective-permute-start(bf16[80,128]{1,0:T(8,128)(2,1)S(1)} %get-tuple-element.24), channel_id=1, source_target_pairs={{0,24},{8,16},{16,8},{24,0},{1,25},{9,17},{17,9},{25,1},{2,26},{10... | collective-permute-start | bytes 61448 | tf_op jit(solution)/shard_map/ppermute | solution.py:19
  13.0 0.4 collective-permute-done.refs_1_
  13.4 3.6 %collective-permute-done.1.refs_2_ = bf16[80,128]{1,0:T(8,128)(2,1)S(1)} collective-permute-done((bf16[80,128]{1,0:T(8,128)(2,1)S(1)}, bf16[80,128]{1,0:T(8,128)(2,1)S(1)}, u32[]{:S(2)}, u32[]{:S(2)}) %collective-permute-start.1) | collective-permute-done | bytes 20512 | tf_op jit(solution)/shard_map/ppermute | solution.py:19
  17.0 0.0 collective-permute-done.2.refs_3_
  17.0 0.0 collective-permute-done.3.refs_4_.refs_1_
  17.0 0.0 copy-start.6
  17.0 0.0 copy-start
  17.1 2.5 %collective-permute-start.8 = (bf16[4,64,128]{2,1,0:T(8,128)(2,1)S(1)}, bf16[4,64,128]{2,1,0:T(8,128)(2,1)S(1)}, u32[]{:S(2)}, u32[]{:S(2)}) collective-permute-start(bf16[4,64,128]{2,1,0:T(8,128)(2,1)S(1)} %get-tuple-element.26.refs_0_), channel_id=1, source_target_pairs={{0,6},{1,7},{2,4},{3,5},{4,2},{5,3},{6,0},{7,1},{8,14},{9,15},{10,... | collective-permute-start | bytes 196616 | tf_op jit(solution)/shard_map/ppermute | solution.py:19
  19.6 0.5 collective-permute-start.7
  20.1 0.5 collective-permute-start.6
  20.6 2.1 %collective-permute-done.8.refs_3_ = bf16[4,64,128]{2,1,0:T(8,128)(2,1)S(1)} collective-permute-done((bf16[4,64,128]{2,1,0:T(8,128)(2,1)S(1)}, bf16[4,64,128]{2,1,0:T(8,128)(2,1)S(1)}, u32[]{:S(2)}, u32[]{:S(2)}) %collective-permute-start.8) | collective-permute-done | bytes 65568 | tf_op jit(solution)/shard_map/ppermute | solution.py:19
  22.7 1.1 %collective-permute-done.7.refs_2_ = bf16[4,64,128]{2,1,0:T(8,128)(2,1)S(1)} collective-permute-done((bf16[4,64,128]{2,1,0:T(8,128)(2,1)S(1)}, bf16[4,64,128]{2,1,0:T(8,128)(2,1)S(1)}, u32[]{:S(2)}, u32[]{:S(2)}) %collective-permute-start.7) | collective-permute-done | bytes 65568 | tf_op jit(solution)/shard_map/ppermute | solution.py:19
  23.8 0.5 collective-permute-done.6.refs_1_
  24.4 0.1 collective-permute-start.9
  24.5 0.8 %collective-permute-start.5 = (bf16[6,128,128]{2,1,0:T(8,128)(2,1)S(1)}, bf16[6,128,128]{2,1,0:T(8,128)(2,1)S(1)}, u32[]{:S(2)}, u32[]{:S(2)}) collective-permute-start(bf16[6,128,128]{2,1,0:T(8,128)(2,1)S(1)} %collective-permute-done.4.refs_2_), channel_id=1, source_target_pairs={{0,8},{8,0},{16,24},{24,16},{1,9},{9,1},{17,25},{25,17},{2,10},{10... | collective-permute-start | bytes 589832 | tf_op jit(solution)/shard_map/ppermute | solution.py:19
  25.3 2.2 %collective-permute-start.14 = (bf16[128,256]{1,0:T(8,128)(2,1)S(1)}, bf16[128,256]{1,0:T(8,128)(2,1)S(1)}, u32[]{:S(2)}, u32[]{:S(2)}) collective-permute-start(bf16[128,256]{1,0:T(8,128)(2,1)S(1)} %copy-done.6), channel_id=1, source_target_pairs={{0,16},{8,24},{16,0},{24,8},{1,17},{9,25},{17,1},{25,9},{2,18},{10... | collective-permute-start | bytes 196616 | tf_op jit(solution)/shard_map/ppermute | solution.py:19
  27.5 0.8 %collective-permute-start.13 = (bf16[128,256]{1,0:T(8,128)(2,1)S(1)}, bf16[128,256]{1,0:T(8,128)(2,1)S(1)}, u32[]{:S(2)}, u32[]{:S(2)}) collective-permute-start(bf16[128,256]{1,0:T(8,128)(2,1)S(1)} %copy-done.6), channel_id=1, source_target_pairs={{0,8},{8,0},{16,24},{24,16},{1,9},{9,1},{17,25},{25,17},{2,10},{10... | collective-permute-start | bytes 196616 | tf_op jit(solution)/shard_map/ppermute | solution.py:19
  28.3 3.6 %collective-permute-done.14.refs_6_ = bf16[128,256]{1,0:T(8,128)(2,1)S(1)} collective-permute-done((bf16[128,256]{1,0:T(8,128)(2,1)S(1)}, bf16[128,256]{1,0:T(8,128)(2,1)S(1)}, u32[]{:S(2)}, u32[]{:S(2)}) %collective-permute-start.14) | collective-permute-done | bytes 65568 | tf_op jit(solution)/shard_map/ppermute | solution.py:19
  31.9 3.5 %collective-permute-start.15 = (bf16[128,256]{1,0:T(8,128)(2,1)S(1)}, bf16[128,256]{1,0:T(8,128)(2,1)S(1)}, u32[]{:S(2)}, u32[]{:S(2)}) collective-permute-start(bf16[128,256]{1,0:T(8,128)(2,1)S(1)} %collective-permute-done.14.refs_6_), channel_id=1, source_target_pairs={{0,8},{8,0},{16,24},{24,16},{1,9},{9,1},{17,25},{25,17},{2,10},{10... | collective-permute-start | bytes 196616 | tf_op jit(solution)/shard_map/ppermute | solution.py:19
  35.4 0.0 copy-start.5
  35.4 1.7 %shard_map.97.refs_0_ = bf16[4,64,128]{2,1,0:T(8,128)(2,1)S(1)} custom-call(s32[4,16,128]{2,1,0:T(8,128)S(1)} %get-tuple-element.25.index, bf16[6,128,128]{2,1,0:T(8,128)(2,1)S(1)} %bitcast.6, bf16[6,128,128]{2,1,0:T(8,128)(2,1)S(1)} %collective-permute-done.3.refs_4_.refs_1_, bf16[6,128,128]{2,1,0:T(8,128)(2,1)S(1)} %collective-permute-done.4.refs_2_, ...), custom_call_target="tpu_custom_call" | custom-call | flops 50331648 | bytes 1310720 | tf_op jit(solution)/shard_map/pallas_call | solution.py:232
  37.2 1.4 %collective-permute-start.12 = (bf16[4,64,128]{2,1,0:T(8,128)(2,1)S(1)}, bf16[4,64,128]{2,1,0:T(8,128)(2,1)S(1)}, u32[]{:S(2)}, u32[]{:S(2)}) collective-permute-start(bf16[4,64,128]{2,1,0:T(8,128)(2,1)S(1)} %shard_map.97.refs_0_), channel_id=1, source_target_pairs={{0,24},{8,16},{16,8},{24,0},{1,25},{9,17},{17,9},{25,1},{2,26},{10... | collective-permute-start | bytes 196616 | tf_op jit(solution)/shard_map/ppermute | solution.py:19
  38.6 0.1 collective-permute-start.11
  38.7 2.9 %collective-permute-start.10 = (bf16[4,64,128]{2,1,0:T(8,128)(2,1)S(1)}, bf16[4,64,128]{2,1,0:T(8,128)(2,1)S(1)}, u32[]{:S(2)}, u32[]{:S(2)}) collective-permute-start(bf16[4,64,128]{2,1,0:T(8,128)(2,1)S(1)} %shard_map.97.refs_0_), channel_id=1, source_target_pairs={{0,8},{8,0},{16,24},{24,16},{1,9},{9,1},{17,25},{25,17},{2,10},{10... | collective-permute-start | bytes 196616 | tf_op jit(solution)/shard_map/ppermute | solution.py:19
  41.6 1.9 %collective-permute-done.12.refs_3_ = bf16[4,64,128]{2,1,0:T(8,128)(2,1)S(1)} collective-permute-done((bf16[4,64,128]{2,1,0:T(8,128)(2,1)S(1)}, bf16[4,64,128]{2,1,0:T(8,128)(2,1)S(1)}, u32[]{:S(2)}, u32[]{:S(2)}) %collective-permute-start.12) | collective-permute-done | bytes 65568 | tf_op jit(solution)/shard_map/ppermute | solution.py:19
  43.5 1.6 %collective-permute-done.11.refs_2_ = bf16[4,64,128]{2,1,0:T(8,128)(2,1)S(1)} collective-permute-done((bf16[4,64,128]{2,1,0:T(8,128)(2,1)S(1)}, bf16[4,64,128]{2,1,0:T(8,128)(2,1)S(1)}, u32[]{:S(2)}, u32[]{:S(2)}) %collective-permute-start.11) | collective-permute-done | bytes 65568 | tf_op jit(solution)/shard_map/ppermute | solution.py:19
  45.1 1.3 %shard_map.98 = (bf16[128,256]{1,0:T(8,128)(2,1)}, bf16[4,128,256]{2,1,0:T(8,128)(2,1)S(1)}, bf16[2,128,256]{2,1,0:T(8,128)(2,1)S(1)}) custom-call(bf16[4,64,128]{2,1,0:T(8,128)(2,1)S(1)} %shard_map.97.refs_0_, bf16[4,64,128]{2,1,0:T(8,128)(2,1)S(1)} %collective-permute-done.10.refs_1_, bf16[4,64,128]{2,1,0:T(8,128)(2,1)S(1)} %collective-permute-done.11.refs_2_, ...), custom_call_target="tpu_custom_call" | custom-call | flops 201326592 | bytes 1310720 | tf_op jit(solution)/shard_map/pallas_call | solution.py:241
  46.5 2.3 %shard_map.99 = (f32[4,128,256]{2,1,0:T(8,128)S(1)}, bf16[5,128,256]{2,1,0:T(8,128)(2,1)S(1)}) custom-call(s32[4,16,128]{2,1,0:T(8,128)S(1)} %get-tuple-element.25.index, bf16[6,128,128]{2,1,0:T(8,128)(2,1)S(1)} %bitcast.7, bf16[6,128,128]{2,1,0:T(8,128)(2,1)S(1)} %collective-permute-done.3.refs_4_.refs_1_, ...), custom_call_target="tpu_custom_call" | custom-call | flops 50331648 | bytes 1310720 | tf_op jit(solution)/shard_map/pallas_call | solution.py:258
  48.8 0.1 collective-permute-start.16
  48.8 1.6 %collective-permute-done.16.arrived = bf16[5,128,256]{2,1,0:T(8,128)(2,1)S(1)} collective-permute-done((bf16[5,128,256]{2,1,0:T(8,128)(2,1)S(1)}, bf16[5,128,256]{2,1,0:T(8,128)(2,1)S(1)}, u32[]{:S(2)}, u32[]{:S(2)}) %collective-permute-start.16) | collective-permute-done | bytes 327712 | tf_op jit(solution)/shard_map/ppermute | solution.py:19
  50.4 0.1 shard_map.100
  50.5 1.0 %collective-permute-start.17 = (bf16[256,256]{1,0:T(8,128)(2,1)S(1)}, bf16[256,256]{1,0:T(8,128)(2,1)S(1)}, u32[]{:S(2)}, u32[]{:S(2)}) collective-permute-start(bf16[256,256]{1,0:T(8,128)(2,1)S(1)} %get-tuple-element.34), channel_id=1, source_target_pairs={{0,2},{1,3},{2,0},{3,1},{4,6},{5,7},{6,4},{7,5},{8,10},{9,11},{10,... | collective-permute-start | bytes 393224 | tf_op jit(solution)/shard_map/ppermute | solution.py:19
  51.5 1.4 %collective-permute-start.18 = (bf16[256,256]{1,0:T(8,128)(2,1)S(1)}, bf16[256,256]{1,0:T(8,128)(2,1)S(1)}, u32[]{:S(2)}, u32[]{:S(2)}) collective-permute-start(bf16[256,256]{1,0:T(8,128)(2,1)S(1)} %get-tuple-element.35), channel_id=1, source_target_pairs={{0,4},{1,5},{2,6},{3,7},{4,0},{5,1},{6,2},{7,3},{8,12},{9,13},{10,... | collective-permute-start | bytes 393224 | tf_op jit(solution)/shard_map/ppermute | solution.py:19
  52.9 1.2 %collective-permute-start.19 = (bf16[256,256]{1,0:T(8,128)(2,1)S(1)}, bf16[256,256]{1,0:T(8,128)(2,1)S(1)}, u32[]{:S(2)}, u32[]{:S(2)}) collective-permute-start(bf16[256,256]{1,0:T(8,128)(2,1)S(1)} %get-tuple-element.36), channel_id=1, source_target_pairs={{0,6},{1,7},{2,4},{3,5},{4,2},{5,3},{6,0},{7,1},{8,14},{9,15},{10,... | collective-permute-start | bytes 393224 | tf_op jit(solution)/shard_map/ppermute | solution.py:19
  54.1 2.9 %collective-permute-done.17.refs_0_ = bf16[256,256]{1,0:T(8,128)(2,1)S(1)} collective-permute-done((bf16[256,256]{1,0:T(8,128)(2,1)S(1)}, bf16[256,256]{1,0:T(8,128)(2,1)S(1)}, u32[]{:S(2)}, u32[]{:S(2)}) %collective-permute-start.17) | collective-permute-done | bytes 131104 | tf_op jit(solution)/shard_map/ppermute | solution.py:19
  56.9 1.6 %collective-permute-done.18.refs_1_ = bf16[256,256]{1,0:T(8,128)(2,1)S(1)} collective-permute-done((bf16[256,256]{1,0:T(8,128)(2,1)S(1)}, bf16[256,256]{1,0:T(8,128)(2,1)S(1)}, u32[]{:S(2)}, u32[]{:S(2)}) %collective-permute-start.18) | collective-permute-done | bytes 131104 | tf_op jit(solution)/shard_map/ppermute | solution.py:19
  58.5 1.2 %collective-permute-done.19.refs_2_ = bf16[256,256]{1,0:T(8,128)(2,1)S(1)} collective-permute-done((bf16[256,256]{1,0:T(8,128)(2,1)S(1)}, bf16[256,256]{1,0:T(8,128)(2,1)S(1)}, u32[]{:S(2)}, u32[]{:S(2)}) %collective-permute-start.19) | collective-permute-done | bytes 131104 | tf_op jit(solution)/shard_map/ppermute | solution.py:19
  59.7 0.7 %shard_map.101 = (f32[128,256]{1,0:T(8,128)}, f32[128,256]{1,0:T(8,128)S(1)}) custom-call(f32[128,256]{1,0:T(8,128)S(1)} %get-tuple-element.32.own, bf16[128,256]{1,0:T(8,128)(2,1)S(1)} %get-tuple-element.33.own_terms, bf16[256,256]{1,0:T(8,128)(2,1)S(1)} %collective-permute-done.17.refs_0_, bf16[256,256]{1,0:T(8,128)(2,1)S(1)} %collective-permute-done.18.refs_1_, ...), custom_call_target="tpu_custom_call" | custom-call | bytes 1048576 | tf_op jit(solution)/shard_map/pallas_call | solution.py:276
  60.5 1.3 %collective-permute-done.20.arrived = f32[128,256]{1,0:T(8,128)S(1)} collective-permute-done((f32[128,256]{1,0:T(8,128)S(1)}, f32[128,256]{1,0:T(8,128)S(1)}, u32[]{:S(2)}, u32[]{:S(2)}) %collective-permute-start.20) | collective-permute-done | bytes 131104 | tf_op jit(solution)/shard_map/ppermute | solution.py:19
  61.8 0.7 %shard_map.102 = f32[256,256]{1,0:T(8,128)} custom-call(f32[128,256]{1,0:T(8,128)S(1)} %get-tuple-element.37.mine, f32[128,256]{1,0:T(8,128)S(1)} %collective-permute-done.20.arrived), custom_call_target="tpu_custom_call" | custom-call | bytes 524288 | tf_op jit(solution)/shard_map/pallas_call | solution.py:283
  (17 shorter events, 0.1 us)
Async XLA Ops:
  0.6 16.4 %collective-permute-start.3 = (bf16[6,128,128]{2,1,0:T(8,128)(2,1)}, bf16[6,128,128]{2,1,0:T(8,128)(2,1)S(1)}, u32[]{:S(2)}, u32[]{:S(2)}) collective-permute-start(bf16[6,128,128]{2,1,0:T(8,128)(2,1)} %bitcast.4), channel_id=1, source_target_pairs={{0,8},{8,0},{16,24},{24,16},{1,9},{9,1},{17,25},{25,17},{2,10},{10... | collective-permute-start | bytes 589832 | tf_op jit(solution)/shard_map/ppermute | solution.py:19
  3.7 20.7 %collective-permute-start.4 = (bf16[6,128,128]{2,1,0:T(8,128)(2,1)}, bf16[6,128,128]{2,1,0:T(8,128)(2,1)S(1)}, u32[]{:S(2)}, u32[]{:S(2)}) collective-permute-start(bf16[6,128,128]{2,1,0:T(8,128)(2,1)} %bitcast.5), channel_id=1, source_target_pairs={{0,16},{8,24},{16,0},{24,8},{1,17},{9,25},{17,1},{25,9},{2,18},{10... | collective-permute-start | bytes 589832 | tf_op jit(solution)/shard_map/ppermute | solution.py:19
  6.3 0.7 %copy-start.3 = (s32[1,1,2,3]{3,2,1,0:T(2,128)S(1)}, s32[1,1,2,3]{3,2,1,0:T(2,128)}, u32[]{:S(2)}) copy-start(s32[1,1,2,3]{3,2,1,0:T(2,128)} %param.12) | copy-start | bytes 76
  6.3 0.7 %copy-start.2 = (s32[1,1,2,3]{3,2,1,0:T(2,128)S(1)}, s32[1,1,2,3]{3,2,1,0:T(2,128)}, u32[]{:S(2)}) copy-start(s32[1,1,2,3]{3,2,1,0:T(2,128)} %param.11) | copy-start | bytes 76
  6.3 0.7 %copy-start.4 = (s32[1,1,2]{2,1,0:T(1,128)S(1)}, s32[1,1,2]{2,1,0:T(1,128)}, u32[]{:S(2)}) copy-start(s32[1,1,2]{2,1,0:T(1,128)} %param.13) | copy-start | bytes 28
  7.0 0.8 %copy-start.1 = (bf16[128,256]{1,0:T(8,128)(2,1)S(1)}, bf16[128,256]{1,0:T(8,128)(2,1)}, u32[]{:S(2)}) copy-start(bf16[128,256]{1,0:T(8,128)(2,1)} %feats.1) | copy-start | bytes 196612
  8.5 4.8 %collective-permute-start = (bf16[80,128]{1,0:T(8,128)(2,1)S(1)}, bf16[80,128]{1,0:T(8,128)(2,1)S(1)}, u32[]{:S(2)}, u32[]{:S(2)}) collective-permute-start(bf16[80,128]{1,0:T(8,128)(2,1)S(1)} %get-tuple-element.22), channel_id=1, source_target_pairs={{0,8},{8,0},{16,24},{24,16},{1,9},{9,1},{17,25},{25,17},{2,10},{10... | collective-permute-start | bytes 61448 | tf_op jit(solution)/shard_map/ppermute | solution.py:19
  9.0 8.0 %collective-permute-start.1 = (bf16[80,128]{1,0:T(8,128)(2,1)S(1)}, bf16[80,128]{1,0:T(8,128)(2,1)S(1)}, u32[]{:S(2)}, u32[]{:S(2)}) collective-permute-start(bf16[80,128]{1,0:T(8,128)(2,1)S(1)} %get-tuple-element.23), channel_id=1, source_target_pairs={{0,16},{8,24},{16,0},{24,8},{1,17},{9,25},{17,1},{25,9},{2,18},{10... | collective-permute-start | bytes 61448 | tf_op jit(solution)/shard_map/ppermute | solution.py:19
  9.0 8.0 %collective-permute-start.2 = (bf16[80,128]{1,0:T(8,128)(2,1)S(1)}, bf16[80,128]{1,0:T(8,128)(2,1)S(1)}, u32[]{:S(2)}, u32[]{:S(2)}) collective-permute-start(bf16[80,128]{1,0:T(8,128)(2,1)S(1)} %get-tuple-element.24), channel_id=1, source_target_pairs={{0,24},{8,16},{16,8},{24,0},{1,25},{9,17},{17,9},{25,1},{2,26},{10... | collective-permute-start | bytes 61448 | tf_op jit(solution)/shard_map/ppermute | solution.py:19
  17.0 8.3 %copy-start.6 = (bf16[128,256]{1,0:T(8,128)(2,1)S(1)}, bf16[128,256]{1,0:T(8,128)(2,1)}, u32[]{:S(2)}) copy-start(bf16[128,256]{1,0:T(8,128)(2,1)} %refs_4_.1) | copy-start | bytes 196612
  17.0 18.4 %copy-start = (bf16[1,1,2,3,128,128]{5,4,3,2,1,0:T(8,128)(2,1)S(1)}, bf16[1,1,2,3,128,128]{5,4,3,2,1,0:T(8,128)(2,1)}, u32[]{:S(2)}) copy-start(bf16[1,1,2,3,128,128]{5,4,3,2,1,0:T(8,128)(2,1)} %param.10) | copy-start | bytes 589828
  17.1 5.7 %collective-permute-start.8 = (bf16[4,64,128]{2,1,0:T(8,128)(2,1)S(1)}, bf16[4,64,128]{2,1,0:T(8,128)(2,1)S(1)}, u32[]{:S(2)}, u32[]{:S(2)}) collective-permute-start(bf16[4,64,128]{2,1,0:T(8,128)(2,1)S(1)} %get-tuple-element.26.refs_0_), channel_id=1, source_target_pairs={{0,6},{1,7},{2,4},{3,5},{4,2},{5,3},{6,0},{7,1},{8,14},{9,15},{10,... | collective-permute-start | bytes 196616 | tf_op jit(solution)/shard_map/ppermute | solution.py:19
  19.6 4.3 %collective-permute-start.7 = (bf16[4,64,128]{2,1,0:T(8,128)(2,1)S(1)}, bf16[4,64,128]{2,1,0:T(8,128)(2,1)S(1)}, u32[]{:S(2)}, u32[]{:S(2)}) collective-permute-start(bf16[4,64,128]{2,1,0:T(8,128)(2,1)S(1)} %get-tuple-element.26.refs_0_), channel_id=1, source_target_pairs={{0,4},{1,5},{2,6},{3,7},{4,0},{5,1},{6,2},{7,3},{8,12},{9,13},{10,... | collective-permute-start | bytes 196616 | tf_op jit(solution)/shard_map/ppermute | solution.py:19
  20.1 4.3 %collective-permute-start.6 = (bf16[4,64,128]{2,1,0:T(8,128)(2,1)S(1)}, bf16[4,64,128]{2,1,0:T(8,128)(2,1)S(1)}, u32[]{:S(2)}, u32[]{:S(2)}) collective-permute-start(bf16[4,64,128]{2,1,0:T(8,128)(2,1)S(1)} %get-tuple-element.26.refs_0_), channel_id=1, source_target_pairs={{0,2},{1,3},{2,0},{3,1},{4,6},{5,7},{6,4},{7,5},{8,10},{9,11},{10,... | collective-permute-start | bytes 196616 | tf_op jit(solution)/shard_map/ppermute | solution.py:19
  24.4 11.0 %collective-permute-start.9 = (bf16[4,4,64,128]{3,2,1,0:T(8,128)(2,1)S(1)}, bf16[4,4,64,128]{3,2,1,0:T(8,128)(2,1)S(1)}, u32[]{:S(2)}, u32[]{:S(2)}) collective-permute-start(bf16[4,4,64,128]{3,2,1,0:T(8,128)(2,1)S(1)} %shard_map.96.refs_4_), channel_id=1, source_target_pairs={{0,1},{1,0},{2,3},{3,2},{4,5},{5,4},{6,7},{7,6},{8,9},{9,8},{10,11... | collective-permute-start | bytes 786440 | tf_op jit(solution)/shard_map/ppermute | solution.py:19
  24.5 11.0 %collective-permute-start.5 = (bf16[6,128,128]{2,1,0:T(8,128)(2,1)S(1)}, bf16[6,128,128]{2,1,0:T(8,128)(2,1)S(1)}, u32[]{:S(2)}, u32[]{:S(2)}) collective-permute-start(bf16[6,128,128]{2,1,0:T(8,128)(2,1)S(1)} %collective-permute-done.4.refs_2_), channel_id=1, source_target_pairs={{0,8},{8,0},{16,24},{24,16},{1,9},{9,1},{17,25},{25,17},{2,10},{10... | collective-permute-start | bytes 589832 | tf_op jit(solution)/shard_map/ppermute | solution.py:19
  25.3 6.6 %collective-permute-start.14 = (bf16[128,256]{1,0:T(8,128)(2,1)S(1)}, bf16[128,256]{1,0:T(8,128)(2,1)S(1)}, u32[]{:S(2)}, u32[]{:S(2)}) collective-permute-start(bf16[128,256]{1,0:T(8,128)(2,1)S(1)} %copy-done.6), channel_id=1, source_target_pairs={{0,16},{8,24},{16,0},{24,8},{1,17},{9,25},{17,1},{25,9},{2,18},{10... | collective-permute-start | bytes 196616 | tf_op jit(solution)/shard_map/ppermute | solution.py:19
  27.5 14.1 %collective-permute-start.13 = (bf16[128,256]{1,0:T(8,128)(2,1)S(1)}, bf16[128,256]{1,0:T(8,128)(2,1)S(1)}, u32[]{:S(2)}, u32[]{:S(2)}) collective-permute-start(bf16[128,256]{1,0:T(8,128)(2,1)S(1)} %copy-done.6), channel_id=1, source_target_pairs={{0,8},{8,0},{16,24},{24,16},{1,9},{9,1},{17,25},{25,17},{2,10},{10... | collective-permute-start | bytes 196616 | tf_op jit(solution)/shard_map/ppermute | solution.py:19
  31.9 9.7 %collective-permute-start.15 = (bf16[128,256]{1,0:T(8,128)(2,1)S(1)}, bf16[128,256]{1,0:T(8,128)(2,1)S(1)}, u32[]{:S(2)}, u32[]{:S(2)}) collective-permute-start(bf16[128,256]{1,0:T(8,128)(2,1)S(1)} %collective-permute-done.14.refs_6_), channel_id=1, source_target_pairs={{0,8},{8,0},{16,24},{24,16},{1,9},{9,1},{17,25},{25,17},{2,10},{10... | collective-permute-start | bytes 196616 | tf_op jit(solution)/shard_map/ppermute | solution.py:19
  35.4 9.7 %copy-start.5 = (bf16[256,256]{1,0:T(8,128)(2,1)S(1)}, bf16[256,256]{1,0:T(8,128)(2,1)}, u32[]{:S(2)}) copy-start(bf16[256,256]{1,0:T(8,128)(2,1)} %refs_8_.1) | copy-start | bytes 393220
  37.2 6.4 %collective-permute-start.12 = (bf16[4,64,128]{2,1,0:T(8,128)(2,1)S(1)}, bf16[4,64,128]{2,1,0:T(8,128)(2,1)S(1)}, u32[]{:S(2)}, u32[]{:S(2)}) collective-permute-start(bf16[4,64,128]{2,1,0:T(8,128)(2,1)S(1)} %shard_map.97.refs_0_), channel_id=1, source_target_pairs={{0,24},{8,16},{16,8},{24,0},{1,25},{9,17},{17,9},{25,1},{2,26},{10... | collective-permute-start | bytes 196616 | tf_op jit(solution)/shard_map/ppermute | solution.py:19
  38.6 6.6 %collective-permute-start.11 = (bf16[4,64,128]{2,1,0:T(8,128)(2,1)S(1)}, bf16[4,64,128]{2,1,0:T(8,128)(2,1)S(1)}, u32[]{:S(2)}, u32[]{:S(2)}) collective-permute-start(bf16[4,64,128]{2,1,0:T(8,128)(2,1)S(1)} %shard_map.97.refs_0_), channel_id=1, source_target_pairs={{0,16},{8,24},{16,0},{24,8},{1,17},{9,25},{17,1},{25,9},{2,18},{10... | collective-permute-start | bytes 196616 | tf_op jit(solution)/shard_map/ppermute | solution.py:19
  38.7 6.5 %collective-permute-start.10 = (bf16[4,64,128]{2,1,0:T(8,128)(2,1)S(1)}, bf16[4,64,128]{2,1,0:T(8,128)(2,1)S(1)}, u32[]{:S(2)}, u32[]{:S(2)}) collective-permute-start(bf16[4,64,128]{2,1,0:T(8,128)(2,1)S(1)} %shard_map.97.refs_0_), channel_id=1, source_target_pairs={{0,8},{8,0},{16,24},{24,16},{1,9},{9,1},{17,25},{25,17},{2,10},{10... | collective-permute-start | bytes 196616 | tf_op jit(solution)/shard_map/ppermute | solution.py:19
  48.8 1.7 %collective-permute-start.16 = (bf16[5,128,256]{2,1,0:T(8,128)(2,1)S(1)}, bf16[5,128,256]{2,1,0:T(8,128)(2,1)S(1)}, u32[]{:S(2)}, u32[]{:S(2)}) collective-permute-start(bf16[5,128,256]{2,1,0:T(8,128)(2,1)S(1)} %get-tuple-element.31), channel_id=1, source_target_pairs={{0,1},{1,0},{2,3},{3,2},{4,5},{5,4},{6,7},{7,6},{8,9},{9,8},{10,11... | collective-permute-start | bytes 983048 | tf_op jit(solution)/shard_map/ppermute | solution.py:19
  50.5 6.4 %collective-permute-start.17 = (bf16[256,256]{1,0:T(8,128)(2,1)S(1)}, bf16[256,256]{1,0:T(8,128)(2,1)S(1)}, u32[]{:S(2)}, u32[]{:S(2)}) collective-permute-start(bf16[256,256]{1,0:T(8,128)(2,1)S(1)} %get-tuple-element.34), channel_id=1, source_target_pairs={{0,2},{1,3},{2,0},{3,1},{4,6},{5,7},{6,4},{7,5},{8,10},{9,11},{10,... | collective-permute-start | bytes 393224 | tf_op jit(solution)/shard_map/ppermute | solution.py:19
  51.5 7.0 %collective-permute-start.18 = (bf16[256,256]{1,0:T(8,128)(2,1)S(1)}, bf16[256,256]{1,0:T(8,128)(2,1)S(1)}, u32[]{:S(2)}, u32[]{:S(2)}) collective-permute-start(bf16[256,256]{1,0:T(8,128)(2,1)S(1)} %get-tuple-element.35), channel_id=1, source_target_pairs={{0,4},{1,5},{2,6},{3,7},{4,0},{5,1},{6,2},{7,3},{8,12},{9,13},{10,... | collective-permute-start | bytes 393224 | tf_op jit(solution)/shard_map/ppermute | solution.py:19
  52.9 6.9 %collective-permute-start.19 = (bf16[256,256]{1,0:T(8,128)(2,1)S(1)}, bf16[256,256]{1,0:T(8,128)(2,1)S(1)}, u32[]{:S(2)}, u32[]{:S(2)}) collective-permute-start(bf16[256,256]{1,0:T(8,128)(2,1)S(1)} %get-tuple-element.36), channel_id=1, source_target_pairs={{0,6},{1,7},{2,4},{3,5},{4,2},{5,3},{6,0},{7,1},{8,14},{9,15},{10,... | collective-permute-start | bytes 393224 | tf_op jit(solution)/shard_map/ppermute | solution.py:19
  60.5 1.3 %collective-permute-start.20 = (f32[128,256]{1,0:T(8,128)S(1)}, f32[128,256]{1,0:T(8,128)S(1)}, u32[]{:S(2)}, u32[]{:S(2)}) collective-permute-start(f32[128,256]{1,0:T(8,128)S(1)} %get-tuple-element.37.mine), channel_id=1, source_target_pairs={{0,1},{1,0},{2,3},{3,2},{4,5},{5,4},{6,7},{7,6},{8,9},{9,8},{10,11... | collective-permute-start | bytes 393224 | tf_op jit(solution)/shard_map/ppermute | solution.py:19

commit v7 on v6

--- a/solution.py
+++ b/solution.py
@@ -19,14 +19,14 @@
     return lax.ppermute(array, axis, [(i, i ^ bit) for i in range(peers)])
 
 
-def spread(array):
+def spread(array, last=1):
     reps = lax.axis_size("rep")
     held = {0: array}
     bit = reps // 2
-    while bit:
+    while bit >= last:
         held.update({x | bit: swap(part, "rep", bit) for x, part in held.items()})
         bit //= 2
-    return [held[x] for x in range(reps)]
+    return [held[x] for x in sorted(held)]
 
 
 def call(body, outs, in_specs, scratch=(), flops=0, moved=0):
@@ -70,16 +70,22 @@
 
 
 def order_chunks(reps, part, *refs):
-    chunks, unread, mine, index = refs[:reps], refs[reps], refs[-2], refs[-1]
+    copies = reps // 2
+    chunks, sources, unread = refs[:reps], refs[reps : reps + copies], refs[reps + copies]
+    mine, index = refs[reps + copies + 1 : reps + copies + 3]
+    for source, target in zip(sources, refs[reps + copies + 3 :]):
+        target[...] = source[...]
     for x in range(reps):
         mine[other("rep", x)] = chunks[x][:part]
         index[x] = chunks[x][part:].astype(F32).astype(jnp.int32)
 
 
-def join(*refs):
-    out = refs[-1]
-    for k, ref in enumerate(refs[:-1]):
+def join(half, *refs):
+    out, pairs = refs[-2:]
+    for k, ref in enumerate(refs[:half]):
         out[k] = ref[...]
+    for k in range(pairs.shape[0]):
+        pairs[k] = refs[half + k][...]
 
 
 def slot_of(index, lists, cap, t, j, c):
@@ -111,12 +117,12 @@
 
 def dense_layer(reps, *refs):
     chunks = refs[:reps]
-    cotangents = refs[reps : 2 * reps]
-    weight, out, dagg, terms, agg, cot, outs = refs[2 * reps :]
+    cotangents = refs[reps : reps + 2]
+    weight, out, dagg, terms, agg, cot, outs = refs[reps + 2 :]
     nodes, width = out.shape
     for x in range(reps):
         origin = other("rep", x)
-        cot[origin] = cotangents[x][...]
+        cot[origin] = cotangents[x % 2][x // 2]
         for b in range(reps):
             agg[b, origin] = chunks[x][b]
     gw = jnp.zeros((width, width), F32)
@@ -204,7 +210,9 @@
     def direct(arrays):
         return [arrays[0]] + [swap(arrays[x], "rep", x) for x in range(1, reps)]
 
-    blocks = spread(block_vals.reshape(slots, block, block))
+    adjacency = block_vals.reshape(slots, block, block)
+    evens = spread(adjacency, 2)
+    odds = [swap(adjacency, "rep", 1)]
     chunks = call(
         functools.partial(split_features, reps, lists, cap),
         [like((part + PAD, nodes), BF16)] * reps,
@@ -212,19 +220,28 @@
         [pltpu.VMEM((reps, part, nodes), BF16)],
         moved=4 * nodes * width,
     )(feats, block_rows[0, 0], block_cols[0, 0], step_counts[0, 0])
-    mine, index = call(
+    mine, index, cotangent, *relayed = call(
         functools.partial(order_chunks, reps, part),
-        [like((reps, part, nodes), BF16), like((reps, PAD, nodes), jnp.int32)],
-        [VMEM] * reps + [pl.BlockSpec(memory_space=pl.ANY)],
+        [like((reps, part, nodes), BF16), like((reps, PAD, nodes), jnp.int32)]
+        + [like((nodes, width), BF16)]
+        + [like((slots, block, block), BF16)] * (reps // 2 - 1),
+        [VMEM] * (reps + reps // 2) + [pl.BlockSpec(memory_space=pl.ANY)],
         moved=4 * nodes * width,
-    )(*direct(chunks), blocks[1])
-
-    near = call(
-        join,
-        like((half, reps, part, nodes), BF16),
-        [VMEM] * half,
+    )(*direct(chunks), cotangent, *evens[1:], odds[0])
+    odds += [swap(array, "rep", 1) for array in relayed]
+    blocks = [array for pair in zip(evens, odds) for array in pair]
+
+    near, cotangents = call(
+        functools.partial(join, half),
+        [like((half, reps, part, nodes), BF16), like((reps // 2, nodes, width), BF16)],
+        [VMEM] * (half + reps // 2) + [pl.BlockSpec(memory_space=pl.ANY)] * (reps // 2 - 1),
         moved=4 * half * nodes * width,
-    )(mine, *[swap(mine, "blk", 2 * k) for k in range(1, half)])
+    )(
+        mine,
+        *[swap(mine, "blk", 2 * k) for k in range(1, half)],
+        *spread(cotangent, 2),
+        *odds[1:],
+    )
     far = swap(near, "blk", 1)
     slot_flops = 2 * groups * cap * part * block * block
     slot_bytes = 2 * (groups * cap * block * block + groups * nodes * width)
@@ -245,7 +262,7 @@
             like((reps, nodes, width), BF16),
             like((2, width // 2, width), BF16),
         ],
-        [VMEM] * (2 * reps + 1),
+        [VMEM] * (reps + 3),
         [
             pltpu.VMEM((reps, reps, part, nodes), BF16),
             pltpu.VMEM((reps, nodes, width), BF16),
@@ -253,7 +270,7 @@
         ],
         flops=6 * reps * nodes * width * width,
         moved=2 * reps * 5 * nodes * width,
-    )(*direct([agg] * reps), *spread(cotangent), weight)
+    )(*direct([agg] * reps), cotangents, swap(cotangents, "rep", 1), weight)
 
     keep, send = call(
         functools.partial(feature_grads, reps, groups, lists, cap),

time: 62.9 us -> 57.4 us (0.913)
  starting transfers between devices: 29.2 us -> 25.6 us
  waiting for transfers between devices: 23.5 us -> 20.1 us
  local copies, waits for them, and re-layouts: 1.55 us -> 2.86 us
    ppermute x21 -> x20, starting transfers between devices: 29.2 us -> 25.6 us  [swap(): return lax.ppermute(array, axis, [(i, i ^ bit) for i in range(peers)])]
    ppermute x21 -> x20, waiting for transfers between devices: 23.5 us -> 20.1 us  [swap(): return lax.ppermute(array, axis, [(i, i ^ bit) for i in range(peers)])]
    unnamed x14, local copies, waits for them, and re-layouts: 1.55 us -> 2.86 us
  transfers between devices with their start and end apart: 21 -> 20, of which waited for: 13 -> 12; matrix products, arithmetic and copies ran while one was open for 0% -> 0% of each run, Pallas kernels for 4% -> 4%
where the time goes in v7:
time: 57.4 us; the launch traced here: 57.3 us
  starting transfers between devices  25.6 us (45%)
  waiting for transfers between devices  20.1 us (35%)
  Pallas kernels  7.91 us (14%)
  local copies, waits for them, and re-layouts  2.86 us (5%)
  between operations  0.73 us (1%)
    ppermute x20, starting transfers between devices, swap(): return lax.ppermute(array, axis, [(i, i ^ bit) for i in range(peers)])  25.6 us
    ppermute x20, waiting for transfers between devices, swap(): return lax.ppermute(array, axis, [(i, i ^ bit) for i in range(peers)])  20.1 us
    unnamed x14, local copies, waits for them, and re-layouts  2.86 us
    pallas_call x1, Pallas kernels, per_device(): call(functools.partial(feature_grads, reps, groups, lists, cap), [like((h...  2.63 us
    pallas_call x1, Pallas kernels, per_device(): call(functools.partial(aggregate, reps, groups, lists, cap), like((reps,...  1.72 us
    pallas_call x1, Pallas kernels, per_device(): call(functools.partial(dense_layer, reps), [like((nodes, width), BF16), l...  1.33 us
  transfers between devices with their start and end apart: 20, of which 12 were waited for; matrix products, arithmetic and copies ran while one was open for 0% of the time, Pallas kernels for 4%

profile of v7, /device:TPU:0, one launch (start us, length us, event | category | flops | bytes accessed | tf_op | source)
XLA Modules:
  0.0 57.3 jit_solution(7307830048825220762)
XLA Ops:
  0.6 3.1 %collective-permute-start.4 = (bf16[6,128,128]{2,1,0:T(8,128)(2,1)}, bf16[6,128,128]{2,1,0:T(8,128)(2,1)S(1)}, u32[]{:S(2)}, u32[]{:S(2)}) collective-permute-start(bf16[6,128,128]{2,1,0:T(8,128)(2,1)} %bitcast.4), channel_id=1, source_target_pairs={{0,8},{8,0},{16,24},{24,16},{1,9},{9,1},{17,25},{25,17},{2,10},{10... | collective-permute-start | bytes 589832 | tf_op jit(solution)/shard_map/ppermute | solution.py:19
  3.7 2.6 %collective-permute-start.3 = (bf16[6,128,128]{2,1,0:T(8,128)(2,1)}, bf16[6,128,128]{2,1,0:T(8,128)(2,1)S(1)}, u32[]{:S(2)}, u32[]{:S(2)}) collective-permute-start(bf16[6,128,128]{2,1,0:T(8,128)(2,1)} %bitcast.5), channel_id=1, source_target_pairs={{0,16},{8,24},{16,0},{24,8},{1,17},{9,25},{17,1},{25,9},{2,18},{10... | collective-permute-start | bytes 589832 | tf_op jit(solution)/shard_map/ppermute | solution.py:19
  6.3 0.8 %copy-done.2 = bf16[128,256]{1,0:T(8,128)(2,1)S(1)} copy-done((bf16[128,256]{1,0:T(8,128)(2,1)S(1)}, bf16[128,256]{1,0:T(8,128)(2,1)}, u32[]{:S(2)}) %copy-start.2) | copy-done | bytes 65560
  7.2 0.7 %copy-done.3 = s32[1,1,2,3]{3,2,1,0:T(2,128)S(1)} copy-done((s32[1,1,2,3]{3,2,1,0:T(2,128)S(1)}, s32[1,1,2,3]{3,2,1,0:T(2,128)}, u32[]{:S(2)}) %copy-start.3) | copy-done | bytes 48
  7.8 0.7 %copy-done.4 = s32[1,1,2,3]{3,2,1,0:T(2,128)S(1)} copy-done((s32[1,1,2,3]{3,2,1,0:T(2,128)S(1)}, s32[1,1,2,3]{3,2,1,0:T(2,128)}, u32[]{:S(2)}) %copy-start.4) | copy-done | bytes 48
  8.5 0.7 %copy-done.5 = s32[1,1,2]{2,1,0:T(1,128)S(1)} copy-done((s32[1,1,2]{2,1,0:T(1,128)S(1)}, s32[1,1,2]{2,1,0:T(1,128)}, u32[]{:S(2)}) %copy-start.5) | copy-done | bytes 32
  9.2 0.7 %shard_map.94 = (bf16[80,128]{1,0:T(8,128)(2,1)S(1)}, bf16[80,128]{1,0:T(8,128)(2,1)S(1)}, bf16[80,128]{1,0:T(8,128)(2,1)S(1)}, bf16[80,128]{1,0:T(8,128)(2,1)S(1)}) custom-call(bf16[128,256]{1,0:T(8,128)(2,1)S(1)} %copy-done.2, s32[2,3]{1,0:T(2,128)S(1)} %bitcast.8, s32[2,3]{1,0:T(2,128)S(1)} %bitcast.9, s32[2]{0:T(128)S(1)} %bitcast.10), custom_call_target="tpu_custom_call" | custom-call | bytes 131072 | tf_op jit(solution)/shard_map/pallas_call | solution.py:216
  9.9 0.5 collective-permute-start
  10.4 0.0 collective-permute-start.1
  10.4 3.9 %collective-permute-start.2 = (bf16[80,128]{1,0:T(8,128)(2,1)S(1)}, bf16[80,128]{1,0:T(8,128)(2,1)S(1)}, u32[]{:S(2)}, u32[]{:S(2)}) collective-permute-start(bf16[80,128]{1,0:T(8,128)(2,1)S(1)} %get-tuple-element.28), channel_id=1, source_target_pairs={{0,24},{8,16},{16,8},{24,0},{1,25},{9,17},{17,9},{25,1},{2,26},{10... | collective-permute-start | bytes 61448 | tf_op jit(solution)/shard_map/ppermute | solution.py:19
  14.3 0.0 collective-permute-done.refs_1_
  14.3 2.5 %collective-permute-done.1.refs_2_ = bf16[80,128]{1,0:T(8,128)(2,1)S(1)} collective-permute-done((bf16[80,128]{1,0:T(8,128)(2,1)S(1)}, bf16[80,128]{1,0:T(8,128)(2,1)S(1)}, u32[]{:S(2)}, u32[]{:S(2)}) %collective-permute-start.1) | collective-permute-done | bytes 20512 | tf_op jit(solution)/shard_map/ppermute | solution.py:19
  16.9 0.0 collective-permute-done.2.refs_3_
  16.9 0.0 collective-permute-done.4.refs_6_.refs_1_
  16.9 0.0 collective-permute-done.3.refs_5_.refs_2_
  16.9 1.0 %collective-permute-start.5 = (bf16[6,128,128]{2,1,0:T(8,128)(2,1)S(1)}, bf16[6,128,128]{2,1,0:T(8,128)(2,1)S(1)}, u32[]{:S(2)}, u32[]{:S(2)}) collective-permute-start(bf16[6,128,128]{2,1,0:T(8,128)(2,1)S(1)} %get-tuple-element.30), channel_id=1, source_target_pairs={{0,8},{8,0},{16,24},{24,16},{1,9},{9,1},{17,25},{25,17},{2,10},{10... | collective-permute-start | bytes 589832 | tf_op jit(solution)/shard_map/ppermute | solution.py:19
  17.9 2.7 %collective-permute-start.9 = (bf16[128,256]{1,0:T(8,128)(2,1)S(1)}, bf16[128,256]{1,0:T(8,128)(2,1)S(1)}, u32[]{:S(2)}, u32[]{:S(2)}) collective-permute-start(bf16[128,256]{1,0:T(8,128)(2,1)S(1)} %get-tuple-element.32.refs_4_), channel_id=1, source_target_pairs={{0,16},{8,24},{16,0},{24,8},{1,17},{9,25},{17,1},{25,9},{2,18},{10... | collective-permute-start | bytes 196616 | tf_op jit(solution)/shard_map/ppermute | solution.py:19
  20.6 2.4 %collective-permute-start.8 = (bf16[4,64,128]{2,1,0:T(8,128)(2,1)S(1)}, bf16[4,64,128]{2,1,0:T(8,128)(2,1)S(1)}, u32[]{:S(2)}, u32[]{:S(2)}) collective-permute-start(bf16[4,64,128]{2,1,0:T(8,128)(2,1)S(1)} %get-tuple-element.31.refs_0_), channel_id=1, source_target_pairs={{0,6},{1,7},{2,4},{3,5},{4,2},{5,3},{6,0},{7,1},{8,14},{9,15},{10,... | collective-permute-start | bytes 196616 | tf_op jit(solution)/shard_map/ppermute | solution.py:19
  23.0 0.5 collective-permute-start.7
  23.5 0.5 collective-permute-start.6
  24.1 0.0 collective-permute-done.9.refs_5_
  24.1 1.7 %collective-permute-done.8.refs_3_ = bf16[4,64,128]{2,1,0:T(8,128)(2,1)S(1)} collective-permute-done((bf16[4,64,128]{2,1,0:T(8,128)(2,1)S(1)}, bf16[4,64,128]{2,1,0:T(8,128)(2,1)S(1)}, u32[]{:S(2)}, u32[]{:S(2)}) %collective-permute-start.8) | collective-permute-done | bytes 65568 | tf_op jit(solution)/shard_map/ppermute | solution.py:19
  25.7 1.5 %collective-permute-done.7.refs_2_ = bf16[4,64,128]{2,1,0:T(8,128)(2,1)S(1)} collective-permute-done((bf16[4,64,128]{2,1,0:T(8,128)(2,1)S(1)}, bf16[4,64,128]{2,1,0:T(8,128)(2,1)S(1)}, u32[]{:S(2)}, u32[]{:S(2)}) %collective-permute-start.7) | collective-permute-done | bytes 65568 | tf_op jit(solution)/shard_map/ppermute | solution.py:19
  27.3 0.5 collective-permute-done.6.refs_1_
  27.8 0.0 collective-permute-done.5.refs_6_.refs_3_
  27.8 0.1 collective-permute-start.10
  27.9 0.2 collective-permute-start.14
  28.1 1.3 %collective-permute-done.10.refs_5_ = bf16[4,4,64,128]{3,2,1,0:T(8,128)(2,1)S(1)} collective-permute-done((bf16[4,4,64,128]{3,2,1,0:T(8,128)(2,1)S(1)}, bf16[4,4,64,128]{3,2,1,0:T(8,128)(2,1)S(1)}, u32[]{:S(2)}, u32[]{:S(2)}) %collective-permute-start.10) | collective-permute-done | bytes 262176 | tf_op jit(solution)/shard_map/ppermute | solution.py:19
  29.4 1.7 %shard_map.97.refs_0_ = bf16[4,64,128]{2,1,0:T(8,128)(2,1)S(1)} custom-call(s32[4,16,128]{2,1,0:T(8,128)S(1)} %get-tuple-element.29.index, bf16[6,128,128]{2,1,0:T(8,128)(2,1)S(1)} %bitcast.6, bf16[6,128,128]{2,1,0:T(8,128)(2,1)S(1)} %collective-permute-done.4.refs_6_.refs_1_, bf16[6,128,128]{2,1,0:T(8,128)(2,1)S(1)} %collective-permute-done.3.refs_5_.refs_2_, ...), custom_call_target="tpu_custom_call" | custom-call | flops 50331648 | bytes 1310720 | tf_op jit(solution)/shard_map/pallas_call | solution.py:249
  31.2 0.9 %collective-permute-start.13 = (bf16[4,64,128]{2,1,0:T(8,128)(2,1)S(1)}, bf16[4,64,128]{2,1,0:T(8,128)(2,1)S(1)}, u32[]{:S(2)}, u32[]{:S(2)}) collective-permute-start(bf16[4,64,128]{2,1,0:T(8,128)(2,1)S(1)} %shard_map.97.refs_0_), channel_id=1, source_target_pairs={{0,24},{8,16},{16,8},{24,0},{1,25},{9,17},{17,9},{25,1},{2,26},{10... | collective-permute-start | bytes 196616 | tf_op jit(solution)/shard_map/ppermute | solution.py:19
  32.0 1.2 %collective-permute-start.12 = (bf16[4,64,128]{2,1,0:T(8,128)(2,1)S(1)}, bf16[4,64,128]{2,1,0:T(8,128)(2,1)S(1)}, u32[]{:S(2)}, u32[]{:S(2)}) collective-permute-start(bf16[4,64,128]{2,1,0:T(8,128)(2,1)S(1)} %shard_map.97.refs_0_), channel_id=1, source_target_pairs={{0,16},{8,24},{16,0},{24,8},{1,17},{9,25},{17,1},{25,9},{2,18},{10... | collective-permute-start | bytes 196616 | tf_op jit(solution)/shard_map/ppermute | solution.py:19
  33.3 2.4 %collective-permute-start.11 = (bf16[4,64,128]{2,1,0:T(8,128)(2,1)S(1)}, bf16[4,64,128]{2,1,0:T(8,128)(2,1)S(1)}, u32[]{:S(2)}, u32[]{:S(2)}) collective-permute-start(bf16[4,64,128]{2,1,0:T(8,128)(2,1)S(1)} %shard_map.97.refs_0_), channel_id=1, source_target_pairs={{0,8},{8,0},{16,24},{24,16},{1,9},{9,1},{17,25},{25,17},{2,10},{10... | collective-permute-start | bytes 196616 | tf_op jit(solution)/shard_map/ppermute | solution.py:19
  35.6 2.4 %collective-permute-done.13.refs_3_ = bf16[4,64,128]{2,1,0:T(8,128)(2,1)S(1)} collective-permute-done((bf16[4,64,128]{2,1,0:T(8,128)(2,1)S(1)}, bf16[4,64,128]{2,1,0:T(8,128)(2,1)S(1)}, u32[]{:S(2)}, u32[]{:S(2)}) %collective-permute-start.13) | collective-permute-done | bytes 65568 | tf_op jit(solution)/shard_map/ppermute | solution.py:19
  38.0 1.7 %collective-permute-done.12.refs_2_ = bf16[4,64,128]{2,1,0:T(8,128)(2,1)S(1)} collective-permute-done((bf16[4,64,128]{2,1,0:T(8,128)(2,1)S(1)}, bf16[4,64,128]{2,1,0:T(8,128)(2,1)S(1)}, u32[]{:S(2)}, u32[]{:S(2)}) %collective-permute-start.12) | collective-permute-done | bytes 65568 | tf_op jit(solution)/shard_map/ppermute | solution.py:19
  39.7 1.3 %shard_map.98 = (bf16[128,256]{1,0:T(8,128)(2,1)}, bf16[4,128,256]{2,1,0:T(8,128)(2,1)S(1)}, bf16[2,128,256]{2,1,0:T(8,128)(2,1)S(1)}) custom-call(bf16[4,64,128]{2,1,0:T(8,128)(2,1)S(1)} %shard_map.97.refs_0_, bf16[4,64,128]{2,1,0:T(8,128)(2,1)S(1)} %collective-permute-done.11.refs_1_, bf16[4,64,128]{2,1,0:T(8,128)(2,1)S(1)} %collective-permute-done.12.refs_2_, ...), custom_call_target="tpu_custom_call" | custom-call | flops 201326592 | bytes 1310720 | tf_op jit(solution)/shard_map/pallas_call | solution.py:258
  41.0 2.6 %shard_map.99 = (f32[4,128,256]{2,1,0:T(8,128)S(1)}, bf16[5,128,256]{2,1,0:T(8,128)(2,1)S(1)}) custom-call(s32[4,16,128]{2,1,0:T(8,128)S(1)} %get-tuple-element.29.index, bf16[6,128,128]{2,1,0:T(8,128)(2,1)S(1)} %bitcast.7, bf16[6,128,128]{2,1,0:T(8,128)(2,1)S(1)} %collective-permute-done.4.refs_6_.refs_1_, ...), custom_call_target="tpu_custom_call" | custom-call | flops 50331648 | bytes 1310720 | tf_op jit(solution)/shard_map/pallas_call | solution.py:275
  43.7 0.1 collective-permute-start.15
  43.8 1.6 %collective-permute-done.15.arrived = bf16[5,128,256]{2,1,0:T(8,128)(2,1)S(1)} collective-permute-done((bf16[5,128,256]{2,1,0:T(8,128)(2,1)S(1)}, bf16[5,128,256]{2,1,0:T(8,128)(2,1)S(1)}, u32[]{:S(2)}, u32[]{:S(2)}) %collective-permute-start.15) | collective-permute-done | bytes 327712 | tf_op jit(solution)/shard_map/ppermute | solution.py:19
  45.4 0.1 shard_map.100
  45.4 0.6 %collective-permute-start.16 = (bf16[256,256]{1,0:T(8,128)(2,1)S(1)}, bf16[256,256]{1,0:T(8,128)(2,1)S(1)}, u32[]{:S(2)}, u32[]{:S(2)}) collective-permute-start(bf16[256,256]{1,0:T(8,128)(2,1)S(1)} %get-tuple-element.42), channel_id=1, source_target_pairs={{0,2},{1,3},{2,0},{3,1},{4,6},{5,7},{6,4},{7,5},{8,10},{9,11},{10,... | collective-permute-start | bytes 393224 | tf_op jit(solution)/shard_map/ppermute | solution.py:19
  46.1 1.5 %collective-permute-start.17 = (bf16[256,256]{1,0:T(8,128)(2,1)S(1)}, bf16[256,256]{1,0:T(8,128)(2,1)S(1)}, u32[]{:S(2)}, u32[]{:S(2)}) collective-permute-start(bf16[256,256]{1,0:T(8,128)(2,1)S(1)} %get-tuple-element.43), channel_id=1, source_target_pairs={{0,4},{1,5},{2,6},{3,7},{4,0},{5,1},{6,2},{7,3},{8,12},{9,13},{10,... | collective-permute-start | bytes 393224 | tf_op jit(solution)/shard_map/ppermute | solution.py:19
  47.6 1.4 %collective-permute-start.18 = (bf16[256,256]{1,0:T(8,128)(2,1)S(1)}, bf16[256,256]{1,0:T(8,128)(2,1)S(1)}, u32[]{:S(2)}, u32[]{:S(2)}) collective-permute-start(bf16[256,256]{1,0:T(8,128)(2,1)S(1)} %get-tuple-element.44), channel_id=1, source_target_pairs={{0,6},{1,7},{2,4},{3,5},{4,2},{5,3},{6,0},{7,1},{8,14},{9,15},{10,... | collective-permute-start | bytes 393224 | tf_op jit(solution)/shard_map/ppermute | solution.py:19
  49.0 2.9 %collective-permute-done.16.refs_0_ = bf16[256,256]{1,0:T(8,128)(2,1)S(1)} collective-permute-done((bf16[256,256]{1,0:T(8,128)(2,1)S(1)}, bf16[256,256]{1,0:T(8,128)(2,1)S(1)}, u32[]{:S(2)}, u32[]{:S(2)}) %collective-permute-start.16) | collective-permute-done | bytes 131104 | tf_op jit(solution)/shard_map/ppermute | solution.py:19
  51.8 1.4 %collective-permute-done.17.refs_1_ = bf16[256,256]{1,0:T(8,128)(2,1)S(1)} collective-permute-done((bf16[256,256]{1,0:T(8,128)(2,1)S(1)}, bf16[256,256]{1,0:T(8,128)(2,1)S(1)}, u32[]{:S(2)}, u32[]{:S(2)}) %collective-permute-start.17) | collective-permute-done | bytes 131104 | tf_op jit(solution)/shard_map/ppermute | solution.py:19
  53.2 1.2 %collective-permute-done.18.refs_2_ = bf16[256,256]{1,0:T(8,128)(2,1)S(1)} collective-permute-done((bf16[256,256]{1,0:T(8,128)(2,1)S(1)}, bf16[256,256]{1,0:T(8,128)(2,1)S(1)}, u32[]{:S(2)}, u32[]{:S(2)}) %collective-permute-start.18) | collective-permute-done | bytes 131104 | tf_op jit(solution)/shard_map/ppermute | solution.py:19
  54.5 0.7 %shard_map.101 = (f32[128,256]{1,0:T(8,128)}, f32[128,256]{1,0:T(8,128)S(1)}) custom-call(f32[128,256]{1,0:T(8,128)S(1)} %get-tuple-element.40.own, bf16[128,256]{1,0:T(8,128)(2,1)S(1)} %get-tuple-element.41.own_terms, bf16[256,256]{1,0:T(8,128)(2,1)S(1)} %collective-permute-done.16.refs_0_, bf16[256,256]{1,0:T(8,128)(2,1)S(1)} %collective-permute-done.17.refs_1_, ...), custom_call_target="tpu_custom_call" | custom-call | bytes 1048576 | tf_op jit(solution)/shard_map/pallas_call | solution.py:293
  55.2 1.3 %collective-permute-done.19.arrived = f32[128,256]{1,0:T(8,128)S(1)} collective-permute-done((f32[128,256]{1,0:T(8,128)S(1)}, f32[128,256]{1,0:T(8,128)S(1)}, u32[]{:S(2)}, u32[]{:S(2)}) %collective-permute-start.19) | collective-permute-done | bytes 131104 | tf_op jit(solution)/shard_map/ppermute | solution.py:19
  56.5 0.7 %shard_map.102 = f32[256,256]{1,0:T(8,128)} custom-call(f32[128,256]{1,0:T(8,128)S(1)} %get-tuple-element.45.mine, f32[128,256]{1,0:T(8,128)S(1)} %collective-permute-done.19.arrived), custom_call_target="tpu_custom_call" | custom-call | bytes 524288 | tf_op jit(solution)/shard_map/pallas_call | solution.py:300
  (15 shorter events, 0.1 us)
Async XLA Ops:
  0.6 16.2 %copy-start.1 = (bf16[128,256]{1,0:T(8,128)(2,1)S(1)}, bf16[128,256]{1,0:T(8,128)(2,1)}, u32[]{:S(2)}) copy-start(bf16[128,256]{1,0:T(8,128)(2,1)} %refs_4_.1) | copy-start | bytes 196612
  0.6 16.2 %collective-permute-start.4 = (bf16[6,128,128]{2,1,0:T(8,128)(2,1)}, bf16[6,128,128]{2,1,0:T(8,128)(2,1)S(1)}, u32[]{:S(2)}, u32[]{:S(2)}) collective-permute-start(bf16[6,128,128]{2,1,0:T(8,128)(2,1)} %bitcast.4), channel_id=1, source_target_pairs={{0,8},{8,0},{16,24},{24,16},{1,9},{9,1},{17,25},{25,17},{2,10},{10... | collective-permute-start | bytes 589832 | tf_op jit(solution)/shard_map/ppermute | solution.py:19
  3.7 13.1 %collective-permute-start.3 = (bf16[6,128,128]{2,1,0:T(8,128)(2,1)}, bf16[6,128,128]{2,1,0:T(8,128)(2,1)S(1)}, u32[]{:S(2)}, u32[]{:S(2)}) collective-permute-start(bf16[6,128,128]{2,1,0:T(8,128)(2,1)} %bitcast.5), channel_id=1, source_target_pairs={{0,16},{8,24},{16,0},{24,8},{1,17},{9,25},{17,1},{25,9},{2,18},{10... | collective-permute-start | bytes 589832 | tf_op jit(solution)/shard_map/ppermute | solution.py:19
  6.3 0.8 %copy-start.2 = (bf16[128,256]{1,0:T(8,128)(2,1)S(1)}, bf16[128,256]{1,0:T(8,128)(2,1)}, u32[]{:S(2)}) copy-start(bf16[128,256]{1,0:T(8,128)(2,1)} %feats.1) | copy-start | bytes 196612
  7.2 0.7 %copy-start.3 = (s32[1,1,2,3]{3,2,1,0:T(2,128)S(1)}, s32[1,1,2,3]{3,2,1,0:T(2,128)}, u32[]{:S(2)}) copy-start(s32[1,1,2,3]{3,2,1,0:T(2,128)} %param.11) | copy-start | bytes 76
  7.8 0.7 %copy-start.4 = (s32[1,1,2,3]{3,2,1,0:T(2,128)S(1)}, s32[1,1,2,3]{3,2,1,0:T(2,128)}, u32[]{:S(2)}) copy-start(s32[1,1,2,3]{3,2,1,0:T(2,128)} %param.12) | copy-start | bytes 76
  8.5 0.7 %copy-start.5 = (s32[1,1,2]{2,1,0:T(1,128)S(1)}, s32[1,1,2]{2,1,0:T(1,128)}, u32[]{:S(2)}) copy-start(s32[1,1,2]{2,1,0:T(1,128)} %param.13) | copy-start | bytes 28
  9.9 4.5 %collective-permute-start = (bf16[80,128]{1,0:T(8,128)(2,1)S(1)}, bf16[80,128]{1,0:T(8,128)(2,1)S(1)}, u32[]{:S(2)}, u32[]{:S(2)}) collective-permute-start(bf16[80,128]{1,0:T(8,128)(2,1)S(1)} %get-tuple-element.26), channel_id=1, source_target_pairs={{0,8},{8,0},{16,24},{24,16},{1,9},{9,1},{17,25},{25,17},{2,10},{10... | collective-permute-start | bytes 61448 | tf_op jit(solution)/shard_map/ppermute | solution.py:19
  10.4 6.5 %collective-permute-start.1 = (bf16[80,128]{1,0:T(8,128)(2,1)S(1)}, bf16[80,128]{1,0:T(8,128)(2,1)S(1)}, u32[]{:S(2)}, u32[]{:S(2)}) collective-permute-start(bf16[80,128]{1,0:T(8,128)(2,1)S(1)} %get-tuple-element.27), channel_id=1, source_target_pairs={{0,16},{8,24},{16,0},{24,8},{1,17},{9,25},{17,1},{25,9},{2,18},{10... | collective-permute-start | bytes 61448 | tf_op jit(solution)/shard_map/ppermute | solution.py:19
  10.4 6.5 %collective-permute-start.2 = (bf16[80,128]{1,0:T(8,128)(2,1)S(1)}, bf16[80,128]{1,0:T(8,128)(2,1)S(1)}, u32[]{:S(2)}, u32[]{:S(2)}) collective-permute-start(bf16[80,128]{1,0:T(8,128)(2,1)S(1)} %get-tuple-element.28), channel_id=1, source_target_pairs={{0,24},{8,16},{16,8},{24,0},{1,25},{9,17},{17,9},{25,1},{2,26},{10... | collective-permute-start | bytes 61448 | tf_op jit(solution)/shard_map/ppermute | solution.py:19
  16.9 10.9 %collective-permute-start.5 = (bf16[6,128,128]{2,1,0:T(8,128)(2,1)S(1)}, bf16[6,128,128]{2,1,0:T(8,128)(2,1)S(1)}, u32[]{:S(2)}, u32[]{:S(2)}) collective-permute-start(bf16[6,128,128]{2,1,0:T(8,128)(2,1)S(1)} %get-tuple-element.30), channel_id=1, source_target_pairs={{0,8},{8,0},{16,24},{24,16},{1,9},{9,1},{17,25},{25,17},{2,10},{10... | collective-permute-start | bytes 589832 | tf_op jit(solution)/shard_map/ppermute | solution.py:19
  17.9 6.2 %collective-permute-start.9 = (bf16[128,256]{1,0:T(8,128)(2,1)S(1)}, bf16[128,256]{1,0:T(8,128)(2,1)S(1)}, u32[]{:S(2)}, u32[]{:S(2)}) collective-permute-start(bf16[128,256]{1,0:T(8,128)(2,1)S(1)} %get-tuple-element.32.refs_4_), channel_id=1, source_target_pairs={{0,16},{8,24},{16,0},{24,8},{1,17},{9,25},{17,1},{25,9},{2,18},{10... | collective-permute-start | bytes 196616 | tf_op jit(solution)/shard_map/ppermute | solution.py:19
  20.6 8.9 %copy-start = (bf16[1,1,2,3,128,128]{5,4,3,2,1,0:T(8,128)(2,1)S(1)}, bf16[1,1,2,3,128,128]{5,4,3,2,1,0:T(8,128)(2,1)}, u32[]{:S(2)}) copy-start(bf16[1,1,2,3,128,128]{5,4,3,2,1,0:T(8,128)(2,1)} %param.10) | copy-start | bytes 589828
  20.6 5.2 %collective-permute-start.8 = (bf16[4,64,128]{2,1,0:T(8,128)(2,1)S(1)}, bf16[4,64,128]{2,1,0:T(8,128)(2,1)S(1)}, u32[]{:S(2)}, u32[]{:S(2)}) collective-permute-start(bf16[4,64,128]{2,1,0:T(8,128)(2,1)S(1)} %get-tuple-element.31.refs_0_), channel_id=1, source_target_pairs={{0,6},{1,7},{2,4},{3,5},{4,2},{5,3},{6,0},{7,1},{8,14},{9,15},{10,... | collective-permute-start | bytes 196616 | tf_op jit(solution)/shard_map/ppermute | solution.py:19
  23.0 4.3 %collective-permute-start.7 = (bf16[4,64,128]{2,1,0:T(8,128)(2,1)S(1)}, bf16[4,64,128]{2,1,0:T(8,128)(2,1)S(1)}, u32[]{:S(2)}, u32[]{:S(2)}) collective-permute-start(bf16[4,64,128]{2,1,0:T(8,128)(2,1)S(1)} %get-tuple-element.31.refs_0_), channel_id=1, source_target_pairs={{0,4},{1,5},{2,6},{3,7},{4,0},{5,1},{6,2},{7,3},{8,12},{9,13},{10,... | collective-permute-start | bytes 196616 | tf_op jit(solution)/shard_map/ppermute | solution.py:19
  23.5 4.3 %collective-permute-start.6 = (bf16[4,64,128]{2,1,0:T(8,128)(2,1)S(1)}, bf16[4,64,128]{2,1,0:T(8,128)(2,1)S(1)}, u32[]{:S(2)}, u32[]{:S(2)}) collective-permute-start(bf16[4,64,128]{2,1,0:T(8,128)(2,1)S(1)} %get-tuple-element.31.refs_0_), channel_id=1, source_target_pairs={{0,2},{1,3},{2,0},{3,1},{4,6},{5,7},{6,4},{7,5},{8,10},{9,11},{10,... | collective-permute-start | bytes 196616 | tf_op jit(solution)/shard_map/ppermute | solution.py:19
  27.8 1.6 %collective-permute-start.10 = (bf16[4,4,64,128]{3,2,1,0:T(8,128)(2,1)S(1)}, bf16[4,4,64,128]{3,2,1,0:T(8,128)(2,1)S(1)}, u32[]{:S(2)}, u32[]{:S(2)}) collective-permute-start(bf16[4,4,64,128]{3,2,1,0:T(8,128)(2,1)S(1)} %get-tuple-element.33.refs_4_), channel_id=1, source_target_pairs={{0,1},{1,0},{2,3},{3,2},{4,5},{5,4},{6,7},{7,6},{8,9},{9,8},{10,11... | collective-permute-start | bytes 786440 | tf_op jit(solution)/shard_map/ppermute | solution.py:19
  27.9 7.7 %collective-permute-start.14 = (bf16[2,128,256]{2,1,0:T(8,128)(2,1)S(1)}, bf16[2,128,256]{2,1,0:T(8,128)(2,1)S(1)}, u32[]{:S(2)}, u32[]{:S(2)}) collective-permute-start(bf16[2,128,256]{2,1,0:T(8,128)(2,1)S(1)} %get-tuple-element.34.refs_4_), channel_id=1, source_target_pairs={{0,8},{8,0},{16,24},{24,16},{1,9},{9,1},{17,25},{25,17},{2,10},{10... | collective-permute-start | bytes 393224 | tf_op jit(solution)/shard_map/ppermute | solution.py:19
  29.4 10.3 %copy-start.6 = (bf16[256,256]{1,0:T(8,128)(2,1)S(1)}, bf16[256,256]{1,0:T(8,128)(2,1)}, u32[]{:S(2)}) copy-start(bf16[256,256]{1,0:T(8,128)(2,1)} %refs_6_.1) | copy-start | bytes 393220
  31.2 6.9 %collective-permute-start.13 = (bf16[4,64,128]{2,1,0:T(8,128)(2,1)S(1)}, bf16[4,64,128]{2,1,0:T(8,128)(2,1)S(1)}, u32[]{:S(2)}, u32[]{:S(2)}) collective-permute-start(bf16[4,64,128]{2,1,0:T(8,128)(2,1)S(1)} %shard_map.97.refs_0_), channel_id=1, source_target_pairs={{0,24},{8,16},{16,8},{24,0},{1,25},{9,17},{17,9},{25,1},{2,26},{10... | collective-permute-start | bytes 196616 | tf_op jit(solution)/shard_map/ppermute | solution.py:19
  32.0 7.7 %collective-permute-start.12 = (bf16[4,64,128]{2,1,0:T(8,128)(2,1)S(1)}, bf16[4,64,128]{2,1,0:T(8,128)(2,1)S(1)}, u32[]{:S(2)}, u32[]{:S(2)}) collective-permute-start(bf16[4,64,128]{2,1,0:T(8,128)(2,1)S(1)} %shard_map.97.refs_0_), channel_id=1, source_target_pairs={{0,16},{8,24},{16,0},{24,8},{1,17},{9,25},{17,1},{25,9},{2,18},{10... | collective-permute-start | bytes 196616 | tf_op jit(solution)/shard_map/ppermute | solution.py:19
  33.3 6.5 %collective-permute-start.11 = (bf16[4,64,128]{2,1,0:T(8,128)(2,1)S(1)}, bf16[4,64,128]{2,1,0:T(8,128)(2,1)S(1)}, u32[]{:S(2)}, u32[]{:S(2)}) collective-permute-start(bf16[4,64,128]{2,1,0:T(8,128)(2,1)S(1)} %shard_map.97.refs_0_), channel_id=1, source_target_pairs={{0,8},{8,0},{16,24},{24,16},{1,9},{9,1},{17,25},{25,17},{2,10},{10... | collective-permute-start | bytes 196616 | tf_op jit(solution)/shard_map/ppermute | solution.py:19
  43.7 1.7 %collective-permute-start.15 = (bf16[5,128,256]{2,1,0:T(8,128)(2,1)S(1)}, bf16[5,128,256]{2,1,0:T(8,128)(2,1)S(1)}, u32[]{:S(2)}, u32[]{:S(2)}) collective-permute-start(bf16[5,128,256]{2,1,0:T(8,128)(2,1)S(1)} %get-tuple-element.39), channel_id=1, source_target_pairs={{0,1},{1,0},{2,3},{3,2},{4,5},{5,4},{6,7},{7,6},{8,9},{9,8},{10,11... | collective-permute-start | bytes 983048 | tf_op jit(solution)/shard_map/ppermute | solution.py:19
  45.4 6.4 %collective-permute-start.16 = (bf16[256,256]{1,0:T(8,128)(2,1)S(1)}, bf16[256,256]{1,0:T(8,128)(2,1)S(1)}, u32[]{:S(2)}, u32[]{:S(2)}) collective-permute-start(bf16[256,256]{1,0:T(8,128)(2,1)S(1)} %get-tuple-element.42), channel_id=1, source_target_pairs={{0,2},{1,3},{2,0},{3,1},{4,6},{5,7},{6,4},{7,5},{8,10},{9,11},{10,... | collective-permute-start | bytes 393224 | tf_op jit(solution)/shard_map/ppermute | solution.py:19
  46.1 7.1 %collective-permute-start.17 = (bf16[256,256]{1,0:T(8,128)(2,1)S(1)}, bf16[256,256]{1,0:T(8,128)(2,1)S(1)}, u32[]{:S(2)}, u32[]{:S(2)}) collective-permute-start(bf16[256,256]{1,0:T(8,128)(2,1)S(1)} %get-tuple-element.43), channel_id=1, source_target_pairs={{0,4},{1,5},{2,6},{3,7},{4,0},{5,1},{6,2},{7,3},{8,12},{9,13},{10,... | collective-permute-start | bytes 393224 | tf_op jit(solution)/shard_map/ppermute | solution.py:19
  47.6 6.9 %collective-permute-start.18 = (bf16[256,256]{1,0:T(8,128)(2,1)S(1)}, bf16[256,256]{1,0:T(8,128)(2,1)S(1)}, u32[]{:S(2)}, u32[]{:S(2)}) collective-permute-start(bf16[256,256]{1,0:T(8,128)(2,1)S(1)} %get-tuple-element.44), channel_id=1, source_target_pairs={{0,6},{1,7},{2,4},{3,5},{4,2},{5,3},{6,0},{7,1},{8,14},{9,15},{10,... | collective-permute-start | bytes 393224 | tf_op jit(solution)/shard_map/ppermute | solution.py:19
  55.2 1.3 %collective-permute-start.19 = (f32[128,256]{1,0:T(8,128)S(1)}, f32[128,256]{1,0:T(8,128)S(1)}, u32[]{:S(2)}, u32[]{:S(2)}) collective-permute-start(f32[128,256]{1,0:T(8,128)S(1)} %get-tuple-element.45.mine), channel_id=1, source_target_pairs={{0,1},{1,0},{2,3},{3,2},{4,5},{5,4},{6,7},{7,6},{8,9},{9,8},{10,11... | collective-permute-start | bytes 393224 | tf_op jit(solution)/shard_map/ppermute | solution.py:19

commit v8 on v7

--- a/solution.py
+++ b/solution.py
@@ -70,14 +70,14 @@
 
 
 def order_chunks(reps, part, *refs):
-    copies = reps // 2
+    copies = reps // 2 - 1
     chunks, sources, unread = refs[:reps], refs[reps : reps + copies], refs[reps + copies]
     mine, index = refs[reps + copies + 1 : reps + copies + 3]
     for source, target in zip(sources, refs[reps + copies + 3 :]):
         target[...] = source[...]
     for x in range(reps):
         mine[other("rep", x)] = chunks[x][:part]
-        index[x] = chunks[x][part:].astype(F32).astype(jnp.int32)
+        index[x] = chunks[x][part:].astype(F32).astype(jnp.int32)[:1]
 
 
 def join(half, *refs):
@@ -100,19 +100,18 @@
     return lax.div(lax.bitwise_xor(mine, lax.rem(mine + groups - offset, groups)), 2)
 
 
-def aggregate(reps, groups, lists, cap, index, *refs):
-    blocks = refs[:reps]
-    near, far, out, total = refs[reps:]
-    total[...] = jnp.zeros_like(total)
-    for x in range(reps):
-        for j in range(lists):
-            held = far if j % 2 else near
+def aggregate(reps, groups, lists, cap, parity, index, *refs):
+    blocks, held, start, out = refs[:reps], refs[reps], refs[reps + 1 : -2], refs[-2]
+    total = refs[-1]
+    total[...] = start[0][...] if start else jnp.zeros_like(total)
+    for x in range(reps):
+        for j in range(parity, lists, 2):
             place = relative(groups, lists, x, j)
             for c in range(cap):
                 row, col, live = slot_of(index, lists, cap, x, j, c)
                 product = dot(held[place, col], blocks[x][j * cap + c], 1, 1)
                 total[row] += jnp.where(live, product, 0.0)
-    out[...] = total[...].astype(BF16)
+    out[...] = total[...].astype(out.dtype)
 
 
 def dense_layer(reps, *refs):
@@ -190,6 +189,11 @@
     terms[...] = gw
 
 
+def store(grads, rows, grad_feats, out_rows):
+    grad_feats[...] = grads[...]
+    out_rows[...] = rows[...]
+
+
 def join_cores(mine, arrived, out):
     core = lax.rem(lax.axis_index("blk"), 2)
     rows = mine.shape[0]
@@ -220,14 +224,13 @@
         [pltpu.VMEM((reps, part, nodes), BF16)],
         moved=4 * nodes * width,
     )(feats, block_rows[0, 0], block_cols[0, 0], step_counts[0, 0])
-    mine, index, cotangent, *relayed = call(
+    mine, index, *relayed = call(
         functools.partial(order_chunks, reps, part),
-        [like((reps, part, nodes), BF16), like((reps, PAD, nodes), jnp.int32)]
-        + [like((nodes, width), BF16)]
+        [like((reps, part, nodes), BF16), like((reps, 1, nodes), jnp.int32)]
         + [like((slots, block, block), BF16)] * (reps // 2 - 1),
-        [VMEM] * (reps + reps // 2) + [pl.BlockSpec(memory_space=pl.ANY)],
+        [VMEM] * (reps + reps // 2 - 1) + [pl.BlockSpec(memory_space=pl.ANY)],
         moved=4 * nodes * width,
-    )(*direct(chunks), cotangent, *evens[1:], odds[0])
+    )(*direct(chunks), *evens[1:], odds[0])
     odds += [swap(array, "rep", 1) for array in relayed]
     blocks = [array for pair in zip(evens, odds) for array in pair]
 
@@ -247,13 +250,21 @@
     slot_bytes = 2 * (groups * cap * block * block + groups * nodes * width)
 
     agg = call(
-        functools.partial(aggregate, reps, groups, lists, cap),
+        functools.partial(aggregate, reps, groups, lists, cap, 0),
+        like((reps, part, nodes), F32),
+        [SMEM] + [VMEM] * (reps + 1),
+        [pltpu.VMEM((reps, part, nodes), F32)],
+        flops=slot_flops // 2,
+        moved=slot_bytes // 2,
+    )(index, *blocks, near)
+    agg = call(
+        functools.partial(aggregate, reps, groups, lists, cap, 1),
         like((reps, part, nodes), BF16),
         [SMEM] + [VMEM] * (reps + 2),
         [pltpu.VMEM((reps, part, nodes), F32)],
-        flops=slot_flops,
-        moved=slot_bytes,
-    )(index, *blocks, near, far)
+        flops=slot_flops // 2,
+        moved=slot_bytes // 2,
+    )(index, *blocks, far, agg)
 
     out_rows, dagg, terms = call(
         functools.partial(dense_layer, reps),
@@ -290,13 +301,19 @@
         [VMEM] * 3,
         moved=10 * half * nodes * width,
     )(keep, terms, swap(send, "blk", 1))
-    grad_feats, terms = call(
+    grads, terms = call(
         functools.partial(add_chips, half),
         [like((nodes, width), F32), like((width // 2, width), F32)],
         [VMEM] * (half + 1),
         [pltpu.VMEM((half, width // 2, width), F32)],
         moved=8 * half * nodes * width,
     )(own, own_terms, *[swap(sends[k - 1], "blk", 2 * k) for k in range(1, half)])
+    grad_feats, out_rows = call(
+        store,
+        [like((nodes, width), F32), like((nodes, width), BF16)],
+        [VMEM] * 2,
+        moved=12 * nodes * width,
+    )(grads, out_rows)
     grad_weight = call(
         join_cores, like((width, width), F32), [VMEM] * 2, moved=8 * width * width
     )(terms, swap(terms, "blk", 1))

time: 57.4 us -> 55.6 us (0.969)
  Pallas kernels: 7.91 us -> 6.35 us
  local copies, waits for them, and re-layouts: 2.86 us -> 1.55 us
  waiting for transfers between devices: 20.1 us -> 20.8 us
    pallas_call x1, Pallas kernels: 2.63 us -> 1.26 us  [per_device(): call(functools.partial(feature_grads, reps, groups, lists, cap), [like((h...]
    unnamed x14, local copies, waits for them, and re-layouts: 2.86 us -> 1.55 us
    pallas_call x1 -> x3, Pallas kernels: 1.72 us -> 2.58 us  [the longest x1 0.95 us: per_device(): call(functools.partial(aggregate, reps, groups, lists, cap, 0), like((rep...]
    ppermute x20, waiting for transfers between devices: 20.1 us -> 20.8 us  [swap(): return lax.ppermute(array, axis, [(i, i ^ bit) for i in range(peers)])]
    pallas_call x1, Pallas kernels: 0.71 us -> 0.09 us  [per_device(): call(functools.partial(add_chips, half), [like((nodes, width), F32), like...]
  transfers between devices with their start and end apart: 20 -> 20, of which waited for: 12 -> 12; matrix products, arithmetic and copies ran while one was open for 0% -> 0% of each run, Pallas kernels for 4% -> 6%
where the time goes in v8:
time: 55.6 us; the launch traced here: 55.2 us
  starting transfers between devices  25.8 us (46%)
  waiting for transfers between devices  20.8 us (37%)
  Pallas kernels  6.35 us (11%)
  local copies, waits for them, and re-layouts  1.55 us (3%)
  between operations  0.76 us (1%)
    ppermute x20, starting transfers between devices, swap(): return lax.ppermute(array, axis, [(i, i ^ bit) for i in range(peers)])  25.8 us
    ppermute x20, waiting for transfers between devices, swap(): return lax.ppermute(array, axis, [(i, i ^ bit) for i in range(peers)])  20.8 us
    unnamed x14, local copies, waits for them, and re-layouts  1.55 us
    pallas_call x1, Pallas kernels, per_device(): call(functools.partial(feature_grads, reps, groups, lists, cap), [like((h...  1.26 us
  transfers between devices with their start and end apart: 20, of which 12 were waited for; matrix products, arithmetic and copies ran while one was open for 0% of the time, Pallas kernels for 6%

profile of v8, /device:TPU:0, one launch (start us, length us, event | category | flops | bytes accessed | tf_op | source)
XLA Modules:
  0.0 55.2 jit_solution(14807114135622119810)
XLA Ops:
  0.6 3.1 %collective-permute-start.4 = (bf16[6,128,128]{2,1,0:T(8,128)(2,1)}, bf16[6,128,128]{2,1,0:T(8,128)(2,1)S(1)}, u32[]{:S(2)}, u32[]{:S(2)}) collective-permute-start(bf16[6,128,128]{2,1,0:T(8,128)(2,1)} %bitcast.4), channel_id=1, source_target_pairs={{0,8},{8,0},{16,24},{24,16},{1,9},{9,1},{17,25},{25,17},{2,10},{10... | collective-permute-start | bytes 589832 | tf_op jit(solution)/shard_map/ppermute | solution.py:19
  3.7 2.6 %collective-permute-start.3 = (bf16[6,128,128]{2,1,0:T(8,128)(2,1)}, bf16[6,128,128]{2,1,0:T(8,128)(2,1)S(1)}, u32[]{:S(2)}, u32[]{:S(2)}) collective-permute-start(bf16[6,128,128]{2,1,0:T(8,128)(2,1)} %bitcast.5), channel_id=1, source_target_pairs={{0,16},{8,24},{16,0},{24,8},{1,17},{9,25},{17,1},{25,9},{2,18},{10... | collective-permute-start | bytes 589832 | tf_op jit(solution)/shard_map/ppermute | solution.py:19
  6.3 0.7 %copy-done.4 = s32[1,1,2,3]{3,2,1,0:T(2,128)S(1)} copy-done((s32[1,1,2,3]{3,2,1,0:T(2,128)S(1)}, s32[1,1,2,3]{3,2,1,0:T(2,128)}, u32[]{:S(2)}) %copy-start.4) | copy-done | bytes 48
  7.0 0.0 copy-done.3
  7.0 0.8 %copy-done.2 = bf16[128,256]{1,0:T(8,128)(2,1)S(1)} copy-done((bf16[128,256]{1,0:T(8,128)(2,1)S(1)}, bf16[128,256]{1,0:T(8,128)(2,1)}, u32[]{:S(2)}) %copy-start.2) | copy-done | bytes 65560
  7.8 0.7 %shard_map.94 = (bf16[80,128]{1,0:T(8,128)(2,1)S(1)}, bf16[80,128]{1,0:T(8,128)(2,1)S(1)}, bf16[80,128]{1,0:T(8,128)(2,1)S(1)}, bf16[80,128]{1,0:T(8,128)(2,1)S(1)}) custom-call(bf16[128,256]{1,0:T(8,128)(2,1)S(1)} %copy-done.2, s32[2,3]{1,0:T(2,128)S(1)} %bitcast.9, s32[2,3]{1,0:T(2,128)S(1)} %bitcast.10, s32[2]{0:T(128)S(1)} %bitcast.11), custom_call_target="tpu_custom_call" | custom-call | bytes 131072 | tf_op jit(solution)/shard_map/pallas_call | solution.py:220
  8.5 0.5 collective-permute-start
  9.0 0.0 collective-permute-start.1
  9.0 3.9 %collective-permute-start.2 = (bf16[80,128]{1,0:T(8,128)(2,1)S(1)}, bf16[80,128]{1,0:T(8,128)(2,1)S(1)}, u32[]{:S(2)}, u32[]{:S(2)}) collective-permute-start(bf16[80,128]{1,0:T(8,128)(2,1)S(1)} %get-tuple-element.29), channel_id=1, source_target_pairs={{0,24},{8,16},{16,8},{24,0},{1,25},{9,17},{17,9},{25,1},{2,26},{10... | collective-permute-start | bytes 61448 | tf_op jit(solution)/shard_map/ppermute | solution.py:19
  13.0 0.4 collective-permute-done.refs_1_
  13.4 3.6 %collective-permute-done.1.refs_2_ = bf16[80,128]{1,0:T(8,128)(2,1)S(1)} collective-permute-done((bf16[80,128]{1,0:T(8,128)(2,1)S(1)}, bf16[80,128]{1,0:T(8,128)(2,1)S(1)}, u32[]{:S(2)}, u32[]{:S(2)}) %collective-permute-start.1) | collective-permute-done | bytes 20512 | tf_op jit(solution)/shard_map/ppermute | solution.py:19
  17.0 0.0 collective-permute-done.2.refs_3_
  17.0 0.0 collective-permute-done.4.refs_5_.refs_1_
  17.0 0.0 copy-start.1
  17.1 0.8 %collective-permute-start.5 = (bf16[6,128,128]{2,1,0:T(8,128)(2,1)S(1)}, bf16[6,128,128]{2,1,0:T(8,128)(2,1)S(1)}, u32[]{:S(2)}, u32[]{:S(2)}) collective-permute-start(bf16[6,128,128]{2,1,0:T(8,128)(2,1)S(1)} %get-tuple-element.31), channel_id=1, source_target_pairs={{0,8},{8,0},{16,24},{24,16},{1,9},{9,1},{17,25},{25,17},{2,10},{10... | collective-permute-start | bytes 589832 | tf_op jit(solution)/shard_map/ppermute | solution.py:19
  17.9 2.3 %collective-permute-start.9 = (bf16[128,256]{1,0:T(8,128)(2,1)S(1)}, bf16[128,256]{1,0:T(8,128)(2,1)S(1)}, u32[]{:S(2)}, u32[]{:S(2)}) collective-permute-start(bf16[128,256]{1,0:T(8,128)(2,1)S(1)} %copy-done.1), channel_id=1, source_target_pairs={{0,16},{8,24},{16,0},{24,8},{1,17},{9,25},{17,1},{25,9},{2,18},{10... | collective-permute-start | bytes 196616 | tf_op jit(solution)/shard_map/ppermute | solution.py:19
  20.2 2.4 %collective-permute-start.8 = (bf16[4,64,128]{2,1,0:T(8,128)(2,1)S(1)}, bf16[4,64,128]{2,1,0:T(8,128)(2,1)S(1)}, u32[]{:S(2)}, u32[]{:S(2)}) collective-permute-start(bf16[4,64,128]{2,1,0:T(8,128)(2,1)S(1)} %get-tuple-element.32.refs_0_), channel_id=1, source_target_pairs={{0,6},{1,7},{2,4},{3,5},{4,2},{5,3},{6,0},{7,1},{8,14},{9,15},{10,... | collective-permute-start | bytes 196616 | tf_op jit(solution)/shard_map/ppermute | solution.py:19
  22.6 0.5 collective-permute-start.7
  23.1 0.5 collective-permute-start.6
  23.6 1.7 %collective-permute-done.8.refs_3_ = bf16[4,64,128]{2,1,0:T(8,128)(2,1)S(1)} collective-permute-done((bf16[4,64,128]{2,1,0:T(8,128)(2,1)S(1)}, bf16[4,64,128]{2,1,0:T(8,128)(2,1)S(1)}, u32[]{:S(2)}, u32[]{:S(2)}) %collective-permute-start.8) | collective-permute-done | bytes 65568 | tf_op jit(solution)/shard_map/ppermute | solution.py:19
  25.3 1.5 %collective-permute-done.7.refs_2_ = bf16[4,64,128]{2,1,0:T(8,128)(2,1)S(1)} collective-permute-done((bf16[4,64,128]{2,1,0:T(8,128)(2,1)S(1)}, bf16[4,64,128]{2,1,0:T(8,128)(2,1)S(1)}, u32[]{:S(2)}, u32[]{:S(2)}) %collective-permute-start.7) | collective-permute-done | bytes 65568 | tf_op jit(solution)/shard_map/ppermute | solution.py:19
  26.9 0.5 collective-permute-done.6.refs_1_
  27.4 0.1 collective-permute-start.10
  27.5 0.8 %collective-permute-start.14 = (bf16[2,128,256]{2,1,0:T(8,128)(2,1)S(1)}, bf16[2,128,256]{2,1,0:T(8,128)(2,1)S(1)}, u32[]{:S(2)}, u32[]{:S(2)}) collective-permute-start(bf16[2,128,256]{2,1,0:T(8,128)(2,1)S(1)} %get-tuple-element.34.refs_4_), channel_id=1, source_target_pairs={{0,8},{8,0},{16,24},{24,16},{1,9},{9,1},{17,25},{25,17},{2,10},{10... | collective-permute-start | bytes 393224 | tf_op jit(solution)/shard_map/ppermute | solution.py:19
  28.3 0.9 %shard_map.97.refs_5_ = f32[4,64,128]{2,1,0:T(8,128)S(1)} custom-call(s32[4,1,128]{2,1,0:T(1,128)S(1)} %get-tuple-element.30.index, bf16[6,128,128]{2,1,0:T(8,128)(2,1)S(1)} %bitcast.6, bf16[6,128,128]{2,1,0:T(8,128)(2,1)S(1)} %collective-permute-done.4.refs_5_.refs_1_, bf16[6,128,128]{2,1,0:T(8,128)(2,1)S(1)} %collective-permute-done.3.refs_4_.refs_2_, ...), custom_call_target="tpu_custom_call" | custom-call | flops 25165824 | bytes 655360 | tf_op jit(solution)/shard_map/pallas_call | solution.py:252
  29.3 0.0 copy-start.6
  29.3 0.9 %shard_map.98.refs_0_ = bf16[4,64,128]{2,1,0:T(8,128)(2,1)S(1)} custom-call(s32[4,1,128]{2,1,0:T(1,128)S(1)} %get-tuple-element.30.index, bf16[6,128,128]{2,1,0:T(8,128)(2,1)S(1)} %bitcast.7, bf16[6,128,128]{2,1,0:T(8,128)(2,1)S(1)} %collective-permute-done.4.refs_5_.refs_1_, bf16[6,128,128]{2,1,0:T(8,128)(2,1)S(1)} %collective-permute-done.3.refs_4_.refs_2_, ...), custom_call_target="tpu_custom_call" | custom-call | flops 25165824 | bytes 655360 | tf_op jit(solution)/shard_map/pallas_call | solution.py:260
  30.3 1.4 %collective-permute-start.13 = (bf16[4,64,128]{2,1,0:T(8,128)(2,1)S(1)}, bf16[4,64,128]{2,1,0:T(8,128)(2,1)S(1)}, u32[]{:S(2)}, u32[]{:S(2)}) collective-permute-start(bf16[4,64,128]{2,1,0:T(8,128)(2,1)S(1)} %shard_map.98.refs_0_), channel_id=1, source_target_pairs={{0,24},{8,16},{16,8},{24,0},{1,25},{9,17},{17,9},{25,1},{2,26},{10... | collective-permute-start | bytes 196616 | tf_op jit(solution)/shard_map/ppermute | solution.py:19
  31.7 1.4 %collective-permute-start.12 = (bf16[4,64,128]{2,1,0:T(8,128)(2,1)S(1)}, bf16[4,64,128]{2,1,0:T(8,128)(2,1)S(1)}, u32[]{:S(2)}, u32[]{:S(2)}) collective-permute-start(bf16[4,64,128]{2,1,0:T(8,128)(2,1)S(1)} %shard_map.98.refs_0_), channel_id=1, source_target_pairs={{0,16},{8,24},{16,0},{24,8},{1,17},{9,25},{17,1},{25,9},{2,18},{10... | collective-permute-start | bytes 196616 | tf_op jit(solution)/shard_map/ppermute | solution.py:19
  33.0 1.7 %collective-permute-start.11 = (bf16[4,64,128]{2,1,0:T(8,128)(2,1)S(1)}, bf16[4,64,128]{2,1,0:T(8,128)(2,1)S(1)}, u32[]{:S(2)}, u32[]{:S(2)}) collective-permute-start(bf16[4,64,128]{2,1,0:T(8,128)(2,1)S(1)} %shard_map.98.refs_0_), channel_id=1, source_target_pairs={{0,8},{8,0},{16,24},{24,16},{1,9},{9,1},{17,25},{25,17},{2,10},{10... | collective-permute-start | bytes 196616 | tf_op jit(solution)/shard_map/ppermute | solution.py:19
  34.7 2.4 %collective-permute-done.13.refs_3_ = bf16[4,64,128]{2,1,0:T(8,128)(2,1)S(1)} collective-permute-done((bf16[4,64,128]{2,1,0:T(8,128)(2,1)S(1)}, bf16[4,64,128]{2,1,0:T(8,128)(2,1)S(1)}, u32[]{:S(2)}, u32[]{:S(2)}) %collective-permute-start.13) | collective-permute-done | bytes 65568 | tf_op jit(solution)/shard_map/ppermute | solution.py:19
  37.1 2.4 %collective-permute-done.12.refs_2_ = bf16[4,64,128]{2,1,0:T(8,128)(2,1)S(1)} collective-permute-done((bf16[4,64,128]{2,1,0:T(8,128)(2,1)S(1)}, bf16[4,64,128]{2,1,0:T(8,128)(2,1)S(1)}, u32[]{:S(2)}, u32[]{:S(2)}) %collective-permute-start.12) | collective-permute-done | bytes 65568 | tf_op jit(solution)/shard_map/ppermute | solution.py:19
  39.5 0.9 %shard_map.99 = (bf16[128,256]{1,0:T(8,128)(2,1)S(1)}, bf16[4,128,256]{2,1,0:T(8,128)(2,1)S(1)}, bf16[2,128,256]{2,1,0:T(8,128)(2,1)S(1)}) custom-call(bf16[4,64,128]{2,1,0:T(8,128)(2,1)S(1)} %shard_map.98.refs_0_, bf16[4,64,128]{2,1,0:T(8,128)(2,1)S(1)} %collective-permute-done.11.refs_1_, bf16[4,64,128]{2,1,0:T(8,128)(2,1)S(1)} %collective-permute-done.12.refs_2_, ...), custom_call_target="tpu_custom_call" | custom-call | flops 201326592 | bytes 1310720 | tf_op jit(solution)/shard_map/pallas_call | solution.py:269
  40.4 1.3 %shard_map.100 = (f32[4,128,256]{2,1,0:T(8,128)S(1)}, bf16[5,128,256]{2,1,0:T(8,128)(2,1)S(1)}) custom-call(s32[4,1,128]{2,1,0:T(1,128)S(1)} %get-tuple-element.30.index, bf16[6,128,128]{2,1,0:T(8,128)(2,1)S(1)} %bitcast.8, bf16[6,128,128]{2,1,0:T(8,128)(2,1)S(1)} %collective-permute-done.4.refs_5_.refs_1_, ...), custom_call_target="tpu_custom_call" | custom-call | flops 50331648 | bytes 1310720 | tf_op jit(solution)/shard_map/pallas_call | solution.py:286
  41.7 0.1 collective-permute-start.15
  41.7 1.6 %collective-permute-done.15.arrived = bf16[5,128,256]{2,1,0:T(8,128)(2,1)S(1)} collective-permute-done((bf16[5,128,256]{2,1,0:T(8,128)(2,1)S(1)}, bf16[5,128,256]{2,1,0:T(8,128)(2,1)S(1)}, u32[]{:S(2)}, u32[]{:S(2)}) %collective-permute-start.15) | collective-permute-done | bytes 327712 | tf_op jit(solution)/shard_map/ppermute | solution.py:19
  43.4 0.1 shard_map.101
  43.4 0.8 %collective-permute-start.16 = (bf16[256,256]{1,0:T(8,128)(2,1)S(1)}, bf16[256,256]{1,0:T(8,128)(2,1)S(1)}, u32[]{:S(2)}, u32[]{:S(2)}) collective-permute-start(bf16[256,256]{1,0:T(8,128)(2,1)S(1)} %get-tuple-element.41), channel_id=1, source_target_pairs={{0,2},{1,3},{2,0},{3,1},{4,6},{5,7},{6,4},{7,5},{8,10},{9,11},{10,... | collective-permute-start | bytes 393224 | tf_op jit(solution)/shard_map/ppermute | solution.py:19
  44.2 1.5 %collective-permute-start.17 = (bf16[256,256]{1,0:T(8,128)(2,1)S(1)}, bf16[256,256]{1,0:T(8,128)(2,1)S(1)}, u32[]{:S(2)}, u32[]{:S(2)}) collective-permute-start(bf16[256,256]{1,0:T(8,128)(2,1)S(1)} %get-tuple-element.42), channel_id=1, source_target_pairs={{0,4},{1,5},{2,6},{3,7},{4,0},{5,1},{6,2},{7,3},{8,12},{9,13},{10,... | collective-permute-start | bytes 393224 | tf_op jit(solution)/shard_map/ppermute | solution.py:19
  45.7 1.2 %collective-permute-start.18 = (bf16[256,256]{1,0:T(8,128)(2,1)S(1)}, bf16[256,256]{1,0:T(8,128)(2,1)S(1)}, u32[]{:S(2)}, u32[]{:S(2)}) collective-permute-start(bf16[256,256]{1,0:T(8,128)(2,1)S(1)} %get-tuple-element.43), channel_id=1, source_target_pairs={{0,6},{1,7},{2,4},{3,5},{4,2},{5,3},{6,0},{7,1},{8,14},{9,15},{10,... | collective-permute-start | bytes 393224 | tf_op jit(solution)/shard_map/ppermute | solution.py:19
  47.0 2.9 %collective-permute-done.16.refs_0_ = bf16[256,256]{1,0:T(8,128)(2,1)S(1)} collective-permute-done((bf16[256,256]{1,0:T(8,128)(2,1)S(1)}, bf16[256,256]{1,0:T(8,128)(2,1)S(1)}, u32[]{:S(2)}, u32[]{:S(2)}) %collective-permute-start.16) | collective-permute-done | bytes 131104 | tf_op jit(solution)/shard_map/ppermute | solution.py:19
  49.8 1.5 %collective-permute-done.17.refs_1_ = bf16[256,256]{1,0:T(8,128)(2,1)S(1)} collective-permute-done((bf16[256,256]{1,0:T(8,128)(2,1)S(1)}, bf16[256,256]{1,0:T(8,128)(2,1)S(1)}, u32[]{:S(2)}, u32[]{:S(2)}) %collective-permute-start.17) | collective-permute-done | bytes 131104 | tf_op jit(solution)/shard_map/ppermute | solution.py:19
  51.4 1.6 %collective-permute-done.18.refs_2_ = bf16[256,256]{1,0:T(8,128)(2,1)S(1)} collective-permute-done((bf16[256,256]{1,0:T(8,128)(2,1)S(1)}, bf16[256,256]{1,0:T(8,128)(2,1)S(1)}, u32[]{:S(2)}, u32[]{:S(2)}) %collective-permute-start.18) | collective-permute-done | bytes 131104 | tf_op jit(solution)/shard_map/ppermute | solution.py:19
  53.0 0.1 shard_map.102
  53.1 0.1 collective-permute-start.19
  53.2 0.7 %shard_map.103 = (f32[128,256]{1,0:T(8,128)}, bf16[128,256]{1,0:T(8,128)(2,1)}) custom-call(f32[128,256]{1,0:T(8,128)S(1)} %get-tuple-element.44.grads, bf16[128,256]{1,0:T(8,128)(2,1)S(1)} %get-tuple-element.45.rows), custom_call_target="tpu_custom_call" | custom-call | bytes 393216 | tf_op jit(solution)/shard_map/pallas_call | solution.py:311
  53.9 0.6 %collective-permute-done.19.arrived = f32[128,256]{1,0:T(8,128)S(1)} collective-permute-done((f32[128,256]{1,0:T(8,128)S(1)}, f32[128,256]{1,0:T(8,128)S(1)}, u32[]{:S(2)}, u32[]{:S(2)}) %collective-permute-start.19) | collective-permute-done | bytes 131104 | tf_op jit(solution)/shard_map/ppermute | solution.py:19
  54.5 0.7 %shard_map.104 = f32[256,256]{1,0:T(8,128)} custom-call(f32[128,256]{1,0:T(8,128)S(1)} %get-tuple-element.47.mine, f32[128,256]{1,0:T(8,128)S(1)} %collective-permute-done.19.arrived), custom_call_target="tpu_custom_call" | custom-call | bytes 524288 | tf_op jit(solution)/shard_map/pallas_call | solution.py:317
  (17 shorter events, 0.1 us)
Async XLA Ops:
  0.6 16.4 %collective-permute-start.4 = (bf16[6,128,128]{2,1,0:T(8,128)(2,1)}, bf16[6,128,128]{2,1,0:T(8,128)(2,1)S(1)}, u32[]{:S(2)}, u32[]{:S(2)}) collective-permute-start(bf16[6,128,128]{2,1,0:T(8,128)(2,1)} %bitcast.4), channel_id=1, source_target_pairs={{0,8},{8,0},{16,24},{24,16},{1,9},{9,1},{17,25},{25,17},{2,10},{10... | collective-permute-start | bytes 589832 | tf_op jit(solution)/shard_map/ppermute | solution.py:19
  3.7 13.3 %collective-permute-start.3 = (bf16[6,128,128]{2,1,0:T(8,128)(2,1)}, bf16[6,128,128]{2,1,0:T(8,128)(2,1)S(1)}, u32[]{:S(2)}, u32[]{:S(2)}) collective-permute-start(bf16[6,128,128]{2,1,0:T(8,128)(2,1)} %bitcast.5), channel_id=1, source_target_pairs={{0,16},{8,24},{16,0},{24,8},{1,17},{9,25},{17,1},{25,9},{2,18},{10... | collective-permute-start | bytes 589832 | tf_op jit(solution)/shard_map/ppermute | solution.py:19
  6.3 0.7 %copy-start.4 = (s32[1,1,2,3]{3,2,1,0:T(2,128)S(1)}, s32[1,1,2,3]{3,2,1,0:T(2,128)}, u32[]{:S(2)}) copy-start(s32[1,1,2,3]{3,2,1,0:T(2,128)} %param.12) | copy-start | bytes 76
  6.3 0.7 %copy-start.3 = (s32[1,1,2,3]{3,2,1,0:T(2,128)S(1)}, s32[1,1,2,3]{3,2,1,0:T(2,128)}, u32[]{:S(2)}) copy-start(s32[1,1,2,3]{3,2,1,0:T(2,128)} %param.11) | copy-start | bytes 76
  6.3 0.7 %copy-start.5 = (s32[1,1,2]{2,1,0:T(1,128)S(1)}, s32[1,1,2]{2,1,0:T(1,128)}, u32[]{:S(2)}) copy-start(s32[1,1,2]{2,1,0:T(1,128)} %param.13) | copy-start | bytes 28
  7.0 0.8 %copy-start.2 = (bf16[128,256]{1,0:T(8,128)(2,1)S(1)}, bf16[128,256]{1,0:T(8,128)(2,1)}, u32[]{:S(2)}) copy-start(bf16[128,256]{1,0:T(8,128)(2,1)} %feats.1) | copy-start | bytes 196612
  8.5 4.8 %collective-permute-start = (bf16[80,128]{1,0:T(8,128)(2,1)S(1)}, bf16[80,128]{1,0:T(8,128)(2,1)S(1)}, u32[]{:S(2)}, u32[]{:S(2)}) collective-permute-start(bf16[80,128]{1,0:T(8,128)(2,1)S(1)} %get-tuple-element.27), channel_id=1, source_target_pairs={{0,8},{8,0},{16,24},{24,16},{1,9},{9,1},{17,25},{25,17},{2,10},{10... | collective-permute-start | bytes 61448 | tf_op jit(solution)/shard_map/ppermute | solution.py:19
  9.0 8.0 %collective-permute-start.1 = (bf16[80,128]{1,0:T(8,128)(2,1)S(1)}, bf16[80,128]{1,0:T(8,128)(2,1)S(1)}, u32[]{:S(2)}, u32[]{:S(2)}) collective-permute-start(bf16[80,128]{1,0:T(8,128)(2,1)S(1)} %get-tuple-element.28), channel_id=1, source_target_pairs={{0,16},{8,24},{16,0},{24,8},{1,17},{9,25},{17,1},{25,9},{2,18},{10... | collective-permute-start | bytes 61448 | tf_op jit(solution)/shard_map/ppermute | solution.py:19
  9.0 8.0 %collective-permute-start.2 = (bf16[80,128]{1,0:T(8,128)(2,1)S(1)}, bf16[80,128]{1,0:T(8,128)(2,1)S(1)}, u32[]{:S(2)}, u32[]{:S(2)}) collective-permute-start(bf16[80,128]{1,0:T(8,128)(2,1)S(1)} %get-tuple-element.29), channel_id=1, source_target_pairs={{0,24},{8,16},{16,8},{24,0},{1,25},{9,17},{17,9},{25,1},{2,26},{10... | collective-permute-start | bytes 61448 | tf_op jit(solution)/shard_map/ppermute | solution.py:19
  17.0 0.9 %copy-start.1 = (bf16[128,256]{1,0:T(8,128)(2,1)S(1)}, bf16[128,256]{1,0:T(8,128)(2,1)}, u32[]{:S(2)}) copy-start(bf16[128,256]{1,0:T(8,128)(2,1)} %refs_4_.1) | copy-start | bytes 196612
  17.1 10.3 %collective-permute-start.5 = (bf16[6,128,128]{2,1,0:T(8,128)(2,1)S(1)}, bf16[6,128,128]{2,1,0:T(8,128)(2,1)S(1)}, u32[]{:S(2)}, u32[]{:S(2)}) collective-permute-start(bf16[6,128,128]{2,1,0:T(8,128)(2,1)S(1)} %get-tuple-element.31), channel_id=1, source_target_pairs={{0,8},{8,0},{16,24},{24,16},{1,9},{9,1},{17,25},{25,17},{2,10},{10... | collective-permute-start | bytes 589832 | tf_op jit(solution)/shard_map/ppermute | solution.py:19
  17.9 5.7 %collective-permute-start.9 = (bf16[128,256]{1,0:T(8,128)(2,1)S(1)}, bf16[128,256]{1,0:T(8,128)(2,1)S(1)}, u32[]{:S(2)}, u32[]{:S(2)}) collective-permute-start(bf16[128,256]{1,0:T(8,128)(2,1)S(1)} %copy-done.1), channel_id=1, source_target_pairs={{0,16},{8,24},{16,0},{24,8},{1,17},{9,25},{17,1},{25,9},{2,18},{10... | collective-permute-start | bytes 196616 | tf_op jit(solution)/shard_map/ppermute | solution.py:19
  20.1 8.2 %copy-start = (bf16[1,1,2,3,128,128]{5,4,3,2,1,0:T(8,128)(2,1)S(1)}, bf16[1,1,2,3,128,128]{5,4,3,2,1,0:T(8,128)(2,1)}, u32[]{:S(2)}) copy-start(bf16[1,1,2,3,128,128]{5,4,3,2,1,0:T(8,128)(2,1)} %param.10) | copy-start | bytes 589828
  20.2 5.2 %collective-permute-start.8 = (bf16[4,64,128]{2,1,0:T(8,128)(2,1)S(1)}, bf16[4,64,128]{2,1,0:T(8,128)(2,1)S(1)}, u32[]{:S(2)}, u32[]{:S(2)}) collective-permute-start(bf16[4,64,128]{2,1,0:T(8,128)(2,1)S(1)} %get-tuple-element.32.refs_0_), channel_id=1, source_target_pairs={{0,6},{1,7},{2,4},{3,5},{4,2},{5,3},{6,0},{7,1},{8,14},{9,15},{10,... | collective-permute-start | bytes 196616 | tf_op jit(solution)/shard_map/ppermute | solution.py:19
  22.6 4.3 %collective-permute-start.7 = (bf16[4,64,128]{2,1,0:T(8,128)(2,1)S(1)}, bf16[4,64,128]{2,1,0:T(8,128)(2,1)S(1)}, u32[]{:S(2)}, u32[]{:S(2)}) collective-permute-start(bf16[4,64,128]{2,1,0:T(8,128)(2,1)S(1)} %get-tuple-element.32.refs_0_), channel_id=1, source_target_pairs={{0,4},{1,5},{2,6},{3,7},{4,0},{5,1},{6,2},{7,3},{8,12},{9,13},{10,... | collective-permute-start | bytes 196616 | tf_op jit(solution)/shard_map/ppermute | solution.py:19
  23.1 4.3 %collective-permute-start.6 = (bf16[4,64,128]{2,1,0:T(8,128)(2,1)S(1)}, bf16[4,64,128]{2,1,0:T(8,128)(2,1)S(1)}, u32[]{:S(2)}, u32[]{:S(2)}) collective-permute-start(bf16[4,64,128]{2,1,0:T(8,128)(2,1)S(1)} %get-tuple-element.32.refs_0_), channel_id=1, source_target_pairs={{0,2},{1,3},{2,0},{3,1},{4,6},{5,7},{6,4},{7,5},{8,10},{9,11},{10,... | collective-permute-start | bytes 196616 | tf_op jit(solution)/shard_map/ppermute | solution.py:19
  27.4 1.9 %collective-permute-start.10 = (bf16[4,4,64,128]{3,2,1,0:T(8,128)(2,1)S(1)}, bf16[4,4,64,128]{3,2,1,0:T(8,128)(2,1)S(1)}, u32[]{:S(2)}, u32[]{:S(2)}) collective-permute-start(bf16[4,4,64,128]{3,2,1,0:T(8,128)(2,1)S(1)} %get-tuple-element.33.refs_4_), channel_id=1, source_target_pairs={{0,1},{1,0},{2,3},{3,2},{4,5},{5,4},{6,7},{7,6},{8,9},{9,8},{10,11... | collective-permute-start | bytes 786440 | tf_op jit(solution)/shard_map/ppermute | solution.py:19
  27.5 7.2 %collective-permute-start.14 = (bf16[2,128,256]{2,1,0:T(8,128)(2,1)S(1)}, bf16[2,128,256]{2,1,0:T(8,128)(2,1)S(1)}, u32[]{:S(2)}, u32[]{:S(2)}) collective-permute-start(bf16[2,128,256]{2,1,0:T(8,128)(2,1)S(1)} %get-tuple-element.34.refs_4_), channel_id=1, source_target_pairs={{0,8},{8,0},{16,24},{24,16},{1,9},{9,1},{17,25},{25,17},{2,10},{10... | collective-permute-start | bytes 393224 | tf_op jit(solution)/shard_map/ppermute | solution.py:19
  29.3 10.2 %copy-start.6 = (bf16[256,256]{1,0:T(8,128)(2,1)S(1)}, bf16[256,256]{1,0:T(8,128)(2,1)}, u32[]{:S(2)}) copy-start(bf16[256,256]{1,0:T(8,128)(2,1)} %refs_6_.1) | copy-start | bytes 393220
  30.3 6.9 %collective-permute-start.13 = (bf16[4,64,128]{2,1,0:T(8,128)(2,1)S(1)}, bf16[4,64,128]{2,1,0:T(8,128)(2,1)S(1)}, u32[]{:S(2)}, u32[]{:S(2)}) collective-permute-start(bf16[4,64,128]{2,1,0:T(8,128)(2,1)S(1)} %shard_map.98.refs_0_), channel_id=1, source_target_pairs={{0,24},{8,16},{16,8},{24,0},{1,25},{9,17},{17,9},{25,1},{2,26},{10... | collective-permute-start | bytes 196616 | tf_op jit(solution)/shard_map/ppermute | solution.py:19
  31.7 7.8 %collective-permute-start.12 = (bf16[4,64,128]{2,1,0:T(8,128)(2,1)S(1)}, bf16[4,64,128]{2,1,0:T(8,128)(2,1)S(1)}, u32[]{:S(2)}, u32[]{:S(2)}) collective-permute-start(bf16[4,64,128]{2,1,0:T(8,128)(2,1)S(1)} %shard_map.98.refs_0_), channel_id=1, source_target_pairs={{0,16},{8,24},{16,0},{24,8},{1,17},{9,25},{17,1},{25,9},{2,18},{10... | collective-permute-start | bytes 196616 | tf_op jit(solution)/shard_map/ppermute | solution.py:19
  33.0 6.5 %collective-permute-start.11 = (bf16[4,64,128]{2,1,0:T(8,128)(2,1)S(1)}, bf16[4,64,128]{2,1,0:T(8,128)(2,1)S(1)}, u32[]{:S(2)}, u32[]{:S(2)}) collective-permute-start(bf16[4,64,128]{2,1,0:T(8,128)(2,1)S(1)} %shard_map.98.refs_0_), channel_id=1, source_target_pairs={{0,8},{8,0},{16,24},{24,16},{1,9},{9,1},{17,25},{25,17},{2,10},{10... | collective-permute-start | bytes 196616 | tf_op jit(solution)/shard_map/ppermute | solution.py:19
  41.7 1.7 %collective-permute-start.15 = (bf16[5,128,256]{2,1,0:T(8,128)(2,1)S(1)}, bf16[5,128,256]{2,1,0:T(8,128)(2,1)S(1)}, u32[]{:S(2)}, u32[]{:S(2)}) collective-permute-start(bf16[5,128,256]{2,1,0:T(8,128)(2,1)S(1)} %get-tuple-element.38), channel_id=1, source_target_pairs={{0,1},{1,0},{2,3},{3,2},{4,5},{5,4},{6,7},{7,6},{8,9},{9,8},{10,11... | collective-permute-start | bytes 983048 | tf_op jit(solution)/shard_map/ppermute | solution.py:19
  43.4 6.4 %collective-permute-start.16 = (bf16[256,256]{1,0:T(8,128)(2,1)S(1)}, bf16[256,256]{1,0:T(8,128)(2,1)S(1)}, u32[]{:S(2)}, u32[]{:S(2)}) collective-permute-start(bf16[256,256]{1,0:T(8,128)(2,1)S(1)} %get-tuple-element.41), channel_id=1, source_target_pairs={{0,2},{1,3},{2,0},{3,1},{4,6},{5,7},{6,4},{7,5},{8,10},{9,11},{10,... | collective-permute-start | bytes 393224 | tf_op jit(solution)/shard_map/ppermute | solution.py:19
  44.2 7.1 %collective-permute-start.17 = (bf16[256,256]{1,0:T(8,128)(2,1)S(1)}, bf16[256,256]{1,0:T(8,128)(2,1)S(1)}, u32[]{:S(2)}, u32[]{:S(2)}) collective-permute-start(bf16[256,256]{1,0:T(8,128)(2,1)S(1)} %get-tuple-element.42), channel_id=1, source_target_pairs={{0,4},{1,5},{2,6},{3,7},{4,0},{5,1},{6,2},{7,3},{8,12},{9,13},{10,... | collective-permute-start | bytes 393224 | tf_op jit(solution)/shard_map/ppermute | solution.py:19
  45.7 7.2 %collective-permute-start.18 = (bf16[256,256]{1,0:T(8,128)(2,1)S(1)}, bf16[256,256]{1,0:T(8,128)(2,1)S(1)}, u32[]{:S(2)}, u32[]{:S(2)}) collective-permute-start(bf16[256,256]{1,0:T(8,128)(2,1)S(1)} %get-tuple-element.43), channel_id=1, source_target_pairs={{0,6},{1,7},{2,4},{3,5},{4,2},{5,3},{6,0},{7,1},{8,14},{9,15},{10,... | collective-permute-start | bytes 393224 | tf_op jit(solution)/shard_map/ppermute | solution.py:19
  53.1 1.4 %collective-permute-start.19 = (f32[128,256]{1,0:T(8,128)S(1)}, f32[128,256]{1,0:T(8,128)S(1)}, u32[]{:S(2)}, u32[]{:S(2)}) collective-permute-start(f32[128,256]{1,0:T(8,128)S(1)} %get-tuple-element.47.mine), channel_id=1, source_target_pairs={{0,1},{1,0},{2,3},{3,2},{4,5},{5,4},{6,7},{7,6},{8,9},{9,8},{10,11... | collective-permute-start | bytes 393224 | tf_op jit(solution)/shard_map/ppermute | solution.py:19

commit v9 on v8

--- a/solution.py
+++ b/solution.py
@@ -70,14 +70,17 @@
 
 
 def order_chunks(reps, part, *refs):
-    copies = reps // 2 - 1
-    chunks, sources, unread = refs[:reps], refs[reps : reps + copies], refs[reps + copies]
-    mine, index = refs[reps + copies + 1 : reps + copies + 3]
-    for source, target in zip(sources, refs[reps + copies + 3 :]):
-        target[...] = source[...]
+    chunks, blocks, mine, index, later = refs[:reps], refs[reps], *refs[-3:]
     for x in range(reps):
         mine[other("rep", x)] = chunks[x][:part]
         index[x] = chunks[x][part:].astype(F32).astype(jnp.int32)[:1]
+    later[...] = blocks[later.shape[0] :]
+
+
+def stack(first, second, out):
+    count = first.shape[0]
+    out[:count] = first[...]
+    out[count:] = second[...]
 
 
 def join(half, *refs):
@@ -100,12 +103,16 @@
     return lax.div(lax.bitwise_xor(mine, lax.rem(mine + groups - offset, groups)), 2)
 
 
-def aggregate(reps, groups, lists, cap, parity, index, *refs):
-    blocks, held, start, out = refs[:reps], refs[reps], refs[reps + 1 : -2], refs[-2]
-    total = refs[-1]
-    total[...] = start[0][...] if start else jnp.zeros_like(total)
-    for x in range(reps):
-        for j in range(parity, lists, 2):
+def aggregate(reps, groups, lists, cap, first, index, *refs):
+    known = reps - 1 if first else reps
+    blocks, near, far = refs[:known], refs[known], refs[-4]
+    start, out, total = refs[-3], refs[-2], refs[-1]
+    total[...] = jnp.zeros_like(total) if first else start[...]
+    for x in range(known):
+        for j in range(lists):
+            if first != (j % 2 == 0 and x < reps - 1):
+                continue
+            held = far if j % 2 else near
             place = relative(groups, lists, x, j)
             for c in range(cap):
                 row, col, live = slot_of(index, lists, cap, x, j, c)
@@ -138,27 +145,27 @@
     terms[...] = gw.astype(BF16).reshape(terms.shape)
 
 
-def feature_grads(reps, groups, lists, cap, index, *refs):
-    blocks = refs[:reps]
-    dagg, terms, keep, send, total = refs[reps:]
+def feature_grads(reps, groups, lists, cap, parity, index, *refs):
+    blocks, dagg, rest = refs[:reps], refs[reps], refs[reps + 1 :]
     me = lax.axis_index("rep")
     half = groups // 2
-    keep[...] = jnp.zeros_like(keep)
+    total = rest[-1]
     total[...] = jnp.zeros_like(total)
     for x in range(reps):
-        for j in range(lists):
-            target = total if j % 2 else keep
+        for j in range(parity, lists, 2):
             place = relative(groups, lists, x, j)
             for c in range(cap):
                 row, col, live = slot_of(index, lists, cap, x, j, c)
 
                 @pl.when(jnp.logical_and(live, col == me))
                 def _():
-                    target[place] += dot(blocks[x][j * cap + c], dagg[row], 0, 0)
-
-    send[:half] = total[...].astype(BF16)
-    core = lax.rem(lax.axis_index("blk"), 2)
-    send[half:] = terms[1 - core].reshape(-1, *send.shape[1:])
+                    total[place] += dot(blocks[x][j * cap + c], dagg[row], 0, 0)
+
+    if parity:
+        terms, send = rest[:2]
+        send[:half] = total[...].astype(BF16)
+        core = lax.rem(lax.axis_index("blk"), 2)
+        send[half:] = terms[1 - core].reshape(-1, *send.shape[1:])
 
 
 def add_core(half, keep, terms, arrived, own, own_terms, *sends):
@@ -214,9 +221,10 @@
     def direct(arrays):
         return [arrays[0]] + [swap(arrays[x], "rep", x) for x in range(1, reps)]
 
+    unread = pl.BlockSpec(memory_space=pl.ANY)
     adjacency = block_vals.reshape(slots, block, block)
-    evens = spread(adjacency, 2)
     odds = [swap(adjacency, "rep", 1)]
+    early = spread(adjacency[: slots // 2], 2)[1:]
     chunks = call(
         functools.partial(split_features, reps, lists, cap),
         [like((part + PAD, nodes), BF16)] * reps,
@@ -224,47 +232,55 @@
         [pltpu.VMEM((reps, part, nodes), BF16)],
         moved=4 * nodes * width,
     )(feats, block_rows[0, 0], block_cols[0, 0], step_counts[0, 0])
-    mine, index, *relayed = call(
+    mine, index, later = call(
         functools.partial(order_chunks, reps, part),
-        [like((reps, part, nodes), BF16), like((reps, 1, nodes), jnp.int32)]
-        + [like((slots, block, block), BF16)] * (reps // 2 - 1),
-        [VMEM] * (reps + reps // 2 - 1) + [pl.BlockSpec(memory_space=pl.ANY)],
+        [
+            like((reps, part, nodes), BF16),
+            like((reps, 1, nodes), jnp.int32),
+            like((slots - slots // 2, block, block), BF16),
+        ],
+        [VMEM] * (reps + 1) + [unread] * (reps // 2),
         moved=4 * nodes * width,
-    )(*direct(chunks), *evens[1:], odds[0])
-    odds += [swap(array, "rep", 1) for array in relayed]
-    blocks = [array for pair in zip(evens, odds) for array in pair]
+    )(*direct(chunks), adjacency, *odds, *early)
+    evens = [
+        call(stack, like(adjacency.shape, BF16), [VMEM] * 2, moved=4 * adjacency.size)(one, two)
+        for one, two in zip(early, spread(later, 2)[1:])
+    ]
+    odds += [swap(array, "rep", 1) for array in evens]
+    blocks = [array for pair in zip([adjacency] + evens, odds) for array in pair]
 
     near, cotangents = call(
         functools.partial(join, half),
         [like((half, reps, part, nodes), BF16), like((reps // 2, nodes, width), BF16)],
-        [VMEM] * (half + reps // 2) + [pl.BlockSpec(memory_space=pl.ANY)] * (reps // 2 - 1),
+        [VMEM] * (half + reps // 2) + [unread] * (reps // 2 - 1),
         moved=4 * half * nodes * width,
     )(
         mine,
         *[swap(mine, "blk", 2 * k) for k in range(1, half)],
         *spread(cotangent, 2),
-        *odds[1:],
+        *evens,
     )
     far = swap(near, "blk", 1)
     slot_flops = 2 * groups * cap * part * block * block
     slot_bytes = 2 * (groups * cap * block * block + groups * nodes * width)
 
     agg = call(
-        functools.partial(aggregate, reps, groups, lists, cap, 0),
+        functools.partial(aggregate, reps, groups, lists, cap, True),
         like((reps, part, nodes), F32),
-        [SMEM] + [VMEM] * (reps + 1),
+        [SMEM] + [VMEM] * reps,
         [pltpu.VMEM((reps, part, nodes), F32)],
         flops=slot_flops // 2,
         moved=slot_bytes // 2,
-    )(index, *blocks, near)
+    )(index, *blocks[:-1], near)
     agg = call(
-        functools.partial(aggregate, reps, groups, lists, cap, 1),
+        functools.partial(aggregate, reps, groups, lists, cap, False),
         like((reps, part, nodes), BF16),
-        [SMEM] + [VMEM] * (reps + 2),
+        [SMEM] + [VMEM] * (reps + 3),
         [pltpu.VMEM((reps, part, nodes), F32)],
         flops=slot_flops // 2,
         moved=slot_bytes // 2,
-    )(index, *blocks, far, agg)
+    )(index, *blocks, near, far, agg)
+    aggs = direct([agg] * reps)
 
     out_rows, dagg, terms = call(
         functools.partial(dense_layer, reps),
@@ -281,19 +297,23 @@
         ],
         flops=6 * reps * nodes * width * width,
         moved=2 * reps * 5 * nodes * width,
-    )(*direct([agg] * reps), cotangents, swap(cotangents, "rep", 1), weight)
-
-    keep, send = call(
-        functools.partial(feature_grads, reps, groups, lists, cap),
-        [
-            like((half, nodes, width), F32),
-            like((half + width // 2 // nodes, nodes, width), BF16),
-        ],
+    )(*aggs, cotangents, swap(cotangents, "rep", 1), weight)
+
+    send = call(
+        functools.partial(feature_grads, reps, groups, lists, cap, 1),
+        like((half + width // 2 // nodes, nodes, width), BF16),
         [SMEM] + [VMEM] * (reps + 2),
         [pltpu.VMEM((half, nodes, width), F32)],
-        flops=slot_flops,
-        moved=slot_bytes,
+        flops=slot_flops // 2,
+        moved=slot_bytes // 2,
     )(index, *blocks, dagg, terms)
+    keep = call(
+        functools.partial(feature_grads, reps, groups, lists, cap, 0),
+        like((half, nodes, width), F32),
+        [SMEM] + [VMEM] * (reps + 1),
+        flops=slot_flops // 2,
+        moved=slot_bytes // 2,
+    )(index, *blocks, dagg)
     own, own_terms, *sends = call(
         functools.partial(add_core, half),
         [like((nodes, width), F32), like((width // 2, width), BF16)]

time: 55.6 us -> 60.8 us (1.094); the launches traced: 55.2 us -> 61.2 us
  waiting for transfers between devices: 20.8 us -> 23 us
  Pallas kernels: 6.35 us -> 7.82 us
  starting transfers between devices: 25.8 us -> 27.1 us
  local copies, waits for them, and re-layouts: 1.55 us -> 2.48 us
    ppermute x20 -> x21, waiting for transfers between devices: 20.8 us -> 23 us  [swap(): return lax.ppermute(array, axis, [(i, i ^ bit) for i in range(peers)])]
    pallas_call x3 -> x5, Pallas kernels: 3.16 us -> 4.64 us  [the longest x1 1.44 us: per_device(): call(functools.partial(feature_grads, reps, groups, lists, cap, 0), like(...]
    ppermute x20 -> x21, starting transfers between devices: 25.8 us -> 27.1 us  [swap(): return lax.ppermute(array, axis, [(i, i ^ bit) for i in range(peers)])]
    slice x0 -> x1, local copies, waits for them, and re-layouts: none -> 0.93 us  [per_device(): early = spread(adjacency[:slots // 2], 2)[1:]]
  transfers between devices with their start and end apart: 20 -> 21, of which waited for: 12 -> 15; matrix products, arithmetic and copies ran while one was open for 0% -> 2% of each run, Pallas kernels for 6% -> 8%
where the time goes in v9:
time: 60.8 us; the launch traced here: 61.2 us
  starting transfers between devices  27.1 us (45%)
  waiting for transfers between devices  23 us (38%)
  Pallas kernels  7.82 us (13%)
  local copies, waits for them, and re-layouts  2.48 us (4%)
  between operations  0.78 us (1%)
    ppermute x21, starting transfers between devices, swap(): return lax.ppermute(array, axis, [(i, i ^ bit) for i in range(peers)])  27.1 us
    ppermute x21, waiting for transfers between devices, swap(): return lax.ppermute(array, axis, [(i, i ^ bit) for i in range(peers)])  23 us
    unnamed x14, local copies, waits for them, and re-layouts  1.55 us
    pallas_call x1, Pallas kernels, per_device(): call(functools.partial(feature_grads, reps, groups, lists, cap, 0), like(...  1.44 us
    pallas_call x1, Pallas kernels, per_device(): call(functools.partial(feature_grads, reps, groups, lists, cap, 1), like(...  1.27 us
  transfers between devices with their start and end apart: 21, of which 15 were waited for; matrix products, arithmetic and copies ran while one was open for 2% of the time, Pallas kernels for 8%

profile of v9, /device:TPU:0, one launch (start us, length us, event | category | flops | bytes accessed | tf_op | source)
XLA Modules:
  0.0 61.2 jit_solution(7144815198972886339)
XLA Ops:
  0.6 3.1 %collective-permute-start.3 = (bf16[6,128,128]{2,1,0:T(8,128)(2,1)}, bf16[6,128,128]{2,1,0:T(8,128)(2,1)S(1)}, u32[]{:S(2)}, u32[]{:S(2)}) collective-permute-start(bf16[6,128,128]{2,1,0:T(8,128)(2,1)} %bitcast.6), channel_id=1, source_target_pairs={{0,8},{8,0},{16,24},{24,16},{1,9},{9,1},{17,25},{25,17},{2,10},{10... | collective-permute-start | bytes 589832 | tf_op jit(solution)/shard_map/ppermute | solution.py:19
  3.7 0.9 %slice_bitcast_fusion = bf16[3,128,128]{2,1,0:T(8,128)(2,1)S(1)} fusion(bf16[1,1,2,3,128,128]{5,4,3,2,1,0:T(8,128)(2,1)} %param.10), kind=kLoop, calls=%fused_computation | loop fusion | bytes 196608 | tf_op jit(solution)/shard_map/slice | solution.py:227
  4.7 2.6 %collective-permute-start.4 = (bf16[3,128,128]{2,1,0:T(8,128)(2,1)S(1)}, bf16[3,128,128]{2,1,0:T(8,128)(2,1)S(1)}, u32[]{:S(2)}, u32[]{:S(2)}) collective-permute-start(bf16[3,128,128]{2,1,0:T(8,128)(2,1)S(1)} %slice_bitcast_fusion), channel_id=1, source_target_pairs={{0,16},{8,24},{16,0},{24,8},{1,17},{9,25},{17,1},{25,9},{2,18},{10... | collective-permute-start | bytes 294920 | tf_op jit(solution)/shard_map/ppermute | solution.py:19
  7.3 0.7 %copy-done.4 = s32[1,1,2,3]{3,2,1,0:T(2,128)S(1)} copy-done((s32[1,1,2,3]{3,2,1,0:T(2,128)S(1)}, s32[1,1,2,3]{3,2,1,0:T(2,128)}, u32[]{:S(2)}) %copy-start.4) | copy-done | bytes 48
  7.9 0.0 copy-done.3
  8.0 0.8 %copy-done.2 = bf16[128,256]{1,0:T(8,128)(2,1)S(1)} copy-done((bf16[128,256]{1,0:T(8,128)(2,1)S(1)}, bf16[128,256]{1,0:T(8,128)(2,1)}, u32[]{:S(2)}) %copy-start.2) | copy-done | bytes 65560
  8.8 0.7 %shard_map.94 = (bf16[80,128]{1,0:T(8,128)(2,1)S(1)}, bf16[80,128]{1,0:T(8,128)(2,1)S(1)}, bf16[80,128]{1,0:T(8,128)(2,1)S(1)}, bf16[80,128]{1,0:T(8,128)(2,1)S(1)}) custom-call(bf16[128,256]{1,0:T(8,128)(2,1)S(1)} %copy-done.2, s32[2,3]{1,0:T(2,128)S(1)} %bitcast.12, s32[2,3]{1,0:T(2,128)S(1)} %bitcast.13, s32[2]{0:T(128)S(1)} %bitcast.14), custom_call_target="tpu_custom_call" | custom-call | bytes 131072 | tf_op jit(solution)/shard_map/pallas_call | solution.py:228
  9.5 0.5 collective-permute-start
  10.0 3.9 %collective-permute-start.2 = (bf16[80,128]{1,0:T(8,128)(2,1)S(1)}, bf16[80,128]{1,0:T(8,128)(2,1)S(1)}, u32[]{:S(2)}, u32[]{:S(2)}) collective-permute-start(bf16[80,128]{1,0:T(8,128)(2,1)S(1)} %get-tuple-element.27), channel_id=1, source_target_pairs={{0,24},{8,16},{16,8},{24,0},{1,25},{9,17},{17,9},{25,1},{2,26},{10... | collective-permute-start | bytes 61448 | tf_op jit(solution)/shard_map/ppermute | solution.py:19
  13.9 0.7 %collective-permute-done.1.refs_2_ = bf16[80,128]{1,0:T(8,128)(2,1)S(1)} collective-permute-done((bf16[80,128]{1,0:T(8,128)(2,1)S(1)}, bf16[80,128]{1,0:T(8,128)(2,1)S(1)}, u32[]{:S(2)}, u32[]{:S(2)}) %collective-permute-start.1) | collective-permute-done | bytes 20512 | tf_op jit(solution)/shard_map/ppermute | solution.py:19
  14.7 1.2 %collective-permute-done.2.refs_3_ = bf16[80,128]{1,0:T(8,128)(2,1)S(1)} collective-permute-done((bf16[80,128]{1,0:T(8,128)(2,1)S(1)}, bf16[80,128]{1,0:T(8,128)(2,1)S(1)}, u32[]{:S(2)}, u32[]{:S(2)}) %collective-permute-start.2) | collective-permute-done | bytes 20512 | tf_op jit(solution)/shard_map/ppermute | solution.py:19
  15.9 0.9 %collective-permute-start.5 = (bf16[3,128,128]{2,1,0:T(8,128)(2,1)S(1)}, bf16[3,128,128]{2,1,0:T(8,128)(2,1)S(1)}, u32[]{:S(2)}, u32[]{:S(2)}) collective-permute-start(bf16[3,128,128]{2,1,0:T(8,128)(2,1)S(1)} %get-tuple-element.29), channel_id=1, source_target_pairs={{0,16},{8,24},{16,0},{24,8},{1,17},{9,25},{17,1},{25,9},{2,18},{10... | collective-permute-start | bytes 294920 | tf_op jit(solution)/shard_map/ppermute | solution.py:19
  16.8 2.1 %collective-permute-start.10 = (bf16[128,256]{1,0:T(8,128)(2,1)S(1)}, bf16[128,256]{1,0:T(8,128)(2,1)S(1)}, u32[]{:S(2)}, u32[]{:S(2)}) collective-permute-start(bf16[128,256]{1,0:T(8,128)(2,1)S(1)} %copy-done.1), channel_id=1, source_target_pairs={{0,16},{8,24},{16,0},{24,8},{1,17},{9,25},{17,1},{25,9},{2,18},{10... | collective-permute-start | bytes 196616 | tf_op jit(solution)/shard_map/ppermute | solution.py:19
  18.9 2.5 %collective-permute-start.9 = (bf16[4,64,128]{2,1,0:T(8,128)(2,1)S(1)}, bf16[4,64,128]{2,1,0:T(8,128)(2,1)S(1)}, u32[]{:S(2)}, u32[]{:S(2)}) collective-permute-start(bf16[4,64,128]{2,1,0:T(8,128)(2,1)S(1)} %get-tuple-element.30.refs_0_), channel_id=1, source_target_pairs={{0,6},{1,7},{2,4},{3,5},{4,2},{5,3},{6,0},{7,1},{8,14},{9,15},{10,... | collective-permute-start | bytes 196616 | tf_op jit(solution)/shard_map/ppermute | solution.py:19
  21.4 0.5 collective-permute-start.8
  21.9 0.5 collective-permute-start.7
  22.4 0.8 %collective-permute-done.5.second = bf16[3,128,128]{2,1,0:T(8,128)(2,1)S(1)} collective-permute-done((bf16[3,128,128]{2,1,0:T(8,128)(2,1)S(1)}, bf16[3,128,128]{2,1,0:T(8,128)(2,1)S(1)}, u32[]{:S(2)}, u32[]{:S(2)}) %collective-permute-start.5) | collective-permute-done | bytes 98336 | tf_op jit(solution)/shard_map/ppermute | solution.py:19
  23.2 0.7 %collective-permute-done.10.refs_5_ = bf16[128,256]{1,0:T(8,128)(2,1)S(1)} collective-permute-done((bf16[128,256]{1,0:T(8,128)(2,1)S(1)}, bf16[128,256]{1,0:T(8,128)(2,1)S(1)}, u32[]{:S(2)}, u32[]{:S(2)}) %collective-permute-start.10) | collective-permute-done | bytes 65568 | tf_op jit(solution)/shard_map/ppermute | solution.py:19
  23.9 0.2 collective-permute-done.9.refs_3_
  24.1 1.6 %collective-permute-done.8.refs_2_ = bf16[4,64,128]{2,1,0:T(8,128)(2,1)S(1)} collective-permute-done((bf16[4,64,128]{2,1,0:T(8,128)(2,1)S(1)}, bf16[4,64,128]{2,1,0:T(8,128)(2,1)S(1)}, u32[]{:S(2)}, u32[]{:S(2)}) %collective-permute-start.8) | collective-permute-done | bytes 65568 | tf_op jit(solution)/shard_map/ppermute | solution.py:19
  25.7 0.5 collective-permute-done.7.refs_1_
  26.2 0.1 collective-permute-start.11
  26.3 2.2 %collective-permute-start.6 = (bf16[6,128,128]{2,1,0:T(8,128)(2,1)S(1)}, bf16[6,128,128]{2,1,0:T(8,128)(2,1)S(1)}, u32[]{:S(2)}, u32[]{:S(2)}) collective-permute-start(bf16[6,128,128]{2,1,0:T(8,128)(2,1)S(1)} %shard_map.96.refs_6_.refs_2_), channel_id=1, source_target_pairs={{0,8},{8,0},{16,24},{24,16},{1,9},{9,1},{17,25},{25,17},{2,10},{10... | collective-permute-start | bytes 589832 | tf_op jit(solution)/shard_map/ppermute | solution.py:19
  28.5 0.1 collective-permute-start.15
  28.6 0.9 %shard_map.98.refs_6_ = f32[4,64,128]{2,1,0:T(8,128)S(1)} custom-call(s32[4,1,128]{2,1,0:T(1,128)S(1)} %get-tuple-element.28.index, bf16[6,128,128]{2,1,0:T(8,128)(2,1)S(1)} %bitcast.8, bf16[6,128,128]{2,1,0:T(8,128)(2,1)S(1)} %collective-permute-done.3.refs_5_.refs_1_, bf16[6,128,128]{2,1,0:T(8,128)(2,1)S(1)} %shard_map.96.refs_6_.refs_2_, ...), custom_call_target="tpu_custom_call" | custom-call | flops 25165824 | bytes 655360 | tf_op jit(solution)/shard_map/pallas_call | solution.py:267
  29.5 4.7 %collective-permute-done.6.refs_3_ = bf16[6,128,128]{2,1,0:T(8,128)(2,1)S(1)} collective-permute-done((bf16[6,128,128]{2,1,0:T(8,128)(2,1)S(1)}, bf16[6,128,128]{2,1,0:T(8,128)(2,1)S(1)}, u32[]{:S(2)}, u32[]{:S(2)}) %collective-permute-start.6) | collective-permute-done | bytes 196640 | tf_op jit(solution)/shard_map/ppermute | solution.py:19
  34.2 1.0 %shard_map.99.refs_0_ = bf16[4,64,128]{2,1,0:T(8,128)(2,1)S(1)} custom-call(s32[4,1,128]{2,1,0:T(1,128)S(1)} %get-tuple-element.28.index, bf16[6,128,128]{2,1,0:T(8,128)(2,1)S(1)} %bitcast.9, bf16[6,128,128]{2,1,0:T(8,128)(2,1)S(1)} %collective-permute-done.3.refs_5_.refs_1_, bf16[6,128,128]{2,1,0:T(8,128)(2,1)S(1)} %shard_map.96.refs_6_.refs_2_, ...), custom_call_target="tpu_custom_call" | custom-call | flops 25165824 | bytes 655360 | tf_op jit(solution)/shard_map/pallas_call | solution.py:275
  35.3 3.6 %collective-permute-start.14 = (bf16[4,64,128]{2,1,0:T(8,128)(2,1)S(1)}, bf16[4,64,128]{2,1,0:T(8,128)(2,1)S(1)}, u32[]{:S(2)}, u32[]{:S(2)}) collective-permute-start(bf16[4,64,128]{2,1,0:T(8,128)(2,1)S(1)} %shard_map.99.refs_0_), channel_id=1, source_target_pairs={{0,24},{8,16},{16,8},{24,0},{1,25},{9,17},{17,9},{25,1},{2,26},{10... | collective-permute-start | bytes 196616 | tf_op jit(solution)/shard_map/ppermute | solution.py:19
  38.9 0.8 %collective-permute-start.12 = (bf16[4,64,128]{2,1,0:T(8,128)(2,1)S(1)}, bf16[4,64,128]{2,1,0:T(8,128)(2,1)S(1)}, u32[]{:S(2)}, u32[]{:S(2)}) collective-permute-start(bf16[4,64,128]{2,1,0:T(8,128)(2,1)S(1)} %shard_map.99.refs_0_), channel_id=1, source_target_pairs={{0,8},{8,0},{16,24},{24,16},{1,9},{9,1},{17,25},{25,17},{2,10},{10... | collective-permute-start | bytes 196616 | tf_op jit(solution)/shard_map/ppermute | solution.py:19
  39.7 2.1 %collective-permute-done.14.refs_3_ = bf16[4,64,128]{2,1,0:T(8,128)(2,1)S(1)} collective-permute-done((bf16[4,64,128]{2,1,0:T(8,128)(2,1)S(1)}, bf16[4,64,128]{2,1,0:T(8,128)(2,1)S(1)}, u32[]{:S(2)}, u32[]{:S(2)}) %collective-permute-start.14) | collective-permute-done | bytes 65568 | tf_op jit(solution)/shard_map/ppermute | solution.py:19
  41.8 2.7 %collective-permute-done.13.refs_2_ = bf16[4,64,128]{2,1,0:T(8,128)(2,1)S(1)} collective-permute-done((bf16[4,64,128]{2,1,0:T(8,128)(2,1)S(1)}, bf16[4,64,128]{2,1,0:T(8,128)(2,1)S(1)}, u32[]{:S(2)}, u32[]{:S(2)}) %collective-permute-start.13) | collective-permute-done | bytes 65568 | tf_op jit(solution)/shard_map/ppermute | solution.py:19
  44.5 0.9 %shard_map.100 = (bf16[128,256]{1,0:T(8,128)(2,1)S(1)}, bf16[4,128,256]{2,1,0:T(8,128)(2,1)S(1)}, bf16[2,128,256]{2,1,0:T(8,128)(2,1)S(1)}) custom-call(bf16[4,64,128]{2,1,0:T(8,128)(2,1)S(1)} %shard_map.99.refs_0_, bf16[4,64,128]{2,1,0:T(8,128)(2,1)S(1)} %collective-permute-done.12.refs_1_, bf16[4,64,128]{2,1,0:T(8,128)(2,1)S(1)} %collective-permute-done.13.refs_2_, ...), custom_call_target="tpu_custom_call" | custom-call | flops 201326592 | bytes 1310720 | tf_op jit(solution)/shard_map/pallas_call | solution.py:285
  45.4 1.3 %shard_map.102 = bf16[5,128,256]{2,1,0:T(8,128)(2,1)S(1)} custom-call(s32[4,1,128]{2,1,0:T(1,128)S(1)} %get-tuple-element.28.index, bf16[6,128,128]{2,1,0:T(8,128)(2,1)S(1)} %bitcast.10, bf16[6,128,128]{2,1,0:T(8,128)(2,1)S(1)} %collective-permute-done.3.refs_5_.refs_1_, bf16[6,128,128]{2,1,0:T(8,128)(2,1)S(1)} %shard_map.96.refs_6_.refs_2_, ...), custom_call_target="tpu_custom_call" | custom-call | flops 25165824 | bytes 655360 | tf_op jit(solution)/shard_map/pallas_call | solution.py:302
  46.7 0.1 collective-permute-start.16
  46.7 1.4 %shard_map.101.keep = f32[4,128,256]{2,1,0:T(8,128)S(1)} custom-call(s32[4,1,128]{2,1,0:T(1,128)S(1)} %get-tuple-element.28.index, bf16[6,128,128]{2,1,0:T(8,128)(2,1)S(1)} %bitcast.11, bf16[6,128,128]{2,1,0:T(8,128)(2,1)S(1)} %collective-permute-done.3.refs_5_.refs_1_, bf16[6,128,128]{2,1,0:T(8,128)(2,1)S(1)} %shard_map.96.refs_6_.refs_2_, ...), custom_call_target="tpu_custom_call" | custom-call | flops 25165824 | bytes 655360 | tf_op jit(solution)/shard_map/pallas_call | solution.py:310
  48.2 0.2 collective-permute-done.16.arrived
  48.4 0.1 shard_map.103
  48.4 0.3 collective-permute-start.17
  48.8 1.8 %collective-permute-start.18 = (bf16[256,256]{1,0:T(8,128)(2,1)S(1)}, bf16[256,256]{1,0:T(8,128)(2,1)S(1)}, u32[]{:S(2)}, u32[]{:S(2)}) collective-permute-start(bf16[256,256]{1,0:T(8,128)(2,1)S(1)} %get-tuple-element.38), channel_id=1, source_target_pairs={{0,4},{1,5},{2,6},{3,7},{4,0},{5,1},{6,2},{7,3},{8,12},{9,13},{10,... | collective-permute-start | bytes 393224 | tf_op jit(solution)/shard_map/ppermute | solution.py:19
  50.5 1.5 %collective-permute-start.19 = (bf16[256,256]{1,0:T(8,128)(2,1)S(1)}, bf16[256,256]{1,0:T(8,128)(2,1)S(1)}, u32[]{:S(2)}, u32[]{:S(2)}) collective-permute-start(bf16[256,256]{1,0:T(8,128)(2,1)S(1)} %get-tuple-element.39), channel_id=1, source_target_pairs={{0,6},{1,7},{2,4},{3,5},{4,2},{5,3},{6,0},{7,1},{8,14},{9,15},{10,... | collective-permute-start | bytes 393224 | tf_op jit(solution)/shard_map/ppermute | solution.py:19
  52.0 2.8 %collective-permute-done.17.refs_0_ = bf16[256,256]{1,0:T(8,128)(2,1)S(1)} collective-permute-done((bf16[256,256]{1,0:T(8,128)(2,1)S(1)}, bf16[256,256]{1,0:T(8,128)(2,1)S(1)}, u32[]{:S(2)}, u32[]{:S(2)}) %collective-permute-start.17) | collective-permute-done | bytes 131104 | tf_op jit(solution)/shard_map/ppermute | solution.py:19
  54.8 2.4 %collective-permute-done.18.refs_1_ = bf16[256,256]{1,0:T(8,128)(2,1)S(1)} collective-permute-done((bf16[256,256]{1,0:T(8,128)(2,1)S(1)}, bf16[256,256]{1,0:T(8,128)(2,1)S(1)}, u32[]{:S(2)}, u32[]{:S(2)}) %collective-permute-start.18) | collective-permute-done | bytes 131104 | tf_op jit(solution)/shard_map/ppermute | solution.py:19
  57.1 1.8 %collective-permute-done.19.refs_2_ = bf16[256,256]{1,0:T(8,128)(2,1)S(1)} collective-permute-done((bf16[256,256]{1,0:T(8,128)(2,1)S(1)}, bf16[256,256]{1,0:T(8,128)(2,1)S(1)}, u32[]{:S(2)}, u32[]{:S(2)}) %collective-permute-start.19) | collective-permute-done | bytes 131104 | tf_op jit(solution)/shard_map/ppermute | solution.py:19
  59.0 0.1 shard_map.104
  59.1 0.1 collective-permute-start.20
  59.1 0.7 %shard_map.105 = (f32[128,256]{1,0:T(8,128)}, bf16[128,256]{1,0:T(8,128)(2,1)}) custom-call(f32[128,256]{1,0:T(8,128)S(1)} %get-tuple-element.40.grads, bf16[128,256]{1,0:T(8,128)(2,1)S(1)} %get-tuple-element.41.rows), custom_call_target="tpu_custom_call" | custom-call | bytes 393216 | tf_op jit(solution)/shard_map/pallas_call | solution.py:331
  59.8 0.6 %collective-permute-done.20.arrived = f32[128,256]{1,0:T(8,128)S(1)} collective-permute-done((f32[128,256]{1,0:T(8,128)S(1)}, f32[128,256]{1,0:T(8,128)S(1)}, u32[]{:S(2)}, u32[]{:S(2)}) %collective-permute-start.20) | collective-permute-done | bytes 131104 | tf_op jit(solution)/shard_map/ppermute | solution.py:19
  60.5 0.7 %shard_map.106 = f32[256,256]{1,0:T(8,128)} custom-call(f32[128,256]{1,0:T(8,128)S(1)} %get-tuple-element.43.mine, f32[128,256]{1,0:T(8,128)S(1)} %collective-permute-done.20.arrived), custom_call_target="tpu_custom_call" | custom-call | bytes 524288 | tf_op jit(solution)/shard_map/pallas_call | solution.py:337
  (22 shorter events, 0.1 us)
Async XLA Ops:
  0.6 15.3 %copy-start = (bf16[1,1,2,3,128,128]{5,4,3,2,1,0:T(8,128)(2,1)S(1)}, bf16[1,1,2,3,128,128]{5,4,3,2,1,0:T(8,128)(2,1)}, u32[]{:S(2)}) copy-start(bf16[1,1,2,3,128,128]{5,4,3,2,1,0:T(8,128)(2,1)} %param.10) | copy-start | bytes 589828
  0.6 15.3 %collective-permute-start.3 = (bf16[6,128,128]{2,1,0:T(8,128)(2,1)}, bf16[6,128,128]{2,1,0:T(8,128)(2,1)S(1)}, u32[]{:S(2)}, u32[]{:S(2)}) collective-permute-start(bf16[6,128,128]{2,1,0:T(8,128)(2,1)} %bitcast.6), channel_id=1, source_target_pairs={{0,8},{8,0},{16,24},{24,16},{1,9},{9,1},{17,25},{25,17},{2,10},{10... | collective-permute-start | bytes 589832 | tf_op jit(solution)/shard_map/ppermute | solution.py:19
  4.7 11.2 %collective-permute-start.4 = (bf16[3,128,128]{2,1,0:T(8,128)(2,1)S(1)}, bf16[3,128,128]{2,1,0:T(8,128)(2,1)S(1)}, u32[]{:S(2)}, u32[]{:S(2)}) collective-permute-start(bf16[3,128,128]{2,1,0:T(8,128)(2,1)S(1)} %slice_bitcast_fusion), channel_id=1, source_target_pairs={{0,16},{8,24},{16,0},{24,8},{1,17},{9,25},{17,1},{25,9},{2,18},{10... | collective-permute-start | bytes 294920 | tf_op jit(solution)/shard_map/ppermute | solution.py:19
  7.3 0.7 %copy-start.4 = (s32[1,1,2,3]{3,2,1,0:T(2,128)S(1)}, s32[1,1,2,3]{3,2,1,0:T(2,128)}, u32[]{:S(2)}) copy-start(s32[1,1,2,3]{3,2,1,0:T(2,128)} %param.12) | copy-start | bytes 76
  7.3 0.7 %copy-start.3 = (s32[1,1,2,3]{3,2,1,0:T(2,128)S(1)}, s32[1,1,2,3]{3,2,1,0:T(2,128)}, u32[]{:S(2)}) copy-start(s32[1,1,2,3]{3,2,1,0:T(2,128)} %param.11) | copy-start | bytes 76
  7.3 0.7 %copy-start.5 = (s32[1,1,2]{2,1,0:T(1,128)S(1)}, s32[1,1,2]{2,1,0:T(1,128)}, u32[]{:S(2)}) copy-start(s32[1,1,2]{2,1,0:T(1,128)} %param.13) | copy-start | bytes 28
  7.9 0.8 %copy-start.2 = (bf16[128,256]{1,0:T(8,128)(2,1)S(1)}, bf16[128,256]{1,0:T(8,128)(2,1)}, u32[]{:S(2)}) copy-start(bf16[128,256]{1,0:T(8,128)(2,1)} %feats.1) | copy-start | bytes 196612
  9.5 4.5 %collective-permute-start = (bf16[80,128]{1,0:T(8,128)(2,1)S(1)}, bf16[80,128]{1,0:T(8,128)(2,1)S(1)}, u32[]{:S(2)}, u32[]{:S(2)}) collective-permute-start(bf16[80,128]{1,0:T(8,128)(2,1)S(1)} %get-tuple-element.25), channel_id=1, source_target_pairs={{0,8},{8,0},{16,24},{24,16},{1,9},{9,1},{17,25},{25,17},{2,10},{10... | collective-permute-start | bytes 61448 | tf_op jit(solution)/shard_map/ppermute | solution.py:19
  10.0 4.7 %collective-permute-start.1 = (bf16[80,128]{1,0:T(8,128)(2,1)S(1)}, bf16[80,128]{1,0:T(8,128)(2,1)S(1)}, u32[]{:S(2)}, u32[]{:S(2)}) collective-permute-start(bf16[80,128]{1,0:T(8,128)(2,1)S(1)} %get-tuple-element.26), channel_id=1, source_target_pairs={{0,16},{8,24},{16,0},{24,8},{1,17},{9,25},{17,1},{25,9},{2,18},{10... | collective-permute-start | bytes 61448 | tf_op jit(solution)/shard_map/ppermute | solution.py:19
  10.0 5.9 %collective-permute-start.2 = (bf16[80,128]{1,0:T(8,128)(2,1)S(1)}, bf16[80,128]{1,0:T(8,128)(2,1)S(1)}, u32[]{:S(2)}, u32[]{:S(2)}) collective-permute-start(bf16[80,128]{1,0:T(8,128)(2,1)S(1)} %get-tuple-element.27), channel_id=1, source_target_pairs={{0,24},{8,16},{16,8},{24,0},{1,25},{9,17},{17,9},{25,1},{2,26},{10... | collective-permute-start | bytes 61448 | tf_op jit(solution)/shard_map/ppermute | solution.py:19
  15.9 0.9 %copy-start.1 = (bf16[128,256]{1,0:T(8,128)(2,1)S(1)}, bf16[128,256]{1,0:T(8,128)(2,1)}, u32[]{:S(2)}) copy-start(bf16[128,256]{1,0:T(8,128)(2,1)} %refs_4_.1) | copy-start | bytes 196612
  15.9 7.3 %collective-permute-start.5 = (bf16[3,128,128]{2,1,0:T(8,128)(2,1)S(1)}, bf16[3,128,128]{2,1,0:T(8,128)(2,1)S(1)}, u32[]{:S(2)}, u32[]{:S(2)}) collective-permute-start(bf16[3,128,128]{2,1,0:T(8,128)(2,1)S(1)} %get-tuple-element.29), channel_id=1, source_target_pairs={{0,16},{8,24},{16,0},{24,8},{1,17},{9,25},{17,1},{25,9},{2,18},{10... | collective-permute-start | bytes 294920 | tf_op jit(solution)/shard_map/ppermute | solution.py:19
  16.8 7.1 %collective-permute-start.10 = (bf16[128,256]{1,0:T(8,128)(2,1)S(1)}, bf16[128,256]{1,0:T(8,128)(2,1)S(1)}, u32[]{:S(2)}, u32[]{:S(2)}) collective-permute-start(bf16[128,256]{1,0:T(8,128)(2,1)S(1)} %copy-done.1), channel_id=1, source_target_pairs={{0,16},{8,24},{16,0},{24,8},{1,17},{9,25},{17,1},{25,9},{2,18},{10... | collective-permute-start | bytes 196616 | tf_op jit(solution)/shard_map/ppermute | solution.py:19
  18.9 5.2 %collective-permute-start.9 = (bf16[4,64,128]{2,1,0:T(8,128)(2,1)S(1)}, bf16[4,64,128]{2,1,0:T(8,128)(2,1)S(1)}, u32[]{:S(2)}, u32[]{:S(2)}) collective-permute-start(bf16[4,64,128]{2,1,0:T(8,128)(2,1)S(1)} %get-tuple-element.30.refs_0_), channel_id=1, source_target_pairs={{0,6},{1,7},{2,4},{3,5},{4,2},{5,3},{6,0},{7,1},{8,14},{9,15},{10,... | collective-permute-start | bytes 196616 | tf_op jit(solution)/shard_map/ppermute | solution.py:19
  21.4 4.3 %collective-permute-start.8 = (bf16[4,64,128]{2,1,0:T(8,128)(2,1)S(1)}, bf16[4,64,128]{2,1,0:T(8,128)(2,1)S(1)}, u32[]{:S(2)}, u32[]{:S(2)}) collective-permute-start(bf16[4,64,128]{2,1,0:T(8,128)(2,1)S(1)} %get-tuple-element.30.refs_0_), channel_id=1, source_target_pairs={{0,4},{1,5},{2,6},{3,7},{4,0},{5,1},{6,2},{7,3},{8,12},{9,13},{10,... | collective-permute-start | bytes 196616 | tf_op jit(solution)/shard_map/ppermute | solution.py:19
  21.9 4.3 %collective-permute-start.7 = (bf16[4,64,128]{2,1,0:T(8,128)(2,1)S(1)}, bf16[4,64,128]{2,1,0:T(8,128)(2,1)S(1)}, u32[]{:S(2)}, u32[]{:S(2)}) collective-permute-start(bf16[4,64,128]{2,1,0:T(8,128)(2,1)S(1)} %get-tuple-element.30.refs_0_), channel_id=1, source_target_pairs={{0,2},{1,3},{2,0},{3,1},{4,6},{5,7},{6,4},{7,5},{8,10},{9,11},{10,... | collective-permute-start | bytes 196616 | tf_op jit(solution)/shard_map/ppermute | solution.py:19
  26.2 8.0 %collective-permute-start.11 = (bf16[4,4,64,128]{3,2,1,0:T(8,128)(2,1)S(1)}, bf16[4,4,64,128]{3,2,1,0:T(8,128)(2,1)S(1)}, u32[]{:S(2)}, u32[]{:S(2)}) collective-permute-start(bf16[4,4,64,128]{3,2,1,0:T(8,128)(2,1)S(1)} %get-tuple-element.31.refs_3_.refs_4_), channel_id=1, source_target_pairs={{0,1},{1,0},{2,3},{3,2},{4,5},{5,4},{6,7},{7,6},{8,9},{9,8},{10,11... | collective-permute-start | bytes 786440 | tf_op jit(solution)/shard_map/ppermute | solution.py:19
  26.3 7.9 %collective-permute-start.6 = (bf16[6,128,128]{2,1,0:T(8,128)(2,1)S(1)}, bf16[6,128,128]{2,1,0:T(8,128)(2,1)S(1)}, u32[]{:S(2)}, u32[]{:S(2)}) collective-permute-start(bf16[6,128,128]{2,1,0:T(8,128)(2,1)S(1)} %shard_map.96.refs_6_.refs_2_), channel_id=1, source_target_pairs={{0,8},{8,0},{16,24},{24,16},{1,9},{9,1},{17,25},{25,17},{2,10},{10... | collective-permute-start | bytes 589832 | tf_op jit(solution)/shard_map/ppermute | solution.py:19
  28.5 11.2 %collective-permute-start.15 = (bf16[2,128,256]{2,1,0:T(8,128)(2,1)S(1)}, bf16[2,128,256]{2,1,0:T(8,128)(2,1)S(1)}, u32[]{:S(2)}, u32[]{:S(2)}) collective-permute-start(bf16[2,128,256]{2,1,0:T(8,128)(2,1)S(1)} %get-tuple-element.32.refs_4_), channel_id=1, source_target_pairs={{0,8},{8,0},{16,24},{24,16},{1,9},{9,1},{17,25},{25,17},{2,10},{10... | collective-permute-start | bytes 393224 | tf_op jit(solution)/shard_map/ppermute | solution.py:19
  29.5 15.0 %copy-start.6 = (bf16[256,256]{1,0:T(8,128)(2,1)S(1)}, bf16[256,256]{1,0:T(8,128)(2,1)}, u32[]{:S(2)}) copy-start(bf16[256,256]{1,0:T(8,128)(2,1)} %refs_6_.1) | copy-start | bytes 393220
  35.3 6.6 %collective-permute-start.14 = (bf16[4,64,128]{2,1,0:T(8,128)(2,1)S(1)}, bf16[4,64,128]{2,1,0:T(8,128)(2,1)S(1)}, u32[]{:S(2)}, u32[]{:S(2)}) collective-permute-start(bf16[4,64,128]{2,1,0:T(8,128)(2,1)S(1)} %shard_map.99.refs_0_), channel_id=1, source_target_pairs={{0,24},{8,16},{16,8},{24,0},{1,25},{9,17},{17,9},{25,1},{2,26},{10... | collective-permute-start | bytes 196616 | tf_op jit(solution)/shard_map/ppermute | solution.py:19
  38.9 5.6 %collective-permute-start.13 = (bf16[4,64,128]{2,1,0:T(8,128)(2,1)S(1)}, bf16[4,64,128]{2,1,0:T(8,128)(2,1)S(1)}, u32[]{:S(2)}, u32[]{:S(2)}) collective-permute-start(bf16[4,64,128]{2,1,0:T(8,128)(2,1)S(1)} %shard_map.99.refs_0_), channel_id=1, source_target_pairs={{0,16},{8,24},{16,0},{24,8},{1,17},{9,25},{17,1},{25,9},{2,18},{10... | collective-permute-start | bytes 196616 | tf_op jit(solution)/shard_map/ppermute | solution.py:19
  38.9 5.6 %collective-permute-start.12 = (bf16[4,64,128]{2,1,0:T(8,128)(2,1)S(1)}, bf16[4,64,128]{2,1,0:T(8,128)(2,1)S(1)}, u32[]{:S(2)}, u32[]{:S(2)}) collective-permute-start(bf16[4,64,128]{2,1,0:T(8,128)(2,1)S(1)} %shard_map.99.refs_0_), channel_id=1, source_target_pairs={{0,8},{8,0},{16,24},{24,16},{1,9},{9,1},{17,25},{25,17},{2,10},{10... | collective-permute-start | bytes 196616 | tf_op jit(solution)/shard_map/ppermute | solution.py:19
  46.7 1.7 %collective-permute-start.16 = (bf16[5,128,256]{2,1,0:T(8,128)(2,1)S(1)}, bf16[5,128,256]{2,1,0:T(8,128)(2,1)S(1)}, u32[]{:S(2)}, u32[]{:S(2)}) collective-permute-start(bf16[5,128,256]{2,1,0:T(8,128)(2,1)S(1)} %shard_map.102), channel_id=1, source_target_pairs={{0,1},{1,0},{2,3},{3,2},{4,5},{5,4},{6,7},{7,6},{8,9},{9,8},{10,11... | collective-permute-start | bytes 983048 | tf_op jit(solution)/shard_map/ppermute | solution.py:19
  48.4 6.3 %collective-permute-start.17 = (bf16[256,256]{1,0:T(8,128)(2,1)S(1)}, bf16[256,256]{1,0:T(8,128)(2,1)S(1)}, u32[]{:S(2)}, u32[]{:S(2)}) collective-permute-start(bf16[256,256]{1,0:T(8,128)(2,1)S(1)} %get-tuple-element.37), channel_id=1, source_target_pairs={{0,2},{1,3},{2,0},{3,1},{4,6},{5,7},{6,4},{7,5},{8,10},{9,11},{10,... | collective-permute-start | bytes 393224 | tf_op jit(solution)/shard_map/ppermute | solution.py:19
  48.8 8.4 %collective-permute-start.18 = (bf16[256,256]{1,0:T(8,128)(2,1)S(1)}, bf16[256,256]{1,0:T(8,128)(2,1)S(1)}, u32[]{:S(2)}, u32[]{:S(2)}) collective-permute-start(bf16[256,256]{1,0:T(8,128)(2,1)S(1)} %get-tuple-element.38), channel_id=1, source_target_pairs={{0,4},{1,5},{2,6},{3,7},{4,0},{5,1},{6,2},{7,3},{8,12},{9,13},{10,... | collective-permute-start | bytes 393224 | tf_op jit(solution)/shard_map/ppermute | solution.py:19
  50.5 8.4 %collective-permute-start.19 = (bf16[256,256]{1,0:T(8,128)(2,1)S(1)}, bf16[256,256]{1,0:T(8,128)(2,1)S(1)}, u32[]{:S(2)}, u32[]{:S(2)}) collective-permute-start(bf16[256,256]{1,0:T(8,128)(2,1)S(1)} %get-tuple-element.39), channel_id=1, source_target_pairs={{0,6},{1,7},{2,4},{3,5},{4,2},{5,3},{6,0},{7,1},{8,14},{9,15},{10,... | collective-permute-start | bytes 393224 | tf_op jit(solution)/shard_map/ppermute | solution.py:19
  59.1 1.4 %collective-permute-start.20 = (f32[128,256]{1,0:T(8,128)S(1)}, f32[128,256]{1,0:T(8,128)S(1)}, u32[]{:S(2)}, u32[]{:S(2)}) collective-permute-start(f32[128,256]{1,0:T(8,128)S(1)} %get-tuple-element.43.mine), channel_id=1, source_target_pairs={{0,1},{1,0},{2,3},{3,2},{4,5},{5,4},{6,7},{7,6},{8,9},{9,8},{10,11... | collective-permute-start | bytes 393224 | tf_op jit(solution)/shard_map/ppermute | solution.py:19

commit v10 on v8

--- a/solution.py
+++ b/solution.py
@@ -138,27 +138,27 @@
     terms[...] = gw.astype(BF16).reshape(terms.shape)
 
 
-def feature_grads(reps, groups, lists, cap, index, *refs):
-    blocks = refs[:reps]
-    dagg, terms, keep, send, total = refs[reps:]
+def feature_grads(reps, groups, lists, cap, parity, index, *refs):
+    blocks, dagg, rest = refs[:reps], refs[reps], refs[reps + 1 :]
     me = lax.axis_index("rep")
     half = groups // 2
-    keep[...] = jnp.zeros_like(keep)
+    total = rest[-1]
     total[...] = jnp.zeros_like(total)
     for x in range(reps):
-        for j in range(lists):
-            target = total if j % 2 else keep
+        for j in range(parity, lists, 2):
             place = relative(groups, lists, x, j)
             for c in range(cap):
                 row, col, live = slot_of(index, lists, cap, x, j, c)
 
                 @pl.when(jnp.logical_and(live, col == me))
                 def _():
-                    target[place] += dot(blocks[x][j * cap + c], dagg[row], 0, 0)
-
-    send[:half] = total[...].astype(BF16)
-    core = lax.rem(lax.axis_index("blk"), 2)
-    send[half:] = terms[1 - core].reshape(-1, *send.shape[1:])
+                    total[place] += dot(blocks[x][j * cap + c], dagg[row], 0, 0)
+
+    if parity:
+        terms, send = rest[:2]
+        send[:half] = total[...].astype(BF16)
+        core = lax.rem(lax.axis_index("blk"), 2)
+        send[half:] = terms[1 - core].reshape(-1, *send.shape[1:])
 
 
 def add_core(half, keep, terms, arrived, own, own_terms, *sends):
@@ -169,8 +169,8 @@
     gw = (mine + arrived[half:].reshape(mine.shape).astype(F32)).astype(BF16)
     own_terms[...] = gw
     for k in range(1, half):
-        sends[k - 1][:nodes] = (keep[k] + arrived[k].astype(F32)).astype(BF16)
-        sends[k - 1][nodes:] = gw
+        sends[half - 1 - k][:nodes] = (keep[k] + arrived[k].astype(F32)).astype(BF16)
+        sends[half - 1 - k][nodes:] = gw
 
 
 def add_chips(half, own, own_terms, *refs):
@@ -180,8 +180,8 @@
     total = own[...]
     held[chip] = own_terms[...].astype(F32)
     for k in range(1, half):
-        total += parts[k - 1][:nodes].astype(F32)
-        held[lax.bitwise_xor(chip, k)] = parts[k - 1][nodes:].astype(F32)
+        total += parts[half - 1 - k][:nodes].astype(F32)
+        held[lax.bitwise_xor(chip, k)] = parts[half - 1 - k][nodes:].astype(F32)
     grads[...] = total
     gw = held[0]
     for k in range(1, half):
@@ -283,17 +283,21 @@
         moved=2 * reps * 5 * nodes * width,
     )(*direct([agg] * reps), cotangents, swap(cotangents, "rep", 1), weight)
 
-    keep, send = call(
-        functools.partial(feature_grads, reps, groups, lists, cap),
-        [
-            like((half, nodes, width), F32),
-            like((half + width // 2 // nodes, nodes, width), BF16),
-        ],
+    send = call(
+        functools.partial(feature_grads, reps, groups, lists, cap, 1),
+        like((half + width // 2 // nodes, nodes, width), BF16),
         [SMEM] + [VMEM] * (reps + 2),
         [pltpu.VMEM((half, nodes, width), F32)],
-        flops=slot_flops,
-        moved=slot_bytes,
+        flops=slot_flops // 2,
+        moved=slot_bytes // 2,
     )(index, *blocks, dagg, terms)
+    keep = call(
+        functools.partial(feature_grads, reps, groups, lists, cap, 0),
+        like((half, nodes, width), F32),
+        [SMEM] + [VMEM] * (reps + 1),
+        flops=slot_flops // 2,
+        moved=slot_bytes // 2,
+    )(index, *blocks, dagg)
     own, own_terms, *sends = call(
         functools.partial(add_core, half),
         [like((nodes, width), F32), like((width // 2, width), BF16)]
@@ -307,7 +311,7 @@
         [VMEM] * (half + 1),
         [pltpu.VMEM((half, width // 2, width), F32)],
         moved=8 * half * nodes * width,
-    )(own, own_terms, *[swap(sends[k - 1], "blk", 2 * k) for k in range(1, half)])
+    )(own, own_terms, *[swap(sends[half - 1 - k], "blk", 2 * k) for k in range(half - 1, 0, -1)])
     grad_feats, out_rows = call(
         store,
         [like((nodes, width), F32), like((nodes, width), BF16)],

time: 55.6 us -> 55.3 us (level)
  waiting for transfers between devices: 20.8 us -> 19.9 us
  Pallas kernels: 6.35 us -> 7.09 us
    ppermute x20, waiting for transfers between devices: 20.8 us -> 19.9 us  [swap(): return lax.ppermute(array, axis, [(i, i ^ bit) for i in range(peers)])]
    pallas_call x1 -> x2, Pallas kernels: 1.26 us -> 2 us  [the longest x1 1.11 us: per_device(): call(functools.partial(feature_grads, reps, groups, lists, cap, 1), like(...]
  transfers between devices with their start and end apart: 20 -> 20, of which waited for: 12 -> 12; matrix products, arithmetic and copies ran while one was open for 0% -> 0% of each run, Pallas kernels for 6% -> 8%
where the time goes in v10:
time: 55.3 us; the launch traced here: 55.1 us
  starting transfers between devices  25.8 us (47%)
  waiting for transfers between devices  19.9 us (36%)
  Pallas kernels  7.09 us (13%)
  local copies, waits for them, and re-layouts  1.55 us (3%)
  between operations  0.77 us (1%)
    ppermute x20, starting transfers between devices, swap(): return lax.ppermute(array, axis, [(i, i ^ bit) for i in range(peers)])  25.8 us
    ppermute x20, waiting for transfers between devices, swap(): return lax.ppermute(array, axis, [(i, i ^ bit) for i in range(peers)])  19.9 us
    unnamed x14, local copies, waits for them, and re-layouts  1.55 us
    pallas_call x1, Pallas kernels, per_device(): call(functools.partial(feature_grads, reps, groups, lists, cap, 1), like(...  1.11 us
  transfers between devices with their start and end apart: 20, of which 12 were waited for; matrix products, arithmetic and copies ran while one was open for 0% of the time, Pallas kernels for 8%

profile of v10, /device:TPU:0, one launch (start us, length us, event | category | flops | bytes accessed | tf_op | source)
XLA Modules:
  0.0 55.1 jit_solution(9827115658372180001)
XLA Ops:
  0.6 3.1 %collective-permute-start.4 = (bf16[6,128,128]{2,1,0:T(8,128)(2,1)}, bf16[6,128,128]{2,1,0:T(8,128)(2,1)S(1)}, u32[]{:S(2)}, u32[]{:S(2)}) collective-permute-start(bf16[6,128,128]{2,1,0:T(8,128)(2,1)} %bitcast.4), channel_id=1, source_target_pairs={{0,8},{8,0},{16,24},{24,16},{1,9},{9,1},{17,25},{25,17},{2,10},{10... | collective-permute-start | bytes 589832 | tf_op jit(solution)/shard_map/ppermute | solution.py:19
  3.7 2.6 %collective-permute-start.3 = (bf16[6,128,128]{2,1,0:T(8,128)(2,1)}, bf16[6,128,128]{2,1,0:T(8,128)(2,1)S(1)}, u32[]{:S(2)}, u32[]{:S(2)}) collective-permute-start(bf16[6,128,128]{2,1,0:T(8,128)(2,1)} %bitcast.5), channel_id=1, source_target_pairs={{0,16},{8,24},{16,0},{24,8},{1,17},{9,25},{17,1},{25,9},{2,18},{10... | collective-permute-start | bytes 589832 | tf_op jit(solution)/shard_map/ppermute | solution.py:19
  6.3 0.7 %copy-done.4 = s32[1,1,2,3]{3,2,1,0:T(2,128)S(1)} copy-done((s32[1,1,2,3]{3,2,1,0:T(2,128)S(1)}, s32[1,1,2,3]{3,2,1,0:T(2,128)}, u32[]{:S(2)}) %copy-start.4) | copy-done | bytes 48
  7.0 0.0 copy-done.3
  7.0 0.8 %copy-done.2 = bf16[128,256]{1,0:T(8,128)(2,1)S(1)} copy-done((bf16[128,256]{1,0:T(8,128)(2,1)S(1)}, bf16[128,256]{1,0:T(8,128)(2,1)}, u32[]{:S(2)}) %copy-start.2) | copy-done | bytes 65560
  7.8 0.7 %shard_map.94 = (bf16[80,128]{1,0:T(8,128)(2,1)S(1)}, bf16[80,128]{1,0:T(8,128)(2,1)S(1)}, bf16[80,128]{1,0:T(8,128)(2,1)S(1)}, bf16[80,128]{1,0:T(8,128)(2,1)S(1)}) custom-call(bf16[128,256]{1,0:T(8,128)(2,1)S(1)} %copy-done.2, s32[2,3]{1,0:T(2,128)S(1)} %bitcast.10, s32[2,3]{1,0:T(2,128)S(1)} %bitcast.11, s32[2]{0:T(128)S(1)} %bitcast.12), custom_call_target="tpu_custom_call" | custom-call | bytes 131072 | tf_op jit(solution)/shard_map/pallas_call | solution.py:220
  8.5 0.5 collective-permute-start
  9.0 0.0 collective-permute-start.1
  9.0 3.9 %collective-permute-start.2 = (bf16[80,128]{1,0:T(8,128)(2,1)S(1)}, bf16[80,128]{1,0:T(8,128)(2,1)S(1)}, u32[]{:S(2)}, u32[]{:S(2)}) collective-permute-start(bf16[80,128]{1,0:T(8,128)(2,1)S(1)} %get-tuple-element.27), channel_id=1, source_target_pairs={{0,24},{8,16},{16,8},{24,0},{1,25},{9,17},{17,9},{25,1},{2,26},{10... | collective-permute-start | bytes 61448 | tf_op jit(solution)/shard_map/ppermute | solution.py:19
  13.0 0.4 collective-permute-done.refs_1_
  13.4 3.6 %collective-permute-done.1.refs_2_ = bf16[80,128]{1,0:T(8,128)(2,1)S(1)} collective-permute-done((bf16[80,128]{1,0:T(8,128)(2,1)S(1)}, bf16[80,128]{1,0:T(8,128)(2,1)S(1)}, u32[]{:S(2)}, u32[]{:S(2)}) %collective-permute-start.1) | collective-permute-done | bytes 20512 | tf_op jit(solution)/shard_map/ppermute | solution.py:19
  17.0 0.0 collective-permute-done.2.refs_3_
  17.0 0.0 copy-start.1
  17.1 0.8 %collective-permute-start.5 = (bf16[6,128,128]{2,1,0:T(8,128)(2,1)S(1)}, bf16[6,128,128]{2,1,0:T(8,128)(2,1)S(1)}, u32[]{:S(2)}, u32[]{:S(2)}) collective-permute-start(bf16[6,128,128]{2,1,0:T(8,128)(2,1)S(1)} %get-tuple-element.29), channel_id=1, source_target_pairs={{0,8},{8,0},{16,24},{24,16},{1,9},{9,1},{17,25},{25,17},{2,10},{10... | collective-permute-start | bytes 589832 | tf_op jit(solution)/shard_map/ppermute | solution.py:19
  17.9 2.3 %collective-permute-start.9 = (bf16[128,256]{1,0:T(8,128)(2,1)S(1)}, bf16[128,256]{1,0:T(8,128)(2,1)S(1)}, u32[]{:S(2)}, u32[]{:S(2)}) collective-permute-start(bf16[128,256]{1,0:T(8,128)(2,1)S(1)} %copy-done.1), channel_id=1, source_target_pairs={{0,16},{8,24},{16,0},{24,8},{1,17},{9,25},{17,1},{25,9},{2,18},{10... | collective-permute-start | bytes 196616 | tf_op jit(solution)/shard_map/ppermute | solution.py:19
  20.2 2.4 %collective-permute-start.8 = (bf16[4,64,128]{2,1,0:T(8,128)(2,1)S(1)}, bf16[4,64,128]{2,1,0:T(8,128)(2,1)S(1)}, u32[]{:S(2)}, u32[]{:S(2)}) collective-permute-start(bf16[4,64,128]{2,1,0:T(8,128)(2,1)S(1)} %get-tuple-element.30.refs_0_), channel_id=1, source_target_pairs={{0,6},{1,7},{2,4},{3,5},{4,2},{5,3},{6,0},{7,1},{8,14},{9,15},{10,... | collective-permute-start | bytes 196616 | tf_op jit(solution)/shard_map/ppermute | solution.py:19
  22.6 0.5 collective-permute-start.7
  23.1 0.5 collective-permute-start.6
  23.6 1.7 %collective-permute-done.8.refs_3_ = bf16[4,64,128]{2,1,0:T(8,128)(2,1)S(1)} collective-permute-done((bf16[4,64,128]{2,1,0:T(8,128)(2,1)S(1)}, bf16[4,64,128]{2,1,0:T(8,128)(2,1)S(1)}, u32[]{:S(2)}, u32[]{:S(2)}) %collective-permute-start.8) | collective-permute-done | bytes 65568 | tf_op jit(solution)/shard_map/ppermute | solution.py:19
  25.3 1.5 %collective-permute-done.7.refs_2_ = bf16[4,64,128]{2,1,0:T(8,128)(2,1)S(1)} collective-permute-done((bf16[4,64,128]{2,1,0:T(8,128)(2,1)S(1)}, bf16[4,64,128]{2,1,0:T(8,128)(2,1)S(1)}, u32[]{:S(2)}, u32[]{:S(2)}) %collective-permute-start.7) | collective-permute-done | bytes 65568 | tf_op jit(solution)/shard_map/ppermute | solution.py:19
  26.9 0.5 collective-permute-done.6.refs_1_
  27.4 0.1 collective-permute-start.10
  27.5 0.8 %collective-permute-start.14 = (bf16[2,128,256]{2,1,0:T(8,128)(2,1)S(1)}, bf16[2,128,256]{2,1,0:T(8,128)(2,1)S(1)}, u32[]{:S(2)}, u32[]{:S(2)}) collective-permute-start(bf16[2,128,256]{2,1,0:T(8,128)(2,1)S(1)} %get-tuple-element.32.refs_4_), channel_id=1, source_target_pairs={{0,8},{8,0},{16,24},{24,16},{1,9},{9,1},{17,25},{25,17},{2,10},{10... | collective-permute-start | bytes 393224 | tf_op jit(solution)/shard_map/ppermute | solution.py:19
  28.3 0.9 %shard_map.97.refs_5_ = f32[4,64,128]{2,1,0:T(8,128)S(1)} custom-call(s32[4,1,128]{2,1,0:T(1,128)S(1)} %get-tuple-element.28.index, bf16[6,128,128]{2,1,0:T(8,128)(2,1)S(1)} %bitcast.6, bf16[6,128,128]{2,1,0:T(8,128)(2,1)S(1)} %collective-permute-done.4.refs_5_.refs_1_, bf16[6,128,128]{2,1,0:T(8,128)(2,1)S(1)} %collective-permute-done.3.refs_4_.refs_2_, ...), custom_call_target="tpu_custom_call" | custom-call | flops 25165824 | bytes 655360 | tf_op jit(solution)/shard_map/pallas_call | solution.py:252
  29.3 0.0 copy-start.6
  29.3 0.9 %shard_map.98.refs_0_ = bf16[4,64,128]{2,1,0:T(8,128)(2,1)S(1)} custom-call(s32[4,1,128]{2,1,0:T(1,128)S(1)} %get-tuple-element.28.index, bf16[6,128,128]{2,1,0:T(8,128)(2,1)S(1)} %bitcast.7, bf16[6,128,128]{2,1,0:T(8,128)(2,1)S(1)} %collective-permute-done.4.refs_5_.refs_1_, bf16[6,128,128]{2,1,0:T(8,128)(2,1)S(1)} %collective-permute-done.3.refs_4_.refs_2_, ...), custom_call_target="tpu_custom_call" | custom-call | flops 25165824 | bytes 655360 | tf_op jit(solution)/shard_map/pallas_call | solution.py:260
  30.2 1.4 %collective-permute-start.13 = (bf16[4,64,128]{2,1,0:T(8,128)(2,1)S(1)}, bf16[4,64,128]{2,1,0:T(8,128)(2,1)S(1)}, u32[]{:S(2)}, u32[]{:S(2)}) collective-permute-start(bf16[4,64,128]{2,1,0:T(8,128)(2,1)S(1)} %shard_map.98.refs_0_), channel_id=1, source_target_pairs={{0,24},{8,16},{16,8},{24,0},{1,25},{9,17},{17,9},{25,1},{2,26},{10... | collective-permute-start | bytes 196616 | tf_op jit(solution)/shard_map/ppermute | solution.py:19
  31.7 1.4 %collective-permute-start.12 = (bf16[4,64,128]{2,1,0:T(8,128)(2,1)S(1)}, bf16[4,64,128]{2,1,0:T(8,128)(2,1)S(1)}, u32[]{:S(2)}, u32[]{:S(2)}) collective-permute-start(bf16[4,64,128]{2,1,0:T(8,128)(2,1)S(1)} %shard_map.98.refs_0_), channel_id=1, source_target_pairs={{0,16},{8,24},{16,0},{24,8},{1,17},{9,25},{17,1},{25,9},{2,18},{10... | collective-permute-start | bytes 196616 | tf_op jit(solution)/shard_map/ppermute | solution.py:19
  33.0 1.7 %collective-permute-start.11 = (bf16[4,64,128]{2,1,0:T(8,128)(2,1)S(1)}, bf16[4,64,128]{2,1,0:T(8,128)(2,1)S(1)}, u32[]{:S(2)}, u32[]{:S(2)}) collective-permute-start(bf16[4,64,128]{2,1,0:T(8,128)(2,1)S(1)} %shard_map.98.refs_0_), channel_id=1, source_target_pairs={{0,8},{8,0},{16,24},{24,16},{1,9},{9,1},{17,25},{25,17},{2,10},{10... | collective-permute-start | bytes 196616 | tf_op jit(solution)/shard_map/ppermute | solution.py:19
  34.7 2.4 %collective-permute-done.13.refs_3_ = bf16[4,64,128]{2,1,0:T(8,128)(2,1)S(1)} collective-permute-done((bf16[4,64,128]{2,1,0:T(8,128)(2,1)S(1)}, bf16[4,64,128]{2,1,0:T(8,128)(2,1)S(1)}, u32[]{:S(2)}, u32[]{:S(2)}) %collective-permute-start.13) | collective-permute-done | bytes 65568 | tf_op jit(solution)/shard_map/ppermute | solution.py:19
  37.1 2.4 %collective-permute-done.12.refs_2_ = bf16[4,64,128]{2,1,0:T(8,128)(2,1)S(1)} collective-permute-done((bf16[4,64,128]{2,1,0:T(8,128)(2,1)S(1)}, bf16[4,64,128]{2,1,0:T(8,128)(2,1)S(1)}, u32[]{:S(2)}, u32[]{:S(2)}) %collective-permute-start.12) | collective-permute-done | bytes 65568 | tf_op jit(solution)/shard_map/ppermute | solution.py:19
  39.5 0.9 %shard_map.99 = (bf16[128,256]{1,0:T(8,128)(2,1)S(1)}, bf16[4,128,256]{2,1,0:T(8,128)(2,1)S(1)}, bf16[2,128,256]{2,1,0:T(8,128)(2,1)S(1)}) custom-call(bf16[4,64,128]{2,1,0:T(8,128)(2,1)S(1)} %shard_map.98.refs_0_, bf16[4,64,128]{2,1,0:T(8,128)(2,1)S(1)} %collective-permute-done.11.refs_1_, bf16[4,64,128]{2,1,0:T(8,128)(2,1)S(1)} %collective-permute-done.12.refs_2_, ...), custom_call_target="tpu_custom_call" | custom-call | flops 201326592 | bytes 1310720 | tf_op jit(solution)/shard_map/pallas_call | solution.py:269
  40.4 1.1 %shard_map.101 = bf16[5,128,256]{2,1,0:T(8,128)(2,1)S(1)} custom-call(s32[4,1,128]{2,1,0:T(1,128)S(1)} %get-tuple-element.28.index, bf16[6,128,128]{2,1,0:T(8,128)(2,1)S(1)} %bitcast.8, bf16[6,128,128]{2,1,0:T(8,128)(2,1)S(1)} %collective-permute-done.4.refs_5_.refs_1_, bf16[6,128,128]{2,1,0:T(8,128)(2,1)S(1)} %collective-permute-done.3.refs_4_.refs_2_, ...), custom_call_target="tpu_custom_call" | custom-call | flops 25165824 | bytes 655360 | tf_op jit(solution)/shard_map/pallas_call | solution.py:286
  41.5 0.1 collective-permute-start.15
  41.6 0.9 %shard_map.100.keep = f32[4,128,256]{2,1,0:T(8,128)S(1)} custom-call(s32[4,1,128]{2,1,0:T(1,128)S(1)} %get-tuple-element.28.index, bf16[6,128,128]{2,1,0:T(8,128)(2,1)S(1)} %bitcast.9, bf16[6,128,128]{2,1,0:T(8,128)(2,1)S(1)} %collective-permute-done.4.refs_5_.refs_1_, bf16[6,128,128]{2,1,0:T(8,128)(2,1)S(1)} %collective-permute-done.3.refs_4_.refs_2_, ...), custom_call_target="tpu_custom_call" | custom-call | flops 25165824 | bytes 655360 | tf_op jit(solution)/shard_map/pallas_call | solution.py:294
  42.5 0.7 %collective-permute-done.15.arrived = bf16[5,128,256]{2,1,0:T(8,128)(2,1)S(1)} collective-permute-done((bf16[5,128,256]{2,1,0:T(8,128)(2,1)S(1)}, bf16[5,128,256]{2,1,0:T(8,128)(2,1)S(1)}, u32[]{:S(2)}, u32[]{:S(2)}) %collective-permute-start.15) | collective-permute-done | bytes 327712 | tf_op jit(solution)/shard_map/ppermute | solution.py:19
  43.2 0.1 shard_map.102
  43.3 1.7 %collective-permute-start.16 = (bf16[256,256]{1,0:T(8,128)(2,1)S(1)}, bf16[256,256]{1,0:T(8,128)(2,1)S(1)}, u32[]{:S(2)}, u32[]{:S(2)}) collective-permute-start(bf16[256,256]{1,0:T(8,128)(2,1)S(1)} %get-tuple-element.37), channel_id=1, source_target_pairs={{0,6},{1,7},{2,4},{3,5},{4,2},{5,3},{6,0},{7,1},{8,14},{9,15},{10,... | collective-permute-start | bytes 393224 | tf_op jit(solution)/shard_map/ppermute | solution.py:19
  45.0 0.1 collective-permute-start.17
  45.1 1.7 %collective-permute-start.18 = (bf16[256,256]{1,0:T(8,128)(2,1)S(1)}, bf16[256,256]{1,0:T(8,128)(2,1)S(1)}, u32[]{:S(2)}, u32[]{:S(2)}) collective-permute-start(bf16[256,256]{1,0:T(8,128)(2,1)S(1)} %get-tuple-element.39), channel_id=1, source_target_pairs={{0,2},{1,3},{2,0},{3,1},{4,6},{5,7},{6,4},{7,5},{8,10},{9,11},{10,... | collective-permute-start | bytes 393224 | tf_op jit(solution)/shard_map/ppermute | solution.py:19
  46.8 3.8 %collective-permute-done.16.refs_0_ = bf16[256,256]{1,0:T(8,128)(2,1)S(1)} collective-permute-done((bf16[256,256]{1,0:T(8,128)(2,1)S(1)}, bf16[256,256]{1,0:T(8,128)(2,1)S(1)}, u32[]{:S(2)}, u32[]{:S(2)}) %collective-permute-start.16) | collective-permute-done | bytes 131104 | tf_op jit(solution)/shard_map/ppermute | solution.py:19
  50.6 2.0 %collective-permute-done.17.refs_1_ = bf16[256,256]{1,0:T(8,128)(2,1)S(1)} collective-permute-done((bf16[256,256]{1,0:T(8,128)(2,1)S(1)}, bf16[256,256]{1,0:T(8,128)(2,1)S(1)}, u32[]{:S(2)}, u32[]{:S(2)}) %collective-permute-start.17) | collective-permute-done | bytes 131104 | tf_op jit(solution)/shard_map/ppermute | solution.py:19
  52.6 0.3 collective-permute-done.18.refs_2_
  52.9 0.1 shard_map.103
  53.0 0.1 collective-permute-start.19
  53.0 0.7 %shard_map.104 = (f32[128,256]{1,0:T(8,128)}, bf16[128,256]{1,0:T(8,128)(2,1)}) custom-call(f32[128,256]{1,0:T(8,128)S(1)} %get-tuple-element.40.grads, bf16[128,256]{1,0:T(8,128)(2,1)S(1)} %get-tuple-element.41.rows), custom_call_target="tpu_custom_call" | custom-call | bytes 393216 | tf_op jit(solution)/shard_map/pallas_call | solution.py:315
  53.7 0.6 %collective-permute-done.19.arrived = f32[128,256]{1,0:T(8,128)S(1)} collective-permute-done((f32[128,256]{1,0:T(8,128)S(1)}, f32[128,256]{1,0:T(8,128)S(1)}, u32[]{:S(2)}, u32[]{:S(2)}) %collective-permute-start.19) | collective-permute-done | bytes 131104 | tf_op jit(solution)/shard_map/ppermute | solution.py:19
  54.4 0.7 %shard_map.105 = f32[256,256]{1,0:T(8,128)} custom-call(f32[128,256]{1,0:T(8,128)S(1)} %get-tuple-element.43.mine, f32[128,256]{1,0:T(8,128)S(1)} %collective-permute-done.19.arrived), custom_call_target="tpu_custom_call" | custom-call | bytes 524288 | tf_op jit(solution)/shard_map/pallas_call | solution.py:321
  (18 shorter events, 0.1 us)
Async XLA Ops:
  0.6 16.4 %collective-permute-start.4 = (bf16[6,128,128]{2,1,0:T(8,128)(2,1)}, bf16[6,128,128]{2,1,0:T(8,128)(2,1)S(1)}, u32[]{:S(2)}, u32[]{:S(2)}) collective-permute-start(bf16[6,128,128]{2,1,0:T(8,128)(2,1)} %bitcast.4), channel_id=1, source_target_pairs={{0,8},{8,0},{16,24},{24,16},{1,9},{9,1},{17,25},{25,17},{2,10},{10... | collective-permute-start | bytes 589832 | tf_op jit(solution)/shard_map/ppermute | solution.py:19
  3.7 13.3 %collective-permute-start.3 = (bf16[6,128,128]{2,1,0:T(8,128)(2,1)}, bf16[6,128,128]{2,1,0:T(8,128)(2,1)S(1)}, u32[]{:S(2)}, u32[]{:S(2)}) collective-permute-start(bf16[6,128,128]{2,1,0:T(8,128)(2,1)} %bitcast.5), channel_id=1, source_target_pairs={{0,16},{8,24},{16,0},{24,8},{1,17},{9,25},{17,1},{25,9},{2,18},{10... | collective-permute-start | bytes 589832 | tf_op jit(solution)/shard_map/ppermute | solution.py:19
  6.3 0.7 %copy-start.4 = (s32[1,1,2,3]{3,2,1,0:T(2,128)S(1)}, s32[1,1,2,3]{3,2,1,0:T(2,128)}, u32[]{:S(2)}) copy-start(s32[1,1,2,3]{3,2,1,0:T(2,128)} %param.12) | copy-start | bytes 76
  6.3 0.7 %copy-start.3 = (s32[1,1,2,3]{3,2,1,0:T(2,128)S(1)}, s32[1,1,2,3]{3,2,1,0:T(2,128)}, u32[]{:S(2)}) copy-start(s32[1,1,2,3]{3,2,1,0:T(2,128)} %param.11) | copy-start | bytes 76
  6.3 0.7 %copy-start.5 = (s32[1,1,2]{2,1,0:T(1,128)S(1)}, s32[1,1,2]{2,1,0:T(1,128)}, u32[]{:S(2)}) copy-start(s32[1,1,2]{2,1,0:T(1,128)} %param.13) | copy-start | bytes 28
  7.0 0.8 %copy-start.2 = (bf16[128,256]{1,0:T(8,128)(2,1)S(1)}, bf16[128,256]{1,0:T(8,128)(2,1)}, u32[]{:S(2)}) copy-start(bf16[128,256]{1,0:T(8,128)(2,1)} %feats.1) | copy-start | bytes 196612
  8.5 4.8 %collective-permute-start = (bf16[80,128]{1,0:T(8,128)(2,1)S(1)}, bf16[80,128]{1,0:T(8,128)(2,1)S(1)}, u32[]{:S(2)}, u32[]{:S(2)}) collective-permute-start(bf16[80,128]{1,0:T(8,128)(2,1)S(1)} %get-tuple-element.25), channel_id=1, source_target_pairs={{0,8},{8,0},{16,24},{24,16},{1,9},{9,1},{17,25},{25,17},{2,10},{10... | collective-permute-start | bytes 61448 | tf_op jit(solution)/shard_map/ppermute | solution.py:19
  9.0 8.0 %collective-permute-start.1 = (bf16[80,128]{1,0:T(8,128)(2,1)S(1)}, bf16[80,128]{1,0:T(8,128)(2,1)S(1)}, u32[]{:S(2)}, u32[]{:S(2)}) collective-permute-start(bf16[80,128]{1,0:T(8,128)(2,1)S(1)} %get-tuple-element.26), channel_id=1, source_target_pairs={{0,16},{8,24},{16,0},{24,8},{1,17},{9,25},{17,1},{25,9},{2,18},{10... | collective-permute-start | bytes 61448 | tf_op jit(solution)/shard_map/ppermute | solution.py:19
  9.0 8.0 %collective-permute-start.2 = (bf16[80,128]{1,0:T(8,128)(2,1)S(1)}, bf16[80,128]{1,0:T(8,128)(2,1)S(1)}, u32[]{:S(2)}, u32[]{:S(2)}) collective-permute-start(bf16[80,128]{1,0:T(8,128)(2,1)S(1)} %get-tuple-element.27), channel_id=1, source_target_pairs={{0,24},{8,16},{16,8},{24,0},{1,25},{9,17},{17,9},{25,1},{2,26},{10... | collective-permute-start | bytes 61448 | tf_op jit(solution)/shard_map/ppermute | solution.py:19
  17.0 0.9 %copy-start.1 = (bf16[128,256]{1,0:T(8,128)(2,1)S(1)}, bf16[128,256]{1,0:T(8,128)(2,1)}, u32[]{:S(2)}) copy-start(bf16[128,256]{1,0:T(8,128)(2,1)} %refs_4_.1) | copy-start | bytes 196612
  17.1 10.3 %collective-permute-start.5 = (bf16[6,128,128]{2,1,0:T(8,128)(2,1)S(1)}, bf16[6,128,128]{2,1,0:T(8,128)(2,1)S(1)}, u32[]{:S(2)}, u32[]{:S(2)}) collective-permute-start(bf16[6,128,128]{2,1,0:T(8,128)(2,1)S(1)} %get-tuple-element.29), channel_id=1, source_target_pairs={{0,8},{8,0},{16,24},{24,16},{1,9},{9,1},{17,25},{25,17},{2,10},{10... | collective-permute-start | bytes 589832 | tf_op jit(solution)/shard_map/ppermute | solution.py:19
  17.9 5.7 %collective-permute-start.9 = (bf16[128,256]{1,0:T(8,128)(2,1)S(1)}, bf16[128,256]{1,0:T(8,128)(2,1)S(1)}, u32[]{:S(2)}, u32[]{:S(2)}) collective-permute-start(bf16[128,256]{1,0:T(8,128)(2,1)S(1)} %copy-done.1), channel_id=1, source_target_pairs={{0,16},{8,24},{16,0},{24,8},{1,17},{9,25},{17,1},{25,9},{2,18},{10... | collective-permute-start | bytes 196616 | tf_op jit(solution)/shard_map/ppermute | solution.py:19
  20.1 8.2 %copy-start = (bf16[1,1,2,3,128,128]{5,4,3,2,1,0:T(8,128)(2,1)S(1)}, bf16[1,1,2,3,128,128]{5,4,3,2,1,0:T(8,128)(2,1)}, u32[]{:S(2)}) copy-start(bf16[1,1,2,3,128,128]{5,4,3,2,1,0:T(8,128)(2,1)} %param.10) | copy-start | bytes 589828
  20.2 5.2 %collective-permute-start.8 = (bf16[4,64,128]{2,1,0:T(8,128)(2,1)S(1)}, bf16[4,64,128]{2,1,0:T(8,128)(2,1)S(1)}, u32[]{:S(2)}, u32[]{:S(2)}) collective-permute-start(bf16[4,64,128]{2,1,0:T(8,128)(2,1)S(1)} %get-tuple-element.30.refs_0_), channel_id=1, source_target_pairs={{0,6},{1,7},{2,4},{3,5},{4,2},{5,3},{6,0},{7,1},{8,14},{9,15},{10,... | collective-permute-start | bytes 196616 | tf_op jit(solution)/shard_map/ppermute | solution.py:19
  22.6 4.3 %collective-permute-start.7 = (bf16[4,64,128]{2,1,0:T(8,128)(2,1)S(1)}, bf16[4,64,128]{2,1,0:T(8,128)(2,1)S(1)}, u32[]{:S(2)}, u32[]{:S(2)}) collective-permute-start(bf16[4,64,128]{2,1,0:T(8,128)(2,1)S(1)} %get-tuple-element.30.refs_0_), channel_id=1, source_target_pairs={{0,4},{1,5},{2,6},{3,7},{4,0},{5,1},{6,2},{7,3},{8,12},{9,13},{10,... | collective-permute-start | bytes 196616 | tf_op jit(solution)/shard_map/ppermute | solution.py:19
  23.1 4.3 %collective-permute-start.6 = (bf16[4,64,128]{2,1,0:T(8,128)(2,1)S(1)}, bf16[4,64,128]{2,1,0:T(8,128)(2,1)S(1)}, u32[]{:S(2)}, u32[]{:S(2)}) collective-permute-start(bf16[4,64,128]{2,1,0:T(8,128)(2,1)S(1)} %get-tuple-element.30.refs_0_), channel_id=1, source_target_pairs={{0,2},{1,3},{2,0},{3,1},{4,6},{5,7},{6,4},{7,5},{8,10},{9,11},{10,... | collective-permute-start | bytes 196616 | tf_op jit(solution)/shard_map/ppermute | solution.py:19
  27.4 1.9 %collective-permute-start.10 = (bf16[4,4,64,128]{3,2,1,0:T(8,128)(2,1)S(1)}, bf16[4,4,64,128]{3,2,1,0:T(8,128)(2,1)S(1)}, u32[]{:S(2)}, u32[]{:S(2)}) collective-permute-start(bf16[4,4,64,128]{3,2,1,0:T(8,128)(2,1)S(1)} %get-tuple-element.31.refs_4_), channel_id=1, source_target_pairs={{0,1},{1,0},{2,3},{3,2},{4,5},{5,4},{6,7},{7,6},{8,9},{9,8},{10,11... | collective-permute-start | bytes 786440 | tf_op jit(solution)/shard_map/ppermute | solution.py:19
  27.5 7.2 %collective-permute-start.14 = (bf16[2,128,256]{2,1,0:T(8,128)(2,1)S(1)}, bf16[2,128,256]{2,1,0:T(8,128)(2,1)S(1)}, u32[]{:S(2)}, u32[]{:S(2)}) collective-permute-start(bf16[2,128,256]{2,1,0:T(8,128)(2,1)S(1)} %get-tuple-element.32.refs_4_), channel_id=1, source_target_pairs={{0,8},{8,0},{16,24},{24,16},{1,9},{9,1},{17,25},{25,17},{2,10},{10... | collective-permute-start | bytes 393224 | tf_op jit(solution)/shard_map/ppermute | solution.py:19
  29.3 10.2 %copy-start.6 = (bf16[256,256]{1,0:T(8,128)(2,1)S(1)}, bf16[256,256]{1,0:T(8,128)(2,1)}, u32[]{:S(2)}) copy-start(bf16[256,256]{1,0:T(8,128)(2,1)} %refs_6_.1) | copy-start | bytes 393220
  30.2 6.8 %collective-permute-start.13 = (bf16[4,64,128]{2,1,0:T(8,128)(2,1)S(1)}, bf16[4,64,128]{2,1,0:T(8,128)(2,1)S(1)}, u32[]{:S(2)}, u32[]{:S(2)}) collective-permute-start(bf16[4,64,128]{2,1,0:T(8,128)(2,1)S(1)} %shard_map.98.refs_0_), channel_id=1, source_target_pairs={{0,24},{8,16},{16,8},{24,0},{1,25},{9,17},{17,9},{25,1},{2,26},{10... | collective-permute-start | bytes 196616 | tf_op jit(solution)/shard_map/ppermute | solution.py:19
  31.7 7.8 %collective-permute-start.12 = (bf16[4,64,128]{2,1,0:T(8,128)(2,1)S(1)}, bf16[4,64,128]{2,1,0:T(8,128)(2,1)S(1)}, u32[]{:S(2)}, u32[]{:S(2)}) collective-permute-start(bf16[4,64,128]{2,1,0:T(8,128)(2,1)S(1)} %shard_map.98.refs_0_), channel_id=1, source_target_pairs={{0,16},{8,24},{16,0},{24,8},{1,17},{9,25},{17,1},{25,9},{2,18},{10... | collective-permute-start | bytes 196616 | tf_op jit(solution)/shard_map/ppermute | solution.py:19
  33.0 6.5 %collective-permute-start.11 = (bf16[4,64,128]{2,1,0:T(8,128)(2,1)S(1)}, bf16[4,64,128]{2,1,0:T(8,128)(2,1)S(1)}, u32[]{:S(2)}, u32[]{:S(2)}) collective-permute-start(bf16[4,64,128]{2,1,0:T(8,128)(2,1)S(1)} %shard_map.98.refs_0_), channel_id=1, source_target_pairs={{0,8},{8,0},{16,24},{24,16},{1,9},{9,1},{17,25},{25,17},{2,10},{10... | collective-permute-start | bytes 196616 | tf_op jit(solution)/shard_map/ppermute | solution.py:19
  41.5 1.7 %collective-permute-start.15 = (bf16[5,128,256]{2,1,0:T(8,128)(2,1)S(1)}, bf16[5,128,256]{2,1,0:T(8,128)(2,1)S(1)}, u32[]{:S(2)}, u32[]{:S(2)}) collective-permute-start(bf16[5,128,256]{2,1,0:T(8,128)(2,1)S(1)} %shard_map.101), channel_id=1, source_target_pairs={{0,1},{1,0},{2,3},{3,2},{4,5},{5,4},{6,7},{7,6},{8,9},{9,8},{10,11... | collective-permute-start | bytes 983048 | tf_op jit(solution)/shard_map/ppermute | solution.py:19
  43.3 7.3 %collective-permute-start.16 = (bf16[256,256]{1,0:T(8,128)(2,1)S(1)}, bf16[256,256]{1,0:T(8,128)(2,1)S(1)}, u32[]{:S(2)}, u32[]{:S(2)}) collective-permute-start(bf16[256,256]{1,0:T(8,128)(2,1)S(1)} %get-tuple-element.37), channel_id=1, source_target_pairs={{0,6},{1,7},{2,4},{3,5},{4,2},{5,3},{6,0},{7,1},{8,14},{9,15},{10,... | collective-permute-start | bytes 393224 | tf_op jit(solution)/shard_map/ppermute | solution.py:19
  45.0 7.6 %collective-permute-start.17 = (bf16[256,256]{1,0:T(8,128)(2,1)S(1)}, bf16[256,256]{1,0:T(8,128)(2,1)S(1)}, u32[]{:S(2)}, u32[]{:S(2)}) collective-permute-start(bf16[256,256]{1,0:T(8,128)(2,1)S(1)} %get-tuple-element.38), channel_id=1, source_target_pairs={{0,4},{1,5},{2,6},{3,7},{4,0},{5,1},{6,2},{7,3},{8,12},{9,13},{10,... | collective-permute-start | bytes 393224 | tf_op jit(solution)/shard_map/ppermute | solution.py:19
  45.1 7.8 %collective-permute-start.18 = (bf16[256,256]{1,0:T(8,128)(2,1)S(1)}, bf16[256,256]{1,0:T(8,128)(2,1)S(1)}, u32[]{:S(2)}, u32[]{:S(2)}) collective-permute-start(bf16[256,256]{1,0:T(8,128)(2,1)S(1)} %get-tuple-element.39), channel_id=1, source_target_pairs={{0,2},{1,3},{2,0},{3,1},{4,6},{5,7},{6,4},{7,5},{8,10},{9,11},{10,... | collective-permute-start | bytes 393224 | tf_op jit(solution)/shard_map/ppermute | solution.py:19
  53.0 1.4 %collective-permute-start.19 = (f32[128,256]{1,0:T(8,128)S(1)}, f32[128,256]{1,0:T(8,128)S(1)}, u32[]{:S(2)}, u32[]{:S(2)}) collective-permute-start(f32[128,256]{1,0:T(8,128)S(1)} %get-tuple-element.43.mine), channel_id=1, source_target_pairs={{0,1},{1,0},{2,3},{3,2},{4,5},{5,4},{6,7},{7,6},{8,9},{9,8},{10,11... | collective-permute-start | bytes 393224 | tf_op jit(solution)/shard_map/ppermute | solution.py:19

commit v11 on v10

--- a/solution.py
+++ b/solution.py
@@ -159,6 +159,14 @@
         send[:half] = total[...].astype(BF16)
         core = lax.rem(lax.axis_index("blk"), 2)
         send[half:] = terms[1 - core].reshape(-1, *send.shape[1:])
+
+
+def dense_and_send(reps, groups, lists, cap, index, *refs):
+    blocks, rest = refs[:reps], refs[reps:]
+    sources, weight, out, dagg, terms, send = rest[:-9], *rest[-9:-4]
+    agg, cot, outs, total = rest[-4:]
+    dense_layer(reps, *sources, weight, out, dagg, terms, agg, cot, outs)
+    feature_grads(reps, groups, lists, cap, 1, index, *blocks, dagg, terms, send, total)
 
 
 def add_core(half, keep, terms, arrived, own, own_terms, *sends):
@@ -266,31 +274,25 @@
         moved=slot_bytes // 2,
     )(index, *blocks, far, agg)
 
-    out_rows, dagg, terms = call(
-        functools.partial(dense_layer, reps),
+    out_rows, dagg, terms, send = call(
+        functools.partial(dense_and_send, reps, groups, lists, cap),
         [
             like((nodes, width), BF16),
             like((reps, nodes, width), BF16),
             like((2, width // 2, width), BF16),
+            like((half + width // 2 // nodes, nodes, width), BF16),
         ],
-        [VMEM] * (reps + 3),
+        [SMEM] + [VMEM] * (2 * reps + 3),
         [
             pltpu.VMEM((reps, reps, part, nodes), BF16),
             pltpu.VMEM((reps, nodes, width), BF16),
             pltpu.VMEM((reps, nodes, width), BF16),
+            pltpu.VMEM((half, nodes, width), F32),
         ],
-        flops=6 * reps * nodes * width * width,
-        moved=2 * reps * 5 * nodes * width,
-    )(*direct([agg] * reps), cotangents, swap(cotangents, "rep", 1), weight)
-
-    send = call(
-        functools.partial(feature_grads, reps, groups, lists, cap, 1),
-        like((half + width // 2 // nodes, nodes, width), BF16),
-        [SMEM] + [VMEM] * (reps + 2),
-        [pltpu.VMEM((half, nodes, width), F32)],
-        flops=slot_flops // 2,
-        moved=slot_bytes // 2,
-    )(index, *blocks, dagg, terms)
+        flops=6 * reps * nodes * width * width + slot_flops // 2,
+        moved=2 * reps * 5 * nodes * width + slot_bytes // 2,
+    )(index, *blocks, *direct([agg] * reps), cotangents, swap(cotangents, "rep", 1), weight)
+
     keep = call(
         functools.partial(feature_grads, reps, groups, lists, cap, 0),
         like((half, nodes, width), F32),

time: 55.3 us -> 55.5 us (level)
  waiting for transfers between devices: 19.9 us -> 19 us
  Pallas kernels: 7.09 us -> 7.95 us
    pallas_call x1, Pallas kernels: 0.89 us -> 1.98 us  [per_device(): call(functools.partial(feature_grads, reps, groups, lists, cap, 0), like(...]
    ppermute x20, waiting for transfers between devices: 19.9 us -> 19 us  [swap(): return lax.ppermute(array, axis, [(i, i ^ bit) for i in range(peers)])]
    pallas_call x2 -> x1, Pallas kernels: 1.99 us -> 1.77 us  [per_device(): call(functools.partial(dense_and_send, reps, groups, lists, cap), [like((...]
  transfers between devices with their start and end apart: 20 -> 20, of which waited for: 12 -> 11; matrix products, arithmetic and copies ran while one was open for 0% -> 0% of each run, Pallas kernels for 8% -> 10%
where the time goes in v11:
time: 55.5 us; the launch traced here: 55.1 us
  starting transfers between devices  25.8 us (46%)
  waiting for transfers between devices  19 us (34%)
  Pallas kernels  7.95 us (14%)
  local copies, waits for them, and re-layouts  1.55 us (3%)
  between operations  0.77 us (1%)
    ppermute x20, starting transfers between devices, swap(): return lax.ppermute(array, axis, [(i, i ^ bit) for i in range(peers)])  25.8 us
    ppermute x20, waiting for transfers between devices, swap(): return lax.ppermute(array, axis, [(i, i ^ bit) for i in range(peers)])  19 us
    pallas_call x1, Pallas kernels, per_device(): call(functools.partial(feature_grads, reps, groups, lists, cap, 0), like(...  1.98 us
    pallas_call x1, Pallas kernels, per_device(): call(functools.partial(dense_and_send, reps, groups, lists, cap), [like((...  1.77 us
    unnamed x14, local copies, waits for them, and re-layouts  1.55 us
  transfers between devices with their start and end apart: 20, of which 11 were waited for; matrix products, arithmetic and copies ran while one was open for 0% of the time, Pallas kernels for 10%

profile of v11, /device:TPU:0, one launch (start us, length us, event | category | flops | bytes accessed | tf_op | source)
XLA Modules:
  0.0 55.1 jit_solution(11461777497443402000)
XLA Ops:
  0.6 3.1 %collective-permute-start.4 = (bf16[6,128,128]{2,1,0:T(8,128)(2,1)}, bf16[6,128,128]{2,1,0:T(8,128)(2,1)S(1)}, u32[]{:S(2)}, u32[]{:S(2)}) collective-permute-start(bf16[6,128,128]{2,1,0:T(8,128)(2,1)} %bitcast.4), channel_id=1, source_target_pairs={{0,8},{8,0},{16,24},{24,16},{1,9},{9,1},{17,25},{25,17},{2,10},{10... | collective-permute-start | bytes 589832 | tf_op jit(solution)/shard_map/ppermute | solution.py:19
  3.7 2.6 %collective-permute-start.3 = (bf16[6,128,128]{2,1,0:T(8,128)(2,1)}, bf16[6,128,128]{2,1,0:T(8,128)(2,1)S(1)}, u32[]{:S(2)}, u32[]{:S(2)}) collective-permute-start(bf16[6,128,128]{2,1,0:T(8,128)(2,1)} %bitcast.5), channel_id=1, source_target_pairs={{0,16},{8,24},{16,0},{24,8},{1,17},{9,25},{17,1},{25,9},{2,18},{10... | collective-permute-start | bytes 589832 | tf_op jit(solution)/shard_map/ppermute | solution.py:19
  6.3 0.7 %copy-done.5 = s32[1,1,2,3]{3,2,1,0:T(2,128)S(1)} copy-done((s32[1,1,2,3]{3,2,1,0:T(2,128)S(1)}, s32[1,1,2,3]{3,2,1,0:T(2,128)}, u32[]{:S(2)}) %copy-start.5) | copy-done | bytes 48
  7.0 0.0 copy-done.4
  7.0 0.8 %copy-done.3 = bf16[128,256]{1,0:T(8,128)(2,1)S(1)} copy-done((bf16[128,256]{1,0:T(8,128)(2,1)S(1)}, bf16[128,256]{1,0:T(8,128)(2,1)}, u32[]{:S(2)}) %copy-start.3) | copy-done | bytes 65560
  7.8 0.7 %shard_map.94 = (bf16[80,128]{1,0:T(8,128)(2,1)S(1)}, bf16[80,128]{1,0:T(8,128)(2,1)S(1)}, bf16[80,128]{1,0:T(8,128)(2,1)S(1)}, bf16[80,128]{1,0:T(8,128)(2,1)S(1)}) custom-call(bf16[128,256]{1,0:T(8,128)(2,1)S(1)} %copy-done.3, s32[2,3]{1,0:T(2,128)S(1)} %bitcast.10, s32[2,3]{1,0:T(2,128)S(1)} %bitcast.11, s32[2]{0:T(128)S(1)} %bitcast.12), custom_call_target="tpu_custom_call" | custom-call | bytes 131072 | tf_op jit(solution)/shard_map/pallas_call | solution.py:228
  8.5 0.5 collective-permute-start
  9.0 0.0 collective-permute-start.1
  9.0 3.9 %collective-permute-start.2 = (bf16[80,128]{1,0:T(8,128)(2,1)S(1)}, bf16[80,128]{1,0:T(8,128)(2,1)S(1)}, u32[]{:S(2)}, u32[]{:S(2)}) collective-permute-start(bf16[80,128]{1,0:T(8,128)(2,1)S(1)} %get-tuple-element.28), channel_id=1, source_target_pairs={{0,24},{8,16},{16,8},{24,0},{1,25},{9,17},{17,9},{25,1},{2,26},{10... | collective-permute-start | bytes 61448 | tf_op jit(solution)/shard_map/ppermute | solution.py:19
  13.0 0.4 collective-permute-done.refs_1_
  13.4 3.6 %collective-permute-done.1.refs_2_ = bf16[80,128]{1,0:T(8,128)(2,1)S(1)} collective-permute-done((bf16[80,128]{1,0:T(8,128)(2,1)S(1)}, bf16[80,128]{1,0:T(8,128)(2,1)S(1)}, u32[]{:S(2)}, u32[]{:S(2)}) %collective-permute-start.1) | collective-permute-done | bytes 20512 | tf_op jit(solution)/shard_map/ppermute | solution.py:19
  17.0 0.0 collective-permute-done.2.refs_3_
  17.0 0.0 collective-permute-done.4.refs_5_.refs_1_
  17.0 0.0 collective-permute-done.3.refs_4_.refs_2_
  17.0 0.0 copy-start.2
  17.1 0.8 %collective-permute-start.5 = (bf16[6,128,128]{2,1,0:T(8,128)(2,1)S(1)}, bf16[6,128,128]{2,1,0:T(8,128)(2,1)S(1)}, u32[]{:S(2)}, u32[]{:S(2)}) collective-permute-start(bf16[6,128,128]{2,1,0:T(8,128)(2,1)S(1)} %get-tuple-element.30), channel_id=1, source_target_pairs={{0,8},{8,0},{16,24},{24,16},{1,9},{9,1},{17,25},{25,17},{2,10},{10... | collective-permute-start | bytes 589832 | tf_op jit(solution)/shard_map/ppermute | solution.py:19
  17.9 2.3 %collective-permute-start.9 = (bf16[128,256]{1,0:T(8,128)(2,1)S(1)}, bf16[128,256]{1,0:T(8,128)(2,1)S(1)}, u32[]{:S(2)}, u32[]{:S(2)}) collective-permute-start(bf16[128,256]{1,0:T(8,128)(2,1)S(1)} %copy-done.2), channel_id=1, source_target_pairs={{0,16},{8,24},{16,0},{24,8},{1,17},{9,25},{17,1},{25,9},{2,18},{10... | collective-permute-start | bytes 196616 | tf_op jit(solution)/shard_map/ppermute | solution.py:19
  20.2 2.4 %collective-permute-start.8 = (bf16[4,64,128]{2,1,0:T(8,128)(2,1)S(1)}, bf16[4,64,128]{2,1,0:T(8,128)(2,1)S(1)}, u32[]{:S(2)}, u32[]{:S(2)}) collective-permute-start(bf16[4,64,128]{2,1,0:T(8,128)(2,1)S(1)} %get-tuple-element.31.refs_0_), channel_id=1, source_target_pairs={{0,6},{1,7},{2,4},{3,5},{4,2},{5,3},{6,0},{7,1},{8,14},{9,15},{10,... | collective-permute-start | bytes 196616 | tf_op jit(solution)/shard_map/ppermute | solution.py:19
  22.6 0.5 collective-permute-start.7
  23.1 0.5 collective-permute-start.6
  23.6 1.7 %collective-permute-done.8.refs_3_ = bf16[4,64,128]{2,1,0:T(8,128)(2,1)S(1)} collective-permute-done((bf16[4,64,128]{2,1,0:T(8,128)(2,1)S(1)}, bf16[4,64,128]{2,1,0:T(8,128)(2,1)S(1)}, u32[]{:S(2)}, u32[]{:S(2)}) %collective-permute-start.8) | collective-permute-done | bytes 65568 | tf_op jit(solution)/shard_map/ppermute | solution.py:19
  25.3 1.5 %collective-permute-done.7.refs_2_ = bf16[4,64,128]{2,1,0:T(8,128)(2,1)S(1)} collective-permute-done((bf16[4,64,128]{2,1,0:T(8,128)(2,1)S(1)}, bf16[4,64,128]{2,1,0:T(8,128)(2,1)S(1)}, u32[]{:S(2)}, u32[]{:S(2)}) %collective-permute-start.7) | collective-permute-done | bytes 65568 | tf_op jit(solution)/shard_map/ppermute | solution.py:19
  26.9 0.5 collective-permute-done.6.refs_1_
  27.4 0.1 collective-permute-start.10
  27.5 0.8 %collective-permute-start.14 = (bf16[2,128,256]{2,1,0:T(8,128)(2,1)S(1)}, bf16[2,128,256]{2,1,0:T(8,128)(2,1)S(1)}, u32[]{:S(2)}, u32[]{:S(2)}) collective-permute-start(bf16[2,128,256]{2,1,0:T(8,128)(2,1)S(1)} %get-tuple-element.33.refs_8_), channel_id=1, source_target_pairs={{0,8},{8,0},{16,24},{24,16},{1,9},{9,1},{17,25},{25,17},{2,10},{10... | collective-permute-start | bytes 393224 | tf_op jit(solution)/shard_map/ppermute | solution.py:19
  28.3 0.9 %shard_map.97.refs_5_ = f32[4,64,128]{2,1,0:T(8,128)S(1)} custom-call(s32[4,1,128]{2,1,0:T(1,128)S(1)} %get-tuple-element.29.index, bf16[6,128,128]{2,1,0:T(8,128)(2,1)S(1)} %bitcast.6, bf16[6,128,128]{2,1,0:T(8,128)(2,1)S(1)} %collective-permute-done.4.refs_5_.refs_1_, bf16[6,128,128]{2,1,0:T(8,128)(2,1)S(1)} %collective-permute-done.3.refs_4_.refs_2_, ...), custom_call_target="tpu_custom_call" | custom-call | flops 25165824 | bytes 655360 | tf_op jit(solution)/shard_map/pallas_call | solution.py:260
  29.3 0.0 copy-start.1
  29.3 0.9 %shard_map.98.refs_4_ = bf16[4,64,128]{2,1,0:T(8,128)(2,1)S(1)} custom-call(s32[4,1,128]{2,1,0:T(1,128)S(1)} %get-tuple-element.29.index, bf16[6,128,128]{2,1,0:T(8,128)(2,1)S(1)} %bitcast.7, bf16[6,128,128]{2,1,0:T(8,128)(2,1)S(1)} %collective-permute-done.4.refs_5_.refs_1_, bf16[6,128,128]{2,1,0:T(8,128)(2,1)S(1)} %collective-permute-done.3.refs_4_.refs_2_, ...), custom_call_target="tpu_custom_call" | custom-call | flops 25165824 | bytes 655360 | tf_op jit(solution)/shard_map/pallas_call | solution.py:268
  30.3 1.4 %collective-permute-start.13 = (bf16[4,64,128]{2,1,0:T(8,128)(2,1)S(1)}, bf16[4,64,128]{2,1,0:T(8,128)(2,1)S(1)}, u32[]{:S(2)}, u32[]{:S(2)}) collective-permute-start(bf16[4,64,128]{2,1,0:T(8,128)(2,1)S(1)} %shard_map.98.refs_4_), channel_id=1, source_target_pairs={{0,24},{8,16},{16,8},{24,0},{1,25},{9,17},{17,9},{25,1},{2,26},{10... | collective-permute-start | bytes 196616 | tf_op jit(solution)/shard_map/ppermute | solution.py:19
  31.7 1.4 %collective-permute-start.12 = (bf16[4,64,128]{2,1,0:T(8,128)(2,1)S(1)}, bf16[4,64,128]{2,1,0:T(8,128)(2,1)S(1)}, u32[]{:S(2)}, u32[]{:S(2)}) collective-permute-start(bf16[4,64,128]{2,1,0:T(8,128)(2,1)S(1)} %shard_map.98.refs_4_), channel_id=1, source_target_pairs={{0,16},{8,24},{16,0},{24,8},{1,17},{9,25},{17,1},{25,9},{2,18},{10... | collective-permute-start | bytes 196616 | tf_op jit(solution)/shard_map/ppermute | solution.py:19
  33.0 1.7 %collective-permute-start.11 = (bf16[4,64,128]{2,1,0:T(8,128)(2,1)S(1)}, bf16[4,64,128]{2,1,0:T(8,128)(2,1)S(1)}, u32[]{:S(2)}, u32[]{:S(2)}) collective-permute-start(bf16[4,64,128]{2,1,0:T(8,128)(2,1)S(1)} %shard_map.98.refs_4_), channel_id=1, source_target_pairs={{0,8},{8,0},{16,24},{24,16},{1,9},{9,1},{17,25},{25,17},{2,10},{10... | collective-permute-start | bytes 196616 | tf_op jit(solution)/shard_map/ppermute | solution.py:19
  34.7 2.4 %collective-permute-done.13.refs_7_ = bf16[4,64,128]{2,1,0:T(8,128)(2,1)S(1)} collective-permute-done((bf16[4,64,128]{2,1,0:T(8,128)(2,1)S(1)}, bf16[4,64,128]{2,1,0:T(8,128)(2,1)S(1)}, u32[]{:S(2)}, u32[]{:S(2)}) %collective-permute-start.13) | collective-permute-done | bytes 65568 | tf_op jit(solution)/shard_map/ppermute | solution.py:19
  37.1 2.4 %collective-permute-done.12.refs_6_ = bf16[4,64,128]{2,1,0:T(8,128)(2,1)S(1)} collective-permute-done((bf16[4,64,128]{2,1,0:T(8,128)(2,1)S(1)}, bf16[4,64,128]{2,1,0:T(8,128)(2,1)S(1)}, u32[]{:S(2)}, u32[]{:S(2)}) %collective-permute-start.12) | collective-permute-done | bytes 65568 | tf_op jit(solution)/shard_map/ppermute | solution.py:19
  39.5 1.8 %shard_map.99 = (bf16[128,256]{1,0:T(8,128)(2,1)S(1)}, bf16[4,128,256]{2,1,0:T(8,128)(2,1)S(1)}, bf16[2,128,256]{2,1,0:T(8,128)(2,1)S(1)}, bf16[5,128,256]{2,1,0:T(8,128)(2,1)S(1)}) custom-call(s32[4,1,128]{2,1,0:T(1,128)S(1)} %get-tuple-element.29.index, bf16[6,128,128]{2,1,0:T(8,128)(2,1)S(1)} %bitcast.8, ...), custom_call_target="tpu_custom_call" | custom-call | flops 226492416 | bytes 1966080 | tf_op jit(solution)/shard_map/pallas_call | solution.py:277
  41.3 0.1 collective-permute-start.15
  41.4 2.0 %shard_map.100.keep = f32[4,128,256]{2,1,0:T(8,128)S(1)} custom-call(s32[4,1,128]{2,1,0:T(1,128)S(1)} %get-tuple-element.29.index, bf16[6,128,128]{2,1,0:T(8,128)(2,1)S(1)} %bitcast.9, bf16[6,128,128]{2,1,0:T(8,128)(2,1)S(1)} %collective-permute-done.4.refs_5_.refs_1_, bf16[6,128,128]{2,1,0:T(8,128)(2,1)S(1)} %collective-permute-done.3.refs_4_.refs_2_, ...), custom_call_target="tpu_custom_call" | custom-call | flops 25165824 | bytes 655360 | tf_op jit(solution)/shard_map/pallas_call | solution.py:296
  43.4 0.1 shard_map.101
  43.4 1.3 %collective-permute-start.16 = (bf16[256,256]{1,0:T(8,128)(2,1)S(1)}, bf16[256,256]{1,0:T(8,128)(2,1)S(1)}, u32[]{:S(2)}, u32[]{:S(2)}) collective-permute-start(bf16[256,256]{1,0:T(8,128)(2,1)S(1)} %get-tuple-element.39), channel_id=1, source_target_pairs={{0,6},{1,7},{2,4},{3,5},{4,2},{5,3},{6,0},{7,1},{8,14},{9,15},{10,... | collective-permute-start | bytes 393224 | tf_op jit(solution)/shard_map/ppermute | solution.py:19
  44.8 0.8 %collective-permute-start.17 = (bf16[256,256]{1,0:T(8,128)(2,1)S(1)}, bf16[256,256]{1,0:T(8,128)(2,1)S(1)}, u32[]{:S(2)}, u32[]{:S(2)}) collective-permute-start(bf16[256,256]{1,0:T(8,128)(2,1)S(1)} %get-tuple-element.40), channel_id=1, source_target_pairs={{0,4},{1,5},{2,6},{3,7},{4,0},{5,1},{6,2},{7,3},{8,12},{9,13},{10,... | collective-permute-start | bytes 393224 | tf_op jit(solution)/shard_map/ppermute | solution.py:19
  45.6 1.4 %collective-permute-start.18 = (bf16[256,256]{1,0:T(8,128)(2,1)S(1)}, bf16[256,256]{1,0:T(8,128)(2,1)S(1)}, u32[]{:S(2)}, u32[]{:S(2)}) collective-permute-start(bf16[256,256]{1,0:T(8,128)(2,1)S(1)} %get-tuple-element.41), channel_id=1, source_target_pairs={{0,2},{1,3},{2,0},{3,1},{4,6},{5,7},{6,4},{7,5},{8,10},{9,11},{10,... | collective-permute-start | bytes 393224 | tf_op jit(solution)/shard_map/ppermute | solution.py:19
  47.0 3.7 %collective-permute-done.16.refs_0_ = bf16[256,256]{1,0:T(8,128)(2,1)S(1)} collective-permute-done((bf16[256,256]{1,0:T(8,128)(2,1)S(1)}, bf16[256,256]{1,0:T(8,128)(2,1)S(1)}, u32[]{:S(2)}, u32[]{:S(2)}) %collective-permute-start.16) | collective-permute-done | bytes 131104 | tf_op jit(solution)/shard_map/ppermute | solution.py:19
  50.7 1.6 %collective-permute-done.17.refs_1_ = bf16[256,256]{1,0:T(8,128)(2,1)S(1)} collective-permute-done((bf16[256,256]{1,0:T(8,128)(2,1)S(1)}, bf16[256,256]{1,0:T(8,128)(2,1)S(1)}, u32[]{:S(2)}, u32[]{:S(2)}) %collective-permute-start.17) | collective-permute-done | bytes 131104 | tf_op jit(solution)/shard_map/ppermute | solution.py:19
  52.4 0.5 collective-permute-done.18.refs_2_
  52.8 0.1 shard_map.102
  52.9 0.1 collective-permute-start.19
  53.0 0.7 %shard_map.103 = (f32[128,256]{1,0:T(8,128)}, bf16[128,256]{1,0:T(8,128)(2,1)}) custom-call(f32[128,256]{1,0:T(8,128)S(1)} %get-tuple-element.42.grads, bf16[128,256]{1,0:T(8,128)(2,1)S(1)} %get-tuple-element.43.rows), custom_call_target="tpu_custom_call" | custom-call | bytes 393216 | tf_op jit(solution)/shard_map/pallas_call | solution.py:317
  53.7 0.6 %collective-permute-done.19.arrived = f32[128,256]{1,0:T(8,128)S(1)} collective-permute-done((f32[128,256]{1,0:T(8,128)S(1)}, f32[128,256]{1,0:T(8,128)S(1)}, u32[]{:S(2)}, u32[]{:S(2)}) %collective-permute-start.19) | collective-permute-done | bytes 131104 | tf_op jit(solution)/shard_map/ppermute | solution.py:19
  54.3 0.7 %shard_map.104 = f32[256,256]{1,0:T(8,128)} custom-call(f32[128,256]{1,0:T(8,128)S(1)} %get-tuple-element.45.mine, f32[128,256]{1,0:T(8,128)S(1)} %collective-permute-done.19.arrived), custom_call_target="tpu_custom_call" | custom-call | bytes 524288 | tf_op jit(solution)/shard_map/pallas_call | solution.py:323
  (17 shorter events, 0.1 us)
Async XLA Ops:
  0.6 16.4 %collective-permute-start.4 = (bf16[6,128,128]{2,1,0:T(8,128)(2,1)}, bf16[6,128,128]{2,1,0:T(8,128)(2,1)S(1)}, u32[]{:S(2)}, u32[]{:S(2)}) collective-permute-start(bf16[6,128,128]{2,1,0:T(8,128)(2,1)} %bitcast.4), channel_id=1, source_target_pairs={{0,8},{8,0},{16,24},{24,16},{1,9},{9,1},{17,25},{25,17},{2,10},{10... | collective-permute-start | bytes 589832 | tf_op jit(solution)/shard_map/ppermute | solution.py:19
  3.7 13.3 %collective-permute-start.3 = (bf16[6,128,128]{2,1,0:T(8,128)(2,1)}, bf16[6,128,128]{2,1,0:T(8,128)(2,1)S(1)}, u32[]{:S(2)}, u32[]{:S(2)}) collective-permute-start(bf16[6,128,128]{2,1,0:T(8,128)(2,1)} %bitcast.5), channel_id=1, source_target_pairs={{0,16},{8,24},{16,0},{24,8},{1,17},{9,25},{17,1},{25,9},{2,18},{10... | collective-permute-start | bytes 589832 | tf_op jit(solution)/shard_map/ppermute | solution.py:19
  6.3 0.7 %copy-start.5 = (s32[1,1,2,3]{3,2,1,0:T(2,128)S(1)}, s32[1,1,2,3]{3,2,1,0:T(2,128)}, u32[]{:S(2)}) copy-start(s32[1,1,2,3]{3,2,1,0:T(2,128)} %param.12) | copy-start | bytes 76
  6.3 0.7 %copy-start.4 = (s32[1,1,2,3]{3,2,1,0:T(2,128)S(1)}, s32[1,1,2,3]{3,2,1,0:T(2,128)}, u32[]{:S(2)}) copy-start(s32[1,1,2,3]{3,2,1,0:T(2,128)} %param.11) | copy-start | bytes 76
  6.3 0.7 %copy-start.6 = (s32[1,1,2]{2,1,0:T(1,128)S(1)}, s32[1,1,2]{2,1,0:T(1,128)}, u32[]{:S(2)}) copy-start(s32[1,1,2]{2,1,0:T(1,128)} %param.13) | copy-start | bytes 28
  7.0 0.8 %copy-start.3 = (bf16[128,256]{1,0:T(8,128)(2,1)S(1)}, bf16[128,256]{1,0:T(8,128)(2,1)}, u32[]{:S(2)}) copy-start(bf16[128,256]{1,0:T(8,128)(2,1)} %feats.1) | copy-start | bytes 196612
  8.5 4.8 %collective-permute-start = (bf16[80,128]{1,0:T(8,128)(2,1)S(1)}, bf16[80,128]{1,0:T(8,128)(2,1)S(1)}, u32[]{:S(2)}, u32[]{:S(2)}) collective-permute-start(bf16[80,128]{1,0:T(8,128)(2,1)S(1)} %get-tuple-element.26), channel_id=1, source_target_pairs={{0,8},{8,0},{16,24},{24,16},{1,9},{9,1},{17,25},{25,17},{2,10},{10... | collective-permute-start | bytes 61448 | tf_op jit(solution)/shard_map/ppermute | solution.py:19
  9.0 8.0 %collective-permute-start.1 = (bf16[80,128]{1,0:T(8,128)(2,1)S(1)}, bf16[80,128]{1,0:T(8,128)(2,1)S(1)}, u32[]{:S(2)}, u32[]{:S(2)}) collective-permute-start(bf16[80,128]{1,0:T(8,128)(2,1)S(1)} %get-tuple-element.27), channel_id=1, source_target_pairs={{0,16},{8,24},{16,0},{24,8},{1,17},{9,25},{17,1},{25,9},{2,18},{10... | collective-permute-start | bytes 61448 | tf_op jit(solution)/shard_map/ppermute | solution.py:19
  9.0 8.0 %collective-permute-start.2 = (bf16[80,128]{1,0:T(8,128)(2,1)S(1)}, bf16[80,128]{1,0:T(8,128)(2,1)S(1)}, u32[]{:S(2)}, u32[]{:S(2)}) collective-permute-start(bf16[80,128]{1,0:T(8,128)(2,1)S(1)} %get-tuple-element.28), channel_id=1, source_target_pairs={{0,24},{8,16},{16,8},{24,0},{1,25},{9,17},{17,9},{25,1},{2,26},{10... | collective-permute-start | bytes 61448 | tf_op jit(solution)/shard_map/ppermute | solution.py:19
  17.0 0.9 %copy-start.2 = (bf16[128,256]{1,0:T(8,128)(2,1)S(1)}, bf16[128,256]{1,0:T(8,128)(2,1)}, u32[]{:S(2)}) copy-start(bf16[128,256]{1,0:T(8,128)(2,1)} %refs_4_.1) | copy-start | bytes 196612
  17.1 10.3 %collective-permute-start.5 = (bf16[6,128,128]{2,1,0:T(8,128)(2,1)S(1)}, bf16[6,128,128]{2,1,0:T(8,128)(2,1)S(1)}, u32[]{:S(2)}, u32[]{:S(2)}) collective-permute-start(bf16[6,128,128]{2,1,0:T(8,128)(2,1)S(1)} %get-tuple-element.30), channel_id=1, source_target_pairs={{0,8},{8,0},{16,24},{24,16},{1,9},{9,1},{17,25},{25,17},{2,10},{10... | collective-permute-start | bytes 589832 | tf_op jit(solution)/shard_map/ppermute | solution.py:19
  17.9 5.7 %collective-permute-start.9 = (bf16[128,256]{1,0:T(8,128)(2,1)S(1)}, bf16[128,256]{1,0:T(8,128)(2,1)S(1)}, u32[]{:S(2)}, u32[]{:S(2)}) collective-permute-start(bf16[128,256]{1,0:T(8,128)(2,1)S(1)} %copy-done.2), channel_id=1, source_target_pairs={{0,16},{8,24},{16,0},{24,8},{1,17},{9,25},{17,1},{25,9},{2,18},{10... | collective-permute-start | bytes 196616 | tf_op jit(solution)/shard_map/ppermute | solution.py:19
  20.1 8.2 %copy-start = (bf16[1,1,2,3,128,128]{5,4,3,2,1,0:T(8,128)(2,1)S(1)}, bf16[1,1,2,3,128,128]{5,4,3,2,1,0:T(8,128)(2,1)}, u32[]{:S(2)}) copy-start(bf16[1,1,2,3,128,128]{5,4,3,2,1,0:T(8,128)(2,1)} %param.10) | copy-start | bytes 589828
  20.2 5.2 %collective-permute-start.8 = (bf16[4,64,128]{2,1,0:T(8,128)(2,1)S(1)}, bf16[4,64,128]{2,1,0:T(8,128)(2,1)S(1)}, u32[]{:S(2)}, u32[]{:S(2)}) collective-permute-start(bf16[4,64,128]{2,1,0:T(8,128)(2,1)S(1)} %get-tuple-element.31.refs_0_), channel_id=1, source_target_pairs={{0,6},{1,7},{2,4},{3,5},{4,2},{5,3},{6,0},{7,1},{8,14},{9,15},{10,... | collective-permute-start | bytes 196616 | tf_op jit(solution)/shard_map/ppermute | solution.py:19
  22.6 4.3 %collective-permute-start.7 = (bf16[4,64,128]{2,1,0:T(8,128)(2,1)S(1)}, bf16[4,64,128]{2,1,0:T(8,128)(2,1)S(1)}, u32[]{:S(2)}, u32[]{:S(2)}) collective-permute-start(bf16[4,64,128]{2,1,0:T(8,128)(2,1)S(1)} %get-tuple-element.31.refs_0_), channel_id=1, source_target_pairs={{0,4},{1,5},{2,6},{3,7},{4,0},{5,1},{6,2},{7,3},{8,12},{9,13},{10,... | collective-permute-start | bytes 196616 | tf_op jit(solution)/shard_map/ppermute | solution.py:19
  23.1 4.3 %collective-permute-start.6 = (bf16[4,64,128]{2,1,0:T(8,128)(2,1)S(1)}, bf16[4,64,128]{2,1,0:T(8,128)(2,1)S(1)}, u32[]{:S(2)}, u32[]{:S(2)}) collective-permute-start(bf16[4,64,128]{2,1,0:T(8,128)(2,1)S(1)} %get-tuple-element.31.refs_0_), channel_id=1, source_target_pairs={{0,2},{1,3},{2,0},{3,1},{4,6},{5,7},{6,4},{7,5},{8,10},{9,11},{10,... | collective-permute-start | bytes 196616 | tf_op jit(solution)/shard_map/ppermute | solution.py:19
  27.4 1.9 %collective-permute-start.10 = (bf16[4,4,64,128]{3,2,1,0:T(8,128)(2,1)S(1)}, bf16[4,4,64,128]{3,2,1,0:T(8,128)(2,1)S(1)}, u32[]{:S(2)}, u32[]{:S(2)}) collective-permute-start(bf16[4,4,64,128]{3,2,1,0:T(8,128)(2,1)S(1)} %get-tuple-element.32.refs_4_), channel_id=1, source_target_pairs={{0,1},{1,0},{2,3},{3,2},{4,5},{5,4},{6,7},{7,6},{8,9},{9,8},{10,11... | collective-permute-start | bytes 786440 | tf_op jit(solution)/shard_map/ppermute | solution.py:19
  27.5 7.2 %collective-permute-start.14 = (bf16[2,128,256]{2,1,0:T(8,128)(2,1)S(1)}, bf16[2,128,256]{2,1,0:T(8,128)(2,1)S(1)}, u32[]{:S(2)}, u32[]{:S(2)}) collective-permute-start(bf16[2,128,256]{2,1,0:T(8,128)(2,1)S(1)} %get-tuple-element.33.refs_8_), channel_id=1, source_target_pairs={{0,8},{8,0},{16,24},{24,16},{1,9},{9,1},{17,25},{25,17},{2,10},{10... | collective-permute-start | bytes 393224 | tf_op jit(solution)/shard_map/ppermute | solution.py:19
  29.3 10.2 %copy-start.1 = (bf16[256,256]{1,0:T(8,128)(2,1)S(1)}, bf16[256,256]{1,0:T(8,128)(2,1)}, u32[]{:S(2)}) copy-start(bf16[256,256]{1,0:T(8,128)(2,1)} %refs_10_.1) | copy-start | bytes 393220
  30.3 6.8 %collective-permute-start.13 = (bf16[4,64,128]{2,1,0:T(8,128)(2,1)S(1)}, bf16[4,64,128]{2,1,0:T(8,128)(2,1)S(1)}, u32[]{:S(2)}, u32[]{:S(2)}) collective-permute-start(bf16[4,64,128]{2,1,0:T(8,128)(2,1)S(1)} %shard_map.98.refs_4_), channel_id=1, source_target_pairs={{0,24},{8,16},{16,8},{24,0},{1,25},{9,17},{17,9},{25,1},{2,26},{10... | collective-permute-start | bytes 196616 | tf_op jit(solution)/shard_map/ppermute | solution.py:19
  31.7 7.8 %collective-permute-start.12 = (bf16[4,64,128]{2,1,0:T(8,128)(2,1)S(1)}, bf16[4,64,128]{2,1,0:T(8,128)(2,1)S(1)}, u32[]{:S(2)}, u32[]{:S(2)}) collective-permute-start(bf16[4,64,128]{2,1,0:T(8,128)(2,1)S(1)} %shard_map.98.refs_4_), channel_id=1, source_target_pairs={{0,16},{8,24},{16,0},{24,8},{1,17},{9,25},{17,1},{25,9},{2,18},{10... | collective-permute-start | bytes 196616 | tf_op jit(solution)/shard_map/ppermute | solution.py:19
  33.0 6.5 %collective-permute-start.11 = (bf16[4,64,128]{2,1,0:T(8,128)(2,1)S(1)}, bf16[4,64,128]{2,1,0:T(8,128)(2,1)S(1)}, u32[]{:S(2)}, u32[]{:S(2)}) collective-permute-start(bf16[4,64,128]{2,1,0:T(8,128)(2,1)S(1)} %shard_map.98.refs_4_), channel_id=1, source_target_pairs={{0,8},{8,0},{16,24},{24,16},{1,9},{9,1},{17,25},{25,17},{2,10},{10... | collective-permute-start | bytes 196616 | tf_op jit(solution)/shard_map/ppermute | solution.py:19
  41.3 2.1 %collective-permute-start.15 = (bf16[5,128,256]{2,1,0:T(8,128)(2,1)S(1)}, bf16[5,128,256]{2,1,0:T(8,128)(2,1)S(1)}, u32[]{:S(2)}, u32[]{:S(2)}) collective-permute-start(bf16[5,128,256]{2,1,0:T(8,128)(2,1)S(1)} %get-tuple-element.36), channel_id=1, source_target_pairs={{0,1},{1,0},{2,3},{3,2},{4,5},{5,4},{6,7},{7,6},{8,9},{9,8},{10,11... | collective-permute-start | bytes 983048 | tf_op jit(solution)/shard_map/ppermute | solution.py:19
  43.4 7.3 %collective-permute-start.16 = (bf16[256,256]{1,0:T(8,128)(2,1)S(1)}, bf16[256,256]{1,0:T(8,128)(2,1)S(1)}, u32[]{:S(2)}, u32[]{:S(2)}) collective-permute-start(bf16[256,256]{1,0:T(8,128)(2,1)S(1)} %get-tuple-element.39), channel_id=1, source_target_pairs={{0,6},{1,7},{2,4},{3,5},{4,2},{5,3},{6,0},{7,1},{8,14},{9,15},{10,... | collective-permute-start | bytes 393224 | tf_op jit(solution)/shard_map/ppermute | solution.py:19
  44.8 7.6 %collective-permute-start.17 = (bf16[256,256]{1,0:T(8,128)(2,1)S(1)}, bf16[256,256]{1,0:T(8,128)(2,1)S(1)}, u32[]{:S(2)}, u32[]{:S(2)}) collective-permute-start(bf16[256,256]{1,0:T(8,128)(2,1)S(1)} %get-tuple-element.40), channel_id=1, source_target_pairs={{0,4},{1,5},{2,6},{3,7},{4,0},{5,1},{6,2},{7,3},{8,12},{9,13},{10,... | collective-permute-start | bytes 393224 | tf_op jit(solution)/shard_map/ppermute | solution.py:19
  45.6 7.2 %collective-permute-start.18 = (bf16[256,256]{1,0:T(8,128)(2,1)S(1)}, bf16[256,256]{1,0:T(8,128)(2,1)S(1)}, u32[]{:S(2)}, u32[]{:S(2)}) collective-permute-start(bf16[256,256]{1,0:T(8,128)(2,1)S(1)} %get-tuple-element.41), channel_id=1, source_target_pairs={{0,2},{1,3},{2,0},{3,1},{4,6},{5,7},{6,4},{7,5},{8,10},{9,11},{10,... | collective-permute-start | bytes 393224 | tf_op jit(solution)/shard_map/ppermute | solution.py:19
  52.9 1.4 %collective-permute-start.19 = (f32[128,256]{1,0:T(8,128)S(1)}, f32[128,256]{1,0:T(8,128)S(1)}, u32[]{:S(2)}, u32[]{:S(2)}) collective-permute-start(f32[128,256]{1,0:T(8,128)S(1)} %get-tuple-element.45.mine), channel_id=1, source_target_pairs={{0,1},{1,0},{2,3},{3,2},{4,5},{5,4},{6,7},{7,6},{8,9},{9,8},{10,11... | collective-permute-start | bytes 393224 | tf_op jit(solution)/shard_map/ppermute | solution.py:19

commit v12 on v10

--- a/solution.py
+++ b/solution.py
@@ -71,7 +71,7 @@
 
 def order_chunks(reps, part, *refs):
     copies = reps // 2 - 1
-    chunks, sources, unread = refs[:reps], refs[reps : reps + copies], refs[reps + copies]
+    chunks, unread, sources = refs[:reps], refs[reps], refs[reps + 1 : reps + 1 + copies]
     mine, index = refs[reps + copies + 1 : reps + copies + 3]
     for source, target in zip(sources, refs[reps + copies + 3 :]):
         target[...] = source[...]
@@ -215,8 +215,8 @@
         return [arrays[0]] + [swap(arrays[x], "rep", x) for x in range(1, reps)]
 
     adjacency = block_vals.reshape(slots, block, block)
+    odds = [swap(adjacency, "rep", 1)]
     evens = spread(adjacency, 2)
-    odds = [swap(adjacency, "rep", 1)]
     chunks = call(
         functools.partial(split_features, reps, lists, cap),
         [like((part + PAD, nodes), BF16)] * reps,
@@ -228,9 +228,9 @@
         functools.partial(order_chunks, reps, part),
         [like((reps, part, nodes), BF16), like((reps, 1, nodes), jnp.int32)]
         + [like((slots, block, block), BF16)] * (reps // 2 - 1),
-        [VMEM] * (reps + reps // 2 - 1) + [pl.BlockSpec(memory_space=pl.ANY)],
+        [VMEM] * reps + [pl.BlockSpec(memory_space=pl.ANY)] + [VMEM] * (reps // 2 - 1),
         moved=4 * nodes * width,
-    )(*direct(chunks), *evens[1:], odds[0])
+    )(*direct(chunks), odds[0], *evens[1:])
     odds += [swap(array, "rep", 1) for array in relayed]
     blocks = [array for pair in zip(evens, odds) for array in pair]
 

time: 55.3 us -> 54.9 us (level)
  waiting for transfers between devices: 19.9 us -> 18.8 us
    ppermute x20, waiting for transfers between devices: 19.9 us -> 18.8 us  [swap(): return lax.ppermute(array, axis, [(i, i ^ bit) for i in range(peers)])]
where the time goes in v12:
time: 54.9 us; the launch traced here: 54.5 us
  starting transfers between devices  25.6 us (47%)
  waiting for transfers between devices  18.8 us (34%)
  Pallas kernels  7.44 us (14%)
  local copies, waits for them, and re-layouts  1.93 us (4%)
  between operations  0.76 us (1%)
    ppermute x20, starting transfers between devices, swap(): return lax.ppermute(array, axis, [(i, i ^ bit) for i in range(peers)])  25.6 us
    ppermute x20, waiting for transfers between devices, swap(): return lax.ppermute(array, axis, [(i, i ^ bit) for i in range(peers)])  18.8 us
    unnamed x14, local copies, waits for them, and re-layouts  1.93 us
    pallas_call x1, Pallas kernels, per_device(): call(functools.partial(feature_grads, reps, groups, lists, cap, 0), like(...  1.25 us
  transfers between devices with their start and end apart: 20, of which 12 were waited for; matrix products, arithmetic and copies ran while one was open for 0% of the time, Pallas kernels for 8%

profile of v12, /device:TPU:0, one launch (start us, length us, event | category | flops | bytes accessed | tf_op | source)
XLA Modules:
  0.0 54.5 jit_solution(1333640420044938091)
XLA Ops:
  0.6 4.1 %collective-permute-start.4 = (bf16[6,128,128]{2,1,0:T(8,128)(2,1)}, bf16[6,128,128]{2,1,0:T(8,128)(2,1)S(1)}, u32[]{:S(2)}, u32[]{:S(2)}) collective-permute-start(bf16[6,128,128]{2,1,0:T(8,128)(2,1)} %bitcast.4), channel_id=1, source_target_pairs={{0,16},{8,24},{16,0},{24,8},{1,17},{9,25},{17,1},{25,9},{2,18},{10... | collective-permute-start | bytes 589832 | tf_op jit(solution)/shard_map/ppermute | solution.py:19
  4.7 1.6 %collective-permute-start.3 = (bf16[6,128,128]{2,1,0:T(8,128)(2,1)}, bf16[6,128,128]{2,1,0:T(8,128)(2,1)S(1)}, u32[]{:S(2)}, u32[]{:S(2)}) collective-permute-start(bf16[6,128,128]{2,1,0:T(8,128)(2,1)} %bitcast.5), channel_id=1, source_target_pairs={{0,8},{8,0},{16,24},{24,16},{1,9},{9,1},{17,25},{25,17},{2,10},{10... | collective-permute-start | bytes 589832 | tf_op jit(solution)/shard_map/ppermute | solution.py:19
  6.3 0.7 %copy-done.4 = s32[1,1,2,3]{3,2,1,0:T(2,128)S(1)} copy-done((s32[1,1,2,3]{3,2,1,0:T(2,128)S(1)}, s32[1,1,2,3]{3,2,1,0:T(2,128)}, u32[]{:S(2)}) %copy-start.4) | copy-done | bytes 48
  7.0 0.0 copy-done.3
  7.0 0.8 %copy-done.2 = bf16[128,256]{1,0:T(8,128)(2,1)S(1)} copy-done((bf16[128,256]{1,0:T(8,128)(2,1)S(1)}, bf16[128,256]{1,0:T(8,128)(2,1)}, u32[]{:S(2)}) %copy-start.2) | copy-done | bytes 65560
  7.8 0.7 %shard_map.94 = (bf16[80,128]{1,0:T(8,128)(2,1)S(1)}, bf16[80,128]{1,0:T(8,128)(2,1)S(1)}, bf16[80,128]{1,0:T(8,128)(2,1)S(1)}, bf16[80,128]{1,0:T(8,128)(2,1)S(1)}) custom-call(bf16[128,256]{1,0:T(8,128)(2,1)S(1)} %copy-done.2, s32[2,3]{1,0:T(2,128)S(1)} %bitcast.10, s32[2,3]{1,0:T(2,128)S(1)} %bitcast.11, s32[2]{0:T(128)S(1)} %bitcast.12), custom_call_target="tpu_custom_call" | custom-call | bytes 131072 | tf_op jit(solution)/shard_map/pallas_call | solution.py:220
  8.5 0.5 collective-permute-start
  9.0 0.1 collective-permute-start.1
  9.1 3.9 %collective-permute-start.2 = (bf16[80,128]{1,0:T(8,128)(2,1)S(1)}, bf16[80,128]{1,0:T(8,128)(2,1)S(1)}, u32[]{:S(2)}, u32[]{:S(2)}) collective-permute-start(bf16[80,128]{1,0:T(8,128)(2,1)S(1)} %get-tuple-element.27), channel_id=1, source_target_pairs={{0,24},{8,16},{16,8},{24,0},{1,25},{9,17},{17,9},{25,1},{2,26},{10... | collective-permute-start | bytes 61448 | tf_op jit(solution)/shard_map/ppermute | solution.py:19
  13.0 2.5 %collective-permute-done.refs_1_ = bf16[80,128]{1,0:T(8,128)(2,1)S(1)} collective-permute-done((bf16[80,128]{1,0:T(8,128)(2,1)S(1)}, bf16[80,128]{1,0:T(8,128)(2,1)S(1)}, u32[]{:S(2)}, u32[]{:S(2)}) %collective-permute-start) | collective-permute-done | bytes 20512 | tf_op jit(solution)/shard_map/ppermute | solution.py:19
  15.5 1.0 %collective-permute-done.2.refs_3_ = bf16[80,128]{1,0:T(8,128)(2,1)S(1)} collective-permute-done((bf16[80,128]{1,0:T(8,128)(2,1)S(1)}, bf16[80,128]{1,0:T(8,128)(2,1)S(1)}, u32[]{:S(2)}, u32[]{:S(2)}) %collective-permute-start.2) | collective-permute-done | bytes 20512 | tf_op jit(solution)/shard_map/ppermute | solution.py:19
  16.5 0.0 collective-permute-done.3.refs_4_.refs_1_
  16.5 0.4 collective-permute-start.5
  17.0 0.4 copy-done.1
  17.3 2.4 %collective-permute-start.9 = (bf16[128,256]{1,0:T(8,128)(2,1)S(1)}, bf16[128,256]{1,0:T(8,128)(2,1)S(1)}, u32[]{:S(2)}, u32[]{:S(2)}) collective-permute-start(bf16[128,256]{1,0:T(8,128)(2,1)S(1)} %copy-done.1), channel_id=1, source_target_pairs={{0,16},{8,24},{16,0},{24,8},{1,17},{9,25},{17,1},{25,9},{2,18},{10... | collective-permute-start | bytes 196616 | tf_op jit(solution)/shard_map/ppermute | solution.py:19
  19.7 2.4 %collective-permute-start.8 = (bf16[4,64,128]{2,1,0:T(8,128)(2,1)S(1)}, bf16[4,64,128]{2,1,0:T(8,128)(2,1)S(1)}, u32[]{:S(2)}, u32[]{:S(2)}) collective-permute-start(bf16[4,64,128]{2,1,0:T(8,128)(2,1)S(1)} %get-tuple-element.30.refs_0_), channel_id=1, source_target_pairs={{0,6},{1,7},{2,4},{3,5},{4,2},{5,3},{6,0},{7,1},{8,14},{9,15},{10,... | collective-permute-start | bytes 196616 | tf_op jit(solution)/shard_map/ppermute | solution.py:19
  22.2 0.5 collective-permute-start.7
  22.7 0.5 collective-permute-start.6
  23.2 1.8 %collective-permute-done.8.refs_3_ = bf16[4,64,128]{2,1,0:T(8,128)(2,1)S(1)} collective-permute-done((bf16[4,64,128]{2,1,0:T(8,128)(2,1)S(1)}, bf16[4,64,128]{2,1,0:T(8,128)(2,1)S(1)}, u32[]{:S(2)}, u32[]{:S(2)}) %collective-permute-start.8) | collective-permute-done | bytes 65568 | tf_op jit(solution)/shard_map/ppermute | solution.py:19
  25.0 1.4 %collective-permute-done.7.refs_2_ = bf16[4,64,128]{2,1,0:T(8,128)(2,1)S(1)} collective-permute-done((bf16[4,64,128]{2,1,0:T(8,128)(2,1)S(1)}, bf16[4,64,128]{2,1,0:T(8,128)(2,1)S(1)}, u32[]{:S(2)}, u32[]{:S(2)}) %collective-permute-start.7) | collective-permute-done | bytes 65568 | tf_op jit(solution)/shard_map/ppermute | solution.py:19
  26.5 0.5 collective-permute-done.6.refs_1_
  27.0 0.1 collective-permute-start.10
  27.1 0.9 %collective-permute-start.14 = (bf16[2,128,256]{2,1,0:T(8,128)(2,1)S(1)}, bf16[2,128,256]{2,1,0:T(8,128)(2,1)S(1)}, u32[]{:S(2)}, u32[]{:S(2)}) collective-permute-start(bf16[2,128,256]{2,1,0:T(8,128)(2,1)S(1)} %get-tuple-element.32.refs_4_), channel_id=1, source_target_pairs={{0,8},{8,0},{16,24},{24,16},{1,9},{9,1},{17,25},{25,17},{2,10},{10... | collective-permute-start | bytes 393224 | tf_op jit(solution)/shard_map/ppermute | solution.py:19
  28.0 1.0 %shard_map.97.refs_5_ = f32[4,64,128]{2,1,0:T(8,128)S(1)} custom-call(s32[4,1,128]{2,1,0:T(1,128)S(1)} %get-tuple-element.28.index, bf16[6,128,128]{2,1,0:T(8,128)(2,1)S(1)} %bitcast.6, bf16[6,128,128]{2,1,0:T(8,128)(2,1)S(1)} %collective-permute-done.3.refs_4_.refs_1_, bf16[6,128,128]{2,1,0:T(8,128)(2,1)S(1)} %collective-permute-done.4.refs_5_.refs_2_, ...), custom_call_target="tpu_custom_call" | custom-call | flops 25165824 | bytes 655360 | tf_op jit(solution)/shard_map/pallas_call | solution.py:252
  29.0 0.0 copy-start.6
  29.0 0.9 %shard_map.98.refs_0_ = bf16[4,64,128]{2,1,0:T(8,128)(2,1)S(1)} custom-call(s32[4,1,128]{2,1,0:T(1,128)S(1)} %get-tuple-element.28.index, bf16[6,128,128]{2,1,0:T(8,128)(2,1)S(1)} %bitcast.7, bf16[6,128,128]{2,1,0:T(8,128)(2,1)S(1)} %collective-permute-done.3.refs_4_.refs_1_, bf16[6,128,128]{2,1,0:T(8,128)(2,1)S(1)} %collective-permute-done.4.refs_5_.refs_2_, ...), custom_call_target="tpu_custom_call" | custom-call | flops 25165824 | bytes 655360 | tf_op jit(solution)/shard_map/pallas_call | solution.py:260
  29.9 1.2 %collective-permute-start.13 = (bf16[4,64,128]{2,1,0:T(8,128)(2,1)S(1)}, bf16[4,64,128]{2,1,0:T(8,128)(2,1)S(1)}, u32[]{:S(2)}, u32[]{:S(2)}) collective-permute-start(bf16[4,64,128]{2,1,0:T(8,128)(2,1)S(1)} %shard_map.98.refs_0_), channel_id=1, source_target_pairs={{0,24},{8,16},{16,8},{24,0},{1,25},{9,17},{17,9},{25,1},{2,26},{10... | collective-permute-start | bytes 196616 | tf_op jit(solution)/shard_map/ppermute | solution.py:19
  31.1 1.5 %collective-permute-start.12 = (bf16[4,64,128]{2,1,0:T(8,128)(2,1)S(1)}, bf16[4,64,128]{2,1,0:T(8,128)(2,1)S(1)}, u32[]{:S(2)}, u32[]{:S(2)}) collective-permute-start(bf16[4,64,128]{2,1,0:T(8,128)(2,1)S(1)} %shard_map.98.refs_0_), channel_id=1, source_target_pairs={{0,16},{8,24},{16,0},{24,8},{1,17},{9,25},{17,1},{25,9},{2,18},{10... | collective-permute-start | bytes 196616 | tf_op jit(solution)/shard_map/ppermute | solution.py:19
  32.6 1.8 %collective-permute-start.11 = (bf16[4,64,128]{2,1,0:T(8,128)(2,1)S(1)}, bf16[4,64,128]{2,1,0:T(8,128)(2,1)S(1)}, u32[]{:S(2)}, u32[]{:S(2)}) collective-permute-start(bf16[4,64,128]{2,1,0:T(8,128)(2,1)S(1)} %shard_map.98.refs_0_), channel_id=1, source_target_pairs={{0,8},{8,0},{16,24},{24,16},{1,9},{9,1},{17,25},{25,17},{2,10},{10... | collective-permute-start | bytes 196616 | tf_op jit(solution)/shard_map/ppermute | solution.py:19
  34.4 2.4 %collective-permute-done.13.refs_3_ = bf16[4,64,128]{2,1,0:T(8,128)(2,1)S(1)} collective-permute-done((bf16[4,64,128]{2,1,0:T(8,128)(2,1)S(1)}, bf16[4,64,128]{2,1,0:T(8,128)(2,1)S(1)}, u32[]{:S(2)}, u32[]{:S(2)}) %collective-permute-start.13) | collective-permute-done | bytes 65568 | tf_op jit(solution)/shard_map/ppermute | solution.py:19
  36.8 2.3 %collective-permute-done.12.refs_2_ = bf16[4,64,128]{2,1,0:T(8,128)(2,1)S(1)} collective-permute-done((bf16[4,64,128]{2,1,0:T(8,128)(2,1)S(1)}, bf16[4,64,128]{2,1,0:T(8,128)(2,1)S(1)}, u32[]{:S(2)}, u32[]{:S(2)}) %collective-permute-start.12) | collective-permute-done | bytes 65568 | tf_op jit(solution)/shard_map/ppermute | solution.py:19
  39.1 0.9 %shard_map.99 = (bf16[128,256]{1,0:T(8,128)(2,1)S(1)}, bf16[4,128,256]{2,1,0:T(8,128)(2,1)S(1)}, bf16[2,128,256]{2,1,0:T(8,128)(2,1)S(1)}) custom-call(bf16[4,64,128]{2,1,0:T(8,128)(2,1)S(1)} %shard_map.98.refs_0_, bf16[4,64,128]{2,1,0:T(8,128)(2,1)S(1)} %collective-permute-done.11.refs_1_, bf16[4,64,128]{2,1,0:T(8,128)(2,1)S(1)} %collective-permute-done.12.refs_2_, ...), custom_call_target="tpu_custom_call" | custom-call | flops 201326592 | bytes 1310720 | tf_op jit(solution)/shard_map/pallas_call | solution.py:269
  40.0 1.1 %shard_map.101 = bf16[5,128,256]{2,1,0:T(8,128)(2,1)S(1)} custom-call(s32[4,1,128]{2,1,0:T(1,128)S(1)} %get-tuple-element.28.index, bf16[6,128,128]{2,1,0:T(8,128)(2,1)S(1)} %bitcast.8, bf16[6,128,128]{2,1,0:T(8,128)(2,1)S(1)} %collective-permute-done.3.refs_4_.refs_1_, bf16[6,128,128]{2,1,0:T(8,128)(2,1)S(1)} %collective-permute-done.4.refs_5_.refs_2_, ...), custom_call_target="tpu_custom_call" | custom-call | flops 25165824 | bytes 655360 | tf_op jit(solution)/shard_map/pallas_call | solution.py:286
  41.1 0.1 collective-permute-start.15
  41.2 1.3 %shard_map.100.keep = f32[4,128,256]{2,1,0:T(8,128)S(1)} custom-call(s32[4,1,128]{2,1,0:T(1,128)S(1)} %get-tuple-element.28.index, bf16[6,128,128]{2,1,0:T(8,128)(2,1)S(1)} %bitcast.9, bf16[6,128,128]{2,1,0:T(8,128)(2,1)S(1)} %collective-permute-done.3.refs_4_.refs_1_, bf16[6,128,128]{2,1,0:T(8,128)(2,1)S(1)} %collective-permute-done.4.refs_5_.refs_2_, ...), custom_call_target="tpu_custom_call" | custom-call | flops 25165824 | bytes 655360 | tf_op jit(solution)/shard_map/pallas_call | solution.py:294
  42.4 0.4 collective-permute-done.15.arrived
  42.8 0.1 shard_map.102
  42.9 1.7 %collective-permute-start.16 = (bf16[256,256]{1,0:T(8,128)(2,1)S(1)}, bf16[256,256]{1,0:T(8,128)(2,1)S(1)}, u32[]{:S(2)}, u32[]{:S(2)}) collective-permute-start(bf16[256,256]{1,0:T(8,128)(2,1)S(1)} %get-tuple-element.37), channel_id=1, source_target_pairs={{0,6},{1,7},{2,4},{3,5},{4,2},{5,3},{6,0},{7,1},{8,14},{9,15},{10,... | collective-permute-start | bytes 393224 | tf_op jit(solution)/shard_map/ppermute | solution.py:19
  44.6 0.0 collective-permute-start.17
  44.6 1.8 %collective-permute-start.18 = (bf16[256,256]{1,0:T(8,128)(2,1)S(1)}, bf16[256,256]{1,0:T(8,128)(2,1)S(1)}, u32[]{:S(2)}, u32[]{:S(2)}) collective-permute-start(bf16[256,256]{1,0:T(8,128)(2,1)S(1)} %get-tuple-element.39), channel_id=1, source_target_pairs={{0,2},{1,3},{2,0},{3,1},{4,6},{5,7},{6,4},{7,5},{8,10},{9,11},{10,... | collective-permute-start | bytes 393224 | tf_op jit(solution)/shard_map/ppermute | solution.py:19
  46.4 3.8 %collective-permute-done.16.refs_0_ = bf16[256,256]{1,0:T(8,128)(2,1)S(1)} collective-permute-done((bf16[256,256]{1,0:T(8,128)(2,1)S(1)}, bf16[256,256]{1,0:T(8,128)(2,1)S(1)}, u32[]{:S(2)}, u32[]{:S(2)}) %collective-permute-start.16) | collective-permute-done | bytes 131104 | tf_op jit(solution)/shard_map/ppermute | solution.py:19
  50.2 2.0 %collective-permute-done.17.refs_1_ = bf16[256,256]{1,0:T(8,128)(2,1)S(1)} collective-permute-done((bf16[256,256]{1,0:T(8,128)(2,1)S(1)}, bf16[256,256]{1,0:T(8,128)(2,1)S(1)}, u32[]{:S(2)}, u32[]{:S(2)}) %collective-permute-start.17) | collective-permute-done | bytes 131104 | tf_op jit(solution)/shard_map/ppermute | solution.py:19
  52.2 0.1 collective-permute-done.18.refs_2_
  52.3 0.1 shard_map.103
  52.4 0.1 collective-permute-start.19
  52.5 0.7 %shard_map.104 = (f32[128,256]{1,0:T(8,128)}, bf16[128,256]{1,0:T(8,128)(2,1)}) custom-call(f32[128,256]{1,0:T(8,128)S(1)} %get-tuple-element.40.grads, bf16[128,256]{1,0:T(8,128)(2,1)S(1)} %get-tuple-element.41.rows), custom_call_target="tpu_custom_call" | custom-call | bytes 393216 | tf_op jit(solution)/shard_map/pallas_call | solution.py:315
  53.2 0.6 %collective-permute-done.19.arrived = f32[128,256]{1,0:T(8,128)S(1)} collective-permute-done((f32[128,256]{1,0:T(8,128)S(1)}, f32[128,256]{1,0:T(8,128)S(1)}, u32[]{:S(2)}, u32[]{:S(2)}) %collective-permute-start.19) | collective-permute-done | bytes 131104 | tf_op jit(solution)/shard_map/ppermute | solution.py:19
  53.8 0.7 %shard_map.105 = f32[256,256]{1,0:T(8,128)} custom-call(f32[128,256]{1,0:T(8,128)S(1)} %get-tuple-element.43.mine, f32[128,256]{1,0:T(8,128)S(1)} %collective-permute-done.19.arrived), custom_call_target="tpu_custom_call" | custom-call | bytes 524288 | tf_op jit(solution)/shard_map/pallas_call | solution.py:321
  (18 shorter events, 0.1 us)
Async XLA Ops:
  0.6 15.9 %collective-permute-start.4 = (bf16[6,128,128]{2,1,0:T(8,128)(2,1)}, bf16[6,128,128]{2,1,0:T(8,128)(2,1)S(1)}, u32[]{:S(2)}, u32[]{:S(2)}) collective-permute-start(bf16[6,128,128]{2,1,0:T(8,128)(2,1)} %bitcast.4), channel_id=1, source_target_pairs={{0,16},{8,24},{16,0},{24,8},{1,17},{9,25},{17,1},{25,9},{2,18},{10... | collective-permute-start | bytes 589832 | tf_op jit(solution)/shard_map/ppermute | solution.py:19
  4.7 11.8 %collective-permute-start.3 = (bf16[6,128,128]{2,1,0:T(8,128)(2,1)}, bf16[6,128,128]{2,1,0:T(8,128)(2,1)S(1)}, u32[]{:S(2)}, u32[]{:S(2)}) collective-permute-start(bf16[6,128,128]{2,1,0:T(8,128)(2,1)} %bitcast.5), channel_id=1, source_target_pairs={{0,8},{8,0},{16,24},{24,16},{1,9},{9,1},{17,25},{25,17},{2,10},{10... | collective-permute-start | bytes 589832 | tf_op jit(solution)/shard_map/ppermute | solution.py:19
  6.3 0.7 %copy-start.4 = (s32[1,1,2,3]{3,2,1,0:T(2,128)S(1)}, s32[1,1,2,3]{3,2,1,0:T(2,128)}, u32[]{:S(2)}) copy-start(s32[1,1,2,3]{3,2,1,0:T(2,128)} %param.12) | copy-start | bytes 76
  6.3 0.7 %copy-start.3 = (s32[1,1,2,3]{3,2,1,0:T(2,128)S(1)}, s32[1,1,2,3]{3,2,1,0:T(2,128)}, u32[]{:S(2)}) copy-start(s32[1,1,2,3]{3,2,1,0:T(2,128)} %param.11) | copy-start | bytes 76
  6.3 0.7 %copy-start.5 = (s32[1,1,2]{2,1,0:T(1,128)S(1)}, s32[1,1,2]{2,1,0:T(1,128)}, u32[]{:S(2)}) copy-start(s32[1,1,2]{2,1,0:T(1,128)} %param.13) | copy-start | bytes 28
  7.0 0.8 %copy-start.2 = (bf16[128,256]{1,0:T(8,128)(2,1)S(1)}, bf16[128,256]{1,0:T(8,128)(2,1)}, u32[]{:S(2)}) copy-start(bf16[128,256]{1,0:T(8,128)(2,1)} %feats.1) | copy-start | bytes 196612
  8.5 6.9 %collective-permute-start = (bf16[80,128]{1,0:T(8,128)(2,1)S(1)}, bf16[80,128]{1,0:T(8,128)(2,1)S(1)}, u32[]{:S(2)}, u32[]{:S(2)}) collective-permute-start(bf16[80,128]{1,0:T(8,128)(2,1)S(1)} %get-tuple-element.25), channel_id=1, source_target_pairs={{0,8},{8,0},{16,24},{24,16},{1,9},{9,1},{17,25},{25,17},{2,10},{10... | collective-permute-start | bytes 61448 | tf_op jit(solution)/shard_map/ppermute | solution.py:19
  9.0 6.4 %collective-permute-start.1 = (bf16[80,128]{1,0:T(8,128)(2,1)S(1)}, bf16[80,128]{1,0:T(8,128)(2,1)S(1)}, u32[]{:S(2)}, u32[]{:S(2)}) collective-permute-start(bf16[80,128]{1,0:T(8,128)(2,1)S(1)} %get-tuple-element.26), channel_id=1, source_target_pairs={{0,16},{8,24},{16,0},{24,8},{1,17},{9,25},{17,1},{25,9},{2,18},{10... | collective-permute-start | bytes 61448 | tf_op jit(solution)/shard_map/ppermute | solution.py:19
  9.1 7.4 %collective-permute-start.2 = (bf16[80,128]{1,0:T(8,128)(2,1)S(1)}, bf16[80,128]{1,0:T(8,128)(2,1)S(1)}, u32[]{:S(2)}, u32[]{:S(2)}) collective-permute-start(bf16[80,128]{1,0:T(8,128)(2,1)S(1)} %get-tuple-element.27), channel_id=1, source_target_pairs={{0,24},{8,16},{16,8},{24,0},{1,25},{9,17},{17,9},{25,1},{2,26},{10... | collective-permute-start | bytes 61448 | tf_op jit(solution)/shard_map/ppermute | solution.py:19
  16.5 0.8 %copy-start.1 = (bf16[128,256]{1,0:T(8,128)(2,1)S(1)}, bf16[128,256]{1,0:T(8,128)(2,1)}, u32[]{:S(2)}) copy-start(bf16[128,256]{1,0:T(8,128)(2,1)} %refs_4_.1) | copy-start | bytes 196612
  16.5 10.4 %collective-permute-start.5 = (bf16[6,128,128]{2,1,0:T(8,128)(2,1)S(1)}, bf16[6,128,128]{2,1,0:T(8,128)(2,1)S(1)}, u32[]{:S(2)}, u32[]{:S(2)}) collective-permute-start(bf16[6,128,128]{2,1,0:T(8,128)(2,1)S(1)} %get-tuple-element.29), channel_id=1, source_target_pairs={{0,8},{8,0},{16,24},{24,16},{1,9},{9,1},{17,25},{25,17},{2,10},{10... | collective-permute-start | bytes 589832 | tf_op jit(solution)/shard_map/ppermute | solution.py:19
  17.3 5.9 %collective-permute-start.9 = (bf16[128,256]{1,0:T(8,128)(2,1)S(1)}, bf16[128,256]{1,0:T(8,128)(2,1)S(1)}, u32[]{:S(2)}, u32[]{:S(2)}) collective-permute-start(bf16[128,256]{1,0:T(8,128)(2,1)S(1)} %copy-done.1), channel_id=1, source_target_pairs={{0,16},{8,24},{16,0},{24,8},{1,17},{9,25},{17,1},{25,9},{2,18},{10... | collective-permute-start | bytes 196616 | tf_op jit(solution)/shard_map/ppermute | solution.py:19
  19.7 8.3 %copy-start = (bf16[1,1,2,3,128,128]{5,4,3,2,1,0:T(8,128)(2,1)S(1)}, bf16[1,1,2,3,128,128]{5,4,3,2,1,0:T(8,128)(2,1)}, u32[]{:S(2)}) copy-start(bf16[1,1,2,3,128,128]{5,4,3,2,1,0:T(8,128)(2,1)} %param.10) | copy-start | bytes 589828
  19.7 5.3 %collective-permute-start.8 = (bf16[4,64,128]{2,1,0:T(8,128)(2,1)S(1)}, bf16[4,64,128]{2,1,0:T(8,128)(2,1)S(1)}, u32[]{:S(2)}, u32[]{:S(2)}) collective-permute-start(bf16[4,64,128]{2,1,0:T(8,128)(2,1)S(1)} %get-tuple-element.30.refs_0_), channel_id=1, source_target_pairs={{0,6},{1,7},{2,4},{3,5},{4,2},{5,3},{6,0},{7,1},{8,14},{9,15},{10,... | collective-permute-start | bytes 196616 | tf_op jit(solution)/shard_map/ppermute | solution.py:19
  22.2 4.3 %collective-permute-start.7 = (bf16[4,64,128]{2,1,0:T(8,128)(2,1)S(1)}, bf16[4,64,128]{2,1,0:T(8,128)(2,1)S(1)}, u32[]{:S(2)}, u32[]{:S(2)}) collective-permute-start(bf16[4,64,128]{2,1,0:T(8,128)(2,1)S(1)} %get-tuple-element.30.refs_0_), channel_id=1, source_target_pairs={{0,4},{1,5},{2,6},{3,7},{4,0},{5,1},{6,2},{7,3},{8,12},{9,13},{10,... | collective-permute-start | bytes 196616 | tf_op jit(solution)/shard_map/ppermute | solution.py:19
  22.7 4.3 %collective-permute-start.6 = (bf16[4,64,128]{2,1,0:T(8,128)(2,1)S(1)}, bf16[4,64,128]{2,1,0:T(8,128)(2,1)S(1)}, u32[]{:S(2)}, u32[]{:S(2)}) collective-permute-start(bf16[4,64,128]{2,1,0:T(8,128)(2,1)S(1)} %get-tuple-element.30.refs_0_), channel_id=1, source_target_pairs={{0,2},{1,3},{2,0},{3,1},{4,6},{5,7},{6,4},{7,5},{8,10},{9,11},{10,... | collective-permute-start | bytes 196616 | tf_op jit(solution)/shard_map/ppermute | solution.py:19
  27.0 2.0 %collective-permute-start.10 = (bf16[4,4,64,128]{3,2,1,0:T(8,128)(2,1)S(1)}, bf16[4,4,64,128]{3,2,1,0:T(8,128)(2,1)S(1)}, u32[]{:S(2)}, u32[]{:S(2)}) collective-permute-start(bf16[4,4,64,128]{3,2,1,0:T(8,128)(2,1)S(1)} %get-tuple-element.31.refs_4_), channel_id=1, source_target_pairs={{0,1},{1,0},{2,3},{3,2},{4,5},{5,4},{6,7},{7,6},{8,9},{9,8},{10,11... | collective-permute-start | bytes 786440 | tf_op jit(solution)/shard_map/ppermute | solution.py:19
  27.1 7.3 %collective-permute-start.14 = (bf16[2,128,256]{2,1,0:T(8,128)(2,1)S(1)}, bf16[2,128,256]{2,1,0:T(8,128)(2,1)S(1)}, u32[]{:S(2)}, u32[]{:S(2)}) collective-permute-start(bf16[2,128,256]{2,1,0:T(8,128)(2,1)S(1)} %get-tuple-element.32.refs_4_), channel_id=1, source_target_pairs={{0,8},{8,0},{16,24},{24,16},{1,9},{9,1},{17,25},{25,17},{2,10},{10... | collective-permute-start | bytes 393224 | tf_op jit(solution)/shard_map/ppermute | solution.py:19
  29.0 10.1 %copy-start.6 = (bf16[256,256]{1,0:T(8,128)(2,1)S(1)}, bf16[256,256]{1,0:T(8,128)(2,1)}, u32[]{:S(2)}) copy-start(bf16[256,256]{1,0:T(8,128)(2,1)} %refs_6_.1) | copy-start | bytes 393220
  29.9 6.8 %collective-permute-start.13 = (bf16[4,64,128]{2,1,0:T(8,128)(2,1)S(1)}, bf16[4,64,128]{2,1,0:T(8,128)(2,1)S(1)}, u32[]{:S(2)}, u32[]{:S(2)}) collective-permute-start(bf16[4,64,128]{2,1,0:T(8,128)(2,1)S(1)} %shard_map.98.refs_0_), channel_id=1, source_target_pairs={{0,24},{8,16},{16,8},{24,0},{1,25},{9,17},{17,9},{25,1},{2,26},{10... | collective-permute-start | bytes 196616 | tf_op jit(solution)/shard_map/ppermute | solution.py:19
  31.1 8.0 %collective-permute-start.12 = (bf16[4,64,128]{2,1,0:T(8,128)(2,1)S(1)}, bf16[4,64,128]{2,1,0:T(8,128)(2,1)S(1)}, u32[]{:S(2)}, u32[]{:S(2)}) collective-permute-start(bf16[4,64,128]{2,1,0:T(8,128)(2,1)S(1)} %shard_map.98.refs_0_), channel_id=1, source_target_pairs={{0,16},{8,24},{16,0},{24,8},{1,17},{9,25},{17,1},{25,9},{2,18},{10... | collective-permute-start | bytes 196616 | tf_op jit(solution)/shard_map/ppermute | solution.py:19
  32.6 6.5 %collective-permute-start.11 = (bf16[4,64,128]{2,1,0:T(8,128)(2,1)S(1)}, bf16[4,64,128]{2,1,0:T(8,128)(2,1)S(1)}, u32[]{:S(2)}, u32[]{:S(2)}) collective-permute-start(bf16[4,64,128]{2,1,0:T(8,128)(2,1)S(1)} %shard_map.98.refs_0_), channel_id=1, source_target_pairs={{0,8},{8,0},{16,24},{24,16},{1,9},{9,1},{17,25},{25,17},{2,10},{10... | collective-permute-start | bytes 196616 | tf_op jit(solution)/shard_map/ppermute | solution.py:19
  41.1 1.7 %collective-permute-start.15 = (bf16[5,128,256]{2,1,0:T(8,128)(2,1)S(1)}, bf16[5,128,256]{2,1,0:T(8,128)(2,1)S(1)}, u32[]{:S(2)}, u32[]{:S(2)}) collective-permute-start(bf16[5,128,256]{2,1,0:T(8,128)(2,1)S(1)} %shard_map.101), channel_id=1, source_target_pairs={{0,1},{1,0},{2,3},{3,2},{4,5},{5,4},{6,7},{7,6},{8,9},{9,8},{10,11... | collective-permute-start | bytes 983048 | tf_op jit(solution)/shard_map/ppermute | solution.py:19
  42.9 7.3 %collective-permute-start.16 = (bf16[256,256]{1,0:T(8,128)(2,1)S(1)}, bf16[256,256]{1,0:T(8,128)(2,1)S(1)}, u32[]{:S(2)}, u32[]{:S(2)}) collective-permute-start(bf16[256,256]{1,0:T(8,128)(2,1)S(1)} %get-tuple-element.37), channel_id=1, source_target_pairs={{0,6},{1,7},{2,4},{3,5},{4,2},{5,3},{6,0},{7,1},{8,14},{9,15},{10,... | collective-permute-start | bytes 393224 | tf_op jit(solution)/shard_map/ppermute | solution.py:19
  44.6 7.6 %collective-permute-start.17 = (bf16[256,256]{1,0:T(8,128)(2,1)S(1)}, bf16[256,256]{1,0:T(8,128)(2,1)S(1)}, u32[]{:S(2)}, u32[]{:S(2)}) collective-permute-start(bf16[256,256]{1,0:T(8,128)(2,1)S(1)} %get-tuple-element.38), channel_id=1, source_target_pairs={{0,4},{1,5},{2,6},{3,7},{4,0},{5,1},{6,2},{7,3},{8,12},{9,13},{10,... | collective-permute-start | bytes 393224 | tf_op jit(solution)/shard_map/ppermute | solution.py:19
  44.6 7.7 %collective-permute-start.18 = (bf16[256,256]{1,0:T(8,128)(2,1)S(1)}, bf16[256,256]{1,0:T(8,128)(2,1)S(1)}, u32[]{:S(2)}, u32[]{:S(2)}) collective-permute-start(bf16[256,256]{1,0:T(8,128)(2,1)S(1)} %get-tuple-element.39), channel_id=1, source_target_pairs={{0,2},{1,3},{2,0},{3,1},{4,6},{5,7},{6,4},{7,5},{8,10},{9,11},{10,... | collective-permute-start | bytes 393224 | tf_op jit(solution)/shard_map/ppermute | solution.py:19
  52.4 1.4 %collective-permute-start.19 = (f32[128,256]{1,0:T(8,128)S(1)}, f32[128,256]{1,0:T(8,128)S(1)}, u32[]{:S(2)}, u32[]{:S(2)}) collective-permute-start(f32[128,256]{1,0:T(8,128)S(1)} %get-tuple-element.43.mine), channel_id=1, source_target_pairs={{0,1},{1,0},{2,3},{3,2},{4,5},{5,4},{6,7},{7,6},{8,9},{9,8},{10,11... | collective-permute-start | bytes 393224 | tf_op jit(solution)/shard_map/ppermute | solution.py:19

commit v13 on v12

--- a/solution.py
+++ b/solution.py
@@ -76,8 +76,8 @@
     for source, target in zip(sources, refs[reps + copies + 3 :]):
         target[...] = source[...]
     for x in range(reps):
-        mine[other("rep", x)] = chunks[x][:part]
-        index[x] = chunks[x][part:].astype(F32).astype(jnp.int32)[:1]
+        mine[other("rep", x)] = chunks[-x][:part]
+        index[x] = chunks[-x][part:].astype(F32).astype(jnp.int32)[:1]
 
 
 def join(half, *refs):
@@ -230,7 +230,7 @@
         + [like((slots, block, block), BF16)] * (reps // 2 - 1),
         [VMEM] * reps + [pl.BlockSpec(memory_space=pl.ANY)] + [VMEM] * (reps // 2 - 1),
         moved=4 * nodes * width,
-    )(*direct(chunks), odds[0], *evens[1:])
+    )(chunks[0], *direct(chunks)[:0:-1], odds[0], *evens[1:])
     odds += [swap(array, "rep", 1) for array in relayed]
     blocks = [array for pair in zip(evens, odds) for array in pair]
 

time: 54.9 us -> 55.4 us (level)
  starting transfers between devices: 25.6 us -> 26.6 us
    ppermute x20, starting transfers between devices: 25.6 us -> 26.6 us  [swap(): return lax.ppermute(array, axis, [(i, i ^ bit) for i in range(peers)])]
  transfers between devices with their start and end apart: 20 -> 20, of which waited for: 12 -> 11; matrix products, arithmetic and copies ran while one was open for 0% -> 0% of each run, Pallas kernels for 8% -> 9%
where the time goes in v13:
time: 55.4 us; the launch traced here: 55 us
  starting transfers between devices  26.6 us (48%)
  waiting for transfers between devices  18.8 us (34%)
  Pallas kernels  7.28 us (13%)
  local copies, waits for them, and re-layouts  1.55 us (3%)
  between operations  0.79 us (1%)
    ppermute x20, starting transfers between devices, swap(): return lax.ppermute(array, axis, [(i, i ^ bit) for i in range(peers)])  26.6 us
    ppermute x20, waiting for transfers between devices, swap(): return lax.ppermute(array, axis, [(i, i ^ bit) for i in range(peers)])  18.8 us
    unnamed x14, local copies, waits for them, and re-layouts  1.55 us
    pallas_call x1, Pallas kernels, per_device(): call(functools.partial(feature_grads, reps, groups, lists, cap, 0), like(...  1.44 us
  transfers between devices with their start and end apart: 20, of which 11 were waited for; matrix products, arithmetic and copies ran while one was open for 0% of the time, Pallas kernels for 9%

profile of v13, /device:TPU:0, one launch (start us, length us, event | category | flops | bytes accessed | tf_op | source)
XLA Modules:
  0.0 55.0 jit_solution(12162889679140913241)
XLA Ops:
  0.6 4.1 %collective-permute-start.4 = (bf16[6,128,128]{2,1,0:T(8,128)(2,1)}, bf16[6,128,128]{2,1,0:T(8,128)(2,1)S(1)}, u32[]{:S(2)}, u32[]{:S(2)}) collective-permute-start(bf16[6,128,128]{2,1,0:T(8,128)(2,1)} %bitcast.4), channel_id=1, source_target_pairs={{0,16},{8,24},{16,0},{24,8},{1,17},{9,25},{17,1},{25,9},{2,18},{10... | collective-permute-start | bytes 589832 | tf_op jit(solution)/shard_map/ppermute | solution.py:19
  4.7 1.6 %collective-permute-start.3 = (bf16[6,128,128]{2,1,0:T(8,128)(2,1)}, bf16[6,128,128]{2,1,0:T(8,128)(2,1)S(1)}, u32[]{:S(2)}, u32[]{:S(2)}) collective-permute-start(bf16[6,128,128]{2,1,0:T(8,128)(2,1)} %bitcast.5), channel_id=1, source_target_pairs={{0,8},{8,0},{16,24},{24,16},{1,9},{9,1},{17,25},{25,17},{2,10},{10... | collective-permute-start | bytes 589832 | tf_op jit(solution)/shard_map/ppermute | solution.py:19
  6.3 0.7 %copy-done.4 = s32[1,1,2,3]{3,2,1,0:T(2,128)S(1)} copy-done((s32[1,1,2,3]{3,2,1,0:T(2,128)S(1)}, s32[1,1,2,3]{3,2,1,0:T(2,128)}, u32[]{:S(2)}) %copy-start.4) | copy-done | bytes 48
  7.0 0.0 copy-done.3
  7.0 0.8 %copy-done.2 = bf16[128,256]{1,0:T(8,128)(2,1)S(1)} copy-done((bf16[128,256]{1,0:T(8,128)(2,1)S(1)}, bf16[128,256]{1,0:T(8,128)(2,1)}, u32[]{:S(2)}) %copy-start.2) | copy-done | bytes 65560
  7.8 0.7 %shard_map.94 = (bf16[80,128]{1,0:T(8,128)(2,1)S(1)}, bf16[80,128]{1,0:T(8,128)(2,1)S(1)}, bf16[80,128]{1,0:T(8,128)(2,1)S(1)}, bf16[80,128]{1,0:T(8,128)(2,1)S(1)}) custom-call(bf16[128,256]{1,0:T(8,128)(2,1)S(1)} %copy-done.2, s32[2,3]{1,0:T(2,128)S(1)} %bitcast.10, s32[2,3]{1,0:T(2,128)S(1)} %bitcast.11, s32[2]{0:T(128)S(1)} %bitcast.12), custom_call_target="tpu_custom_call" | custom-call | bytes 131072 | tf_op jit(solution)/shard_map/pallas_call | solution.py:220
  8.5 0.1 collective-permute-start
  8.6 1.9 %collective-permute-start.1 = (bf16[80,128]{1,0:T(8,128)(2,1)S(1)}, bf16[80,128]{1,0:T(8,128)(2,1)S(1)}, u32[]{:S(2)}, u32[]{:S(2)}) collective-permute-start(bf16[80,128]{1,0:T(8,128)(2,1)S(1)} %get-tuple-element.26), channel_id=1, source_target_pairs={{0,16},{8,24},{16,0},{24,8},{1,17},{9,25},{17,1},{25,9},{2,18},{10... | collective-permute-start | bytes 61448 | tf_op jit(solution)/shard_map/ppermute | solution.py:19
  10.5 2.5 %collective-permute-start.2 = (bf16[80,128]{1,0:T(8,128)(2,1)S(1)}, bf16[80,128]{1,0:T(8,128)(2,1)S(1)}, u32[]{:S(2)}, u32[]{:S(2)}) collective-permute-start(bf16[80,128]{1,0:T(8,128)(2,1)S(1)} %get-tuple-element.27), channel_id=1, source_target_pairs={{0,8},{8,0},{16,24},{24,16},{1,9},{9,1},{17,25},{25,17},{2,10},{10... | collective-permute-start | bytes 61448 | tf_op jit(solution)/shard_map/ppermute | solution.py:19
  13.0 3.1 %collective-permute-done.refs_1_ = bf16[80,128]{1,0:T(8,128)(2,1)S(1)} collective-permute-done((bf16[80,128]{1,0:T(8,128)(2,1)S(1)}, bf16[80,128]{1,0:T(8,128)(2,1)S(1)}, u32[]{:S(2)}, u32[]{:S(2)}) %collective-permute-start) | collective-permute-done | bytes 20512 | tf_op jit(solution)/shard_map/ppermute | solution.py:19
  16.0 0.0 collective-permute-done.1.refs_2_
  16.0 0.0 collective-permute-done.2.refs_3_
  16.1 0.0 collective-permute-done.4.refs_5_.refs_2_
  16.1 0.0 copy-start.1
  16.1 1.2 %collective-permute-start.5 = (bf16[6,128,128]{2,1,0:T(8,128)(2,1)S(1)}, bf16[6,128,128]{2,1,0:T(8,128)(2,1)S(1)}, u32[]{:S(2)}, u32[]{:S(2)}) collective-permute-start(bf16[6,128,128]{2,1,0:T(8,128)(2,1)S(1)} %get-tuple-element.29), channel_id=1, source_target_pairs={{0,8},{8,0},{16,24},{24,16},{1,9},{9,1},{17,25},{25,17},{2,10},{10... | collective-permute-start | bytes 589832 | tf_op jit(solution)/shard_map/ppermute | solution.py:19
  17.3 2.8 %collective-permute-start.9 = (bf16[128,256]{1,0:T(8,128)(2,1)S(1)}, bf16[128,256]{1,0:T(8,128)(2,1)S(1)}, u32[]{:S(2)}, u32[]{:S(2)}) collective-permute-start(bf16[128,256]{1,0:T(8,128)(2,1)S(1)} %copy-done.1), channel_id=1, source_target_pairs={{0,16},{8,24},{16,0},{24,8},{1,17},{9,25},{17,1},{25,9},{2,18},{10... | collective-permute-start | bytes 196616 | tf_op jit(solution)/shard_map/ppermute | solution.py:19
  20.0 2.4 %collective-permute-start.8 = (bf16[4,64,128]{2,1,0:T(8,128)(2,1)S(1)}, bf16[4,64,128]{2,1,0:T(8,128)(2,1)S(1)}, u32[]{:S(2)}, u32[]{:S(2)}) collective-permute-start(bf16[4,64,128]{2,1,0:T(8,128)(2,1)S(1)} %get-tuple-element.30.refs_0_), channel_id=1, source_target_pairs={{0,6},{1,7},{2,4},{3,5},{4,2},{5,3},{6,0},{7,1},{8,14},{9,15},{10,... | collective-permute-start | bytes 196616 | tf_op jit(solution)/shard_map/ppermute | solution.py:19
  22.5 0.5 collective-permute-start.7
  23.0 0.5 collective-permute-start.6
  23.5 1.8 %collective-permute-done.8.refs_3_ = bf16[4,64,128]{2,1,0:T(8,128)(2,1)S(1)} collective-permute-done((bf16[4,64,128]{2,1,0:T(8,128)(2,1)S(1)}, bf16[4,64,128]{2,1,0:T(8,128)(2,1)S(1)}, u32[]{:S(2)}, u32[]{:S(2)}) %collective-permute-start.8) | collective-permute-done | bytes 65568 | tf_op jit(solution)/shard_map/ppermute | solution.py:19
  25.3 1.4 %collective-permute-done.7.refs_2_ = bf16[4,64,128]{2,1,0:T(8,128)(2,1)S(1)} collective-permute-done((bf16[4,64,128]{2,1,0:T(8,128)(2,1)S(1)}, bf16[4,64,128]{2,1,0:T(8,128)(2,1)S(1)}, u32[]{:S(2)}, u32[]{:S(2)}) %collective-permute-start.7) | collective-permute-done | bytes 65568 | tf_op jit(solution)/shard_map/ppermute | solution.py:19
  26.8 0.5 collective-permute-done.6.refs_1_
  27.3 0.1 collective-permute-start.10
  27.4 0.8 %collective-permute-start.14 = (bf16[2,128,256]{2,1,0:T(8,128)(2,1)S(1)}, bf16[2,128,256]{2,1,0:T(8,128)(2,1)S(1)}, u32[]{:S(2)}, u32[]{:S(2)}) collective-permute-start(bf16[2,128,256]{2,1,0:T(8,128)(2,1)S(1)} %get-tuple-element.32.refs_4_), channel_id=1, source_target_pairs={{0,8},{8,0},{16,24},{24,16},{1,9},{9,1},{17,25},{25,17},{2,10},{10... | collective-permute-start | bytes 393224 | tf_op jit(solution)/shard_map/ppermute | solution.py:19
  28.2 0.9 %shard_map.97.refs_5_ = f32[4,64,128]{2,1,0:T(8,128)S(1)} custom-call(s32[4,1,128]{2,1,0:T(1,128)S(1)} %get-tuple-element.28.index, bf16[6,128,128]{2,1,0:T(8,128)(2,1)S(1)} %bitcast.6, bf16[6,128,128]{2,1,0:T(8,128)(2,1)S(1)} %collective-permute-done.3.refs_4_.refs_1_, bf16[6,128,128]{2,1,0:T(8,128)(2,1)S(1)} %collective-permute-done.4.refs_5_.refs_2_, ...), custom_call_target="tpu_custom_call" | custom-call | flops 25165824 | bytes 655360 | tf_op jit(solution)/shard_map/pallas_call | solution.py:252
  29.1 0.0 copy-start.6
  29.2 1.0 %shard_map.98.refs_0_ = bf16[4,64,128]{2,1,0:T(8,128)(2,1)S(1)} custom-call(s32[4,1,128]{2,1,0:T(1,128)S(1)} %get-tuple-element.28.index, bf16[6,128,128]{2,1,0:T(8,128)(2,1)S(1)} %bitcast.7, bf16[6,128,128]{2,1,0:T(8,128)(2,1)S(1)} %collective-permute-done.3.refs_4_.refs_1_, bf16[6,128,128]{2,1,0:T(8,128)(2,1)S(1)} %collective-permute-done.4.refs_5_.refs_2_, ...), custom_call_target="tpu_custom_call" | custom-call | flops 25165824 | bytes 655360 | tf_op jit(solution)/shard_map/pallas_call | solution.py:260
  30.1 0.9 %collective-permute-start.13 = (bf16[4,64,128]{2,1,0:T(8,128)(2,1)S(1)}, bf16[4,64,128]{2,1,0:T(8,128)(2,1)S(1)}, u32[]{:S(2)}, u32[]{:S(2)}) collective-permute-start(bf16[4,64,128]{2,1,0:T(8,128)(2,1)S(1)} %shard_map.98.refs_0_), channel_id=1, source_target_pairs={{0,24},{8,16},{16,8},{24,0},{1,25},{9,17},{17,9},{25,1},{2,26},{10... | collective-permute-start | bytes 196616 | tf_op jit(solution)/shard_map/ppermute | solution.py:19
  31.1 1.9 %collective-permute-start.12 = (bf16[4,64,128]{2,1,0:T(8,128)(2,1)S(1)}, bf16[4,64,128]{2,1,0:T(8,128)(2,1)S(1)}, u32[]{:S(2)}, u32[]{:S(2)}) collective-permute-start(bf16[4,64,128]{2,1,0:T(8,128)(2,1)S(1)} %shard_map.98.refs_0_), channel_id=1, source_target_pairs={{0,16},{8,24},{16,0},{24,8},{1,17},{9,25},{17,1},{25,9},{2,18},{10... | collective-permute-start | bytes 196616 | tf_op jit(solution)/shard_map/ppermute | solution.py:19
  32.9 1.6 %collective-permute-start.11 = (bf16[4,64,128]{2,1,0:T(8,128)(2,1)S(1)}, bf16[4,64,128]{2,1,0:T(8,128)(2,1)S(1)}, u32[]{:S(2)}, u32[]{:S(2)}) collective-permute-start(bf16[4,64,128]{2,1,0:T(8,128)(2,1)S(1)} %shard_map.98.refs_0_), channel_id=1, source_target_pairs={{0,8},{8,0},{16,24},{24,16},{1,9},{9,1},{17,25},{25,17},{2,10},{10... | collective-permute-start | bytes 196616 | tf_op jit(solution)/shard_map/ppermute | solution.py:19
  34.6 2.4 %collective-permute-done.13.refs_3_ = bf16[4,64,128]{2,1,0:T(8,128)(2,1)S(1)} collective-permute-done((bf16[4,64,128]{2,1,0:T(8,128)(2,1)S(1)}, bf16[4,64,128]{2,1,0:T(8,128)(2,1)S(1)}, u32[]{:S(2)}, u32[]{:S(2)}) %collective-permute-start.13) | collective-permute-done | bytes 65568 | tf_op jit(solution)/shard_map/ppermute | solution.py:19
  37.0 2.4 %collective-permute-done.12.refs_2_ = bf16[4,64,128]{2,1,0:T(8,128)(2,1)S(1)} collective-permute-done((bf16[4,64,128]{2,1,0:T(8,128)(2,1)S(1)}, bf16[4,64,128]{2,1,0:T(8,128)(2,1)S(1)}, u32[]{:S(2)}, u32[]{:S(2)}) %collective-permute-start.12) | collective-permute-done | bytes 65568 | tf_op jit(solution)/shard_map/ppermute | solution.py:19
  39.4 0.9 %shard_map.99 = (bf16[128,256]{1,0:T(8,128)(2,1)S(1)}, bf16[4,128,256]{2,1,0:T(8,128)(2,1)S(1)}, bf16[2,128,256]{2,1,0:T(8,128)(2,1)S(1)}) custom-call(bf16[4,64,128]{2,1,0:T(8,128)(2,1)S(1)} %shard_map.98.refs_0_, bf16[4,64,128]{2,1,0:T(8,128)(2,1)S(1)} %collective-permute-done.11.refs_1_, bf16[4,64,128]{2,1,0:T(8,128)(2,1)S(1)} %collective-permute-done.12.refs_2_, ...), custom_call_target="tpu_custom_call" | custom-call | flops 201326592 | bytes 1310720 | tf_op jit(solution)/shard_map/pallas_call | solution.py:269
  40.3 0.7 %shard_map.101 = bf16[5,128,256]{2,1,0:T(8,128)(2,1)S(1)} custom-call(s32[4,1,128]{2,1,0:T(1,128)S(1)} %get-tuple-element.28.index, bf16[6,128,128]{2,1,0:T(8,128)(2,1)S(1)} %bitcast.8, bf16[6,128,128]{2,1,0:T(8,128)(2,1)S(1)} %collective-permute-done.3.refs_4_.refs_1_, bf16[6,128,128]{2,1,0:T(8,128)(2,1)S(1)} %collective-permute-done.4.refs_5_.refs_2_, ...), custom_call_target="tpu_custom_call" | custom-call | flops 25165824 | bytes 655360 | tf_op jit(solution)/shard_map/pallas_call | solution.py:286
  41.0 0.1 collective-permute-start.15
  41.1 1.4 %shard_map.100.keep = f32[4,128,256]{2,1,0:T(8,128)S(1)} custom-call(s32[4,1,128]{2,1,0:T(1,128)S(1)} %get-tuple-element.28.index, bf16[6,128,128]{2,1,0:T(8,128)(2,1)S(1)} %bitcast.9, bf16[6,128,128]{2,1,0:T(8,128)(2,1)S(1)} %collective-permute-done.3.refs_4_.refs_1_, bf16[6,128,128]{2,1,0:T(8,128)(2,1)S(1)} %collective-permute-done.4.refs_5_.refs_2_, ...), custom_call_target="tpu_custom_call" | custom-call | flops 25165824 | bytes 655360 | tf_op jit(solution)/shard_map/pallas_call | solution.py:294
  42.5 0.2 collective-permute-done.15.arrived
  42.7 0.1 shard_map.102
  42.8 2.1 %collective-permute-start.16 = (bf16[256,256]{1,0:T(8,128)(2,1)S(1)}, bf16[256,256]{1,0:T(8,128)(2,1)S(1)}, u32[]{:S(2)}, u32[]{:S(2)}) collective-permute-start(bf16[256,256]{1,0:T(8,128)(2,1)S(1)} %get-tuple-element.37), channel_id=1, source_target_pairs={{0,6},{1,7},{2,4},{3,5},{4,2},{5,3},{6,0},{7,1},{8,14},{9,15},{10,... | collective-permute-start | bytes 393224 | tf_op jit(solution)/shard_map/ppermute | solution.py:19
  44.9 1.4 %collective-permute-start.18 = (bf16[256,256]{1,0:T(8,128)(2,1)S(1)}, bf16[256,256]{1,0:T(8,128)(2,1)S(1)}, u32[]{:S(2)}, u32[]{:S(2)}) collective-permute-start(bf16[256,256]{1,0:T(8,128)(2,1)S(1)} %get-tuple-element.39), channel_id=1, source_target_pairs={{0,2},{1,3},{2,0},{3,1},{4,6},{5,7},{6,4},{7,5},{8,10},{9,11},{10,... | collective-permute-start | bytes 393224 | tf_op jit(solution)/shard_map/ppermute | solution.py:19
  46.3 3.7 %collective-permute-done.16.refs_0_ = bf16[256,256]{1,0:T(8,128)(2,1)S(1)} collective-permute-done((bf16[256,256]{1,0:T(8,128)(2,1)S(1)}, bf16[256,256]{1,0:T(8,128)(2,1)S(1)}, u32[]{:S(2)}, u32[]{:S(2)}) %collective-permute-start.16) | collective-permute-done | bytes 131104 | tf_op jit(solution)/shard_map/ppermute | solution.py:19
  50.1 2.2 %collective-permute-done.17.refs_1_ = bf16[256,256]{1,0:T(8,128)(2,1)S(1)} collective-permute-done((bf16[256,256]{1,0:T(8,128)(2,1)S(1)}, bf16[256,256]{1,0:T(8,128)(2,1)S(1)}, u32[]{:S(2)}, u32[]{:S(2)}) %collective-permute-start.17) | collective-permute-done | bytes 131104 | tf_op jit(solution)/shard_map/ppermute | solution.py:19
  52.3 0.5 collective-permute-done.18.refs_2_
  52.8 0.1 shard_map.103
  52.8 0.1 collective-permute-start.19
  52.9 0.7 %shard_map.104 = (f32[128,256]{1,0:T(8,128)}, bf16[128,256]{1,0:T(8,128)(2,1)}) custom-call(f32[128,256]{1,0:T(8,128)S(1)} %get-tuple-element.40.grads, bf16[128,256]{1,0:T(8,128)(2,1)S(1)} %get-tuple-element.41.rows), custom_call_target="tpu_custom_call" | custom-call | bytes 393216 | tf_op jit(solution)/shard_map/pallas_call | solution.py:315
  53.6 0.6 %collective-permute-done.19.arrived = f32[128,256]{1,0:T(8,128)S(1)} collective-permute-done((f32[128,256]{1,0:T(8,128)S(1)}, f32[128,256]{1,0:T(8,128)S(1)}, u32[]{:S(2)}, u32[]{:S(2)}) %collective-permute-start.19) | collective-permute-done | bytes 131104 | tf_op jit(solution)/shard_map/ppermute | solution.py:19
  54.3 0.7 %shard_map.105 = f32[256,256]{1,0:T(8,128)} custom-call(f32[128,256]{1,0:T(8,128)S(1)} %get-tuple-element.43.mine, f32[128,256]{1,0:T(8,128)S(1)} %collective-permute-done.19.arrived), custom_call_target="tpu_custom_call" | custom-call | bytes 524288 | tf_op jit(solution)/shard_map/pallas_call | solution.py:321
  (18 shorter events, 0.1 us)
Async XLA Ops:
  0.6 15.4 %collective-permute-start.4 = (bf16[6,128,128]{2,1,0:T(8,128)(2,1)}, bf16[6,128,128]{2,1,0:T(8,128)(2,1)S(1)}, u32[]{:S(2)}, u32[]{:S(2)}) collective-permute-start(bf16[6,128,128]{2,1,0:T(8,128)(2,1)} %bitcast.4), channel_id=1, source_target_pairs={{0,16},{8,24},{16,0},{24,8},{1,17},{9,25},{17,1},{25,9},{2,18},{10... | collective-permute-start | bytes 589832 | tf_op jit(solution)/shard_map/ppermute | solution.py:19
  4.7 11.3 %collective-permute-start.3 = (bf16[6,128,128]{2,1,0:T(8,128)(2,1)}, bf16[6,128,128]{2,1,0:T(8,128)(2,1)S(1)}, u32[]{:S(2)}, u32[]{:S(2)}) collective-permute-start(bf16[6,128,128]{2,1,0:T(8,128)(2,1)} %bitcast.5), channel_id=1, source_target_pairs={{0,8},{8,0},{16,24},{24,16},{1,9},{9,1},{17,25},{25,17},{2,10},{10... | collective-permute-start | bytes 589832 | tf_op jit(solution)/shard_map/ppermute | solution.py:19
  6.3 0.7 %copy-start.4 = (s32[1,1,2,3]{3,2,1,0:T(2,128)S(1)}, s32[1,1,2,3]{3,2,1,0:T(2,128)}, u32[]{:S(2)}) copy-start(s32[1,1,2,3]{3,2,1,0:T(2,128)} %param.12) | copy-start | bytes 76
  6.3 0.7 %copy-start.3 = (s32[1,1,2,3]{3,2,1,0:T(2,128)S(1)}, s32[1,1,2,3]{3,2,1,0:T(2,128)}, u32[]{:S(2)}) copy-start(s32[1,1,2,3]{3,2,1,0:T(2,128)} %param.11) | copy-start | bytes 76
  6.3 0.7 %copy-start.5 = (s32[1,1,2]{2,1,0:T(1,128)S(1)}, s32[1,1,2]{2,1,0:T(1,128)}, u32[]{:S(2)}) copy-start(s32[1,1,2]{2,1,0:T(1,128)} %param.13) | copy-start | bytes 28
  7.0 0.8 %copy-start.2 = (bf16[128,256]{1,0:T(8,128)(2,1)S(1)}, bf16[128,256]{1,0:T(8,128)(2,1)}, u32[]{:S(2)}) copy-start(bf16[128,256]{1,0:T(8,128)(2,1)} %feats.1) | copy-start | bytes 196612
  8.5 7.5 %collective-permute-start = (bf16[80,128]{1,0:T(8,128)(2,1)S(1)}, bf16[80,128]{1,0:T(8,128)(2,1)S(1)}, u32[]{:S(2)}, u32[]{:S(2)}) collective-permute-start(bf16[80,128]{1,0:T(8,128)(2,1)S(1)} %get-tuple-element.25), channel_id=1, source_target_pairs={{0,24},{8,16},{16,8},{24,0},{1,25},{9,17},{17,9},{25,1},{2,26},{10... | collective-permute-start | bytes 61448 | tf_op jit(solution)/shard_map/ppermute | solution.py:19
  8.6 7.4 %collective-permute-start.1 = (bf16[80,128]{1,0:T(8,128)(2,1)S(1)}, bf16[80,128]{1,0:T(8,128)(2,1)S(1)}, u32[]{:S(2)}, u32[]{:S(2)}) collective-permute-start(bf16[80,128]{1,0:T(8,128)(2,1)S(1)} %get-tuple-element.26), channel_id=1, source_target_pairs={{0,16},{8,24},{16,0},{24,8},{1,17},{9,25},{17,1},{25,9},{2,18},{10... | collective-permute-start | bytes 61448 | tf_op jit(solution)/shard_map/ppermute | solution.py:19
  10.5 5.5 %collective-permute-start.2 = (bf16[80,128]{1,0:T(8,128)(2,1)S(1)}, bf16[80,128]{1,0:T(8,128)(2,1)S(1)}, u32[]{:S(2)}, u32[]{:S(2)}) collective-permute-start(bf16[80,128]{1,0:T(8,128)(2,1)S(1)} %get-tuple-element.27), channel_id=1, source_target_pairs={{0,8},{8,0},{16,24},{24,16},{1,9},{9,1},{17,25},{25,17},{2,10},{10... | collective-permute-start | bytes 61448 | tf_op jit(solution)/shard_map/ppermute | solution.py:19
  16.1 1.2 %copy-start.1 = (bf16[128,256]{1,0:T(8,128)(2,1)S(1)}, bf16[128,256]{1,0:T(8,128)(2,1)}, u32[]{:S(2)}) copy-start(bf16[128,256]{1,0:T(8,128)(2,1)} %refs_4_.1) | copy-start | bytes 196612
  16.1 11.2 %collective-permute-start.5 = (bf16[6,128,128]{2,1,0:T(8,128)(2,1)S(1)}, bf16[6,128,128]{2,1,0:T(8,128)(2,1)S(1)}, u32[]{:S(2)}, u32[]{:S(2)}) collective-permute-start(bf16[6,128,128]{2,1,0:T(8,128)(2,1)S(1)} %get-tuple-element.29), channel_id=1, source_target_pairs={{0,8},{8,0},{16,24},{24,16},{1,9},{9,1},{17,25},{25,17},{2,10},{10... | collective-permute-start | bytes 589832 | tf_op jit(solution)/shard_map/ppermute | solution.py:19
  17.3 6.3 %collective-permute-start.9 = (bf16[128,256]{1,0:T(8,128)(2,1)S(1)}, bf16[128,256]{1,0:T(8,128)(2,1)S(1)}, u32[]{:S(2)}, u32[]{:S(2)}) collective-permute-start(bf16[128,256]{1,0:T(8,128)(2,1)S(1)} %copy-done.1), channel_id=1, source_target_pairs={{0,16},{8,24},{16,0},{24,8},{1,17},{9,25},{17,1},{25,9},{2,18},{10... | collective-permute-start | bytes 196616 | tf_op jit(solution)/shard_map/ppermute | solution.py:19
  20.0 8.1 %copy-start = (bf16[1,1,2,3,128,128]{5,4,3,2,1,0:T(8,128)(2,1)S(1)}, bf16[1,1,2,3,128,128]{5,4,3,2,1,0:T(8,128)(2,1)}, u32[]{:S(2)}) copy-start(bf16[1,1,2,3,128,128]{5,4,3,2,1,0:T(8,128)(2,1)} %param.10) | copy-start | bytes 589828
  20.0 5.3 %collective-permute-start.8 = (bf16[4,64,128]{2,1,0:T(8,128)(2,1)S(1)}, bf16[4,64,128]{2,1,0:T(8,128)(2,1)S(1)}, u32[]{:S(2)}, u32[]{:S(2)}) collective-permute-start(bf16[4,64,128]{2,1,0:T(8,128)(2,1)S(1)} %get-tuple-element.30.refs_0_), channel_id=1, source_target_pairs={{0,6},{1,7},{2,4},{3,5},{4,2},{5,3},{6,0},{7,1},{8,14},{9,15},{10,... | collective-permute-start | bytes 196616 | tf_op jit(solution)/shard_map/ppermute | solution.py:19
  22.5 4.3 %collective-permute-start.7 = (bf16[4,64,128]{2,1,0:T(8,128)(2,1)S(1)}, bf16[4,64,128]{2,1,0:T(8,128)(2,1)S(1)}, u32[]{:S(2)}, u32[]{:S(2)}) collective-permute-start(bf16[4,64,128]{2,1,0:T(8,128)(2,1)S(1)} %get-tuple-element.30.refs_0_), channel_id=1, source_target_pairs={{0,4},{1,5},{2,6},{3,7},{4,0},{5,1},{6,2},{7,3},{8,12},{9,13},{10,... | collective-permute-start | bytes 196616 | tf_op jit(solution)/shard_map/ppermute | solution.py:19
  23.0 4.3 %collective-permute-start.6 = (bf16[4,64,128]{2,1,0:T(8,128)(2,1)S(1)}, bf16[4,64,128]{2,1,0:T(8,128)(2,1)S(1)}, u32[]{:S(2)}, u32[]{:S(2)}) collective-permute-start(bf16[4,64,128]{2,1,0:T(8,128)(2,1)S(1)} %get-tuple-element.30.refs_0_), channel_id=1, source_target_pairs={{0,2},{1,3},{2,0},{3,1},{4,6},{5,7},{6,4},{7,5},{8,10},{9,11},{10,... | collective-permute-start | bytes 196616 | tf_op jit(solution)/shard_map/ppermute | solution.py:19
  27.3 1.8 %collective-permute-start.10 = (bf16[4,4,64,128]{3,2,1,0:T(8,128)(2,1)S(1)}, bf16[4,4,64,128]{3,2,1,0:T(8,128)(2,1)S(1)}, u32[]{:S(2)}, u32[]{:S(2)}) collective-permute-start(bf16[4,4,64,128]{3,2,1,0:T(8,128)(2,1)S(1)} %get-tuple-element.31.refs_4_), channel_id=1, source_target_pairs={{0,1},{1,0},{2,3},{3,2},{4,5},{5,4},{6,7},{7,6},{8,9},{9,8},{10,11... | collective-permute-start | bytes 786440 | tf_op jit(solution)/shard_map/ppermute | solution.py:19
  27.4 7.2 %collective-permute-start.14 = (bf16[2,128,256]{2,1,0:T(8,128)(2,1)S(1)}, bf16[2,128,256]{2,1,0:T(8,128)(2,1)S(1)}, u32[]{:S(2)}, u32[]{:S(2)}) collective-permute-start(bf16[2,128,256]{2,1,0:T(8,128)(2,1)S(1)} %get-tuple-element.32.refs_4_), channel_id=1, source_target_pairs={{0,8},{8,0},{16,24},{24,16},{1,9},{9,1},{17,25},{25,17},{2,10},{10... | collective-permute-start | bytes 393224 | tf_op jit(solution)/shard_map/ppermute | solution.py:19
  29.1 10.2 %copy-start.6 = (bf16[256,256]{1,0:T(8,128)(2,1)S(1)}, bf16[256,256]{1,0:T(8,128)(2,1)}, u32[]{:S(2)}) copy-start(bf16[256,256]{1,0:T(8,128)(2,1)} %refs_6_.1) | copy-start | bytes 393220
  30.1 6.8 %collective-permute-start.13 = (bf16[4,64,128]{2,1,0:T(8,128)(2,1)S(1)}, bf16[4,64,128]{2,1,0:T(8,128)(2,1)S(1)}, u32[]{:S(2)}, u32[]{:S(2)}) collective-permute-start(bf16[4,64,128]{2,1,0:T(8,128)(2,1)S(1)} %shard_map.98.refs_0_), channel_id=1, source_target_pairs={{0,24},{8,16},{16,8},{24,0},{1,25},{9,17},{17,9},{25,1},{2,26},{10... | collective-permute-start | bytes 196616 | tf_op jit(solution)/shard_map/ppermute | solution.py:19
  31.1 8.3 %collective-permute-start.12 = (bf16[4,64,128]{2,1,0:T(8,128)(2,1)S(1)}, bf16[4,64,128]{2,1,0:T(8,128)(2,1)S(1)}, u32[]{:S(2)}, u32[]{:S(2)}) collective-permute-start(bf16[4,64,128]{2,1,0:T(8,128)(2,1)S(1)} %shard_map.98.refs_0_), channel_id=1, source_target_pairs={{0,16},{8,24},{16,0},{24,8},{1,17},{9,25},{17,1},{25,9},{2,18},{10... | collective-permute-start | bytes 196616 | tf_op jit(solution)/shard_map/ppermute | solution.py:19
  32.9 6.4 %collective-permute-start.11 = (bf16[4,64,128]{2,1,0:T(8,128)(2,1)S(1)}, bf16[4,64,128]{2,1,0:T(8,128)(2,1)S(1)}, u32[]{:S(2)}, u32[]{:S(2)}) collective-permute-start(bf16[4,64,128]{2,1,0:T(8,128)(2,1)S(1)} %shard_map.98.refs_0_), channel_id=1, source_target_pairs={{0,8},{8,0},{16,24},{24,16},{1,9},{9,1},{17,25},{25,17},{2,10},{10... | collective-permute-start | bytes 196616 | tf_op jit(solution)/shard_map/ppermute | solution.py:19
  41.0 1.7 %collective-permute-start.15 = (bf16[5,128,256]{2,1,0:T(8,128)(2,1)S(1)}, bf16[5,128,256]{2,1,0:T(8,128)(2,1)S(1)}, u32[]{:S(2)}, u32[]{:S(2)}) collective-permute-start(bf16[5,128,256]{2,1,0:T(8,128)(2,1)S(1)} %shard_map.101), channel_id=1, source_target_pairs={{0,1},{1,0},{2,3},{3,2},{4,5},{5,4},{6,7},{7,6},{8,9},{9,8},{10,11... | collective-permute-start | bytes 983048 | tf_op jit(solution)/shard_map/ppermute | solution.py:19
  42.8 7.3 %collective-permute-start.16 = (bf16[256,256]{1,0:T(8,128)(2,1)S(1)}, bf16[256,256]{1,0:T(8,128)(2,1)S(1)}, u32[]{:S(2)}, u32[]{:S(2)}) collective-permute-start(bf16[256,256]{1,0:T(8,128)(2,1)S(1)} %get-tuple-element.37), channel_id=1, source_target_pairs={{0,6},{1,7},{2,4},{3,5},{4,2},{5,3},{6,0},{7,1},{8,14},{9,15},{10,... | collective-permute-start | bytes 393224 | tf_op jit(solution)/shard_map/ppermute | solution.py:19
  44.9 7.4 %collective-permute-start.17 = (bf16[256,256]{1,0:T(8,128)(2,1)S(1)}, bf16[256,256]{1,0:T(8,128)(2,1)S(1)}, u32[]{:S(2)}, u32[]{:S(2)}) collective-permute-start(bf16[256,256]{1,0:T(8,128)(2,1)S(1)} %get-tuple-element.38), channel_id=1, source_target_pairs={{0,4},{1,5},{2,6},{3,7},{4,0},{5,1},{6,2},{7,3},{8,12},{9,13},{10,... | collective-permute-start | bytes 393224 | tf_op jit(solution)/shard_map/ppermute | solution.py:19
  44.9 7.8 %collective-permute-start.18 = (bf16[256,256]{1,0:T(8,128)(2,1)S(1)}, bf16[256,256]{1,0:T(8,128)(2,1)S(1)}, u32[]{:S(2)}, u32[]{:S(2)}) collective-permute-start(bf16[256,256]{1,0:T(8,128)(2,1)S(1)} %get-tuple-element.39), channel_id=1, source_target_pairs={{0,2},{1,3},{2,0},{3,1},{4,6},{5,7},{6,4},{7,5},{8,10},{9,11},{10,... | collective-permute-start | bytes 393224 | tf_op jit(solution)/shard_map/ppermute | solution.py:19
  52.8 1.4 %collective-permute-start.19 = (f32[128,256]{1,0:T(8,128)S(1)}, f32[128,256]{1,0:T(8,128)S(1)}, u32[]{:S(2)}, u32[]{:S(2)}) collective-permute-start(f32[128,256]{1,0:T(8,128)S(1)} %get-tuple-element.43.mine), channel_id=1, source_target_pairs={{0,1},{1,0},{2,3},{3,2},{4,5},{5,4},{6,7},{7,6},{8,9},{9,8},{10,11... | collective-permute-start | bytes 393224 | tf_op jit(solution)/shard_map/ppermute | solution.py:19

commit v14 on v12

--- a/solution.py
+++ b/solution.py
@@ -186,7 +186,7 @@
     gw = held[0]
     for k in range(1, half):
         gw += held[k]
-    terms[...] = gw
+    terms[...] = gw.astype(BF16)
 
 
 def store(grads, rows, grad_feats, out_rows):
@@ -197,8 +197,8 @@
 def join_cores(mine, arrived, out):
     core = lax.rem(lax.axis_index("blk"), 2)
     rows = mine.shape[0]
-    out[pl.ds(pl.multiple_of(core * rows, rows), rows), :] = mine[...]
-    out[pl.ds(pl.multiple_of((1 - core) * rows, rows), rows), :] = arrived[...]
+    out[pl.ds(pl.multiple_of(core * rows, rows), rows), :] = mine[...].astype(F32)
+    out[pl.ds(pl.multiple_of((1 - core) * rows, rows), rows), :] = arrived[...].astype(F32)
 
 
 def per_device(feats, weight, cotangent, block_vals, block_rows, block_cols, step_counts):
@@ -307,7 +307,7 @@
     )(keep, terms, swap(send, "blk", 1))
     grads, terms = call(
         functools.partial(add_chips, half),
-        [like((nodes, width), F32), like((width // 2, width), F32)],
+        [like((nodes, width), F32), like((width // 2, width), BF16)],
         [VMEM] * (half + 1),
         [pltpu.VMEM((half, width // 2, width), F32)],
         moved=8 * half * nodes * width,

time: 54.9 us -> 55 us (level)
    pallas_call x1, Pallas kernels: 1.09 us -> 1.65 us  [per_device(): call(functools.partial(feature_grads, reps, groups, lists, cap, 1), like(...]
  transfers between devices with their start and end apart: 20 -> 20, of which waited for: 12 -> 11; matrix products, arithmetic and copies ran while one was open for 0% -> 0% of each run, Pallas kernels for 8% -> 8%
where the time goes in v14:
time: 55 us; the launch traced here: 54.9 us
  starting transfers between devices  25.7 us (47%)
  waiting for transfers between devices  18.7 us (34%)
  Pallas kernels  7.8 us (14%)
  local copies, waits for them, and re-layouts  1.93 us (4%)
  between operations  0.76 us (1%)
    ppermute x20, starting transfers between devices, swap(): return lax.ppermute(array, axis, [(i, i ^ bit) for i in range(peers)])  25.7 us
    ppermute x20, waiting for transfers between devices, swap(): return lax.ppermute(array, axis, [(i, i ^ bit) for i in range(peers)])  18.7 us
    unnamed x14, local copies, waits for them, and re-layouts  1.93 us
    pallas_call x1, Pallas kernels, per_device(): call(functools.partial(feature_grads, reps, groups, lists, cap, 1), like(...  1.65 us
  transfers between devices with their start and end apart: 20, of which 11 were waited for; matrix products, arithmetic and copies ran while one was open for 0% of the time, Pallas kernels for 8%

profile of v14, /device:TPU:0, one launch (start us, length us, event | category | flops | bytes accessed | tf_op | source)
XLA Modules:
  0.0 54.9 jit_solution(10120145837201929757)
XLA Ops:
  0.6 4.1 %collective-permute-start.4 = (bf16[6,128,128]{2,1,0:T(8,128)(2,1)}, bf16[6,128,128]{2,1,0:T(8,128)(2,1)S(1)}, u32[]{:S(2)}, u32[]{:S(2)}) collective-permute-start(bf16[6,128,128]{2,1,0:T(8,128)(2,1)} %bitcast.4), channel_id=1, source_target_pairs={{0,16},{8,24},{16,0},{24,8},{1,17},{9,25},{17,1},{25,9},{2,18},{10... | collective-permute-start | bytes 589832 | tf_op jit(solution)/shard_map/ppermute | solution.py:19
  4.7 1.6 %collective-permute-start.3 = (bf16[6,128,128]{2,1,0:T(8,128)(2,1)}, bf16[6,128,128]{2,1,0:T(8,128)(2,1)S(1)}, u32[]{:S(2)}, u32[]{:S(2)}) collective-permute-start(bf16[6,128,128]{2,1,0:T(8,128)(2,1)} %bitcast.5), channel_id=1, source_target_pairs={{0,8},{8,0},{16,24},{24,16},{1,9},{9,1},{17,25},{25,17},{2,10},{10... | collective-permute-start | bytes 589832 | tf_op jit(solution)/shard_map/ppermute | solution.py:19
  6.3 0.7 %copy-done.4 = s32[1,1,2,3]{3,2,1,0:T(2,128)S(1)} copy-done((s32[1,1,2,3]{3,2,1,0:T(2,128)S(1)}, s32[1,1,2,3]{3,2,1,0:T(2,128)}, u32[]{:S(2)}) %copy-start.4) | copy-done | bytes 48
  7.0 0.0 copy-done.3
  7.0 0.8 %copy-done.2 = bf16[128,256]{1,0:T(8,128)(2,1)S(1)} copy-done((bf16[128,256]{1,0:T(8,128)(2,1)S(1)}, bf16[128,256]{1,0:T(8,128)(2,1)}, u32[]{:S(2)}) %copy-start.2) | copy-done | bytes 65560
  7.8 0.7 %shard_map.94 = (bf16[80,128]{1,0:T(8,128)(2,1)S(1)}, bf16[80,128]{1,0:T(8,128)(2,1)S(1)}, bf16[80,128]{1,0:T(8,128)(2,1)S(1)}, bf16[80,128]{1,0:T(8,128)(2,1)S(1)}) custom-call(bf16[128,256]{1,0:T(8,128)(2,1)S(1)} %copy-done.2, s32[2,3]{1,0:T(2,128)S(1)} %bitcast.10, s32[2,3]{1,0:T(2,128)S(1)} %bitcast.11, s32[2]{0:T(128)S(1)} %bitcast.12), custom_call_target="tpu_custom_call" | custom-call | bytes 131072 | tf_op jit(solution)/shard_map/pallas_call | solution.py:220
  8.5 0.5 collective-permute-start
  9.0 0.1 collective-permute-start.1
  9.1 3.9 %collective-permute-start.2 = (bf16[80,128]{1,0:T(8,128)(2,1)S(1)}, bf16[80,128]{1,0:T(8,128)(2,1)S(1)}, u32[]{:S(2)}, u32[]{:S(2)}) collective-permute-start(bf16[80,128]{1,0:T(8,128)(2,1)S(1)} %get-tuple-element.27), channel_id=1, source_target_pairs={{0,24},{8,16},{16,8},{24,0},{1,25},{9,17},{17,9},{25,1},{2,26},{10... | collective-permute-start | bytes 61448 | tf_op jit(solution)/shard_map/ppermute | solution.py:19
  13.0 2.5 %collective-permute-done.refs_1_ = bf16[80,128]{1,0:T(8,128)(2,1)S(1)} collective-permute-done((bf16[80,128]{1,0:T(8,128)(2,1)S(1)}, bf16[80,128]{1,0:T(8,128)(2,1)S(1)}, u32[]{:S(2)}, u32[]{:S(2)}) %collective-permute-start) | collective-permute-done | bytes 20512 | tf_op jit(solution)/shard_map/ppermute | solution.py:19
  15.5 1.0 %collective-permute-done.2.refs_3_ = bf16[80,128]{1,0:T(8,128)(2,1)S(1)} collective-permute-done((bf16[80,128]{1,0:T(8,128)(2,1)S(1)}, bf16[80,128]{1,0:T(8,128)(2,1)S(1)}, u32[]{:S(2)}, u32[]{:S(2)}) %collective-permute-start.2) | collective-permute-done | bytes 20512 | tf_op jit(solution)/shard_map/ppermute | solution.py:19
  16.5 0.4 collective-permute-start.5
  17.0 0.4 copy-done.1
  17.3 2.4 %collective-permute-start.9 = (bf16[128,256]{1,0:T(8,128)(2,1)S(1)}, bf16[128,256]{1,0:T(8,128)(2,1)S(1)}, u32[]{:S(2)}, u32[]{:S(2)}) collective-permute-start(bf16[128,256]{1,0:T(8,128)(2,1)S(1)} %copy-done.1), channel_id=1, source_target_pairs={{0,16},{8,24},{16,0},{24,8},{1,17},{9,25},{17,1},{25,9},{2,18},{10... | collective-permute-start | bytes 196616 | tf_op jit(solution)/shard_map/ppermute | solution.py:19
  19.7 2.4 %collective-permute-start.8 = (bf16[4,64,128]{2,1,0:T(8,128)(2,1)S(1)}, bf16[4,64,128]{2,1,0:T(8,128)(2,1)S(1)}, u32[]{:S(2)}, u32[]{:S(2)}) collective-permute-start(bf16[4,64,128]{2,1,0:T(8,128)(2,1)S(1)} %get-tuple-element.30.refs_0_), channel_id=1, source_target_pairs={{0,6},{1,7},{2,4},{3,5},{4,2},{5,3},{6,0},{7,1},{8,14},{9,15},{10,... | collective-permute-start | bytes 196616 | tf_op jit(solution)/shard_map/ppermute | solution.py:19
  22.2 0.5 collective-permute-start.7
  22.7 0.5 collective-permute-start.6
  23.2 0.0 collective-permute-done.9.refs_5_
  23.2 1.8 %collective-permute-done.8.refs_3_ = bf16[4,64,128]{2,1,0:T(8,128)(2,1)S(1)} collective-permute-done((bf16[4,64,128]{2,1,0:T(8,128)(2,1)S(1)}, bf16[4,64,128]{2,1,0:T(8,128)(2,1)S(1)}, u32[]{:S(2)}, u32[]{:S(2)}) %collective-permute-start.8) | collective-permute-done | bytes 65568 | tf_op jit(solution)/shard_map/ppermute | solution.py:19
  25.0 1.4 %collective-permute-done.7.refs_2_ = bf16[4,64,128]{2,1,0:T(8,128)(2,1)S(1)} collective-permute-done((bf16[4,64,128]{2,1,0:T(8,128)(2,1)S(1)}, bf16[4,64,128]{2,1,0:T(8,128)(2,1)S(1)}, u32[]{:S(2)}, u32[]{:S(2)}) %collective-permute-start.7) | collective-permute-done | bytes 65568 | tf_op jit(solution)/shard_map/ppermute | solution.py:19
  26.5 0.5 collective-permute-done.6.refs_1_
  27.0 0.0 collective-permute-done.5.refs_6_.refs_3_
  27.0 0.1 collective-permute-start.10
  27.1 0.9 %collective-permute-start.14 = (bf16[2,128,256]{2,1,0:T(8,128)(2,1)S(1)}, bf16[2,128,256]{2,1,0:T(8,128)(2,1)S(1)}, u32[]{:S(2)}, u32[]{:S(2)}) collective-permute-start(bf16[2,128,256]{2,1,0:T(8,128)(2,1)S(1)} %get-tuple-element.32.refs_4_), channel_id=1, source_target_pairs={{0,8},{8,0},{16,24},{24,16},{1,9},{9,1},{17,25},{25,17},{2,10},{10... | collective-permute-start | bytes 393224 | tf_op jit(solution)/shard_map/ppermute | solution.py:19
  28.0 0.9 %shard_map.97.refs_5_ = f32[4,64,128]{2,1,0:T(8,128)S(1)} custom-call(s32[4,1,128]{2,1,0:T(1,128)S(1)} %get-tuple-element.28.index, bf16[6,128,128]{2,1,0:T(8,128)(2,1)S(1)} %bitcast.6, bf16[6,128,128]{2,1,0:T(8,128)(2,1)S(1)} %collective-permute-done.3.refs_4_.refs_1_, bf16[6,128,128]{2,1,0:T(8,128)(2,1)S(1)} %collective-permute-done.4.refs_5_.refs_2_, ...), custom_call_target="tpu_custom_call" | custom-call | flops 25165824 | bytes 655360 | tf_op jit(solution)/shard_map/pallas_call | solution.py:252
  28.9 0.0 copy-start.6
  29.0 0.9 %shard_map.98.refs_0_ = bf16[4,64,128]{2,1,0:T(8,128)(2,1)S(1)} custom-call(s32[4,1,128]{2,1,0:T(1,128)S(1)} %get-tuple-element.28.index, bf16[6,128,128]{2,1,0:T(8,128)(2,1)S(1)} %bitcast.7, bf16[6,128,128]{2,1,0:T(8,128)(2,1)S(1)} %collective-permute-done.3.refs_4_.refs_1_, bf16[6,128,128]{2,1,0:T(8,128)(2,1)S(1)} %collective-permute-done.4.refs_5_.refs_2_, ...), custom_call_target="tpu_custom_call" | custom-call | flops 25165824 | bytes 655360 | tf_op jit(solution)/shard_map/pallas_call | solution.py:260
  29.9 1.2 %collective-permute-start.13 = (bf16[4,64,128]{2,1,0:T(8,128)(2,1)S(1)}, bf16[4,64,128]{2,1,0:T(8,128)(2,1)S(1)}, u32[]{:S(2)}, u32[]{:S(2)}) collective-permute-start(bf16[4,64,128]{2,1,0:T(8,128)(2,1)S(1)} %shard_map.98.refs_0_), channel_id=1, source_target_pairs={{0,24},{8,16},{16,8},{24,0},{1,25},{9,17},{17,9},{25,1},{2,26},{10... | collective-permute-start | bytes 196616 | tf_op jit(solution)/shard_map/ppermute | solution.py:19
  31.1 1.5 %collective-permute-start.12 = (bf16[4,64,128]{2,1,0:T(8,128)(2,1)S(1)}, bf16[4,64,128]{2,1,0:T(8,128)(2,1)S(1)}, u32[]{:S(2)}, u32[]{:S(2)}) collective-permute-start(bf16[4,64,128]{2,1,0:T(8,128)(2,1)S(1)} %shard_map.98.refs_0_), channel_id=1, source_target_pairs={{0,16},{8,24},{16,0},{24,8},{1,17},{9,25},{17,1},{25,9},{2,18},{10... | collective-permute-start | bytes 196616 | tf_op jit(solution)/shard_map/ppermute | solution.py:19
  32.6 1.7 %collective-permute-start.11 = (bf16[4,64,128]{2,1,0:T(8,128)(2,1)S(1)}, bf16[4,64,128]{2,1,0:T(8,128)(2,1)S(1)}, u32[]{:S(2)}, u32[]{:S(2)}) collective-permute-start(bf16[4,64,128]{2,1,0:T(8,128)(2,1)S(1)} %shard_map.98.refs_0_), channel_id=1, source_target_pairs={{0,8},{8,0},{16,24},{24,16},{1,9},{9,1},{17,25},{25,17},{2,10},{10... | collective-permute-start | bytes 196616 | tf_op jit(solution)/shard_map/ppermute | solution.py:19
  34.4 2.4 %collective-permute-done.13.refs_3_ = bf16[4,64,128]{2,1,0:T(8,128)(2,1)S(1)} collective-permute-done((bf16[4,64,128]{2,1,0:T(8,128)(2,1)S(1)}, bf16[4,64,128]{2,1,0:T(8,128)(2,1)S(1)}, u32[]{:S(2)}, u32[]{:S(2)}) %collective-permute-start.13) | collective-permute-done | bytes 65568 | tf_op jit(solution)/shard_map/ppermute | solution.py:19
  36.8 2.3 %collective-permute-done.12.refs_2_ = bf16[4,64,128]{2,1,0:T(8,128)(2,1)S(1)} collective-permute-done((bf16[4,64,128]{2,1,0:T(8,128)(2,1)S(1)}, bf16[4,64,128]{2,1,0:T(8,128)(2,1)S(1)}, u32[]{:S(2)}, u32[]{:S(2)}) %collective-permute-start.12) | collective-permute-done | bytes 65568 | tf_op jit(solution)/shard_map/ppermute | solution.py:19
  39.1 0.9 %shard_map.99 = (bf16[128,256]{1,0:T(8,128)(2,1)S(1)}, bf16[4,128,256]{2,1,0:T(8,128)(2,1)S(1)}, bf16[2,128,256]{2,1,0:T(8,128)(2,1)S(1)}) custom-call(bf16[4,64,128]{2,1,0:T(8,128)(2,1)S(1)} %shard_map.98.refs_0_, bf16[4,64,128]{2,1,0:T(8,128)(2,1)S(1)} %collective-permute-done.11.refs_1_, bf16[4,64,128]{2,1,0:T(8,128)(2,1)S(1)} %collective-permute-done.12.refs_2_, ...), custom_call_target="tpu_custom_call" | custom-call | flops 201326592 | bytes 1310720 | tf_op jit(solution)/shard_map/pallas_call | solution.py:269
  40.0 1.6 %shard_map.101 = bf16[5,128,256]{2,1,0:T(8,128)(2,1)S(1)} custom-call(s32[4,1,128]{2,1,0:T(1,128)S(1)} %get-tuple-element.28.index, bf16[6,128,128]{2,1,0:T(8,128)(2,1)S(1)} %bitcast.8, bf16[6,128,128]{2,1,0:T(8,128)(2,1)S(1)} %collective-permute-done.3.refs_4_.refs_1_, bf16[6,128,128]{2,1,0:T(8,128)(2,1)S(1)} %collective-permute-done.4.refs_5_.refs_2_, ...), custom_call_target="tpu_custom_call" | custom-call | flops 25165824 | bytes 655360 | tf_op jit(solution)/shard_map/pallas_call | solution.py:286
  41.6 0.1 collective-permute-start.15
  41.7 1.1 %shard_map.100.keep = f32[4,128,256]{2,1,0:T(8,128)S(1)} custom-call(s32[4,1,128]{2,1,0:T(1,128)S(1)} %get-tuple-element.28.index, bf16[6,128,128]{2,1,0:T(8,128)(2,1)S(1)} %bitcast.9, bf16[6,128,128]{2,1,0:T(8,128)(2,1)S(1)} %collective-permute-done.3.refs_4_.refs_1_, bf16[6,128,128]{2,1,0:T(8,128)(2,1)S(1)} %collective-permute-done.4.refs_5_.refs_2_, ...), custom_call_target="tpu_custom_call" | custom-call | flops 25165824 | bytes 655360 | tf_op jit(solution)/shard_map/pallas_call | solution.py:294
  42.8 0.5 collective-permute-done.15.arrived
  43.3 0.1 shard_map.102
  43.4 1.2 %collective-permute-start.16 = (bf16[256,256]{1,0:T(8,128)(2,1)S(1)}, bf16[256,256]{1,0:T(8,128)(2,1)S(1)}, u32[]{:S(2)}, u32[]{:S(2)}) collective-permute-start(bf16[256,256]{1,0:T(8,128)(2,1)S(1)} %get-tuple-element.37), channel_id=1, source_target_pairs={{0,6},{1,7},{2,4},{3,5},{4,2},{5,3},{6,0},{7,1},{8,14},{9,15},{10,... | collective-permute-start | bytes 393224 | tf_op jit(solution)/shard_map/ppermute | solution.py:19
  44.6 0.1 collective-permute-start.17
  44.8 2.2 %collective-permute-start.18 = (bf16[256,256]{1,0:T(8,128)(2,1)S(1)}, bf16[256,256]{1,0:T(8,128)(2,1)S(1)}, u32[]{:S(2)}, u32[]{:S(2)}) collective-permute-start(bf16[256,256]{1,0:T(8,128)(2,1)S(1)} %get-tuple-element.39), channel_id=1, source_target_pairs={{0,2},{1,3},{2,0},{3,1},{4,6},{5,7},{6,4},{7,5},{8,10},{9,11},{10,... | collective-permute-start | bytes 393224 | tf_op jit(solution)/shard_map/ppermute | solution.py:19
  47.0 3.4 %collective-permute-done.16.refs_0_ = bf16[256,256]{1,0:T(8,128)(2,1)S(1)} collective-permute-done((bf16[256,256]{1,0:T(8,128)(2,1)S(1)}, bf16[256,256]{1,0:T(8,128)(2,1)S(1)}, u32[]{:S(2)}, u32[]{:S(2)}) %collective-permute-start.16) | collective-permute-done | bytes 131104 | tf_op jit(solution)/shard_map/ppermute | solution.py:19
  50.4 2.3 %collective-permute-done.17.refs_1_ = bf16[256,256]{1,0:T(8,128)(2,1)S(1)} collective-permute-done((bf16[256,256]{1,0:T(8,128)(2,1)S(1)}, bf16[256,256]{1,0:T(8,128)(2,1)S(1)}, u32[]{:S(2)}, u32[]{:S(2)}) %collective-permute-start.17) | collective-permute-done | bytes 131104 | tf_op jit(solution)/shard_map/ppermute | solution.py:19
  52.7 0.1 shard_map.103
  52.8 0.2 collective-permute-start.19
  53.0 0.7 %shard_map.104 = (f32[128,256]{1,0:T(8,128)}, bf16[128,256]{1,0:T(8,128)(2,1)}) custom-call(f32[128,256]{1,0:T(8,128)S(1)} %get-tuple-element.40.grads, bf16[128,256]{1,0:T(8,128)(2,1)S(1)} %get-tuple-element.41.rows), custom_call_target="tpu_custom_call" | custom-call | bytes 393216 | tf_op jit(solution)/shard_map/pallas_call | solution.py:315
  53.7 0.5 collective-permute-done.19.arrived
  54.1 0.7 %shard_map.105 = f32[256,256]{1,0:T(8,128)} custom-call(bf16[128,256]{1,0:T(8,128)(2,1)S(1)} %get-tuple-element.43.mine, bf16[128,256]{1,0:T(8,128)(2,1)S(1)} %collective-permute-done.19.arrived), custom_call_target="tpu_custom_call" | custom-call | bytes 524288 | tf_op jit(solution)/shard_map/pallas_call | solution.py:321
  (18 shorter events, 0.1 us)
Async XLA Ops:
  0.6 15.9 %collective-permute-start.4 = (bf16[6,128,128]{2,1,0:T(8,128)(2,1)}, bf16[6,128,128]{2,1,0:T(8,128)(2,1)S(1)}, u32[]{:S(2)}, u32[]{:S(2)}) collective-permute-start(bf16[6,128,128]{2,1,0:T(8,128)(2,1)} %bitcast.4), channel_id=1, source_target_pairs={{0,16},{8,24},{16,0},{24,8},{1,17},{9,25},{17,1},{25,9},{2,18},{10... | collective-permute-start | bytes 589832 | tf_op jit(solution)/shard_map/ppermute | solution.py:19
  4.7 11.8 %collective-permute-start.3 = (bf16[6,128,128]{2,1,0:T(8,128)(2,1)}, bf16[6,128,128]{2,1,0:T(8,128)(2,1)S(1)}, u32[]{:S(2)}, u32[]{:S(2)}) collective-permute-start(bf16[6,128,128]{2,1,0:T(8,128)(2,1)} %bitcast.5), channel_id=1, source_target_pairs={{0,8},{8,0},{16,24},{24,16},{1,9},{9,1},{17,25},{25,17},{2,10},{10... | collective-permute-start | bytes 589832 | tf_op jit(solution)/shard_map/ppermute | solution.py:19
  6.3 0.7 %copy-start.4 = (s32[1,1,2,3]{3,2,1,0:T(2,128)S(1)}, s32[1,1,2,3]{3,2,1,0:T(2,128)}, u32[]{:S(2)}) copy-start(s32[1,1,2,3]{3,2,1,0:T(2,128)} %param.12) | copy-start | bytes 76
  6.3 0.7 %copy-start.3 = (s32[1,1,2,3]{3,2,1,0:T(2,128)S(1)}, s32[1,1,2,3]{3,2,1,0:T(2,128)}, u32[]{:S(2)}) copy-start(s32[1,1,2,3]{3,2,1,0:T(2,128)} %param.11) | copy-start | bytes 76
  6.3 0.7 %copy-start.5 = (s32[1,1,2]{2,1,0:T(1,128)S(1)}, s32[1,1,2]{2,1,0:T(1,128)}, u32[]{:S(2)}) copy-start(s32[1,1,2]{2,1,0:T(1,128)} %param.13) | copy-start | bytes 28
  7.0 0.8 %copy-start.2 = (bf16[128,256]{1,0:T(8,128)(2,1)S(1)}, bf16[128,256]{1,0:T(8,128)(2,1)}, u32[]{:S(2)}) copy-start(bf16[128,256]{1,0:T(8,128)(2,1)} %feats.1) | copy-start | bytes 196612
  8.5 6.9 %collective-permute-start = (bf16[80,128]{1,0:T(8,128)(2,1)S(1)}, bf16[80,128]{1,0:T(8,128)(2,1)S(1)}, u32[]{:S(2)}, u32[]{:S(2)}) collective-permute-start(bf16[80,128]{1,0:T(8,128)(2,1)S(1)} %get-tuple-element.25), channel_id=1, source_target_pairs={{0,8},{8,0},{16,24},{24,16},{1,9},{9,1},{17,25},{25,17},{2,10},{10... | collective-permute-start | bytes 61448 | tf_op jit(solution)/shard_map/ppermute | solution.py:19
  9.0 6.4 %collective-permute-start.1 = (bf16[80,128]{1,0:T(8,128)(2,1)S(1)}, bf16[80,128]{1,0:T(8,128)(2,1)S(1)}, u32[]{:S(2)}, u32[]{:S(2)}) collective-permute-start(bf16[80,128]{1,0:T(8,128)(2,1)S(1)} %get-tuple-element.26), channel_id=1, source_target_pairs={{0,16},{8,24},{16,0},{24,8},{1,17},{9,25},{17,1},{25,9},{2,18},{10... | collective-permute-start | bytes 61448 | tf_op jit(solution)/shard_map/ppermute | solution.py:19
  9.1 7.4 %collective-permute-start.2 = (bf16[80,128]{1,0:T(8,128)(2,1)S(1)}, bf16[80,128]{1,0:T(8,128)(2,1)S(1)}, u32[]{:S(2)}, u32[]{:S(2)}) collective-permute-start(bf16[80,128]{1,0:T(8,128)(2,1)S(1)} %get-tuple-element.27), channel_id=1, source_target_pairs={{0,24},{8,16},{16,8},{24,0},{1,25},{9,17},{17,9},{25,1},{2,26},{10... | collective-permute-start | bytes 61448 | tf_op jit(solution)/shard_map/ppermute | solution.py:19
  16.5 0.8 %copy-start.1 = (bf16[128,256]{1,0:T(8,128)(2,1)S(1)}, bf16[128,256]{1,0:T(8,128)(2,1)}, u32[]{:S(2)}) copy-start(bf16[128,256]{1,0:T(8,128)(2,1)} %refs_4_.1) | copy-start | bytes 196612
  16.5 10.4 %collective-permute-start.5 = (bf16[6,128,128]{2,1,0:T(8,128)(2,1)S(1)}, bf16[6,128,128]{2,1,0:T(8,128)(2,1)S(1)}, u32[]{:S(2)}, u32[]{:S(2)}) collective-permute-start(bf16[6,128,128]{2,1,0:T(8,128)(2,1)S(1)} %get-tuple-element.29), channel_id=1, source_target_pairs={{0,8},{8,0},{16,24},{24,16},{1,9},{9,1},{17,25},{25,17},{2,10},{10... | collective-permute-start | bytes 589832 | tf_op jit(solution)/shard_map/ppermute | solution.py:19
  17.3 5.9 %collective-permute-start.9 = (bf16[128,256]{1,0:T(8,128)(2,1)S(1)}, bf16[128,256]{1,0:T(8,128)(2,1)S(1)}, u32[]{:S(2)}, u32[]{:S(2)}) collective-permute-start(bf16[128,256]{1,0:T(8,128)(2,1)S(1)} %copy-done.1), channel_id=1, source_target_pairs={{0,16},{8,24},{16,0},{24,8},{1,17},{9,25},{17,1},{25,9},{2,18},{10... | collective-permute-start | bytes 196616 | tf_op jit(solution)/shard_map/ppermute | solution.py:19
  19.7 8.3 %copy-start = (bf16[1,1,2,3,128,128]{5,4,3,2,1,0:T(8,128)(2,1)S(1)}, bf16[1,1,2,3,128,128]{5,4,3,2,1,0:T(8,128)(2,1)}, u32[]{:S(2)}) copy-start(bf16[1,1,2,3,128,128]{5,4,3,2,1,0:T(8,128)(2,1)} %param.10) | copy-start | bytes 589828
  19.7 5.3 %collective-permute-start.8 = (bf16[4,64,128]{2,1,0:T(8,128)(2,1)S(1)}, bf16[4,64,128]{2,1,0:T(8,128)(2,1)S(1)}, u32[]{:S(2)}, u32[]{:S(2)}) collective-permute-start(bf16[4,64,128]{2,1,0:T(8,128)(2,1)S(1)} %get-tuple-element.30.refs_0_), channel_id=1, source_target_pairs={{0,6},{1,7},{2,4},{3,5},{4,2},{5,3},{6,0},{7,1},{8,14},{9,15},{10,... | collective-permute-start | bytes 196616 | tf_op jit(solution)/shard_map/ppermute | solution.py:19
  22.2 4.3 %collective-permute-start.7 = (bf16[4,64,128]{2,1,0:T(8,128)(2,1)S(1)}, bf16[4,64,128]{2,1,0:T(8,128)(2,1)S(1)}, u32[]{:S(2)}, u32[]{:S(2)}) collective-permute-start(bf16[4,64,128]{2,1,0:T(8,128)(2,1)S(1)} %get-tuple-element.30.refs_0_), channel_id=1, source_target_pairs={{0,4},{1,5},{2,6},{3,7},{4,0},{5,1},{6,2},{7,3},{8,12},{9,13},{10,... | collective-permute-start | bytes 196616 | tf_op jit(solution)/shard_map/ppermute | solution.py:19
  22.7 4.3 %collective-permute-start.6 = (bf16[4,64,128]{2,1,0:T(8,128)(2,1)S(1)}, bf16[4,64,128]{2,1,0:T(8,128)(2,1)S(1)}, u32[]{:S(2)}, u32[]{:S(2)}) collective-permute-start(bf16[4,64,128]{2,1,0:T(8,128)(2,1)S(1)} %get-tuple-element.30.refs_0_), channel_id=1, source_target_pairs={{0,2},{1,3},{2,0},{3,1},{4,6},{5,7},{6,4},{7,5},{8,10},{9,11},{10,... | collective-permute-start | bytes 196616 | tf_op jit(solution)/shard_map/ppermute | solution.py:19
  27.0 2.0 %collective-permute-start.10 = (bf16[4,4,64,128]{3,2,1,0:T(8,128)(2,1)S(1)}, bf16[4,4,64,128]{3,2,1,0:T(8,128)(2,1)S(1)}, u32[]{:S(2)}, u32[]{:S(2)}) collective-permute-start(bf16[4,4,64,128]{3,2,1,0:T(8,128)(2,1)S(1)} %get-tuple-element.31.refs_4_), channel_id=1, source_target_pairs={{0,1},{1,0},{2,3},{3,2},{4,5},{5,4},{6,7},{7,6},{8,9},{9,8},{10,11... | collective-permute-start | bytes 786440 | tf_op jit(solution)/shard_map/ppermute | solution.py:19
  27.1 7.3 %collective-permute-start.14 = (bf16[2,128,256]{2,1,0:T(8,128)(2,1)S(1)}, bf16[2,128,256]{2,1,0:T(8,128)(2,1)S(1)}, u32[]{:S(2)}, u32[]{:S(2)}) collective-permute-start(bf16[2,128,256]{2,1,0:T(8,128)(2,1)S(1)} %get-tuple-element.32.refs_4_), channel_id=1, source_target_pairs={{0,8},{8,0},{16,24},{24,16},{1,9},{9,1},{17,25},{25,17},{2,10},{10... | collective-permute-start | bytes 393224 | tf_op jit(solution)/shard_map/ppermute | solution.py:19
  28.9 10.1 %copy-start.6 = (bf16[256,256]{1,0:T(8,128)(2,1)S(1)}, bf16[256,256]{1,0:T(8,128)(2,1)}, u32[]{:S(2)}) copy-start(bf16[256,256]{1,0:T(8,128)(2,1)} %refs_6_.1) | copy-start | bytes 393220
  29.9 6.8 %collective-permute-start.13 = (bf16[4,64,128]{2,1,0:T(8,128)(2,1)S(1)}, bf16[4,64,128]{2,1,0:T(8,128)(2,1)S(1)}, u32[]{:S(2)}, u32[]{:S(2)}) collective-permute-start(bf16[4,64,128]{2,1,0:T(8,128)(2,1)S(1)} %shard_map.98.refs_0_), channel_id=1, source_target_pairs={{0,24},{8,16},{16,8},{24,0},{1,25},{9,17},{17,9},{25,1},{2,26},{10... | collective-permute-start | bytes 196616 | tf_op jit(solution)/shard_map/ppermute | solution.py:19
  31.1 8.0 %collective-permute-start.12 = (bf16[4,64,128]{2,1,0:T(8,128)(2,1)S(1)}, bf16[4,64,128]{2,1,0:T(8,128)(2,1)S(1)}, u32[]{:S(2)}, u32[]{:S(2)}) collective-permute-start(bf16[4,64,128]{2,1,0:T(8,128)(2,1)S(1)} %shard_map.98.refs_0_), channel_id=1, source_target_pairs={{0,16},{8,24},{16,0},{24,8},{1,17},{9,25},{17,1},{25,9},{2,18},{10... | collective-permute-start | bytes 196616 | tf_op jit(solution)/shard_map/ppermute | solution.py:19
  32.6 6.5 %collective-permute-start.11 = (bf16[4,64,128]{2,1,0:T(8,128)(2,1)S(1)}, bf16[4,64,128]{2,1,0:T(8,128)(2,1)S(1)}, u32[]{:S(2)}, u32[]{:S(2)}) collective-permute-start(bf16[4,64,128]{2,1,0:T(8,128)(2,1)S(1)} %shard_map.98.refs_0_), channel_id=1, source_target_pairs={{0,8},{8,0},{16,24},{24,16},{1,9},{9,1},{17,25},{25,17},{2,10},{10... | collective-permute-start | bytes 196616 | tf_op jit(solution)/shard_map/ppermute | solution.py:19
  41.6 1.7 %collective-permute-start.15 = (bf16[5,128,256]{2,1,0:T(8,128)(2,1)S(1)}, bf16[5,128,256]{2,1,0:T(8,128)(2,1)S(1)}, u32[]{:S(2)}, u32[]{:S(2)}) collective-permute-start(bf16[5,128,256]{2,1,0:T(8,128)(2,1)S(1)} %shard_map.101), channel_id=1, source_target_pairs={{0,1},{1,0},{2,3},{3,2},{4,5},{5,4},{6,7},{7,6},{8,9},{9,8},{10,11... | collective-permute-start | bytes 983048 | tf_op jit(solution)/shard_map/ppermute | solution.py:19
  43.4 7.0 %collective-permute-start.16 = (bf16[256,256]{1,0:T(8,128)(2,1)S(1)}, bf16[256,256]{1,0:T(8,128)(2,1)S(1)}, u32[]{:S(2)}, u32[]{:S(2)}) collective-permute-start(bf16[256,256]{1,0:T(8,128)(2,1)S(1)} %get-tuple-element.37), channel_id=1, source_target_pairs={{0,6},{1,7},{2,4},{3,5},{4,2},{5,3},{6,0},{7,1},{8,14},{9,15},{10,... | collective-permute-start | bytes 393224 | tf_op jit(solution)/shard_map/ppermute | solution.py:19
  44.6 8.1 %collective-permute-start.17 = (bf16[256,256]{1,0:T(8,128)(2,1)S(1)}, bf16[256,256]{1,0:T(8,128)(2,1)S(1)}, u32[]{:S(2)}, u32[]{:S(2)}) collective-permute-start(bf16[256,256]{1,0:T(8,128)(2,1)S(1)} %get-tuple-element.38), channel_id=1, source_target_pairs={{0,4},{1,5},{2,6},{3,7},{4,0},{5,1},{6,2},{7,3},{8,12},{9,13},{10,... | collective-permute-start | bytes 393224 | tf_op jit(solution)/shard_map/ppermute | solution.py:19
  44.8 8.0 %collective-permute-start.18 = (bf16[256,256]{1,0:T(8,128)(2,1)S(1)}, bf16[256,256]{1,0:T(8,128)(2,1)S(1)}, u32[]{:S(2)}, u32[]{:S(2)}) collective-permute-start(bf16[256,256]{1,0:T(8,128)(2,1)S(1)} %get-tuple-element.39), channel_id=1, source_target_pairs={{0,2},{1,3},{2,0},{3,1},{4,6},{5,7},{6,4},{7,5},{8,10},{9,11},{10,... | collective-permute-start | bytes 393224 | tf_op jit(solution)/shard_map/ppermute | solution.py:19
  52.8 1.3 %collective-permute-start.19 = (bf16[128,256]{1,0:T(8,128)(2,1)S(1)}, bf16[128,256]{1,0:T(8,128)(2,1)S(1)}, u32[]{:S(2)}, u32[]{:S(2)}) collective-permute-start(bf16[128,256]{1,0:T(8,128)(2,1)S(1)} %get-tuple-element.43.mine), channel_id=1, source_target_pairs={{0,1},{1,0},{2,3},{3,2},{4,5},{5,4},{6,7},{7,6},{8,9},{9,8},{10,11... | collective-permute-start | bytes 196616 | tf_op jit(solution)/shard_map/ppermute | solution.py:19

commit v15 on v12

--- a/solution.py
+++ b/solution.py
@@ -83,7 +83,7 @@
 def join(half, *refs):
     out, pairs = refs[-2:]
     for k, ref in enumerate(refs[:half]):
-        out[k] = ref[...]
+        out[(half - k) % half] = ref[...]
     for k in range(pairs.shape[0]):
         pairs[k] = refs[half + k][...]
 
@@ -241,7 +241,7 @@
         moved=4 * half * nodes * width,
     )(
         mine,
-        *[swap(mine, "blk", 2 * k) for k in range(1, half)],
+        *[swap(mine, "blk", 2 * k) for k in range(half - 1, 0, -1)],
         *spread(cotangent, 2),
         *odds[1:],
     )

time: 54.9 us -> 55.4 us (level)
  waiting for transfers between devices: 18.8 us -> 19.7 us
    ppermute x20, waiting for transfers between devices: 18.8 us -> 19.7 us  [swap(): return lax.ppermute(array, axis, [(i, i ^ bit) for i in range(peers)])]
  transfers between devices with their start and end apart: 20 -> 20, of which waited for: 12 -> 11; matrix products, arithmetic and copies ran while one was open for 0% -> 0% of each run, Pallas kernels for 8% -> 8%
where the time goes in v15:
time: 55.4 us
  starting transfers between devices  25.6 us (46%)
  waiting for transfers between devices  19.7 us (36%)
  Pallas kernels  7.45 us (13%)
  local copies, waits for them, and re-layouts  1.93 us (3%)
  between operations  0.77 us (1%)
    ppermute x20, starting transfers between devices, swap(): return lax.ppermute(array, axis, [(i, i ^ bit) for i in range(peers)])  25.6 us
    ppermute x20, waiting for transfers between devices, swap(): return lax.ppermute(array, axis, [(i, i ^ bit) for i in range(peers)])  19.7 us
    unnamed x14, local copies, waits for them, and re-layouts  1.93 us
    pallas_call x1, Pallas kernels, per_device(): call(functools.partial(feature_grads, reps, groups, lists, cap, 1), like(...  1.28 us
  transfers between devices with their start and end apart: 20, of which 11 were waited for; matrix products, arithmetic and copies ran while one was open for 0% of the time, Pallas kernels for 8%

profile of v15, /device:TPU:0, one launch (start us, length us, event | category | flops | bytes accessed | tf_op | source)
XLA Modules:
  0.0 55.4 jit_solution(10999810823943477943)
XLA Ops:
  0.6 4.1 %collective-permute-start.4 = (bf16[6,128,128]{2,1,0:T(8,128)(2,1)}, bf16[6,128,128]{2,1,0:T(8,128)(2,1)S(1)}, u32[]{:S(2)}, u32[]{:S(2)}) collective-permute-start(bf16[6,128,128]{2,1,0:T(8,128)(2,1)} %bitcast.4), channel_id=1, source_target_pairs={{0,16},{8,24},{16,0},{24,8},{1,17},{9,25},{17,1},{25,9},{2,18},{10... | collective-permute-start | bytes 589832 | tf_op jit(solution)/shard_map/ppermute | solution.py:19
  4.7 1.6 %collective-permute-start.3 = (bf16[6,128,128]{2,1,0:T(8,128)(2,1)}, bf16[6,128,128]{2,1,0:T(8,128)(2,1)S(1)}, u32[]{:S(2)}, u32[]{:S(2)}) collective-permute-start(bf16[6,128,128]{2,1,0:T(8,128)(2,1)} %bitcast.5), channel_id=1, source_target_pairs={{0,8},{8,0},{16,24},{24,16},{1,9},{9,1},{17,25},{25,17},{2,10},{10... | collective-permute-start | bytes 589832 | tf_op jit(solution)/shard_map/ppermute | solution.py:19
  6.3 0.7 %copy-done.4 = s32[1,1,2,3]{3,2,1,0:T(2,128)S(1)} copy-done((s32[1,1,2,3]{3,2,1,0:T(2,128)S(1)}, s32[1,1,2,3]{3,2,1,0:T(2,128)}, u32[]{:S(2)}) %copy-start.4) | copy-done | bytes 48
  7.0 0.0 copy-done.3
  7.0 0.8 %copy-done.2 = bf16[128,256]{1,0:T(8,128)(2,1)S(1)} copy-done((bf16[128,256]{1,0:T(8,128)(2,1)S(1)}, bf16[128,256]{1,0:T(8,128)(2,1)}, u32[]{:S(2)}) %copy-start.2) | copy-done | bytes 65560
  7.8 0.7 %shard_map.94 = (bf16[80,128]{1,0:T(8,128)(2,1)S(1)}, bf16[80,128]{1,0:T(8,128)(2,1)S(1)}, bf16[80,128]{1,0:T(8,128)(2,1)S(1)}, bf16[80,128]{1,0:T(8,128)(2,1)S(1)}) custom-call(bf16[128,256]{1,0:T(8,128)(2,1)S(1)} %copy-done.2, s32[2,3]{1,0:T(2,128)S(1)} %bitcast.10, s32[2,3]{1,0:T(2,128)S(1)} %bitcast.11, s32[2]{0:T(128)S(1)} %bitcast.12), custom_call_target="tpu_custom_call" | custom-call | bytes 131072 | tf_op jit(solution)/shard_map/pallas_call | solution.py:220
  8.5 0.5 collective-permute-start
  9.0 0.1 collective-permute-start.1
  9.1 3.9 %collective-permute-start.2 = (bf16[80,128]{1,0:T(8,128)(2,1)S(1)}, bf16[80,128]{1,0:T(8,128)(2,1)S(1)}, u32[]{:S(2)}, u32[]{:S(2)}) collective-permute-start(bf16[80,128]{1,0:T(8,128)(2,1)S(1)} %get-tuple-element.27), channel_id=1, source_target_pairs={{0,24},{8,16},{16,8},{24,0},{1,25},{9,17},{17,9},{25,1},{2,26},{10... | collective-permute-start | bytes 61448 | tf_op jit(solution)/shard_map/ppermute | solution.py:19
  13.0 2.5 %collective-permute-done.refs_1_ = bf16[80,128]{1,0:T(8,128)(2,1)S(1)} collective-permute-done((bf16[80,128]{1,0:T(8,128)(2,1)S(1)}, bf16[80,128]{1,0:T(8,128)(2,1)S(1)}, u32[]{:S(2)}, u32[]{:S(2)}) %collective-permute-start) | collective-permute-done | bytes 20512 | tf_op jit(solution)/shard_map/ppermute | solution.py:19
  15.5 0.0 collective-permute-done.1.refs_2_
  15.5 1.0 %collective-permute-done.2.refs_3_ = bf16[80,128]{1,0:T(8,128)(2,1)S(1)} collective-permute-done((bf16[80,128]{1,0:T(8,128)(2,1)S(1)}, bf16[80,128]{1,0:T(8,128)(2,1)S(1)}, u32[]{:S(2)}, u32[]{:S(2)}) %collective-permute-start.2) | collective-permute-done | bytes 20512 | tf_op jit(solution)/shard_map/ppermute | solution.py:19
  16.5 0.0 collective-permute-done.4.refs_5_.refs_2_
  16.5 0.4 collective-permute-start.5
  17.0 0.4 copy-done.1
  17.3 2.4 %collective-permute-start.9 = (bf16[128,256]{1,0:T(8,128)(2,1)S(1)}, bf16[128,256]{1,0:T(8,128)(2,1)S(1)}, u32[]{:S(2)}, u32[]{:S(2)}) collective-permute-start(bf16[128,256]{1,0:T(8,128)(2,1)S(1)} %copy-done.1), channel_id=1, source_target_pairs={{0,16},{8,24},{16,0},{24,8},{1,17},{9,25},{17,1},{25,9},{2,18},{10... | collective-permute-start | bytes 196616 | tf_op jit(solution)/shard_map/ppermute | solution.py:19
  19.7 1.5 %collective-permute-start.8 = (bf16[4,64,128]{2,1,0:T(8,128)(2,1)S(1)}, bf16[4,64,128]{2,1,0:T(8,128)(2,1)S(1)}, u32[]{:S(2)}, u32[]{:S(2)}) collective-permute-start(bf16[4,64,128]{2,1,0:T(8,128)(2,1)S(1)} %get-tuple-element.30.refs_0_), channel_id=1, source_target_pairs={{0,2},{1,3},{2,0},{3,1},{4,6},{5,7},{6,4},{7,5},{8,10},{9,11},{10,... | collective-permute-start | bytes 196616 | tf_op jit(solution)/shard_map/ppermute | solution.py:19
  21.2 1.5 %collective-permute-start.7 = (bf16[4,64,128]{2,1,0:T(8,128)(2,1)S(1)}, bf16[4,64,128]{2,1,0:T(8,128)(2,1)S(1)}, u32[]{:S(2)}, u32[]{:S(2)}) collective-permute-start(bf16[4,64,128]{2,1,0:T(8,128)(2,1)S(1)} %get-tuple-element.30.refs_0_), channel_id=1, source_target_pairs={{0,4},{1,5},{2,6},{3,7},{4,0},{5,1},{6,2},{7,3},{8,12},{9,13},{10,... | collective-permute-start | bytes 196616 | tf_op jit(solution)/shard_map/ppermute | solution.py:19
  22.7 0.5 collective-permute-start.6
  23.2 0.8 %collective-permute-done.8.refs_3_ = bf16[4,64,128]{2,1,0:T(8,128)(2,1)S(1)} collective-permute-done((bf16[4,64,128]{2,1,0:T(8,128)(2,1)S(1)}, bf16[4,64,128]{2,1,0:T(8,128)(2,1)S(1)}, u32[]{:S(2)}, u32[]{:S(2)}) %collective-permute-start.8) | collective-permute-done | bytes 65568 | tf_op jit(solution)/shard_map/ppermute | solution.py:19
  24.0 2.2 %collective-permute-done.7.refs_2_ = bf16[4,64,128]{2,1,0:T(8,128)(2,1)S(1)} collective-permute-done((bf16[4,64,128]{2,1,0:T(8,128)(2,1)S(1)}, bf16[4,64,128]{2,1,0:T(8,128)(2,1)S(1)}, u32[]{:S(2)}, u32[]{:S(2)}) %collective-permute-start.7) | collective-permute-done | bytes 65568 | tf_op jit(solution)/shard_map/ppermute | solution.py:19
  26.2 1.7 %collective-permute-done.6.refs_1_ = bf16[4,64,128]{2,1,0:T(8,128)(2,1)S(1)} collective-permute-done((bf16[4,64,128]{2,1,0:T(8,128)(2,1)S(1)}, bf16[4,64,128]{2,1,0:T(8,128)(2,1)S(1)}, u32[]{:S(2)}, u32[]{:S(2)}) %collective-permute-start.6) | collective-permute-done | bytes 65568 | tf_op jit(solution)/shard_map/ppermute | solution.py:19
  27.9 0.1 collective-permute-start.10
  28.0 0.9 %collective-permute-start.14 = (bf16[2,128,256]{2,1,0:T(8,128)(2,1)S(1)}, bf16[2,128,256]{2,1,0:T(8,128)(2,1)S(1)}, u32[]{:S(2)}, u32[]{:S(2)}) collective-permute-start(bf16[2,128,256]{2,1,0:T(8,128)(2,1)S(1)} %get-tuple-element.32.refs_4_), channel_id=1, source_target_pairs={{0,8},{8,0},{16,24},{24,16},{1,9},{9,1},{17,25},{25,17},{2,10},{10... | collective-permute-start | bytes 393224 | tf_op jit(solution)/shard_map/ppermute | solution.py:19
  28.9 1.0 %shard_map.97.refs_5_ = f32[4,64,128]{2,1,0:T(8,128)S(1)} custom-call(s32[4,1,128]{2,1,0:T(1,128)S(1)} %get-tuple-element.28.index, bf16[6,128,128]{2,1,0:T(8,128)(2,1)S(1)} %bitcast.6, bf16[6,128,128]{2,1,0:T(8,128)(2,1)S(1)} %collective-permute-done.3.refs_4_.refs_1_, bf16[6,128,128]{2,1,0:T(8,128)(2,1)S(1)} %collective-permute-done.4.refs_5_.refs_2_, ...), custom_call_target="tpu_custom_call" | custom-call | flops 25165824 | bytes 655360 | tf_op jit(solution)/shard_map/pallas_call | solution.py:252
  29.9 0.0 copy-start.6
  29.9 0.9 %shard_map.98.refs_0_ = bf16[4,64,128]{2,1,0:T(8,128)(2,1)S(1)} custom-call(s32[4,1,128]{2,1,0:T(1,128)S(1)} %get-tuple-element.28.index, bf16[6,128,128]{2,1,0:T(8,128)(2,1)S(1)} %bitcast.7, bf16[6,128,128]{2,1,0:T(8,128)(2,1)S(1)} %collective-permute-done.3.refs_4_.refs_1_, bf16[6,128,128]{2,1,0:T(8,128)(2,1)S(1)} %collective-permute-done.4.refs_5_.refs_2_, ...), custom_call_target="tpu_custom_call" | custom-call | flops 25165824 | bytes 655360 | tf_op jit(solution)/shard_map/pallas_call | solution.py:260
  30.9 1.2 %collective-permute-start.13 = (bf16[4,64,128]{2,1,0:T(8,128)(2,1)S(1)}, bf16[4,64,128]{2,1,0:T(8,128)(2,1)S(1)}, u32[]{:S(2)}, u32[]{:S(2)}) collective-permute-start(bf16[4,64,128]{2,1,0:T(8,128)(2,1)S(1)} %shard_map.98.refs_0_), channel_id=1, source_target_pairs={{0,24},{8,16},{16,8},{24,0},{1,25},{9,17},{17,9},{25,1},{2,26},{10... | collective-permute-start | bytes 196616 | tf_op jit(solution)/shard_map/ppermute | solution.py:19
  32.1 1.5 %collective-permute-start.12 = (bf16[4,64,128]{2,1,0:T(8,128)(2,1)S(1)}, bf16[4,64,128]{2,1,0:T(8,128)(2,1)S(1)}, u32[]{:S(2)}, u32[]{:S(2)}) collective-permute-start(bf16[4,64,128]{2,1,0:T(8,128)(2,1)S(1)} %shard_map.98.refs_0_), channel_id=1, source_target_pairs={{0,16},{8,24},{16,0},{24,8},{1,17},{9,25},{17,1},{25,9},{2,18},{10... | collective-permute-start | bytes 196616 | tf_op jit(solution)/shard_map/ppermute | solution.py:19
  33.6 1.8 %collective-permute-start.11 = (bf16[4,64,128]{2,1,0:T(8,128)(2,1)S(1)}, bf16[4,64,128]{2,1,0:T(8,128)(2,1)S(1)}, u32[]{:S(2)}, u32[]{:S(2)}) collective-permute-start(bf16[4,64,128]{2,1,0:T(8,128)(2,1)S(1)} %shard_map.98.refs_0_), channel_id=1, source_target_pairs={{0,8},{8,0},{16,24},{24,16},{1,9},{9,1},{17,25},{25,17},{2,10},{10... | collective-permute-start | bytes 196616 | tf_op jit(solution)/shard_map/ppermute | solution.py:19
  35.3 2.4 %collective-permute-done.13.refs_3_ = bf16[4,64,128]{2,1,0:T(8,128)(2,1)S(1)} collective-permute-done((bf16[4,64,128]{2,1,0:T(8,128)(2,1)S(1)}, bf16[4,64,128]{2,1,0:T(8,128)(2,1)S(1)}, u32[]{:S(2)}, u32[]{:S(2)}) %collective-permute-start.13) | collective-permute-done | bytes 65568 | tf_op jit(solution)/shard_map/ppermute | solution.py:19
  37.7 2.3 %collective-permute-done.12.refs_2_ = bf16[4,64,128]{2,1,0:T(8,128)(2,1)S(1)} collective-permute-done((bf16[4,64,128]{2,1,0:T(8,128)(2,1)S(1)}, bf16[4,64,128]{2,1,0:T(8,128)(2,1)S(1)}, u32[]{:S(2)}, u32[]{:S(2)}) %collective-permute-start.12) | collective-permute-done | bytes 65568 | tf_op jit(solution)/shard_map/ppermute | solution.py:19
  40.0 0.9 %shard_map.99 = (bf16[128,256]{1,0:T(8,128)(2,1)S(1)}, bf16[4,128,256]{2,1,0:T(8,128)(2,1)S(1)}, bf16[2,128,256]{2,1,0:T(8,128)(2,1)S(1)}) custom-call(bf16[4,64,128]{2,1,0:T(8,128)(2,1)S(1)} %shard_map.98.refs_0_, bf16[4,64,128]{2,1,0:T(8,128)(2,1)S(1)} %collective-permute-done.11.refs_1_, bf16[4,64,128]{2,1,0:T(8,128)(2,1)S(1)} %collective-permute-done.12.refs_2_, ...), custom_call_target="tpu_custom_call" | custom-call | flops 201326592 | bytes 1310720 | tf_op jit(solution)/shard_map/pallas_call | solution.py:269
  40.9 1.3 %shard_map.101 = bf16[5,128,256]{2,1,0:T(8,128)(2,1)S(1)} custom-call(s32[4,1,128]{2,1,0:T(1,128)S(1)} %get-tuple-element.28.index, bf16[6,128,128]{2,1,0:T(8,128)(2,1)S(1)} %bitcast.8, bf16[6,128,128]{2,1,0:T(8,128)(2,1)S(1)} %collective-permute-done.3.refs_4_.refs_1_, bf16[6,128,128]{2,1,0:T(8,128)(2,1)S(1)} %collective-permute-done.4.refs_5_.refs_2_, ...), custom_call_target="tpu_custom_call" | custom-call | flops 25165824 | bytes 655360 | tf_op jit(solution)/shard_map/pallas_call | solution.py:286
  42.2 0.1 collective-permute-start.15
  42.3 1.1 %shard_map.100.keep = f32[4,128,256]{2,1,0:T(8,128)S(1)} custom-call(s32[4,1,128]{2,1,0:T(1,128)S(1)} %get-tuple-element.28.index, bf16[6,128,128]{2,1,0:T(8,128)(2,1)S(1)} %bitcast.9, bf16[6,128,128]{2,1,0:T(8,128)(2,1)S(1)} %collective-permute-done.3.refs_4_.refs_1_, bf16[6,128,128]{2,1,0:T(8,128)(2,1)S(1)} %collective-permute-done.4.refs_5_.refs_2_, ...), custom_call_target="tpu_custom_call" | custom-call | flops 25165824 | bytes 655360 | tf_op jit(solution)/shard_map/pallas_call | solution.py:294
  43.4 0.5 collective-permute-done.15.arrived
  43.9 0.1 shard_map.102
  44.0 0.9 %collective-permute-start.16 = (bf16[256,256]{1,0:T(8,128)(2,1)S(1)}, bf16[256,256]{1,0:T(8,128)(2,1)S(1)}, u32[]{:S(2)}, u32[]{:S(2)}) collective-permute-start(bf16[256,256]{1,0:T(8,128)(2,1)S(1)} %get-tuple-element.37), channel_id=1, source_target_pairs={{0,6},{1,7},{2,4},{3,5},{4,2},{5,3},{6,0},{7,1},{8,14},{9,15},{10,... | collective-permute-start | bytes 393224 | tf_op jit(solution)/shard_map/ppermute | solution.py:19
  44.9 1.4 %collective-permute-start.17 = (bf16[256,256]{1,0:T(8,128)(2,1)S(1)}, bf16[256,256]{1,0:T(8,128)(2,1)S(1)}, u32[]{:S(2)}, u32[]{:S(2)}) collective-permute-start(bf16[256,256]{1,0:T(8,128)(2,1)S(1)} %get-tuple-element.38), channel_id=1, source_target_pairs={{0,4},{1,5},{2,6},{3,7},{4,0},{5,1},{6,2},{7,3},{8,12},{9,13},{10,... | collective-permute-start | bytes 393224 | tf_op jit(solution)/shard_map/ppermute | solution.py:19
  46.3 1.3 %collective-permute-start.18 = (bf16[256,256]{1,0:T(8,128)(2,1)S(1)}, bf16[256,256]{1,0:T(8,128)(2,1)S(1)}, u32[]{:S(2)}, u32[]{:S(2)}) collective-permute-start(bf16[256,256]{1,0:T(8,128)(2,1)S(1)} %get-tuple-element.39), channel_id=1, source_target_pairs={{0,2},{1,3},{2,0},{3,1},{4,6},{5,7},{6,4},{7,5},{8,10},{9,11},{10,... | collective-permute-start | bytes 393224 | tf_op jit(solution)/shard_map/ppermute | solution.py:19
  47.6 3.8 %collective-permute-done.16.refs_0_ = bf16[256,256]{1,0:T(8,128)(2,1)S(1)} collective-permute-done((bf16[256,256]{1,0:T(8,128)(2,1)S(1)}, bf16[256,256]{1,0:T(8,128)(2,1)S(1)}, u32[]{:S(2)}, u32[]{:S(2)}) %collective-permute-start.16) | collective-permute-done | bytes 131104 | tf_op jit(solution)/shard_map/ppermute | solution.py:19
  51.4 1.8 %collective-permute-done.17.refs_1_ = bf16[256,256]{1,0:T(8,128)(2,1)S(1)} collective-permute-done((bf16[256,256]{1,0:T(8,128)(2,1)S(1)}, bf16[256,256]{1,0:T(8,128)(2,1)S(1)}, u32[]{:S(2)}, u32[]{:S(2)}) %collective-permute-start.17) | collective-permute-done | bytes 131104 | tf_op jit(solution)/shard_map/ppermute | solution.py:19
  53.2 0.1 shard_map.103
  53.3 0.1 collective-permute-start.19
  53.3 0.7 %shard_map.104 = (f32[128,256]{1,0:T(8,128)}, bf16[128,256]{1,0:T(8,128)(2,1)}) custom-call(f32[128,256]{1,0:T(8,128)S(1)} %get-tuple-element.40.grads, bf16[128,256]{1,0:T(8,128)(2,1)S(1)} %get-tuple-element.41.rows), custom_call_target="tpu_custom_call" | custom-call | bytes 393216 | tf_op jit(solution)/shard_map/pallas_call | solution.py:315
  54.0 0.6 %collective-permute-done.19.arrived = f32[128,256]{1,0:T(8,128)S(1)} collective-permute-done((f32[128,256]{1,0:T(8,128)S(1)}, f32[128,256]{1,0:T(8,128)S(1)}, u32[]{:S(2)}, u32[]{:S(2)}) %collective-permute-start.19) | collective-permute-done | bytes 131104 | tf_op jit(solution)/shard_map/ppermute | solution.py:19
  54.7 0.7 %shard_map.105 = f32[256,256]{1,0:T(8,128)} custom-call(f32[128,256]{1,0:T(8,128)S(1)} %get-tuple-element.43.mine, f32[128,256]{1,0:T(8,128)S(1)} %collective-permute-done.19.arrived), custom_call_target="tpu_custom_call" | custom-call | bytes 524288 | tf_op jit(solution)/shard_map/pallas_call | solution.py:321
  (18 shorter events, 0.1 us)
Async XLA Ops:
  0.6 15.9 %collective-permute-start.4 = (bf16[6,128,128]{2,1,0:T(8,128)(2,1)}, bf16[6,128,128]{2,1,0:T(8,128)(2,1)S(1)}, u32[]{:S(2)}, u32[]{:S(2)}) collective-permute-start(bf16[6,128,128]{2,1,0:T(8,128)(2,1)} %bitcast.4), channel_id=1, source_target_pairs={{0,16},{8,24},{16,0},{24,8},{1,17},{9,25},{17,1},{25,9},{2,18},{10... | collective-permute-start | bytes 589832 | tf_op jit(solution)/shard_map/ppermute | solution.py:19
  4.7 11.8 %collective-permute-start.3 = (bf16[6,128,128]{2,1,0:T(8,128)(2,1)}, bf16[6,128,128]{2,1,0:T(8,128)(2,1)S(1)}, u32[]{:S(2)}, u32[]{:S(2)}) collective-permute-start(bf16[6,128,128]{2,1,0:T(8,128)(2,1)} %bitcast.5), channel_id=1, source_target_pairs={{0,8},{8,0},{16,24},{24,16},{1,9},{9,1},{17,25},{25,17},{2,10},{10... | collective-permute-start | bytes 589832 | tf_op jit(solution)/shard_map/ppermute | solution.py:19
  6.3 0.7 %copy-start.4 = (s32[1,1,2,3]{3,2,1,0:T(2,128)S(1)}, s32[1,1,2,3]{3,2,1,0:T(2,128)}, u32[]{:S(2)}) copy-start(s32[1,1,2,3]{3,2,1,0:T(2,128)} %param.12) | copy-start | bytes 76
  6.3 0.7 %copy-start.3 = (s32[1,1,2,3]{3,2,1,0:T(2,128)S(1)}, s32[1,1,2,3]{3,2,1,0:T(2,128)}, u32[]{:S(2)}) copy-start(s32[1,1,2,3]{3,2,1,0:T(2,128)} %param.11) | copy-start | bytes 76
  6.3 0.7 %copy-start.5 = (s32[1,1,2]{2,1,0:T(1,128)S(1)}, s32[1,1,2]{2,1,0:T(1,128)}, u32[]{:S(2)}) copy-start(s32[1,1,2]{2,1,0:T(1,128)} %param.13) | copy-start | bytes 28
  7.0 0.8 %copy-start.2 = (bf16[128,256]{1,0:T(8,128)(2,1)S(1)}, bf16[128,256]{1,0:T(8,128)(2,1)}, u32[]{:S(2)}) copy-start(bf16[128,256]{1,0:T(8,128)(2,1)} %feats.1) | copy-start | bytes 196612
  8.5 6.9 %collective-permute-start = (bf16[80,128]{1,0:T(8,128)(2,1)S(1)}, bf16[80,128]{1,0:T(8,128)(2,1)S(1)}, u32[]{:S(2)}, u32[]{:S(2)}) collective-permute-start(bf16[80,128]{1,0:T(8,128)(2,1)S(1)} %get-tuple-element.25), channel_id=1, source_target_pairs={{0,8},{8,0},{16,24},{24,16},{1,9},{9,1},{17,25},{25,17},{2,10},{10... | collective-permute-start | bytes 61448 | tf_op jit(solution)/shard_map/ppermute | solution.py:19
  9.0 6.4 %collective-permute-start.1 = (bf16[80,128]{1,0:T(8,128)(2,1)S(1)}, bf16[80,128]{1,0:T(8,128)(2,1)S(1)}, u32[]{:S(2)}, u32[]{:S(2)}) collective-permute-start(bf16[80,128]{1,0:T(8,128)(2,1)S(1)} %get-tuple-element.26), channel_id=1, source_target_pairs={{0,16},{8,24},{16,0},{24,8},{1,17},{9,25},{17,1},{25,9},{2,18},{10... | collective-permute-start | bytes 61448 | tf_op jit(solution)/shard_map/ppermute | solution.py:19
  9.1 7.4 %collective-permute-start.2 = (bf16[80,128]{1,0:T(8,128)(2,1)S(1)}, bf16[80,128]{1,0:T(8,128)(2,1)S(1)}, u32[]{:S(2)}, u32[]{:S(2)}) collective-permute-start(bf16[80,128]{1,0:T(8,128)(2,1)S(1)} %get-tuple-element.27), channel_id=1, source_target_pairs={{0,24},{8,16},{16,8},{24,0},{1,25},{9,17},{17,9},{25,1},{2,26},{10... | collective-permute-start | bytes 61448 | tf_op jit(solution)/shard_map/ppermute | solution.py:19
  16.5 0.8 %copy-start.1 = (bf16[128,256]{1,0:T(8,128)(2,1)S(1)}, bf16[128,256]{1,0:T(8,128)(2,1)}, u32[]{:S(2)}) copy-start(bf16[128,256]{1,0:T(8,128)(2,1)} %refs_4_.1) | copy-start | bytes 196612
  16.5 11.4 %collective-permute-start.5 = (bf16[6,128,128]{2,1,0:T(8,128)(2,1)S(1)}, bf16[6,128,128]{2,1,0:T(8,128)(2,1)S(1)}, u32[]{:S(2)}, u32[]{:S(2)}) collective-permute-start(bf16[6,128,128]{2,1,0:T(8,128)(2,1)S(1)} %get-tuple-element.29), channel_id=1, source_target_pairs={{0,8},{8,0},{16,24},{24,16},{1,9},{9,1},{17,25},{25,17},{2,10},{10... | collective-permute-start | bytes 589832 | tf_op jit(solution)/shard_map/ppermute | solution.py:19
  17.3 5.9 %collective-permute-start.9 = (bf16[128,256]{1,0:T(8,128)(2,1)S(1)}, bf16[128,256]{1,0:T(8,128)(2,1)S(1)}, u32[]{:S(2)}, u32[]{:S(2)}) collective-permute-start(bf16[128,256]{1,0:T(8,128)(2,1)S(1)} %copy-done.1), channel_id=1, source_target_pairs={{0,16},{8,24},{16,0},{24,8},{1,17},{9,25},{17,1},{25,9},{2,18},{10... | collective-permute-start | bytes 196616 | tf_op jit(solution)/shard_map/ppermute | solution.py:19
  19.7 9.2 %copy-start = (bf16[1,1,2,3,128,128]{5,4,3,2,1,0:T(8,128)(2,1)S(1)}, bf16[1,1,2,3,128,128]{5,4,3,2,1,0:T(8,128)(2,1)}, u32[]{:S(2)}) copy-start(bf16[1,1,2,3,128,128]{5,4,3,2,1,0:T(8,128)(2,1)} %param.10) | copy-start | bytes 589828
  19.7 4.3 %collective-permute-start.8 = (bf16[4,64,128]{2,1,0:T(8,128)(2,1)S(1)}, bf16[4,64,128]{2,1,0:T(8,128)(2,1)S(1)}, u32[]{:S(2)}, u32[]{:S(2)}) collective-permute-start(bf16[4,64,128]{2,1,0:T(8,128)(2,1)S(1)} %get-tuple-element.30.refs_0_), channel_id=1, source_target_pairs={{0,2},{1,3},{2,0},{3,1},{4,6},{5,7},{6,4},{7,5},{8,10},{9,11},{10,... | collective-permute-start | bytes 196616 | tf_op jit(solution)/shard_map/ppermute | solution.py:19
  21.2 5.0 %collective-permute-start.7 = (bf16[4,64,128]{2,1,0:T(8,128)(2,1)S(1)}, bf16[4,64,128]{2,1,0:T(8,128)(2,1)S(1)}, u32[]{:S(2)}, u32[]{:S(2)}) collective-permute-start(bf16[4,64,128]{2,1,0:T(8,128)(2,1)S(1)} %get-tuple-element.30.refs_0_), channel_id=1, source_target_pairs={{0,4},{1,5},{2,6},{3,7},{4,0},{5,1},{6,2},{7,3},{8,12},{9,13},{10,... | collective-permute-start | bytes 196616 | tf_op jit(solution)/shard_map/ppermute | solution.py:19
  22.7 5.2 %collective-permute-start.6 = (bf16[4,64,128]{2,1,0:T(8,128)(2,1)S(1)}, bf16[4,64,128]{2,1,0:T(8,128)(2,1)S(1)}, u32[]{:S(2)}, u32[]{:S(2)}) collective-permute-start(bf16[4,64,128]{2,1,0:T(8,128)(2,1)S(1)} %get-tuple-element.30.refs_0_), channel_id=1, source_target_pairs={{0,6},{1,7},{2,4},{3,5},{4,2},{5,3},{6,0},{7,1},{8,14},{9,15},{10,... | collective-permute-start | bytes 196616 | tf_op jit(solution)/shard_map/ppermute | solution.py:19
  27.9 2.0 %collective-permute-start.10 = (bf16[4,4,64,128]{3,2,1,0:T(8,128)(2,1)S(1)}, bf16[4,4,64,128]{3,2,1,0:T(8,128)(2,1)S(1)}, u32[]{:S(2)}, u32[]{:S(2)}) collective-permute-start(bf16[4,4,64,128]{3,2,1,0:T(8,128)(2,1)S(1)} %get-tuple-element.31.refs_4_), channel_id=1, source_target_pairs={{0,1},{1,0},{2,3},{3,2},{4,5},{5,4},{6,7},{7,6},{8,9},{9,8},{10,11... | collective-permute-start | bytes 786440 | tf_op jit(solution)/shard_map/ppermute | solution.py:19
  28.0 7.3 %collective-permute-start.14 = (bf16[2,128,256]{2,1,0:T(8,128)(2,1)S(1)}, bf16[2,128,256]{2,1,0:T(8,128)(2,1)S(1)}, u32[]{:S(2)}, u32[]{:S(2)}) collective-permute-start(bf16[2,128,256]{2,1,0:T(8,128)(2,1)S(1)} %get-tuple-element.32.refs_4_), channel_id=1, source_target_pairs={{0,8},{8,0},{16,24},{24,16},{1,9},{9,1},{17,25},{25,17},{2,10},{10... | collective-permute-start | bytes 393224 | tf_op jit(solution)/shard_map/ppermute | solution.py:19
  29.9 10.1 %copy-start.6 = (bf16[256,256]{1,0:T(8,128)(2,1)S(1)}, bf16[256,256]{1,0:T(8,128)(2,1)}, u32[]{:S(2)}) copy-start(bf16[256,256]{1,0:T(8,128)(2,1)} %refs_6_.1) | copy-start | bytes 393220
  30.9 6.8 %collective-permute-start.13 = (bf16[4,64,128]{2,1,0:T(8,128)(2,1)S(1)}, bf16[4,64,128]{2,1,0:T(8,128)(2,1)S(1)}, u32[]{:S(2)}, u32[]{:S(2)}) collective-permute-start(bf16[4,64,128]{2,1,0:T(8,128)(2,1)S(1)} %shard_map.98.refs_0_), channel_id=1, source_target_pairs={{0,24},{8,16},{16,8},{24,0},{1,25},{9,17},{17,9},{25,1},{2,26},{10... | collective-permute-start | bytes 196616 | tf_op jit(solution)/shard_map/ppermute | solution.py:19
  32.1 8.0 %collective-permute-start.12 = (bf16[4,64,128]{2,1,0:T(8,128)(2,1)S(1)}, bf16[4,64,128]{2,1,0:T(8,128)(2,1)S(1)}, u32[]{:S(2)}, u32[]{:S(2)}) collective-permute-start(bf16[4,64,128]{2,1,0:T(8,128)(2,1)S(1)} %shard_map.98.refs_0_), channel_id=1, source_target_pairs={{0,16},{8,24},{16,0},{24,8},{1,17},{9,25},{17,1},{25,9},{2,18},{10... | collective-permute-start | bytes 196616 | tf_op jit(solution)/shard_map/ppermute | solution.py:19
  33.6 6.5 %collective-permute-start.11 = (bf16[4,64,128]{2,1,0:T(8,128)(2,1)S(1)}, bf16[4,64,128]{2,1,0:T(8,128)(2,1)S(1)}, u32[]{:S(2)}, u32[]{:S(2)}) collective-permute-start(bf16[4,64,128]{2,1,0:T(8,128)(2,1)S(1)} %shard_map.98.refs_0_), channel_id=1, source_target_pairs={{0,8},{8,0},{16,24},{24,16},{1,9},{9,1},{17,25},{25,17},{2,10},{10... | collective-permute-start | bytes 196616 | tf_op jit(solution)/shard_map/ppermute | solution.py:19
  42.2 1.7 %collective-permute-start.15 = (bf16[5,128,256]{2,1,0:T(8,128)(2,1)S(1)}, bf16[5,128,256]{2,1,0:T(8,128)(2,1)S(1)}, u32[]{:S(2)}, u32[]{:S(2)}) collective-permute-start(bf16[5,128,256]{2,1,0:T(8,128)(2,1)S(1)} %shard_map.101), channel_id=1, source_target_pairs={{0,1},{1,0},{2,3},{3,2},{4,5},{5,4},{6,7},{7,6},{8,9},{9,8},{10,11... | collective-permute-start | bytes 983048 | tf_op jit(solution)/shard_map/ppermute | solution.py:19
  44.0 7.3 %collective-permute-start.16 = (bf16[256,256]{1,0:T(8,128)(2,1)S(1)}, bf16[256,256]{1,0:T(8,128)(2,1)S(1)}, u32[]{:S(2)}, u32[]{:S(2)}) collective-permute-start(bf16[256,256]{1,0:T(8,128)(2,1)S(1)} %get-tuple-element.37), channel_id=1, source_target_pairs={{0,6},{1,7},{2,4},{3,5},{4,2},{5,3},{6,0},{7,1},{8,14},{9,15},{10,... | collective-permute-start | bytes 393224 | tf_op jit(solution)/shard_map/ppermute | solution.py:19
  44.9 8.3 %collective-permute-start.17 = (bf16[256,256]{1,0:T(8,128)(2,1)S(1)}, bf16[256,256]{1,0:T(8,128)(2,1)S(1)}, u32[]{:S(2)}, u32[]{:S(2)}) collective-permute-start(bf16[256,256]{1,0:T(8,128)(2,1)S(1)} %get-tuple-element.38), channel_id=1, source_target_pairs={{0,4},{1,5},{2,6},{3,7},{4,0},{5,1},{6,2},{7,3},{8,12},{9,13},{10,... | collective-permute-start | bytes 393224 | tf_op jit(solution)/shard_map/ppermute | solution.py:19
  46.3 6.9 %collective-permute-start.18 = (bf16[256,256]{1,0:T(8,128)(2,1)S(1)}, bf16[256,256]{1,0:T(8,128)(2,1)S(1)}, u32[]{:S(2)}, u32[]{:S(2)}) collective-permute-start(bf16[256,256]{1,0:T(8,128)(2,1)S(1)} %get-tuple-element.39), channel_id=1, source_target_pairs={{0,2},{1,3},{2,0},{3,1},{4,6},{5,7},{6,4},{7,5},{8,10},{9,11},{10,... | collective-permute-start | bytes 393224 | tf_op jit(solution)/shard_map/ppermute | solution.py:19
  53.3 1.4 %collective-permute-start.19 = (f32[128,256]{1,0:T(8,128)S(1)}, f32[128,256]{1,0:T(8,128)S(1)}, u32[]{:S(2)}, u32[]{:S(2)}) collective-permute-start(f32[128,256]{1,0:T(8,128)S(1)} %get-tuple-element.43.mine), channel_id=1, source_target_pairs={{0,1},{1,0},{2,3},{3,2},{4,5},{5,4},{6,7},{7,6},{8,9},{9,8},{10,11... | collective-permute-start | bytes 393224 | tf_op jit(solution)/shard_map/ppermute | solution.py:19
